TPU v7x, 256 devices: a whole 4x4x8 slice. The times are simulated.
256 devices in a mesh: row: 16 (over y_hi, x, core), col: 16 (over z, y_lo).
Axes of the slice: x: 4, y: 4 (y_hi: 2, y_lo: 2; y = y_hi * 2 + y_lo), z: 8, core: 2. Of those that a mesh axis runs over, the one named last changes fastest.
Arguments:
- homolog_features: bfloat16 [64, 4096, 256], P('row', 'col'), may hold values from -6 to 6
- presence_indicator: int32 [64, 4096], P('row', 'col'), may hold values from 0 to 1
- polymer_label: int32 [4096], P('col'), may hold values from 0 to 3, as said below
- lowering_matrix: bfloat16 [256, 64], replicated, may hold values from -0.375 to 0.375
- lowering_offset: float32 [64], replicated, may hold values from -3 to 3
- outgoing_matrix: bfloat16 [1024, 128], replicated, may hold values from -0.1875 to 0.1875
- outgoing_offset: float32 [128], replicated, may hold values from -4 to 4
- update_adjoint: bfloat16 [256, 4096, 128], P('row', 'col'), may hold values from -6 to 6
Outputs:
- pair_increment: bfloat16 [256, 4096, 128], P('row', 'col')
- alignment_gradient: bfloat16 [64, 4096, 256], P('row', 'col')
- projector_weight_gradient: float32 [256, 64], replicated
- projector_bias_gradient: float32 [64], replicated
- out_weight_grad: float32 [1024, 128], replicated
- out_bias_grad: float32 [128], replicated
Inputs may be any that keep to these rules, and one draw needn't show every extreme that they name: `polymer_label`: never falls along the residues: each chain is one contiguous run.
All inputs are finite; a program needn't handle non-finite values.
Results may differ from a plain program's by a relative error of at most 0.0077.
Values may be sent and summed in bfloat16 or wider, within the bound.
No kernel may reach another device: no remote copies, remote signals or barrier semaphores. Data moves between devices by JAX's collectives and lax.ppermute only.
A program may use at most 64 MiB of HBM per device.

v0:
```python
import jax
import jax.numpy as jnp
from jax import lax
from jax.sharding import PartitionSpec as P

PAIRED = 16
CHAINS = 4


def broadcast(block, axis, source):
    block = jnp.where(lax.axis_index(axis) == source, block, jnp.zeros_like(block))
    return lax.psum(block, axis)


def layer_normalize(values):
    center = values - jnp.mean(values, axis=-1, keepdims=True)
    spread = jnp.mean(center * center, axis=-1, keepdims=True)
    return center * lax.rsqrt(spread + 1e-05)


def per_device(
    homolog_features,
    presence_indicator,
    polymer_label,
    lowering_matrix,
    lowering_offset,
    outgoing_matrix,
    outgoing_offset,
    update_adjoint,
):
    homolog_portion = homolog_features.shape[0]
    position_portion = homolog_features.shape[1]
    hidden = lowering_matrix.shape[1] // 2
    channels = outgoing_matrix.shape[1]
    row_dev = update_adjoint.shape[0]
    row_index = lax.axis_index("row")
    col_index = lax.axis_index("col")
    presence_real = homolog_features.astype(jnp.float32)
    normalized_alignment = layer_normalize(presence_real).astype(jnp.bfloat16)
    seq_index = row_index * homolog_portion + jnp.arange(homolog_portion, dtype=jnp.int32)
    seq_chain = (seq_index - PAIRED) % CHAINS
    permitted_pairs = (seq_index[:, None] < PAIRED) | (seq_chain[:, None] == polymer_label[None, :])
    active_mask = jnp.where(permitted_pairs & (presence_indicator == 1), 1.0, 0.0).astype(
        jnp.float32
    )
    projected = (
        jnp.einsum(
            "src,ch->shr", normalized_alignment, lowering_matrix, preferred_element_type=jnp.float32
        )
        + lowering_offset[None, :, None]
    )
    proj_pair = (projected * active_mask[:, None, :]).astype(jnp.bfloat16)
    gathered, mask_whole = (
        lax.all_gather(proj_pair, "row", axis=0, tiled=True),
        lax.all_gather(active_mask.astype(jnp.bfloat16), "row", axis=0, tiled=True),
    )
    seq_total = gathered.shape[0]
    holder = row_index * row_dev // position_portion
    offset = jnp.clip(
        row_index * row_dev - col_index * position_portion, 0, position_portion - row_dev
    )
    left_piece = lax.dynamic_slice_in_dim(gathered[:, :hidden, :], offset, row_dev, 2)
    mask_piece = lax.dynamic_slice_in_dim(mask_whole, offset, row_dev, 1)
    left_rows, mask_rows = (
        broadcast(left_piece, "col", holder),
        broadcast(mask_piece, "col", holder),
    )
    right_cols = gathered[:, hidden:, :]
    counts = jnp.dot(mask_rows.T, mask_whole, preferred_element_type=jnp.float32)
    divisor = jnp.maximum(counts, 1.0)
    out_tensor = outgoing_matrix.reshape(hidden, hidden, channels)

    def block_step(carry, block_index):
        right_grad, weight_gradient, bias_gradient = carry
        start = block_index * 8
        left_block = lax.dynamic_slice_in_dim(left_rows, start, 8, 2)
        div_block = lax.dynamic_slice_in_dim(divisor, start, 8, 0)[..., None]
        grad_block = lax.dynamic_slice_in_dim(update_adjoint, start, 8, 0)
        outer = jnp.einsum(
            "sci,sej->icej", left_block, right_cols, preferred_element_type=jnp.float32
        ).astype(jnp.bfloat16)
        before = (
            jnp.einsum("icej,ceo->ijo", outer, out_tensor, preferred_element_type=jnp.float32)
            + outgoing_offset
        )
        pair_block = (before / div_block).astype(jnp.bfloat16)
        scaled = (grad_block.astype(jnp.float32) / div_block).astype(jnp.bfloat16)
        bias_gradient = bias_gradient + jnp.sum(scaled.astype(jnp.float32), axis=(0, 1))
        weight_gradient = weight_gradient + jnp.einsum(
            "icej,ijo->ceo", outer, scaled, preferred_element_type=jnp.float32
        )
        outer_grad = jnp.einsum(
            "ijo,ceo->icej", scaled, out_tensor, preferred_element_type=jnp.float32
        ).astype(jnp.bfloat16)
        left_grad = jnp.einsum(
            "icej,sej->sci", outer_grad, right_cols, preferred_element_type=jnp.float32
        )
        right_grad = right_grad + jnp.einsum(
            "icej,sci->sej", outer_grad, left_block, preferred_element_type=jnp.float32
        )
        return ((right_grad, weight_gradient, bias_gradient), (pair_block, left_grad))

    initial = (
        jnp.zeros((seq_total, hidden, position_portion), jnp.float32),
        jnp.zeros((hidden, hidden, channels), jnp.float32),
        jnp.zeros((channels,), jnp.float32),
    )
    (right_grad, weight_gradient, bias_gradient), (pair_blocks, left_blocks) = lax.scan(
        block_step, initial, jnp.arange(row_dev // 8, dtype=jnp.int32)
    )
    pair_increment = pair_blocks.reshape(row_dev, position_portion, channels)
    left_grad = jnp.transpose(left_blocks, (1, 2, 0, 3)).reshape(seq_total, hidden, row_dev)
    left_total = lax.psum(left_grad, "col")
    placed = lax.dynamic_update_slice_in_dim(jnp.zeros_like(right_grad), left_total, offset, 2)
    placed = jnp.where(col_index == holder, placed, 0.0)
    left_local, right_local = (
        lax.psum_scatter(placed, "row", scatter_dimension=0, tiled=True),
        lax.psum_scatter(right_grad, "row", scatter_dimension=0, tiled=True),
    )
    both = jnp.concatenate([left_local, right_local], axis=1)
    proj_grad = (both * active_mask[:, None, :]).astype(jnp.bfloat16)
    projector_weight_gradient = jnp.einsum(
        "src,shr->ch", normalized_alignment, proj_grad, preferred_element_type=jnp.float32
    )
    projector_bias_gradient = jnp.sum(proj_grad.astype(jnp.float32), axis=(0, 2))
    normalized_gradient = jnp.einsum(
        "shr,ch->src", proj_grad, lowering_matrix, preferred_element_type=jnp.float32
    )
    discarded_value, backward_function = jax.vjp(layer_normalize, presence_real)
    alignment_gradient = backward_function(normalized_gradient)[0].astype(jnp.bfloat16)
    grand_totals = lax.psum(
        (
            projector_weight_gradient,
            projector_bias_gradient,
            weight_gradient.reshape(hidden * hidden, channels),
            bias_gradient,
        ),
        ("row", "col"),
    )
    return (
        pair_increment,
        alignment_gradient,
        grand_totals[0],
        grand_totals[1],
        grand_totals[2],
        grand_totals[3],
    )


def solution(mesh):
    in_specs = (
        P("row", "col", None),
        P("row", "col"),
        P("col"),
        P(),
        P(),
        P(),
        P(),
        P("row", "col", None),
    )
    out_specs = (P("row", "col", None), P("row", "col", None), P(), P(), P(), P())
    return jax.shard_map(
        per_device, mesh=mesh, in_specs=in_specs, out_specs=out_specs, check_vma=False
    )
```

profile of v0, /device:TPU:1, one launch (start us, length us, event | category | flops | bytes accessed | tf_op | source)
XLA Modules:
  0.0 836.4 jit_solution(14909911531324635415)
XLA Ops:
  7.3 1.2 copy.50
  9.6 1.6 fusion.51
  11.2 25.7 %all-gather = bf16[16,4,256]{2,1,0:T(4,128)(2,1)S(1)} all-gather(bf16[1,4,256]{2,1,0:T(4,128)(2,1)S(1)} %get-tuple-element.213), channel_id=1, replica_groups=mesh['row'=16,'col'=16] {'row'}, dimensions={0}, use_global_device_ids=true | all-gather | bytes 34816 | tf_op jit(solution)/shard_map/all_gather | solution.py:55
  37.1 52.3 %psum.50 = bf16[64,16]{1,0:T(8,128)(2,1)S(1)} all-reduce(bf16[64,16]{1,0:T(8,128)(2,1)S(1)} %dynamic-slice_select_fusion), channel_id=1, replica_groups=mesh['row'=16,'col'=16] {'col'}, use_global_device_ids=true, to_apply=%region_3.4 | all-reduce | flops 1024 | bytes 4096 | tf_op jit(solution)/shard_map/psum | solution.py:12
  89.4 2.7 fusion.66
  93.9 1.8 copy.54
  95.7 129.9 %all-reduce.6.cloned.1.call-done = bf16[64,32,16]{0,2,1:T(8,128)(2,1)} async-done(((bf16[64,32,16]{0,2,1:T(8,128)(2,1)}), bf16[64,32,16]{0,2,1:T(8,128)(2,1)}) %all-reduce.6.cloned.1.call-update) | async-done | bytes 65552 | tf_op jit(solution)/shard_map/psum | solution.py:12
  225.6 34.4 %while.19 = (s32[]{:T(128)}, f32[64,32,256]{2,0,1:T(8,128)S(1)}, f32[32,32,128]{2,1,0:T(8,128)}, f32[128]{0:T(128)S(1)}, bf16[2,8,256,128]{3,2,1,0:T(8,128)(2,1)...) while((s32[]{:T(128)}, f32[64,32,256]{2,0,1:T(8,128)S(1)}, ...), condition=%wide.region_6.7_spmd.clone, body=%wide.region_4.6_spmd.clone.sunk | while | flops 2425094144 | bytes 53529516 | solution.py:108
  226.8 1.5 convert_reduce_fusion.4
  230.5 1.5 fusion.97
  232.1 1.7 fusion.99
  233.8 1.4 convert_bitcast_fusion.5
  235.2 4.5 fusion.100
  239.7 2.8 bitcast_add_fusion.2
  243.9 1.5 convert_reduce_fusion.4
  246.3 1.2 convert_bitcast_fusion.6
  247.6 1.5 fusion.97
  249.1 1.7 fusion.99
  250.9 1.4 convert_bitcast_fusion.5
  252.3 4.5 fusion.100
  256.8 2.8 bitcast_add_fusion.2
  260.7 2.6 copy.57
  263.4 133.0 %all-reduce.8.cloned.1.call-done = f32[64,32,16]{0,2,1:T(8,128)} async-done(((f32[64,32,16]{0,2,1:T(8,128)}), f32[64,32,16]{0,2,1:T(8,128)}) %all-reduce.8.cloned.1.call-update) | async-done | bytes 131088 | tf_op jit(solution)/shard_map/psum | solution.py:113
  397.4 1.8 copy.56
  399.4 12.9 %select_n.62 = f32[64,32,256]{2,1,0:T(8,128)S(1)} dynamic-update-slice(f32[64,32,256]{2,1,0:T(8,128)S(1)} %broadcast.101, f32[64,32,16]{2,1,0:T(8,128)} %copy.56, s32[]{:T(128)} %constant.40.clone.1, s32[]{:T(128)} %constant.40.clone.1, s32[]{:T(128)S(6)} %min.4) | dynamic-update-slice | bytes 262148 | tf_op jit(solution)/shard_map/jit(_where)/select_n | solution.py:115
  412.3 1.3 copy-done.3
  413.6 73.4 %reduce-scatter.5.cloned.1.call-done = f32[4,32,256]{2,1,0:T(8,128)} async-done(((f32[64,32,256]{2,1,0:T(8,128)}), f32[4,32,256]{2,1,0:T(8,128)}) %reduce-scatter.5.cloned.1.call-update) | async-done | bytes 131088 | tf_op jit(solution)/shard_map/reduce_scatter | solution.py:118
  487.1 81.8 %reduce-scatter.3.cloned.1.call-done = f32[4,32,256]{2,1,0:T(8,128)} async-done(((f32[64,32,256]{2,1,0:T(8,128)}), f32[4,32,256]{2,1,0:T(8,128)}) %reduce-scatter.3.cloned.1.call-update) | async-done | bytes 131088 | tf_op jit(solution)/shard_map/reduce_scatter | solution.py:117
  572.9 77.4 %all-reduce = (f32[64]{0:T(128)}, f32[128]{0:T(128)}) all-reduce(f32[64]{0:T(128)S(1)} %get-tuple-element.211, f32[128]{0:T(128)S(1)} %get-tuple-element.81), channel_id=1, replica_groups=mesh['row'=16,'col'=16] {'row','col'}, use_global_device_ids=true, to_apply=%region_14.15 | all-reduce | flops 192 | bytes 1536 | tf_op jit(solution)/shard_map/psum | solution.py:131
  650.2 176.0 %all-reduce.10.cloned.1.call-done = (f32[256,64]{0,1:T(8,128)}, f32[1024,128]{1,0:T(8,128)}) async-done(((f32[256,64]{0,1:T(8,128)}, f32[1024,128]{1,0:T(8,128)}), (f32[256,64]{0,1:T(8,128)}, f32[1024,128]{1,0:T(8,128)})) %all-reduce.10.cloned.1.call-update) | async-done | bytes 589840 | tf_op jit(solution)/shard_map/psum | solution.py:131
  826.2 1.5 copy.155
  827.7 1.9 copy.156
  (89 shorter events, 13.4 us)
Async XLA Ops:
  7.2 2.4 copy-start
  7.2 82.2 %all-gather.3.cloned.1.call-start = ((), (), s32[]{:S(2)}) async-start(), calls=%async_computation.2 | async-start | bytes 2228224 | tf_op jit(solution)/shard_map/all_gather | solution.py:54
  8.5 85.1 %copy-start.1 = (bf16[4,256,256]{1,2,0:T(8,128)(2,1)}, bf16[4,256,256]{1,2,0:T(8,128)(2,1)S(1)}, u32[]{:S(2)}) copy-start(bf16[4,256,256]{1,2,0:T(8,128)(2,1)S(1)} %copy.50) | copy-start | bytes 1572868
  11.2 214.4 %all-reduce.6.cloned.1.call-start = ((), (), s32[]{:S(2)}) async-start(), calls=%async_computation.3 | async-start | bytes 262144 | tf_op jit(solution)/shard_map/psum | solution.py:12
  89.4 136.2 %copy-start.9 = (f32[128]{0:T(128)S(1)}, f32[128]{0:T(128)}, u32[]{:S(2)}) copy-start(f32[128]{0:T(128)} %param.16) | copy-start | bytes 1540
  93.6 302.8 %all-reduce.8.cloned.1.call-start = ((), (), s32[]{:S(2)}) async-start(), calls=%async_computation.4 | async-start | bytes 524288 | tf_op jit(solution)/shard_map/psum | solution.py:113
  226.8 3.7 copy-start.4
  226.8 3.7 copy-start.5
  230.5 1.5 copy-start.8
  230.5 1.5 copy-start.10
  232.1 1.8 copy-start.6
  233.8 5.9 copy-start.11
  243.9 3.7 copy-start.4
  243.9 3.7 copy-start.5
  247.6 1.5 copy-start.8
  247.6 1.5 copy-start.10
  249.1 1.8 copy-start.6
  250.9 5.9 copy-start.11
  259.9 0.7 copy-start.7
  260.7 226.4 %reduce-scatter.5.cloned.1.call-start = ((), (), s32[]{:S(2)}) async-start(), calls=%async_computation.6 | async-start | bytes 2228224 | tf_op jit(solution)/shard_map/reduce_scatter | solution.py:118
  263.3 306.7 %copy-start.2 = (bf16[4,256,256]{1,2,0:T(8,128)(2,1)S(1)}, bf16[4,256,256]{1,2,0:T(8,128)(2,1)}, u32[]{:S(2)}) copy-start(bf16[4,256,256]{1,2,0:T(8,128)(2,1)} %copy-done.1) | copy-start | bytes 1572868
  263.3 305.6 %reduce-scatter.3.cloned.1.call-start = ((), (), s32[]{:S(2)}) async-start(), calls=%async_computation.5 | async-start | bytes 2228224 | tf_op jit(solution)/shard_map/reduce_scatter | solution.py:117
  412.2 1.3 copy-start.3
  413.6 412.6 %all-reduce.10.cloned.1.call-start = ((), (), s32[]{:S(2)}) async-start(), calls=%async_computation.7 | async-start | bytes 1179648 | tf_op jit(solution)/shard_map/psum | solution.py:131
Sparse Core Ops, SparseCore 0:
  11.3 58.0 all-gather.2
  93.7 131.7 all-reduce.5
  260.8 135.5 all-reduce.7
  400.5 86.5 reduce-scatter.4
  491.1 77.7 reduce-scatter.2
  575.0 251.1 all-reduce.9
where the time goes:
time: 837 us; the launch traced here: 836 us
  waiting for transfers between devices  594 us (71%)
  blocking collectives  155 us (19%)
  local copies, waits for them, and re-layouts  33.6 us (4%)
  matrix products  29.3 us (4%)
  between operations  14.3 us (2%)
    psum x1, waiting for transfers between devices, per_device(): lax.psum((projector_weight_gradient, projector_bias_gradient, weight_grad...  176 us
    psum x1, waiting for transfers between devices, per_device(): left_total = lax.psum(left_grad, 'col')  133 us
    psum x1, waiting for transfers between devices, broadcast(): return lax.psum(block, axis)  130 us
    reduce_scatter x1, waiting for transfers between devices, per_device(): lax.psum_scatter(placed, 'row', scatter_dimension=0, tiled=True)  81.8 us
    psum x1, blocking collectives, per_device(): lax.psum((projector_weight_gradient, projector_bias_gradient, weight_grad...  77.4 us
    reduce_scatter x1, waiting for transfers between devices, per_device(): lax.psum_scatter(right_grad, 'row', scatter_dimension=0, tiled=True)  73.4 us
    psum x1, blocking collectives, broadcast(): return lax.psum(block, axis)  52.3 us
    all_gather x1, blocking collectives, per_device(): lax.all_gather(active_mask.astype(jnp.bfloat16), 'row', axis=0, tiled=True)  25.7 us
  transfers between devices with their start and end apart: 6, of which 5 were waited for; matrix products, arithmetic and copies ran while one was open for 3% of the time, Pallas kernels for 0%

commit v1 on v0

v1 whole, which is shorter than its diff:
```python
import jax
import jax.numpy as jnp
from jax import lax
from jax.sharding import PartitionSpec as P

PAIRED = 16
CHAINS = 4
BF = jnp.bfloat16
F32 = jnp.float32
STEP = 4


def layer_normalize(values):
    center = values - jnp.mean(values, axis=-1, keepdims=True)
    spread = jnp.mean(center * center, axis=-1, keepdims=True)
    return center * lax.rsqrt(spread + 1e-05)


def column_spread(block, col_index, cols):
    far = [lax.ppermute(block, "col", [(0, d)]) for d in range(STEP, cols, STEP)]
    block = jnp.where(col_index == 0, block, sum(far[1:], far[0]))
    near = [
        lax.ppermute(block, "col", [(a, a + d) for a in range(0, cols, STEP)])
        for d in range(1, STEP)
    ]
    return jnp.where(col_index % STEP == 0, block, sum(near[1:], near[0]))


def column_collect(block, cols):
    sent = block.astype(BF)
    for d in range(1, STEP):
        block = block + lax.ppermute(
            sent, "col", [(a + d, a) for a in range(0, cols, STEP)]
        ).astype(F32)
    sent = block.astype(BF)
    for d in range(STEP, cols, STEP):
        block = block + lax.ppermute(sent, "col", [(d, 0)]).astype(F32)
    return block


def high_low(values):
    high = values.astype(BF)
    return high, (values - high.astype(F32)).astype(BF)


def per_device(
    homolog_features,
    presence_indicator,
    polymer_label,
    lowering_matrix,
    lowering_offset,
    outgoing_matrix,
    outgoing_offset,
    update_adjoint,
):
    seqs, places, depth = homolog_features.shape
    hidden = lowering_matrix.shape[1] // 2
    channels = outgoing_matrix.shape[1]
    row_dev = update_adjoint.shape[0]
    rows, cols = lax.axis_size("row"), lax.axis_size("col")
    row_index, col_index = lax.axis_index("row"), lax.axis_index("col")

    presence_real = homolog_features.astype(F32)
    normalized_alignment = layer_normalize(presence_real).astype(BF)
    seq_index = row_index * seqs + jnp.arange(seqs, dtype=jnp.int32)
    seq_chain = (seq_index - PAIRED) % CHAINS
    permitted_pairs = (seq_index[:, None] < PAIRED) | (seq_chain[:, None] == polymer_label[None, :])
    active_mask = jnp.where(permitted_pairs & (presence_indicator == 1), 1.0, 0.0).astype(F32)
    projected = (
        jnp.einsum("src,ch->hsr", normalized_alignment, lowering_matrix, preferred_element_type=F32)
        + lowering_offset[:, None, None]
    )
    proj_pair = (projected * active_mask[None]).astype(BF)
    live_own = active_mask.astype(BF)

    pieces = hidden * seqs
    spread = column_spread(
        jnp.concatenate([proj_pair[:hidden].reshape(pieces, places), live_own], axis=0),
        col_index,
        cols,
    )
    per_row = spread.reshape(pieces + seqs, rows, row_dev).transpose(1, 0, 2)
    left_part = per_row[:, :pieces].reshape(rows, pieces * row_dev // places, places)
    live_part = per_row[:, pieces:].reshape(rows, 1, seqs * row_dev)
    live_part = jnp.pad(live_part, ((0, 0), (0, 0), (0, places - seqs * row_dev)))
    lines = left_part.shape[1]
    packed = jnp.concatenate(
        [
            jnp.broadcast_to(proj_pair[hidden:].reshape(1, pieces, places), (rows, pieces, places)),
            left_part,
            jnp.broadcast_to(live_own[None], (rows, seqs, places)),
            live_part,
            jnp.zeros((rows, 16 - lines - seqs - 1, places), BF),
        ],
        axis=1,
    )
    arrived = lax.all_to_all(packed, "row", 0, 0, tiled=True)
    right_cols = (
        arrived[:, :pieces].reshape(rows, hidden, seqs, places).transpose(0, 2, 1, 3)
    ).reshape(rows * seqs, hidden, places)
    left_rows = (
        arrived[:, pieces : pieces + lines]
        .reshape(rows, hidden, seqs, row_dev)
        .transpose(0, 2, 1, 3)
        .reshape(rows * seqs, hidden, row_dev)
    )
    at = pieces + lines
    mask_whole = arrived[:, at : at + seqs].reshape(rows * seqs, places)
    mask_rows = arrived[:, at + seqs, : seqs * row_dev].reshape(rows * seqs, row_dev)
    seq_total = rows * seqs
    counts = jnp.dot(mask_rows.T, mask_whole, preferred_element_type=F32)
    divisor = jnp.maximum(counts, 1.0)
    out_tensor = outgoing_matrix.reshape(hidden, hidden, channels)

    def block_step(carry, block_index):
        right_grad, weight_gradient, bias_gradient = carry
        start = block_index * 8
        left_block = lax.dynamic_slice_in_dim(left_rows, start, 8, 2)
        div_block = lax.dynamic_slice_in_dim(divisor, start, 8, 0)[..., None]
        grad_block = lax.dynamic_slice_in_dim(update_adjoint, start, 8, 0)
        outer = jnp.einsum(
            "sci,sej->icej", left_block, right_cols, preferred_element_type=F32
        ).astype(BF)
        before = (
            jnp.einsum("icej,ceo->ijo", outer, out_tensor, preferred_element_type=F32)
            + outgoing_offset
        )
        pair_block = (before / div_block).astype(BF)
        scaled = (grad_block.astype(F32) / div_block).astype(BF)
        bias_gradient = bias_gradient + jnp.sum(scaled.astype(F32), axis=(0, 1))
        weight_gradient = weight_gradient + jnp.einsum(
            "icej,ijo->ceo", outer, scaled, preferred_element_type=F32
        )
        outer_grad = jnp.einsum(
            "ijo,ceo->icej", scaled, out_tensor, preferred_element_type=F32
        ).astype(BF)
        left_grad = jnp.einsum("icej,sej->sci", outer_grad, right_cols, preferred_element_type=F32)
        right_grad = right_grad + jnp.einsum(
            "icej,sci->sej", outer_grad, left_block, preferred_element_type=F32
        )
        return ((right_grad, weight_gradient, bias_gradient), (pair_block, left_grad))

    initial = (
        jnp.zeros((seq_total, hidden, places), F32),
        jnp.zeros((hidden, hidden, channels), F32),
        jnp.zeros((channels,), F32),
    )
    (right_grad, weight_gradient, bias_gradient), (pair_blocks, left_blocks) = lax.scan(
        block_step, initial, jnp.arange(row_dev // 8, dtype=jnp.int32)
    )
    pair_increment = pair_blocks.reshape(row_dev, places, channels)
    left_grad = jnp.transpose(left_blocks, (1, 2, 0, 3)).reshape(seq_total * hidden * row_dev // places, places)
    left_total = column_collect(left_grad, cols)

    weight_gradient = weight_gradient.reshape(places // channels, -1, channels)
    weight_lines = weight_gradient.shape[1] // rows
    weight_pack = jnp.concatenate(list(weight_gradient), axis=1).reshape(rows, weight_lines, places)
    packed = jnp.concatenate(
        [
            right_grad.astype(BF).reshape(rows, pieces, places),
            weight_pack.astype(BF),
            left_total.astype(BF).reshape(rows, lines, places),
            jnp.zeros((rows, 16 - lines, places), BF),
        ],
        axis=1,
    )
    arrived = lax.all_to_all(packed, "row", 0, 0, tiled=True)
    added = jnp.sum(arrived[:, : pieces + weight_lines].astype(F32), axis=0)
    right_local = added[:pieces].reshape(seqs, hidden, places)
    weight_chunk = added[pieces:].astype(BF)
    at = pieces + weight_lines
    left_local = (
        arrived[:, at : at + lines]
        .reshape(rows, seqs, hidden, row_dev)
        .transpose(1, 2, 0, 3)
        .reshape(seqs, hidden, places)
        .astype(F32)
    )
    left_local = jnp.where(col_index == 0, left_local, 0.0)
    both = jnp.concatenate([left_local, right_local], axis=1)
    proj_grad = (both * active_mask[:, None, :]).astype(BF)
    projector_weight_gradient = jnp.einsum(
        "src,shr->hc", normalized_alignment, proj_grad, preferred_element_type=F32
    )
    projector_bias_gradient = jnp.sum(proj_grad.astype(F32), axis=(0, 2))

    bias_rows = jnp.concatenate(
        list(high_low(bias_gradient)) + list(high_low(projector_bias_gradient)), axis=0
    )
    bias_rows = jnp.pad(bias_rows, (0, 16 * places - bias_rows.shape[0])).reshape(16, places)
    own = jnp.concatenate([projector_weight_gradient.astype(BF), weight_chunk, bias_rows], axis=0)
    count = own.shape[0]
    arrived = lax.all_to_all(
        jnp.broadcast_to(own[None], (cols, count, places)), "col", 0, 0, tiled=True
    )
    added = jnp.sum(arrived.astype(F32), axis=0)
    bias_at = 2 * hidden + weight_lines

    def split_bias(lines_of):
        flat = lines_of.reshape(-1)
        out = flat[:channels] + flat[channels : 2 * channels]
        flat = flat[2 * channels :]
        return out, flat[: 2 * hidden] + flat[2 * hidden : 4 * hidden]

    first, second = split_bias(added[bias_at:])
    bias_rows = jnp.concatenate(list(high_low(first)) + list(high_low(second)), axis=0)
    bias_rows = jnp.pad(bias_rows, (0, 16 * places - bias_rows.shape[0])).reshape(16, places)
    own = jnp.concatenate([added[:bias_at].astype(BF), bias_rows], axis=0)
    arrived = lax.all_to_all(
        jnp.broadcast_to(own[None], (rows, count, places)), "row", 0, 0, tiled=True
    ).astype(F32)
    weight_total = arrived[:, 2 * hidden : bias_at].reshape(rows * weight_lines, places)
    weight_total = jnp.concatenate(
        [weight_total[:, i : i + channels] for i in range(0, places, channels)], axis=0
    )
    projector_total = jnp.sum(arrived[:, : 2 * hidden], axis=0).T
    first, second = split_bias(jnp.sum(arrived[:, bias_at:], axis=0))

    normalized_gradient = jnp.einsum(
        "shr,ch->src", proj_grad, lowering_matrix, preferred_element_type=F32
    )
    discarded_value, backward_function = jax.vjp(layer_normalize, presence_real)
    alignment_gradient = backward_function(normalized_gradient)[0].astype(BF)
    return (
        pair_increment,
        alignment_gradient,
        projector_total,
        second,
        weight_total,
        first,
    )


def solution(mesh):
    in_specs = (
        P("row", "col", None),
        P("row", "col"),
        P("col"),
        P(),
        P(),
        P(),
        P(),
        P("row", "col", None),
    )
    out_specs = (P("row", "col", None), P("row", "col", None), P(), P(), P(), P())
    return jax.shard_map(
        per_device, mesh=mesh, in_specs=in_specs, out_specs=out_specs, check_vma=False
    )
```

time: 837 us -> 211 us (0.25)
  waiting for transfers between devices: 594 us -> 89.7 us
  blocking collectives: 155 us -> 0 us
  starting transfers between devices: 0.25 us -> 49.1 us
  between operations: 14.3 us -> 1.27 us
    psum x3 -> x0, waiting for transfers between devices: 439 us -> none  [the longest x1 176 us: per_device(): lax.psum((projector_weight_gradient, projector_bias_gradient, weight_grad...]
    reduce_scatter x2 -> x0, waiting for transfers between devices: 155 us -> none  [the longest x1 81.8 us: per_device(): lax.psum_scatter(placed, 'row', scatter_dimension=0, tiled=True)]
    psum x2 -> x0, blocking collectives: 130 us -> none  [the longest x1 77.4 us: per_device(): lax.psum((projector_weight_gradient, projector_bias_gradient, weight_grad...]
    all_to_all x0 -> x4, waiting for transfers between devices: none -> 77.5 us  [the longest x2 40.4 us: per_device(): arrived = lax.all_to_all(packed, 'row', 0, 0, tiled=True)]
    all_to_all x0 -> x4, starting transfers between devices: none -> 25.9 us  [the longest x2 14.8 us: per_device(): arrived = lax.all_to_all(packed, 'row', 0, 0, tiled=True)]
    all_gather x1 -> x0, blocking collectives: 25.7 us -> none  [per_device(): lax.all_gather(active_mask.astype(jnp.bfloat16), 'row', axis=0, tiled=True)]
    ppermute x0 -> x12, starting transfers between devices: none -> 23.2 us  [the longest x3 11.6 us: column_spread(): lax.ppermute(block, 'col', [(0, d)])]
    select_n x2 -> x3, local copies, waits for them, and re-layouts: 14.6 us -> 0.75 us  [the longest x2 0.65 us: per_device(): left_local = jnp.where(col_index == 0, left_local, 0.0)]
  transfers between devices with their start and end apart: 6 -> 16, of which waited for: 5 -> 12; matrix products, arithmetic and copies ran while one was open for 3% -> 2% of each run, Pallas kernels for 0% -> 0%
where the time goes in v1:
time: 211 us; the launch traced here: 210 us
  waiting for transfers between devices  89.7 us (43%)
  starting transfers between devices  49.1 us (23%)
  local copies, waits for them, and re-layouts  29.2 us (14%)
  matrix products  28 us (13%)
  other arithmetic  10.3 us (5%)
    all_to_all x2, waiting for transfers between devices, per_device(): arrived = lax.all_to_all(packed, 'row', 0, 0, tiled=True)  40.4 us
    all_to_all x1, waiting for transfers between devices, per_device(): lax.all_to_all(jnp.broadcast_to(own[None], (cols, count, places)), 'col',...  22.7 us
    all_to_all x2, starting transfers between devices, per_device(): arrived = lax.all_to_all(packed, 'row', 0, 0, tiled=True)  14.8 us
    all_to_all x1, waiting for transfers between devices, per_device(): lax.all_to_all(jnp.broadcast_to(own[None], (rows, count, places)), 'row',...  14.4 us
    ppermute x3, starting transfers between devices, column_spread(): lax.ppermute(block, 'col', [(0, d)])  11.6 us
    dot_general x2, matrix products, block_step(): jnp.einsum('icej,sej->sci', outer_grad, right_cols, preferred_element_typ...  8.98 us
    all_to_all x1, starting transfers between devices, per_device(): lax.all_to_all(jnp.broadcast_to(own[None], (rows, count, places)), 'row',...  7.42 us
    dot_general x2, matrix products, block_step(): jnp.einsum('icej,sci->sej', outer_grad, left_block, preferred_element_typ...  5.61 us
  transfers between devices with their start and end apart: 16, of which 12 were waited for; matrix products, arithmetic and copies ran while one was open for 2% of the time, Pallas kernels for 0%

profile of v1, /device:TPU:1, one launch (start us, length us, event | category | flops | bytes accessed | tf_op | source)
XLA Modules:
  0.0 209.6 jit_solution(6721607376144351321)
XLA Ops:
  4.0 8.8 %collective-permute-start.2 = (bf16[132,256]{1,0:T(8,128)(2,1)S(1)}, bf16[132,256]{1,0:T(8,128)(2,1)S(1)}, u32[]{:S(2)}, u32[]{:S(2)}) collective-permute-start(bf16[132,256]{1,0:T(8,128)(2,1)S(1)} %pad_maximum_fusion.1), channel_id=1, source_target_pairs={{0,12},{16,28},{32,44},{48,60},{64,76},{80,92},{96,108},{112,124},... | collective-permute-start | bytes 202760 | tf_op jit(solution)/shard_map/ppermute | solution.py:20
  12.8 1.6 collective-permute-start.1
  15.7 1.9 collective-permute-done
  24.3 4.2 %concatenate.33 = bf16[16,144,256]{2,1,0:T(8,128)(2,1)} concatenate(bf16[16,128,256]{2,1,0:T(8,128)(2,1)S(1)} %broadcast_in_dim.92, bf16[16,8,256]{2,1,0:T(8,128)(2,1)S(1)} %reshape.153, bf16[16,4,256]{2,1,0:T(4,128)(2,1)S(1)} %broadcast_in_dim.93, bf16[16,1,256]{2,1,0:T(2,128)(2,1)S(1)} %pad.11.clone, bf16[16,3,256]{2,1,0:T(4,128)(2,1)S(1)} %broadcast_in_dim.94), dimensions={1} | concatenate | bytes 2359296 | tf_op jit(solution)/shard_map/concatenate | solution.py:87
  28.5 8.5 %all-to-all-start = ((bf16[16,144,256]{2,1,0:T(8,128)(2,1)}), bf16[16,144,256]{2,1,0:T(8,128)(2,1)S(1)}, u32[]{:S(2)}, u32[]{:S(2)}) async-start(bf16[16,144,256]{2,1,0:T(8,128)(2,1)} %concatenate.33), calls=%async_computation | async-start | bytes 2359296 | tf_op jit(solution)/shard_map/all_to_all | solution.py:97
  37.0 18.7 %all-to-all-done = bf16[16,144,256]{2,1,0:T(8,128)(2,1)S(1)} async-done(((bf16[16,144,256]{2,1,0:T(8,128)(2,1)}), bf16[16,144,256]{2,1,0:T(8,128)(2,1)S(1)}, u32[]{:S(2)}, u32[]{:S(2)}) %all-to-all-start) | async-done | bytes 1179680 | tf_op jit(solution)/shard_map/all_to_all | solution.py:97
  59.8 2.0 copy.113
  63.1 32.7 %while.19 = (s32[]{:T(128)}, f32[64,32,256]{2,0,1:T(8,128)S(1)}, f32[32,32,128]{2,1,0:T(8,128)}, f32[128]{0:T(128)S(1)}, bf16[2,8,256,128]{3,2,1,0:T(8,128)(2,1)...) while((s32[]{:T(128)}, f32[64,32,256]{2,0,1:T(8,128)S(1)}, ...), condition=%wide.region_4.5_spmd.clone, body=%wide.region_2.4_spmd.clone.sunk | while | flops 2425094144 | bytes 54316004 | solution.py:148
  64.5 1.5 convert_reduce_fusion.6
  67.4 1.5 fusion.127
  68.9 1.7 fusion.129
  70.7 1.4 convert_bitcast_fusion.4
  72.1 4.5 %fusion.130 = f32[2,64,32,8]{1,2,3,0:T(8,128)S(1)} fusion(f32[2,64,32,8]{1,2,3,0:T(8,128)S(1)} %copy-done.8, s32[]{:T(128)S(6)} %copy.194, bf16[8,32,32,256]{3,2,1,0:T(8,128)(2,1)S(1)} %convert_bitcast_fusion.4, bf16[64,32,256]{2,0,1:T(8,128)(2,1)S(1)} %get-tuple-element.377), kind=kOutput, calls=%fused_computation.20.clone.1 | convolution fusion | flops 268435456 | bytes 5373956 | tf_op jit(solution)/shard_map/while/body/eval_jaxpr/icej,sej->sci/dot_general | solution.py:137
  76.6 2.8 %bitcast_add_fusion.2 = f32[64,32,256]{2,0,1:T(8,128)S(1)} fusion(f32[64,32,256]{2,0,1:T(8,128)S(1)} %get-tuple-element.350, bf16[64,32,8,1]{0,1,2,3:T(8,128)(2,1)S(1)} %dynamic-slice_bitcast_fusion.2, bf16[8,32,32,256]{3,2,1,0:T(8,128)(2,1)S(1)} %convert_bitcast_fusion.4, pred[]{:T(512)S(6)} %compare.60), kind=kOutput, calls=%fused_computation.10.clone.1 | convolution fusion | flops 269484032 | bytes 8421377 | tf_op jit(solution)/shard_map/while/body/eval_jaxpr/icej,sci->sej/dot_general | solution.py:138
  80.7 1.5 convert_reduce_fusion.6
  83.6 1.5 fusion.127
  85.1 1.7 fusion.129
  88.3 4.5 %fusion.130 = f32[2,64,32,8]{1,2,3,0:T(8,128)S(1)} fusion(f32[2,64,32,8]{1,2,3,0:T(8,128)S(1)} %copy-done.8, s32[]{:T(128)S(6)} %copy.194, bf16[8,32,32,256]{3,2,1,0:T(8,128)(2,1)S(1)} %convert_bitcast_fusion.4, bf16[64,32,256]{2,0,1:T(8,128)(2,1)S(1)} %get-tuple-element.377), kind=kOutput, calls=%fused_computation.20.clone.1 | convolution fusion | flops 268435456 | bytes 5373956 | tf_op jit(solution)/shard_map/while/body/eval_jaxpr/icej,sej->sci/dot_general | solution.py:137
  92.8 2.8 %bitcast_add_fusion.2 = f32[64,32,256]{2,0,1:T(8,128)S(1)} fusion(f32[64,32,256]{2,0,1:T(8,128)S(1)} %get-tuple-element.350, bf16[64,32,8,1]{0,1,2,3:T(8,128)(2,1)S(1)} %dynamic-slice_bitcast_fusion.2, bf16[8,32,32,256]{3,2,1,0:T(8,128)(2,1)S(1)} %convert_bitcast_fusion.4, pred[]{:T(512)S(6)} %compare.60), kind=kOutput, calls=%fused_computation.10.clone.1 | convolution fusion | flops 269484032 | bytes 8421377 | tf_op jit(solution)/shard_map/while/body/eval_jaxpr/icej,sci->sej/dot_general | solution.py:138
  95.9 3.9 %copy.119 = f32[64,32,2,8]{3,2,1,0:T(2,128)} copy(f32[64,32,2,8]{0,1,3,2:T(8,128)} %bitcast.145) | data formatting | bytes 262144 | tf_op jit(solution)/shard_map/transpose | solution.py:152
  99.8 4.7 %reshape.163 = f32[128,256]{1,0:T(8,128)S(1)} reshape(f32[64,32,2,8]{3,2,1,0:T(2,128)} %copy.119) | data formatting | bytes 262144 | tf_op jit(solution)/shard_map/reshape | solution.py:152
  108.5 1.9 collective-permute-done.8
  110.8 1.5 collective-permute-done.6
  117.4 2.1 collective-permute-done.11
  119.4 3.1 %collective-permute-done.10 = bf16[128,256]{1,0:T(8,128)(2,1)S(1)} collective-permute-done((bf16[128,256]{1,0:T(8,128)(2,1)S(1)}, bf16[128,256]{1,0:T(8,128)(2,1)S(1)}, u32[]{:S(2)}, u32[]{:S(2)}) %collective-permute-start.10) | collective-permute-done | bytes 65568 | tf_op jit(solution)/shard_map/ppermute | solution.py:37
  122.6 1.7 maximum_maximum_fusion
  124.3 6.3 %all-to-all-start.1 = ((bf16[16,176,256]{2,1,0:T(8,128)(2,1)}), bf16[16,176,256]{2,1,0:T(8,128)(2,1)S(1)}, u32[]{:S(2)}, u32[]{:S(2)}) async-start(bf16[16,176,256]{2,1,0:T(8,128)(2,1)} %maximum_maximum_fusion), calls=%async_computation.1 | async-start | bytes 2883584 | tf_op jit(solution)/shard_map/all_to_all | solution.py:167
  130.6 21.7 %all-to-all-done.1 = bf16[16,176,256]{2,1,0:T(8,128)(2,1)S(1)} async-done(((bf16[16,176,256]{2,1,0:T(8,128)(2,1)}), bf16[16,176,256]{2,1,0:T(8,128)(2,1)S(1)}, u32[]{:S(2)}, u32[]{:S(2)}) %all-to-all-start.1) | async-done | bytes 1441824 | tf_op jit(solution)/shard_map/all_to_all | solution.py:167
  155.2 3.6 %all-to-all-start.2 = ((bf16[16,112,256]{2,1,0:T(8,128)(2,1)}), bf16[16,112,256]{2,1,0:T(8,128)(2,1)S(1)}, u32[]{:S(2)}, u32[]{:S(2)}) async-start(bf16[16,112,256]{2,1,0:T(8,128)(2,1)} %broadcast_in_dim.99), calls=%async_computation.2 | async-start | bytes 1835008 | tf_op jit(solution)/shard_map/all_to_all | solution.py:193
  159.1 22.7 %all-to-all-done.2 = bf16[16,112,256]{2,1,0:T(8,128)(2,1)S(1)} async-done(((bf16[16,112,256]{2,1,0:T(8,128)(2,1)}), bf16[16,112,256]{2,1,0:T(8,128)(2,1)S(1)}, u32[]{:S(2)}, u32[]{:S(2)}) %all-to-all-start.2) | async-done | bytes 917536 | tf_op jit(solution)/shard_map/all_to_all | solution.py:193
  183.2 7.4 %all-to-all-start.3 = ((bf16[16,112,256]{2,1,0:T(8,128)(2,1)}), bf16[16,112,256]{2,1,0:T(8,128)(2,1)S(1)}, u32[]{:S(2)}, u32[]{:S(2)}) async-start(bf16[16,112,256]{2,1,0:T(8,128)(2,1)} %broadcast_in_dim.100), calls=%async_computation.3 | async-start | bytes 1835008 | tf_op jit(solution)/shard_map/all_to_all | solution.py:209
  192.2 14.4 %all-to-all-done.3 = bf16[16,112,256]{2,1,0:T(8,128)(2,1)S(1)} async-done(((bf16[16,112,256]{2,1,0:T(8,128)(2,1)}), bf16[16,112,256]{2,1,0:T(8,128)(2,1)S(1)}, u32[]{:S(2)}, u32[]{:S(2)}) %all-to-all-start.3) | async-done | bytes 917536 | tf_op jit(solution)/shard_map/all_to_all | solution.py:209
  (169 shorter events, 40.2 us)
Async XLA Ops:
  0.6 2.3 %copy-start = (bf16[256,64]{0,1:T(8,128)(2,1)S(1)}, bf16[256,64]{0,1:T(8,128)(2,1)}, u32[]{:S(2)}) copy-start(bf16[256,64]{0,1:T(8,128)(2,1)} %param.13) | copy-start | bytes 98308
  1.9 22.3 %copy-start.1 = (bf16[4,256,256]{1,2,0:T(8,128)(2,1)}, bf16[4,256,256]{1,2,0:T(8,128)(2,1)S(1)}, u32[]{:S(2)}) copy-start(bf16[4,256,256]{1,2,0:T(8,128)(2,1)S(1)} %copy.105) | copy-start | bytes 1572868
  4.0 11.6 %collective-permute-start.2 = (bf16[132,256]{1,0:T(8,128)(2,1)S(1)}, bf16[132,256]{1,0:T(8,128)(2,1)S(1)}, u32[]{:S(2)}, u32[]{:S(2)}) collective-permute-start(bf16[132,256]{1,0:T(8,128)(2,1)S(1)} %pad_maximum_fusion.1), channel_id=1, source_target_pairs={{0,12},{16,28},{32,44},{48,60},{64,76},{80,92},{96,108},{112,124},... | collective-permute-start | bytes 202760 | tf_op jit(solution)/shard_map/ppermute | solution.py:20
  12.8 2.9 %collective-permute-start.1 = (bf16[132,256]{1,0:T(8,128)(2,1)S(1)}, bf16[132,256]{1,0:T(8,128)(2,1)S(1)}, u32[]{:S(2)}, u32[]{:S(2)}) collective-permute-start(bf16[132,256]{1,0:T(8,128)(2,1)S(1)} %pad_maximum_fusion.1), channel_id=1, source_target_pairs={{0,8},{16,24},{32,40},{48,56},{64,72},{80,88},{96,104},{112,120},{... | collective-permute-start | bytes 202760 | tf_op jit(solution)/shard_map/ppermute | solution.py:20
  14.4 3.3 %collective-permute-start = (bf16[132,256]{1,0:T(8,128)(2,1)S(1)}, bf16[132,256]{1,0:T(8,128)(2,1)S(1)}, u32[]{:S(2)}, u32[]{:S(2)}) collective-permute-start(bf16[132,256]{1,0:T(8,128)(2,1)S(1)} %pad_maximum_fusion.1), channel_id=1, source_target_pairs={{0,4},{16,20},{32,36},{48,52},{64,68},{80,84},{96,100},{112,116},{... | collective-permute-start | bytes 202760 | tf_op jit(solution)/shard_map/ppermute | solution.py:20
  17.7 4.0 %collective-permute-start.5 = (bf16[132,256]{1,0:T(8,128)(2,1)S(1)}, bf16[132,256]{1,0:T(8,128)(2,1)S(1)}, u32[]{:S(2)}, u32[]{:S(2)}) collective-permute-start(bf16[132,256]{1,0:T(8,128)(2,1)S(1)} %add_select_fusion.1), channel_id=1, source_target_pairs={{0,3},{4,7},{8,11},{12,15},{16,19},{20,23},{24,27},{28,31},{32,35}... | collective-permute-start | bytes 202760 | tf_op jit(solution)/shard_map/ppermute | solution.py:23
  19.0 3.3 %collective-permute-start.4 = (bf16[132,256]{1,0:T(8,128)(2,1)S(1)}, bf16[132,256]{1,0:T(8,128)(2,1)S(1)}, u32[]{:S(2)}, u32[]{:S(2)}) collective-permute-start(bf16[132,256]{1,0:T(8,128)(2,1)S(1)} %add_select_fusion.1), channel_id=1, source_target_pairs={{0,2},{4,6},{8,10},{12,14},{16,18},{20,22},{24,26},{28,30},{32,34}... | collective-permute-start | bytes 202760 | tf_op jit(solution)/shard_map/ppermute | solution.py:23
  20.3 2.7 %collective-permute-start.3 = (bf16[132,256]{1,0:T(8,128)(2,1)S(1)}, bf16[132,256]{1,0:T(8,128)(2,1)S(1)}, u32[]{:S(2)}, u32[]{:S(2)}) collective-permute-start(bf16[132,256]{1,0:T(8,128)(2,1)S(1)} %add_select_fusion.1), channel_id=1, source_target_pairs={{0,1},{4,5},{8,9},{12,13},{16,17},{20,21},{24,25},{28,29},{32,33},... | collective-permute-start | bytes 202760 | tf_op jit(solution)/shard_map/ppermute | solution.py:23
  28.5 27.3 %all-to-all-start = ((bf16[16,144,256]{2,1,0:T(8,128)(2,1)}), bf16[16,144,256]{2,1,0:T(8,128)(2,1)S(1)}, u32[]{:S(2)}, u32[]{:S(2)}) async-start(bf16[16,144,256]{2,1,0:T(8,128)(2,1)} %concatenate.33), calls=%async_computation | async-start | bytes 2359296 | tf_op jit(solution)/shard_map/all_to_all | solution.py:97
  56.6 6.5 %copy-start.11 = (f32[128]{0:T(128)S(1)}, f32[128]{0:T(128)}, u32[]{:S(2)}) copy-start(f32[128]{0:T(128)} %param.16) | copy-start | bytes 1540
  64.5 2.8 %copy-start.3 = (bf16[16,256,128]{2,1,0:T(8,128)(2,1)S(1)}, bf16[16,256,128]{2,1,0:T(8,128)(2,1)}, u32[]{:S(2)}) copy-start(bf16[16,256,128]{2,1,0:T(8,128)(2,1)} %get-tuple-element.374) | copy-start | bytes 3145732 | tf_op jit(solution)/shard_map/while
  64.5 2.8 %copy-start.5 = (f32[32,32,128]{2,1,0:T(8,128)S(1)}, f32[32,32,128]{2,1,0:T(8,128)}, u32[]{:S(2)}) copy-start(f32[32,32,128]{2,1,0:T(8,128)} %get-tuple-element.351) | copy-start | bytes 1572868 | tf_op jit(solution)/shard_map/while
  67.4 1.5 copy-start.10
  68.9 1.8 copy-start.6
  70.7 5.9 %copy-start.13 = (bf16[2,8,256,128]{3,2,1,0:T(8,128)(2,1)}, bf16[2,8,256,128]{3,2,1,0:T(8,128)(2,1)S(1)}, u32[]{:S(2)}) copy-start(bf16[2,8,256,128]{3,2,1,0:T(8,128)(2,1)S(1)} %fusion.129) | copy-start | bytes 3145732 | tf_op jit(solution)/shard_map/while
  76.6 2.8 %copy-start.9 = (f32[2,64,32,8]{1,2,3,0:T(8,128)}, f32[2,64,32,8]{1,2,3,0:T(8,128)S(1)}, u32[]{:S(2)}) copy-start(f32[2,64,32,8]{1,2,3,0:T(8,128)S(1)} %fusion.130) | copy-start | bytes 393220 | tf_op jit(solution)/shard_map/while
  80.7 2.8 %copy-start.3 = (bf16[16,256,128]{2,1,0:T(8,128)(2,1)S(1)}, bf16[16,256,128]{2,1,0:T(8,128)(2,1)}, u32[]{:S(2)}) copy-start(bf16[16,256,128]{2,1,0:T(8,128)(2,1)} %get-tuple-element.374) | copy-start | bytes 3145732 | tf_op jit(solution)/shard_map/while
  80.7 2.8 %copy-start.5 = (f32[32,32,128]{2,1,0:T(8,128)S(1)}, f32[32,32,128]{2,1,0:T(8,128)}, u32[]{:S(2)}) copy-start(f32[32,32,128]{2,1,0:T(8,128)} %get-tuple-element.351) | copy-start | bytes 1572868 | tf_op jit(solution)/shard_map/while
  83.5 1.5 copy-start.10
  85.1 1.8 copy-start.6
  86.9 5.9 %copy-start.13 = (bf16[2,8,256,128]{3,2,1,0:T(8,128)(2,1)}, bf16[2,8,256,128]{3,2,1,0:T(8,128)(2,1)S(1)}, u32[]{:S(2)}) copy-start(bf16[2,8,256,128]{3,2,1,0:T(8,128)(2,1)S(1)} %fusion.129) | copy-start | bytes 3145732 | tf_op jit(solution)/shard_map/while
  92.8 2.8 %copy-start.9 = (f32[2,64,32,8]{1,2,3,0:T(8,128)}, f32[2,64,32,8]{1,2,3,0:T(8,128)S(1)}, u32[]{:S(2)}) copy-start(f32[2,64,32,8]{1,2,3,0:T(8,128)S(1)} %fusion.130) | copy-start | bytes 393220 | tf_op jit(solution)/shard_map/while
  95.9 12.6 %copy-start.7 = (f32[32,32,128]{2,1,0:T(8,128)S(1)}, f32[32,32,128]{2,1,0:T(8,128)}, u32[]{:S(2)}) copy-start(f32[32,32,128]{2,1,0:T(8,128)} %get-tuple-element.79) | copy-start | bytes 1572868
  104.5 5.9 %collective-permute-start.8 = (bf16[128,256]{1,0:T(8,128)(2,1)S(1)}, bf16[128,256]{1,0:T(8,128)(2,1)S(1)}, u32[]{:S(2)}, u32[]{:S(2)}) collective-permute-start(bf16[128,256]{1,0:T(8,128)(2,1)S(1)} %convert_element_type.146), channel_id=1, source_target_pairs={{3,0},{7,4},{11,8},{15,12},{19,16},{23,20},{27,24},{31,28},{35,32}... | collective-permute-start | bytes 196616 | tf_op jit(solution)/shard_map/ppermute | solution.py:32
  105.8 5.0 %collective-permute-start.7 = (bf16[128,256]{1,0:T(8,128)(2,1)S(1)}, bf16[128,256]{1,0:T(8,128)(2,1)S(1)}, u32[]{:S(2)}, u32[]{:S(2)}) collective-permute-start(bf16[128,256]{1,0:T(8,128)(2,1)S(1)} %convert_element_type.146), channel_id=1, source_target_pairs={{2,0},{6,4},{10,8},{14,12},{18,16},{22,20},{26,24},{30,28},{34,32}... | collective-permute-start | bytes 196616 | tf_op jit(solution)/shard_map/ppermute | solution.py:32
  107.1 5.2 %collective-permute-start.6 = (bf16[128,256]{1,0:T(8,128)(2,1)S(1)}, bf16[128,256]{1,0:T(8,128)(2,1)S(1)}, u32[]{:S(2)}, u32[]{:S(2)}) collective-permute-start(bf16[128,256]{1,0:T(8,128)(2,1)S(1)} %convert_element_type.146), channel_id=1, source_target_pairs={{1,0},{5,4},{9,8},{13,12},{17,16},{21,20},{25,24},{29,28},{33,32},... | collective-permute-start | bytes 196616 | tf_op jit(solution)/shard_map/ppermute | solution.py:32
  112.3 7.1 %collective-permute-start.11 = (bf16[128,256]{1,0:T(8,128)(2,1)S(1)}, bf16[128,256]{1,0:T(8,128)(2,1)S(1)}, u32[]{:S(2)}, u32[]{:S(2)}) collective-permute-start(bf16[128,256]{1,0:T(8,128)(2,1)S(1)} %fusion.75), channel_id=1, source_target_pairs={{12,0},{28,16},{44,32},{60,48},{76,64},{92,80},{108,96},{124,112},... | collective-permute-start | bytes 196616 | tf_op jit(solution)/shard_map/ppermute | solution.py:37
  113.6 8.9 %collective-permute-start.10 = (bf16[128,256]{1,0:T(8,128)(2,1)S(1)}, bf16[128,256]{1,0:T(8,128)(2,1)S(1)}, u32[]{:S(2)}, u32[]{:S(2)}) collective-permute-start(bf16[128,256]{1,0:T(8,128)(2,1)S(1)} %fusion.75), channel_id=1, source_target_pairs={{8,0},{24,16},{40,32},{56,48},{72,64},{88,80},{104,96},{120,112},{... | collective-permute-start | bytes 196616 | tf_op jit(solution)/shard_map/ppermute | solution.py:37
  114.9 7.6 %collective-permute-start.9 = (bf16[128,256]{1,0:T(8,128)(2,1)S(1)}, bf16[128,256]{1,0:T(8,128)(2,1)S(1)}, u32[]{:S(2)}, u32[]{:S(2)}) collective-permute-start(bf16[128,256]{1,0:T(8,128)(2,1)S(1)} %fusion.75), channel_id=1, source_target_pairs={{4,0},{20,16},{36,32},{52,48},{68,64},{84,80},{100,96},{116,112},{... | collective-permute-start | bytes 196616 | tf_op jit(solution)/shard_map/ppermute | solution.py:37
  124.3 28.0 %all-to-all-start.1 = ((bf16[16,176,256]{2,1,0:T(8,128)(2,1)}), bf16[16,176,256]{2,1,0:T(8,128)(2,1)S(1)}, u32[]{:S(2)}, u32[]{:S(2)}) async-start(bf16[16,176,256]{2,1,0:T(8,128)(2,1)} %maximum_maximum_fusion), calls=%async_computation.1 | async-start | bytes 2883584 | tf_op jit(solution)/shard_map/all_to_all | solution.py:167
  155.2 26.7 %all-to-all-start.2 = ((bf16[16,112,256]{2,1,0:T(8,128)(2,1)}), bf16[16,112,256]{2,1,0:T(8,128)(2,1)S(1)}, u32[]{:S(2)}, u32[]{:S(2)}) async-start(bf16[16,112,256]{2,1,0:T(8,128)(2,1)} %broadcast_in_dim.99), calls=%async_computation.2 | async-start | bytes 1835008 | tf_op jit(solution)/shard_map/all_to_all | solution.py:193
  183.2 23.4 %all-to-all-start.3 = ((bf16[16,112,256]{2,1,0:T(8,128)(2,1)}), bf16[16,112,256]{2,1,0:T(8,128)(2,1)S(1)}, u32[]{:S(2)}, u32[]{:S(2)}) async-start(bf16[16,112,256]{2,1,0:T(8,128)(2,1)} %broadcast_in_dim.100), calls=%async_computation.3 | async-start | bytes 1835008 | tf_op jit(solution)/shard_map/all_to_all | solution.py:209
  (6 other events, 8.7 us)

commit v2 on v1

v2 whole, which is shorter than its diff:
```python
import functools

import jax
import jax.numpy as jnp
from jax import lax
from jax.experimental import pallas as pl
from jax.experimental.pallas import tpu as pltpu
from jax.sharding import PartitionSpec as P

PAIRED = 16
CHAINS = 4
BF = jnp.bfloat16
F32 = jnp.float32
STEP = 4


def layer_normalize(values):
    center = values - jnp.mean(values, axis=-1, keepdims=True)
    spread = jnp.mean(center * center, axis=-1, keepdims=True)
    return center * lax.rsqrt(spread + 1e-05)


def column_spread(block, col_index, cols):
    far = [lax.ppermute(block, "col", [(0, d)]) for d in range(STEP, cols, STEP)]
    block = jnp.where(col_index == 0, block, sum(far[1:], far[0]))
    near = [
        lax.ppermute(block, "col", [(a, a + d) for a in range(0, cols, STEP)])
        for d in range(1, STEP)
    ]
    return jnp.where(col_index % STEP == 0, block, sum(near[1:], near[0]))


def column_near(block, cols):
    sent = block.astype(BF)
    parts = [
        lax.ppermute(sent, "col", [(a + d, a) for a in range(0, cols, STEP)])
        for d in range(1, STEP)
    ]
    return block + sum(p.astype(F32) for p in parts)


def column_far(block, cols):
    sent = block.astype(BF)
    parts = [lax.ppermute(sent, "col", [(d, 0)]) for d in range(STEP, cols, STEP)]
    return block + sum(p.astype(F32) for p in parts)


def dot(a, b, lhs, rhs):
    return lax.dot_general(a, b, (((lhs,), (rhs,)), ((), ())), preferred_element_type=F32)


def first_kernel(shape, arrived, adjoint, weights, g_ref, s_ref, d_ref, r_ref, left_ref, bias_ref, r_all, tiles, total):
    src, seqs, hidden, row_dev, places, channels, e_block = shape
    step = pl.program_id(0)
    pieces = seqs * hidden

    @pl.when(step == 0)
    def _():
        lines = src * pieces
        spans = [(h, pl.ds(h * channels, channels)) for h in range(places // channels)]
        for d in range(src):
            for h, span in spans:
                r_all[pl.ds(h * lines + d * pieces, pieces), :] = arrived[d, :pieces, span].astype(F32)
            tiles[pl.ds(d * row_dev, row_dev), :] = arrived[d, pieces : pieces + row_dev, channels:].astype(F32)
        for e in range(hidden):
            for h, span in spans:
                rows = [r_all[pl.ds(h * lines + s * hidden + e, src, stride=pieces), :] for s in range(seqs)]
                r_ref[e, :, span] = jnp.concatenate(rows, axis=0).astype(BF)
        for h, span in spans:
            for d in range(src):
                r_all[pl.ds((h * src + d) * 16, 16), :] = arrived[d, pieces + row_dev :, span].astype(F32)
        live_t = []
        for h, span in spans:
            rows = [r_all[pl.ds(h * src * 16 + s, src, stride=16), :] for s in range(seqs)]
            live_t.append(jnp.concatenate(rows, axis=0).T)
        live_t = jnp.concatenate(live_t, axis=0).astype(BF)
        bias = jnp.zeros((1, channels), F32)
        for i in range(row_dev):
            tile = tiles[pl.ds(i, src, stride=row_dev), :]
            column = jnp.concatenate([tile[:, s * hidden : s * hidden + 1] for s in range(seqs)], axis=0)
            column = jnp.broadcast_to(column, (src * seqs, channels)).astype(BF)
            divisor = jnp.maximum(dot(live_t, column, 1, 0), 1.0)
            scaled = (adjoint[i].astype(F32) / divisor).astype(BF)
            d_ref[i] = divisor.astype(BF)
            s_ref[i] = scaled
            bias = bias + jnp.sum(scaled.astype(F32), axis=0, keepdims=True)
        bias_ref[...] = bias
        total[...] = jnp.zeros_like(total)

    part = weights[pl.ds(step * e_block * hidden, e_block * hidden), :]
    for i in range(row_dev):
        g = dot(part, s_ref[i], 1, 1).astype(BF)
        g_ref[:, pl.ds(i * hidden, hidden), :] = g.reshape(e_block, hidden, places)
    acc = total[...]
    for e in range(e_block):
        acc = acc + dot(r_ref[step * e_block + e], g_ref[e], 1, 1)
    total[...] = acc

    @pl.when(step == pl.num_programs(0) - 1)
    def _():
        for i in range(row_dev):
            block = acc[:, i * hidden : (i + 1) * hidden]
            left_ref[pl.ds(i, src, stride=row_dev), :] = jnp.concatenate(
                [block[s * src : (s + 1) * src] for s in range(seqs)], axis=1
            )


def unpack_left(shape, arrived, tiles, left_ref, left_t_ref):
    src, seqs, hidden, row_dev, places, channels, e_block = shape
    pieces = seqs * hidden
    for d in range(src):
        tiles[pl.ds(d * row_dev, row_dev), :] = arrived[d, pieces : pieces + row_dev, :channels].astype(F32)
    blocks = []
    for i in range(row_dev):
        tile = tiles[pl.ds(i, src, stride=row_dev), :]
        blocks.append(jnp.concatenate([tile[:, s * hidden : (s + 1) * hidden] for s in range(seqs)], axis=0))
    left = jnp.concatenate(blocks, axis=1)
    left_ref[...] = left.astype(BF)
    left_t_ref[...] = left.T.astype(BF)


def second_kernel(shape, arrived, r_ref, s_ref, d_ref, weights_t, offset, pair_ref, wgrad_ref, left_out, tiles, left_t, outer, before):
    src, seqs, hidden, row_dev, places, channels, e_block = shape
    step = pl.program_id(0)

    @pl.when(step == 0)
    def _():
        unpack_left(shape, arrived, tiles, left_out, left_t)
        before[...] = jnp.zeros_like(before)

    for e in range(e_block):
        outer[e] = dot(left_t[...], r_ref[e], 1, 0).astype(BF)
    acc = jnp.zeros((e_block * hidden, channels), F32)
    for i in range(row_dev):
        block = outer[:, pl.ds(i * hidden, hidden), :].reshape(e_block * hidden, places)
        before[i] = before[i] + dot(weights_t[...], block, 1, 0)
        acc = acc + dot(block, s_ref[i], 1, 0)
    wgrad_ref[...] = acc

    @pl.when(step == pl.num_programs(0) - 1)
    def _():
        for i in range(row_dev):
            pair_ref[i] = ((before[i].T + offset[...]) / d_ref[i].astype(F32)).astype(BF)


def third_kernel(shape, left, g_ref, out_ref, held):
    src, seqs, hidden, row_dev, places, channels, e_block = shape
    step = pl.program_id(0)
    for e in range(e_block):
        grad = dot(left[...], g_ref[e], 1, 0)
        for h in range(places // channels):
            for s in range(seqs):
                at = h * src * seqs * hidden + s * hidden + step * e_block + e
                held[pl.ds(at, src, stride=seqs * hidden), :] = grad[
                    s * src : (s + 1) * src, h * channels : (h + 1) * channels
                ]

    @pl.when(step == pl.num_programs(0) - 1)
    def _():
        lines = src * seqs * hidden
        for h in range(places // channels):
            out_ref[:, pl.ds(h * channels, channels)] = held[pl.ds(h * lines, lines), :].astype(BF)


def vmem(*block):
    return pl.BlockSpec(block, lambda t: (0,) * len(block))


def params():
    return pltpu.CompilerParams(dimension_semantics=("arbitrary",), vmem_limit_bytes=52 * 2**20)


def main_first(shape, arrived, adjoint, weights):
    src, seqs, hidden, row_dev, places, channels, e_block = shape
    total, lines = src * seqs, row_dev * hidden
    S = jax.ShapeDtypeStruct
    return pl.pallas_call(
        functools.partial(first_kernel, shape),
        grid=(hidden // e_block,),
        in_specs=[vmem(*arrived.shape), vmem(*adjoint.shape), vmem(*weights.shape)],
        out_specs=[
            pl.BlockSpec((e_block, lines, places), lambda t: (t, 0, 0)),
            vmem(row_dev, places, channels),
            vmem(row_dev, places, channels),
            vmem(hidden, total, places),
            vmem(src * row_dev, channels),
            vmem(1, channels),
        ],
        out_shape=[
            S((hidden, lines, places), BF),
            S((row_dev, places, channels), BF),
            S((row_dev, places, channels), BF),
            S((hidden, total, places), BF),
            S((src * row_dev, channels), F32),
            S((1, channels), F32),
        ],
        scratch_shapes=[
            pltpu.VMEM((total * hidden * places // channels, channels), F32),
            pltpu.VMEM((src * row_dev, channels), F32),
            pltpu.VMEM((total, lines), F32),
        ],
        compiler_params=params(),
        cost_estimate=pl.CostEstimate(flops=2 * 800_000_000, bytes_accessed=16 * 2**20, transcendentals=0),
        name="scaled_outer_grad",
    )(arrived, adjoint, weights)


def main_second(shape, arrived, right, scaled, divisor, weights_t, offset):
    src, seqs, hidden, row_dev, places, channels, e_block = shape
    total, lines = src * seqs, row_dev * hidden
    S = jax.ShapeDtypeStruct
    folds = places // channels
    halves = hidden // e_block // folds
    return pl.pallas_call(
        functools.partial(second_kernel, shape),
        grid=(hidden // e_block,),
        in_specs=[
            vmem(*arrived.shape),
            pl.BlockSpec((e_block, total, places), lambda t: (t, 0, 0)),
            vmem(*scaled.shape),
            vmem(*divisor.shape),
            pl.BlockSpec((channels, e_block * hidden), lambda t: (0, t)),
            vmem(1, channels),
        ],
        out_specs=[
            vmem(row_dev, places, channels),
            pl.BlockSpec((e_block * hidden, channels), lambda t: (t % halves, t // halves)),
            vmem(total, lines),
        ],
        out_shape=[
            S((row_dev, places, channels), BF),
            S((hidden * hidden // folds, places), F32),
            S((total, lines), BF),
        ],
        scratch_shapes=[
            pltpu.VMEM((src * row_dev, channels), F32),
            pltpu.VMEM((lines, total), BF),
            pltpu.VMEM((e_block, lines, places), BF),
            pltpu.VMEM((row_dev, channels, places), F32),
        ],
        compiler_params=params(),
        cost_estimate=pl.CostEstimate(flops=2 * 1_300_000_000, bytes_accessed=8 * 2**20, transcendentals=0),
        name="outer_pair",
    )(arrived, right, scaled, divisor, weights_t, offset)


def main_third(shape, left, outer_grad):
    src, seqs, hidden, row_dev, places, channels, e_block = shape
    total, lines = src * seqs, row_dev * hidden
    return pl.pallas_call(
        functools.partial(third_kernel, shape),
        grid=(hidden // e_block,),
        in_specs=[vmem(total, lines), pl.BlockSpec((e_block, lines, places), lambda t: (t, 0, 0))],
        out_specs=vmem(total * hidden, places),
        out_shape=jax.ShapeDtypeStruct((total * hidden, places), BF),
        scratch_shapes=[pltpu.VMEM((total * hidden * places // channels, channels), F32)],
        compiler_params=params(),
        cost_estimate=pl.CostEstimate(flops=2 * 270_000_000, bytes_accessed=10 * 2**20, transcendentals=0),
        name="right_grad",
    )(left, outer_grad)


def high_low(values):
    high = values.astype(BF)
    return high, (values - high.astype(F32)).astype(BF)


def per_device(
    homolog_features,
    presence_indicator,
    polymer_label,
    lowering_matrix,
    lowering_offset,
    outgoing_matrix,
    outgoing_offset,
    update_adjoint,
):
    seqs, places, depth = homolog_features.shape
    hidden = lowering_matrix.shape[1] // 2
    channels = outgoing_matrix.shape[1]
    row_dev = update_adjoint.shape[0]
    rows, cols = lax.axis_size("row"), lax.axis_size("col")
    row_index, col_index = lax.axis_index("row"), lax.axis_index("col")

    presence_real = homolog_features.astype(F32)
    normalized_alignment = layer_normalize(presence_real).astype(BF)
    seq_index = row_index * seqs + jnp.arange(seqs, dtype=jnp.int32)
    seq_chain = (seq_index - PAIRED) % CHAINS
    permitted_pairs = (seq_index[:, None] < PAIRED) | (seq_chain[:, None] == polymer_label[None, :])
    active_mask = jnp.where(permitted_pairs & (presence_indicator == 1), 1.0, 0.0).astype(F32)
    pieces = seqs * hidden
    tile = row_dev
    right_own = (
        jnp.einsum(
            "src,ch->shr", normalized_alignment, lowering_matrix[:, hidden:], preferred_element_type=F32
        )
        + lowering_offset[hidden:, None]
    )
    right_own = (right_own * active_mask[:, None, :]).astype(BF).reshape(pieces, places)
    live_t = active_mask.T[:, :, None]
    left_own = (
        jnp.einsum(
            "src,ch->rsh", normalized_alignment, lowering_matrix[:, :hidden], preferred_element_type=F32
        )
        + lowering_offset[:hidden]
    )
    left_own = jnp.concatenate(
        [
            (left_own * live_t).astype(BF).reshape(places, pieces),
            jnp.broadcast_to(live_t, left_own.shape).astype(BF).reshape(places, pieces),
        ],
        axis=1,
    )
    spread = column_spread(left_own, col_index, cols)
    live_own = jnp.pad(active_mask.astype(BF), ((0, 16 - seqs), (0, 0)))
    packed = jnp.concatenate(
        [
            jnp.broadcast_to(right_own[None], (rows, pieces, places)),
            spread.reshape(rows, tile, places),
            jnp.broadcast_to(live_own[None], (rows, 16, places)),
        ],
        axis=1,
    )
    arrived = lax.all_to_all(packed, "row", 0, 0, tiled=True)

    shape = (rows, seqs, hidden, row_dev, places, channels, 8)
    weights = outgoing_matrix.reshape(hidden, hidden, channels).transpose(1, 0, 2)
    weights = weights.reshape(hidden * hidden, channels)
    outer_grad, scaled, divisor, right_cols, left_grad, bias_gradient = main_first(
        shape, arrived, update_adjoint, weights
    )
    bias_gradient = bias_gradient[0]

    left_grad = column_near(left_grad, cols)
    pair_increment, weight_gradient, left_rows = main_second(
        shape, arrived, right_cols, scaled, divisor, weights.T, outgoing_offset[None]
    )
    left_grad = column_far(left_grad, cols)
    right_grad = main_third(shape, left_rows, outer_grad)

    weight_lines = weight_gradient.shape[0] // rows
    left_lines = jnp.pad(
        left_grad.astype(BF).reshape(rows, tile, channels), ((0, 0), (0, 0), (0, places - channels))
    )
    packed = jnp.concatenate(
        [
            right_grad.reshape(rows, pieces, places),
            weight_gradient.astype(BF).reshape(rows, weight_lines, places),
            left_lines,
        ],
        axis=1,
    )
    arrived = lax.all_to_all(packed, "row", 0, 0, tiled=True)
    added = jnp.sum(arrived[:, : pieces + weight_lines].astype(F32), axis=0)
    right_local = added[:pieces].reshape(seqs, hidden, places)
    weight_chunk = added[pieces:].astype(BF)
    left_local = arrived[:, pieces + weight_lines :, :channels].reshape(places, seqs, hidden)
    left_local = left_local.transpose(1, 2, 0).astype(F32)
    left_local = jnp.where(col_index == 0, left_local, 0.0)
    both = jnp.concatenate([left_local, right_local], axis=1)
    proj_grad = (both * active_mask[:, None, :]).astype(BF)
    projector_weight_gradient = jnp.einsum(
        "src,shr->hc", normalized_alignment, proj_grad, preferred_element_type=F32
    )
    projector_bias_gradient = jnp.sum(proj_grad.astype(F32), axis=(0, 2))

    bias_rows = jnp.concatenate(
        list(high_low(bias_gradient)) + list(high_low(projector_bias_gradient)), axis=0
    )
    bias_rows = jnp.pad(bias_rows, (0, 16 * places - bias_rows.shape[0])).reshape(16, places)
    own = jnp.concatenate([projector_weight_gradient.astype(BF), weight_chunk, bias_rows], axis=0)
    count = own.shape[0]
    arrived = lax.all_to_all(
        jnp.broadcast_to(own[None], (cols, count, places)), "col", 0, 0, tiled=True
    )
    added = jnp.sum(arrived.astype(F32), axis=0)
    bias_at = 2 * hidden + weight_lines

    def split_bias(lines_of):
        flat = lines_of.reshape(-1)
        out = flat[:channels] + flat[channels : 2 * channels]
        flat = flat[2 * channels :]
        return out, flat[: 2 * hidden] + flat[2 * hidden : 4 * hidden]

    first, second = split_bias(added[bias_at:])
    bias_rows = jnp.concatenate(list(high_low(first)) + list(high_low(second)), axis=0)
    bias_rows = jnp.pad(bias_rows, (0, 16 * places - bias_rows.shape[0])).reshape(16, places)
    own = jnp.concatenate([added[:bias_at].astype(BF), bias_rows], axis=0)
    arrived = lax.all_to_all(
        jnp.broadcast_to(own[None], (rows, count, places)), "row", 0, 0, tiled=True
    ).astype(F32)
    weight_total = arrived[:, 2 * hidden : bias_at].reshape(rows * weight_lines, places)
    weight_total = jnp.concatenate(
        [weight_total[:, i : i + channels] for i in range(0, places, channels)], axis=0
    )
    weight_total = weight_total.reshape(hidden, hidden, channels).transpose(1, 0, 2)
    weight_total = weight_total.reshape(hidden * hidden, channels)
    projector_total = jnp.sum(arrived[:, : 2 * hidden], axis=0).T
    first, second = split_bias(jnp.sum(arrived[:, bias_at:], axis=0))

    normalized_gradient = jnp.einsum(
        "shr,ch->src", proj_grad, lowering_matrix, preferred_element_type=F32
    )
    discarded_value, backward_function = jax.vjp(layer_normalize, presence_real)
    alignment_gradient = backward_function(normalized_gradient)[0].astype(BF)
    return (
        pair_increment,
        alignment_gradient,
        projector_total,
        second,
        weight_total,
        first,
    )


def solution(mesh):
    in_specs = (
        P("row", "col", None),
        P("row", "col"),
        P("col"),
        P(),
        P(),
        P(),
        P(),
        P("row", "col", None),
    )
    out_specs = (P("row", "col", None), P("row", "col", None), P(), P(), P(), P())
    return jax.shard_map(
        per_device, mesh=mesh, in_specs=in_specs, out_specs=out_specs, check_vma=False
    )
```

time: 211 us -> 187 us (0.89)
  Pallas kernels: 0 us -> 27.3 us
  matrix products: 28 us -> 1.16 us
  local copies, waits for them, and re-layouts: 29.2 us -> 10.6 us
  other arithmetic: 10.3 us -> 6.28 us
  starting transfers between devices: 49.1 us -> 52.2 us
    pallas_call x0 -> x3, Pallas kernels: none -> 27.3 us  [the longest x1 11.4 us: main_first(): pl.pallas_call(functools.partial(first_kernel, shape), grid=(hidden // e_...]
    dot_general x14 -> x2, matrix products: 27.4 us -> 0.52 us  [the longest x1 0.26 us: per_device(): jnp.einsum('src,ch->rsh', normalized_alignment, lowering_matrix[:, :hidde...]
    reshape x7 -> x1, local copies, waits for them, and re-layouts: 6.67 us -> 0.15 us  [per_device(): weights = weights.reshape(hidden * hidden, channels)]
    transpose x3 -> x2, local copies, waits for them, and re-layouts: 6.44 us -> 1.21 us  [the longest x1 1.1 us: per_device(): weight_total.reshape(hidden, hidden, channels).transpose(1, 0, 2)]
    ppermute x6, waiting for transfers between devices: 8.93 us -> 3.75 us  [the longest x3 3.74 us: column_near(): lax.ppermute(sent, 'col', [(a + d, a) for a in range(0, cols, STEP)])]
    concatenate x2 -> x0, local copies, waits for them, and re-layouts: 4.23 us -> none  [the longest x1 4.16 us: per_device(): jnp.concatenate([jnp.broadcast_to(proj_pair[hidden:].reshape(1, pieces, p...]
    all_to_all x1, starting transfers between devices: 3.63 us -> 7.02 us  [per_device(): lax.all_to_all(jnp.broadcast_to(own[None], (cols, count, places)), 'col',...]
    reduce_sum x2 -> x0, other arithmetic: 3.03 us -> none  [block_step(): bias_gradient = bias_gradient + jnp.sum(scaled.astype(F32), axis=(0, 1))]
  transfers between devices with their start and end apart: 16 -> 16, of which waited for: 12 -> 11; matrix products, arithmetic and copies ran while one was open for 2% -> 1% of each run, Pallas kernels for 0% -> 9%
where the time goes in v2:
time: 187 us; the launch traced here: 186 us
  waiting for transfers between devices  87.7 us (47%)
  starting transfers between devices  52.2 us (28%)
  Pallas kernels  27.3 us (15%)
  local copies, waits for them, and re-layouts  10.6 us (6%)
  other arithmetic  6.28 us (3%)
    all_to_all x2, waiting for transfers between devices, per_device(): arrived = lax.all_to_all(packed, 'row', 0, 0, tiled=True)  41.7 us
    all_to_all x1, waiting for transfers between devices, per_device(): lax.all_to_all(jnp.broadcast_to(own[None], (cols, count, places)), 'col',...  22.6 us
    all_to_all x1, waiting for transfers between devices, per_device(): lax.all_to_all(jnp.broadcast_to(own[None], (rows, count, places)), 'row',...  14.4 us
    all_to_all x2, starting transfers between devices, per_device(): arrived = lax.all_to_all(packed, 'row', 0, 0, tiled=True)  14.4 us
    ppermute x3, starting transfers between devices, column_spread(): lax.ppermute(block, 'col', [(0, d)])  11.6 us
    pallas_call x1, Pallas kernels, main_first(): pl.pallas_call(functools.partial(first_kernel, shape), grid=(hidden // e_...  11.4 us
    pallas_call x1, Pallas kernels, main_second(): pl.pallas_call(functools.partial(second_kernel, shape), grid=(hidden // e...  10.4 us
    all_to_all x1, starting transfers between devices, per_device(): lax.all_to_all(jnp.broadcast_to(own[None], (rows, count, places)), 'row',...  7.57 us
  transfers between devices with their start and end apart: 16, of which 11 were waited for; matrix products, arithmetic and copies ran while one was open for 1% of the time, Pallas kernels for 9%

profile of v2, /device:TPU:1, one launch (start us, length us, event | category | flops | bytes accessed | tf_op | source)
XLA Modules:
  0.0 186.4 jit_solution(8798822236140014564)
XLA Ops:
  1.5 1.2 copy.61
  3.4 8.8 %collective-permute-start.2 = (bf16[256,256]{0,1:T(8,128)(2,1)S(1)}, bf16[256,256]{0,1:T(8,128)(2,1)S(1)}, u32[]{:S(2)}, u32[]{:S(2)}) collective-permute-start(bf16[256,256]{0,1:T(8,128)(2,1)S(1)} %pad_maximum_fusion.2), channel_id=1, source_target_pairs={{0,12},{16,28},{32,44},{48,60},{64,76},{80,92},{96,108},{112,124},... | collective-permute-start | bytes 393224 | tf_op jit(solution)/shard_map/ppermute | solution.py:24
  12.2 1.6 collective-permute-start.1
  13.7 1.3 collective-permute-start
  15.9 2.8 %collective-permute-done = bf16[256,256]{0,1:T(8,128)(2,1)S(1)} collective-permute-done((bf16[256,256]{0,1:T(8,128)(2,1)S(1)}, bf16[256,256]{0,1:T(8,128)(2,1)S(1)}, u32[]{:S(2)}, u32[]{:S(2)}) %collective-permute-start) | collective-permute-done | bytes 131104 | tf_op jit(solution)/shard_map/ppermute | solution.py:24
  18.8 1.3 collective-permute-start.5
  20.1 1.3 collective-permute-start.4
  21.4 1.3 collective-permute-start.3
  22.9 1.4 collective-permute-done.4
  24.9 1.2 pad_maximum_fusion
  26.0 9.2 %all-to-all-start = ((bf16[16,160,256]{2,1,0:T(8,128)(2,1)}), bf16[16,160,256]{2,1,0:T(8,128)(2,1)S(1)}, u32[]{:S(2)}, u32[]{:S(2)}) async-start(bf16[16,160,256]{2,1,0:T(8,128)(2,1)} %pad_maximum_fusion), calls=%async_computation | async-start | bytes 2621440 | tf_op jit(solution)/shard_map/all_to_all | solution.py:324
  35.4 20.1 %all-to-all-done.arrived = bf16[16,160,256]{2,1,0:T(8,128)(2,1)S(1)} async-done(((bf16[16,160,256]{2,1,0:T(8,128)(2,1)}), bf16[16,160,256]{2,1,0:T(8,128)(2,1)S(1)}, u32[]{:S(2)}, u32[]{:S(2)}) %all-to-all-start) | async-done | bytes 1310752 | tf_op jit(solution)/shard_map/all_to_all | solution.py:324
  55.4 1.2 copy-done.3
  56.6 11.4 %scaled_outer_grad.1 = (bf16[32,512,256]{2,1,0:T(8,128)(2,1)}, bf16[16,256,128]{2,1,0:T(8,128)(2,1)S(1)}, bf16[16,256,128]{2,1,0:T(8,128)(2,1)}, bf16[32,64,256]...) custom-call(bf16[16,160,256]{2,1,0:T(8,128)(2,1)} %copy-done.3, bf16[16,256,128]{2,1,0:T(8,128)(2,1)} %adjoint.1, ...), custom_call_target="tpu_custom_call" | custom-call | flops 1600000000 | bytes 16777216 | tf_op jit(solution)/shard_map/scaled_outer_grad/pallas_call | solution.py:177
  69.0 1.3 collective-permute-start.8
  70.3 1.3 collective-permute-start.7
  71.6 1.3 collective-permute-start.6
  73.0 1.9 collective-permute-done.8
  75.3 1.5 collective-permute-done.6
  76.8 1.3 collective-permute-start.11
  78.1 1.3 collective-permute-start.10
  79.4 1.3 collective-permute-start.9
  80.7 1.2 copy-done.2
  82.0 10.4 %outer_pair.1 = (bf16[16,256,128]{2,1,0:T(8,128)(2,1)}, f32[512,256]{1,0:T(8,128)S(1)}, bf16[64,512]{1,0:T(8,128)(2,1)S(1)}) custom-call(bf16[16,160,256]{2,1,0:T(8,128)(2,1)} %copy-done.3, bf16[32,64,256]{2,1,0:T(8,128)(2,1)S(1)} %copy-done.2, bf16[16,256,128]{2,1,0:T(8,128)(2,1)} %copy-done.1, bf16[16,256,128]{2,1,0:T(8,128)(2,1)} %get-tuple-element.17.d_ref, ...), custom_call_target="tpu_custom_call" | custom-call | flops 2600000000 | bytes 8388608 | tf_op jit(solution)/shard_map/outer_pair/pallas_call | solution.py:214
  92.3 5.5 %right_grad.1 = bf16[2048,256]{1,0:T(8,128)(2,1)S(1)} custom-call(bf16[64,512]{1,0:T(8,128)(2,1)S(1)} %get-tuple-element.19.left, bf16[32,512,256]{2,1,0:T(8,128)(2,1)} %get-tuple-element.20.g_ref), custom_call_target="tpu_custom_call" | custom-call | flops 540000000 | bytes 10485760 | tf_op jit(solution)/shard_map/right_grad/pallas_call | solution.py:250
  98.0 1.2 fusion.1
  99.2 5.2 %all-to-all-start.1 = ((bf16[16,176,256]{2,1,0:T(8,128)(2,1)}), bf16[16,176,256]{2,1,0:T(8,128)(2,1)S(1)}, u32[]{:S(2)}, u32[]{:S(2)}) async-start(bf16[16,176,256]{2,1,0:T(8,128)(2,1)} %fusion.1), calls=%async_computation.1 | async-start | bytes 2883584 | tf_op jit(solution)/shard_map/all_to_all | solution.py:353
  104.4 21.7 %all-to-all-done.1 = bf16[16,176,256]{2,1,0:T(8,128)(2,1)S(1)} async-done(((bf16[16,176,256]{2,1,0:T(8,128)(2,1)}), bf16[16,176,256]{2,1,0:T(8,128)(2,1)S(1)}, u32[]{:S(2)}, u32[]{:S(2)}) %all-to-all-start.1) | async-done | bytes 1441824 | tf_op jit(solution)/shard_map/all_to_all | solution.py:353
  128.3 7.0 %all-to-all-start.2 = ((bf16[16,112,256]{2,1,0:T(8,128)(2,1)}), bf16[16,112,256]{2,1,0:T(8,128)(2,1)S(1)}, u32[]{:S(2)}, u32[]{:S(2)}) async-start(bf16[16,112,256]{2,1,0:T(8,128)(2,1)} %broadcast_in_dim.37), calls=%async_computation.2 | async-start | bytes 1835008 | tf_op jit(solution)/shard_map/all_to_all | solution.py:373
  135.6 22.6 %all-to-all-done.2 = bf16[16,112,256]{2,1,0:T(8,128)(2,1)S(1)} async-done(((bf16[16,112,256]{2,1,0:T(8,128)(2,1)}), bf16[16,112,256]{2,1,0:T(8,128)(2,1)S(1)}, u32[]{:S(2)}, u32[]{:S(2)}) %all-to-all-start.2) | async-done | bytes 917536 | tf_op jit(solution)/shard_map/all_to_all | solution.py:373
  159.6 7.6 %all-to-all-start.3 = ((bf16[16,112,256]{2,1,0:T(8,128)(2,1)}), bf16[16,112,256]{2,1,0:T(8,128)(2,1)S(1)}, u32[]{:S(2)}, u32[]{:S(2)}) async-start(bf16[16,112,256]{2,1,0:T(8,128)(2,1)} %broadcast_in_dim.70), calls=%async_computation.3 | async-start | bytes 1835008 | tf_op jit(solution)/shard_map/all_to_all | solution.py:389
  168.7 14.4 %all-to-all-done.3 = bf16[16,112,256]{2,1,0:T(8,128)(2,1)S(1)} async-done(((bf16[16,112,256]{2,1,0:T(8,128)(2,1)}), bf16[16,112,256]{2,1,0:T(8,128)(2,1)S(1)}, u32[]{:S(2)}, u32[]{:S(2)}) %all-to-all-start.3) | async-done | bytes 917536 | tf_op jit(solution)/shard_map/all_to_all | solution.py:389
  (91 shorter events, 13.4 us)
Async XLA Ops:
  0.6 2.4 %copy-start.7 = (s32[256]{0:T(256)S(1)}, s32[256]{0:T(256)}, u32[]{:S(2)}) copy-start(s32[256]{0:T(256)} %param.10) | copy-start | bytes 3076
  0.6 2.4 %copy-start.6 = (s32[4,256]{1,0:T(4,128)S(1)}, s32[4,256]{1,0:T(4,128)}, u32[]{:S(2)}) copy-start(s32[4,256]{1,0:T(4,128)} %param.9) | copy-start | bytes 12292
  0.7 2.5 %copy-start.5 = (bf16[256,64]{0,1:T(8,128)(2,1)S(1)}, bf16[256,64]{0,1:T(8,128)(2,1)}, u32[]{:S(2)}) copy-start(bf16[256,64]{0,1:T(8,128)(2,1)} %param.11) | copy-start | bytes 98308
  3.4 11.7 %collective-permute-start.2 = (bf16[256,256]{0,1:T(8,128)(2,1)S(1)}, bf16[256,256]{0,1:T(8,128)(2,1)S(1)}, u32[]{:S(2)}, u32[]{:S(2)}) collective-permute-start(bf16[256,256]{0,1:T(8,128)(2,1)S(1)} %pad_maximum_fusion.2), channel_id=1, source_target_pairs={{0,12},{16,28},{32,44},{48,60},{64,76},{80,92},{96,108},{112,124},... | collective-permute-start | bytes 393224 | tf_op jit(solution)/shard_map/ppermute | solution.py:24
  12.2 3.7 %collective-permute-start.1 = (bf16[256,256]{0,1:T(8,128)(2,1)S(1)}, bf16[256,256]{0,1:T(8,128)(2,1)S(1)}, u32[]{:S(2)}, u32[]{:S(2)}) collective-permute-start(bf16[256,256]{0,1:T(8,128)(2,1)S(1)} %pad_maximum_fusion.2), channel_id=1, source_target_pairs={{0,8},{16,24},{32,40},{48,56},{64,72},{80,88},{96,104},{112,120},{... | collective-permute-start | bytes 393224 | tf_op jit(solution)/shard_map/ppermute | solution.py:24
  13.7 4.9 %collective-permute-start = (bf16[256,256]{0,1:T(8,128)(2,1)S(1)}, bf16[256,256]{0,1:T(8,128)(2,1)S(1)}, u32[]{:S(2)}, u32[]{:S(2)}) collective-permute-start(bf16[256,256]{0,1:T(8,128)(2,1)S(1)} %pad_maximum_fusion.2), channel_id=1, source_target_pairs={{0,4},{16,20},{32,36},{48,52},{64,68},{80,84},{96,100},{112,116},{... | collective-permute-start | bytes 393224 | tf_op jit(solution)/shard_map/ppermute | solution.py:24
  18.8 4.2 %collective-permute-start.5 = (bf16[256,256]{0,1:T(8,128)(2,1)S(1)}, bf16[256,256]{0,1:T(8,128)(2,1)S(1)}, u32[]{:S(2)}, u32[]{:S(2)}) collective-permute-start(bf16[256,256]{0,1:T(8,128)(2,1)S(1)} %add_select_fusion.1), channel_id=1, source_target_pairs={{0,3},{4,7},{8,11},{12,15},{16,19},{20,23},{24,27},{28,31},{32,35}... | collective-permute-start | bytes 393224 | tf_op jit(solution)/shard_map/ppermute | solution.py:27
  20.1 4.3 %collective-permute-start.4 = (bf16[256,256]{0,1:T(8,128)(2,1)S(1)}, bf16[256,256]{0,1:T(8,128)(2,1)S(1)}, u32[]{:S(2)}, u32[]{:S(2)}) collective-permute-start(bf16[256,256]{0,1:T(8,128)(2,1)S(1)} %add_select_fusion.1), channel_id=1, source_target_pairs={{0,2},{4,6},{8,10},{12,14},{16,18},{20,22},{24,26},{28,30},{32,34}... | collective-permute-start | bytes 393224 | tf_op jit(solution)/shard_map/ppermute | solution.py:27
  21.4 3.2 %collective-permute-start.3 = (bf16[256,256]{0,1:T(8,128)(2,1)S(1)}, bf16[256,256]{0,1:T(8,128)(2,1)S(1)}, u32[]{:S(2)}, u32[]{:S(2)}) collective-permute-start(bf16[256,256]{0,1:T(8,128)(2,1)S(1)} %add_select_fusion.1), channel_id=1, source_target_pairs={{0,1},{4,5},{8,9},{12,13},{16,17},{20,21},{24,25},{28,29},{32,33},... | collective-permute-start | bytes 393224 | tf_op jit(solution)/shard_map/ppermute | solution.py:27
  26.0 9.2 %copy-start.4 = (bf16[1024,128]{1,0:T(8,128)(2,1)S(1)}, bf16[1024,128]{1,0:T(8,128)(2,1)}, u32[]{:S(2)}) copy-start(bf16[1024,128]{1,0:T(8,128)(2,1)} %param.13) | copy-start | bytes 786436
  26.0 29.4 %all-to-all-start = ((bf16[16,160,256]{2,1,0:T(8,128)(2,1)}), bf16[16,160,256]{2,1,0:T(8,128)(2,1)S(1)}, u32[]{:S(2)}, u32[]{:S(2)}) async-start(bf16[16,160,256]{2,1,0:T(8,128)(2,1)} %pad_maximum_fusion), calls=%async_computation | async-start | bytes 2621440 | tf_op jit(solution)/shard_map/all_to_all | solution.py:324
  55.4 1.2 copy-start.3
  56.6 24.2 %copy-start = (f32[128]{0:T(128)S(1)}, f32[128]{0:T(128)}, u32[]{:S(2)}) copy-start(f32[128]{0:T(128)} %param.14) | copy-start | bytes 1540
  68.0 1.0 copy-start.1
  69.0 5.9 %collective-permute-start.8 = (bf16[256,128]{1,0:T(8,128)(2,1)S(1)}, bf16[256,128]{1,0:T(8,128)(2,1)S(1)}, u32[]{:S(2)}, u32[]{:S(2)}) collective-permute-start(bf16[256,128]{1,0:T(8,128)(2,1)S(1)} %convert_element_type.131), channel_id=1, source_target_pairs={{3,0},{7,4},{11,8},{15,12},{19,16},{23,20},{27,24},{31,28},{35,32}... | collective-permute-start | bytes 196616 | tf_op jit(solution)/shard_map/ppermute | solution.py:36
  70.3 5.0 %collective-permute-start.7 = (bf16[256,128]{1,0:T(8,128)(2,1)S(1)}, bf16[256,128]{1,0:T(8,128)(2,1)S(1)}, u32[]{:S(2)}, u32[]{:S(2)}) collective-permute-start(bf16[256,128]{1,0:T(8,128)(2,1)S(1)} %convert_element_type.131), channel_id=1, source_target_pairs={{2,0},{6,4},{10,8},{14,12},{18,16},{22,20},{26,24},{30,28},{34,32}... | collective-permute-start | bytes 196616 | tf_op jit(solution)/shard_map/ppermute | solution.py:36
  71.6 5.2 %collective-permute-start.6 = (bf16[256,128]{1,0:T(8,128)(2,1)S(1)}, bf16[256,128]{1,0:T(8,128)(2,1)S(1)}, u32[]{:S(2)}, u32[]{:S(2)}) collective-permute-start(bf16[256,128]{1,0:T(8,128)(2,1)S(1)} %convert_element_type.131), channel_id=1, source_target_pairs={{1,0},{5,4},{9,8},{13,12},{17,16},{21,20},{25,24},{29,28},{33,32},... | collective-permute-start | bytes 196616 | tf_op jit(solution)/shard_map/ppermute | solution.py:36
  76.8 21.1 %collective-permute-start.11 = (bf16[256,128]{1,0:T(8,128)(2,1)S(1)}, bf16[256,128]{1,0:T(8,128)(2,1)S(1)}, u32[]{:S(2)}, u32[]{:S(2)}) collective-permute-start(bf16[256,128]{1,0:T(8,128)(2,1)S(1)} %fusion.34), channel_id=1, source_target_pairs={{12,0},{28,16},{44,32},{60,48},{76,64},{92,80},{108,96},{124,112},... | collective-permute-start | bytes 196616 | tf_op jit(solution)/shard_map/ppermute | solution.py:44
  78.1 19.8 %collective-permute-start.10 = (bf16[256,128]{1,0:T(8,128)(2,1)S(1)}, bf16[256,128]{1,0:T(8,128)(2,1)S(1)}, u32[]{:S(2)}, u32[]{:S(2)}) collective-permute-start(bf16[256,128]{1,0:T(8,128)(2,1)S(1)} %fusion.34), channel_id=1, source_target_pairs={{8,0},{24,16},{40,32},{56,48},{72,64},{88,80},{104,96},{120,112},{... | collective-permute-start | bytes 196616 | tf_op jit(solution)/shard_map/ppermute | solution.py:44
  79.4 18.5 %collective-permute-start.9 = (bf16[256,128]{1,0:T(8,128)(2,1)S(1)}, bf16[256,128]{1,0:T(8,128)(2,1)S(1)}, u32[]{:S(2)}, u32[]{:S(2)}) collective-permute-start(bf16[256,128]{1,0:T(8,128)(2,1)S(1)} %fusion.34), channel_id=1, source_target_pairs={{4,0},{20,16},{36,32},{52,48},{68,64},{84,80},{100,96},{116,112},{... | collective-permute-start | bytes 196616 | tf_op jit(solution)/shard_map/ppermute | solution.py:44
  80.7 1.2 copy-start.2
  99.2 26.8 %all-to-all-start.1 = ((bf16[16,176,256]{2,1,0:T(8,128)(2,1)}), bf16[16,176,256]{2,1,0:T(8,128)(2,1)S(1)}, u32[]{:S(2)}, u32[]{:S(2)}) async-start(bf16[16,176,256]{2,1,0:T(8,128)(2,1)} %fusion.1), calls=%async_computation.1 | async-start | bytes 2883584 | tf_op jit(solution)/shard_map/all_to_all | solution.py:353
  128.3 30.0 %all-to-all-start.2 = ((bf16[16,112,256]{2,1,0:T(8,128)(2,1)}), bf16[16,112,256]{2,1,0:T(8,128)(2,1)S(1)}, u32[]{:S(2)}, u32[]{:S(2)}) async-start(bf16[16,112,256]{2,1,0:T(8,128)(2,1)} %broadcast_in_dim.37), calls=%async_computation.2 | async-start | bytes 1835008 | tf_op jit(solution)/shard_map/all_to_all | solution.py:373
  159.6 23.5 %all-to-all-start.3 = ((bf16[16,112,256]{2,1,0:T(8,128)(2,1)}), bf16[16,112,256]{2,1,0:T(8,128)(2,1)S(1)}, u32[]{:S(2)}, u32[]{:S(2)}) async-start(bf16[16,112,256]{2,1,0:T(8,128)(2,1)} %broadcast_in_dim.70), calls=%async_computation.3 | async-start | bytes 1835008 | tf_op jit(solution)/shard_map/all_to_all | solution.py:389

commit v3 on v0

v3 whole, which is shorter than its diff:
```python
import functools

import jax
import jax.numpy as jnp
from jax import lax
from jax.experimental import pallas as pl
from jax.experimental.pallas import tpu as pltpu
from jax.sharding import PartitionSpec as P

PAIRED = 16
CHAINS = 4
BF = jnp.bfloat16
F32 = jnp.float32
STEP = 4
GROUP = 16
E_BLOCK = 8


def dot(a, b, lhs, rhs):
    return lax.dot_general(a, b, (((lhs,), (rhs,)), ((), ())), preferred_element_type=F32)


def rows_at(start, size):
    return pl.ds(pl.multiple_of(start, GROUP), size)


def normal(values):
    center = values - jnp.mean(values, axis=-1, keepdims=True)
    spread = jnp.mean(center * center, axis=-1, keepdims=True)
    scale = lax.rsqrt(spread + 1e-05)
    return center * scale, scale


def project_kernel(dims, info, msa, present, label, weights, offset, normed, live_ref, send, keep, right, left):
    src, seqs, hidden, row_dev, places, half = dims
    pairs = src // 2
    me, core = info[0], lax.rem(info[0], 2)
    first = info[1] == 0
    seq = me * seqs + lax.broadcasted_iota(jnp.int32, (seqs, places), 0)
    chain = lax.rem(seq + (CHAINS - PAIRED % CHAINS), CHAINS)
    permitted = (seq < PAIRED) | (chain == jnp.broadcast_to(label[...], (seqs, places)))
    live = jnp.where(permitted & (present[...] == 1), 1.0, 0.0).astype(F32)
    live = jnp.concatenate([live, jnp.zeros((8 - seqs, places), F32)], axis=0)
    live_ref[...] = live
    weight = weights[...].astype(F32)
    right_w = weight[hidden:].astype(BF)
    left_w = jnp.concatenate([weight[:hidden]] * seqs, axis=0).T.astype(BF)
    lane = lax.broadcasted_iota(jnp.int32, left_w.shape, 1) // hidden
    column = jnp.broadcast_to(offset[...], (8, 2 * hidden)).T[hidden:, :1]
    total = jnp.zeros((places, seqs * hidden), F32)
    for s in range(seqs):
        value = normal(msa[s].astype(F32))[0].astype(BF)
        normed[s] = value
        out = (dot(right_w, value, 1, 1) + column) * live[s : s + 1]
        for h in range(2):
            right[pl.ds(h * seqs * hidden + s * hidden, hidden), :] = out[:, h * half : (h + 1) * half]
        total = total + dot(value, jnp.where(lane == s, left_w, jnp.zeros_like(left_w)), 1, 0)
    total = total + jnp.concatenate([offset[:, :hidden]] * seqs, axis=1)
    spot = lax.broadcasted_iota(jnp.int32, (8, seqs * hidden), 0)
    expand = jnp.where(spot == lax.broadcasted_iota(jnp.int32, (8, seqs * hidden), 1) // hidden, 1.0, 0.0)
    total = total * dot(live.T.astype(BF), expand.astype(BF), 1, 0)
    left[...] = jnp.where(first, total, 0.0)
    place = lax.broadcasted_iota(jnp.int32, (places, half), 0)
    slot = lax.broadcasted_iota(jnp.int32, (places, half), 1)
    base = seqs * hidden
    for ref, to in ((send, 1 - core), (keep, core)):
        pick = jnp.where(place == slot // row_dev * 2 * row_dev + to * row_dev + lax.rem(slot, row_dev), 1.0, 0.0)
        band = dot(live.astype(BF), pick.astype(BF), 1, 0)[:seqs]
        band = jnp.where(first, band, 0.0)
        own = jnp.where(to == 0, live[:seqs, :half], live[:seqs, half:])
        flags = jnp.concatenate([own, band, jnp.zeros((GROUP - 2 * seqs, half), F32)], axis=0)
        ref[pl.ds(0, base), :] = right[rows_at(to * base, base), :].astype(BF)
        ref[pl.ds(base, GROUP), :] = flags.astype(BF)
        for q in range(pairs):
            ref[pl.ds(base + GROUP + q * row_dev, row_dev), :] = left[
                rows_at(q * 2 * row_dev + to * row_dev, row_dev), :
            ].astype(BF)


def pack_right_kernel(dims, info, keep, came, out):
    src, seqs, hidden, row_dev, places, half = dims
    core = lax.rem(info[0], 2)
    base = seqs * hidden
    for ref, who in ((keep, core), (came, 1 - core)):
        value = ref[pl.ds(0, base), :]
        flags = ref[pl.ds(base, GROUP), :]
        for q in range(src // 2):
            out[q, rows_at(who * base, base), :] = value
            out[q, rows_at(2 * base + who * GROUP, GROUP), :] = flags


def pack_left_kernel(dims, info, tree, near_1, near_2, near_3, out):
    src, seqs, hidden, row_dev, places, half = dims
    pairs = src // 2
    core = lax.rem(info[0], 2)
    mixed = GROUP + pairs * row_dev
    for n, who in enumerate((core, 1 - core)):
        span = pl.ds(n * mixed, mixed)
        spread = tree[span, :] + near_1[span, :] + near_2[span, :] + near_3[span, :]
        for q in range(pairs):
            out[q, rows_at(who * row_dev, row_dev), :] = spread[GROUP + q * row_dev : GROUP + (q + 1) * row_dev]
            out[q, rows_at(2 * row_dev + who * GROUP, GROUP), :] = spread[:GROUP]


def unpack_right_kernel(dims, info, mine, other, weights, r_ref, live_t_ref, by_e, by_e_t, r_all, flags, w_all):
    src, seqs, hidden, row_dev, places, half = dims
    base = seqs * hidden
    lines = src * base
    core = lax.rem(info[0], 2)
    for ref, h in ((mine, core), (other, 1 - core)):
        for q in range(src // 2):
            r_all[rows_at(h * lines + q * 2 * base, 2 * base), :] = ref[q, : 2 * base, :].astype(F32)
            flags[rows_at((h * src + 2 * q) * GROUP, 2 * GROUP), :] = ref[q, 2 * base :, :].astype(F32)
    w_all[...] = weights[...].astype(F32)
    for e in range(hidden):
        for h in range(2):
            rows = [r_all[pl.ds(h * lines + s * hidden + e, src, stride=base), :] for s in range(seqs)]
            r_ref[e, :, pl.ds(h * half, half)] = jnp.concatenate(rows, axis=0).astype(BF)
    for e in range(0, hidden, 4):
        rows = [w_all[pl.ds(e + n, hidden, stride=hidden), :] for n in range(4)]
        part = jnp.concatenate(rows, axis=0)
        by_e[pl.ds(e * hidden, 4 * hidden), :] = part.astype(BF)
        by_e_t[:, pl.ds(e * hidden, 4 * hidden)] = part.T.astype(BF)
    for h in range(2):
        rows = [flags[pl.ds(h * src * GROUP + s, src, stride=GROUP), :] for s in range(seqs)]
        live_t_ref[pl.ds(h * half, half), :] = jnp.concatenate(rows, axis=0).T.astype(BF)


def first_kernel(dims, info, arrived, r_ref, live_t, adjoint, weights, g_ref, s_ref, d_ref, left_ref, bias_ref, left_out, left_t, tiles, total):
    src, seqs, hidden, row_dev, places, half = dims
    step = pl.program_id(0)

    @pl.when(step == 0)
    def _():
        pair = info[0] // 2
        for q in range(src // 2):
            tiles[pl.ds(q * 2 * GROUP, 2 * GROUP), :] = arrived[q, 2 * row_dev :, :].astype(F32)
        rows = [tiles[pl.ds(seqs + s, src, stride=GROUP), :] for s in range(seqs)]
        band = jnp.concatenate(rows, axis=0).astype(BF)
        for q in range(src // 2):
            tiles[pl.ds(q * 2 * row_dev, 2 * row_dev), :] = arrived[q, : 2 * row_dev, :].astype(F32)
        blocks = []
        for i in range(row_dev):
            tile = tiles[pl.ds(i, src, stride=row_dev), :]
            blocks.append(jnp.concatenate([tile[:, s * hidden : (s + 1) * hidden] for s in range(seqs)], axis=0))
        left = jnp.concatenate(blocks, axis=1)
        left_out[...] = left.astype(BF)
        left_t[...] = left.T.astype(BF)
        spot = lax.broadcasted_iota(jnp.int32, (half, half), 0) - pair * row_dev
        bias = jnp.zeros((1, half), F32)
        for i in range(row_dev):
            column = dot(band, jnp.where(spot == i, 1.0, 0.0).astype(BF), 1, 0).astype(BF)
            divisor = jnp.maximum(dot(live_t[...], column, 1, 0), 1.0)
            scaled = (adjoint[i].astype(F32) / divisor).astype(BF)
            d_ref[i] = divisor.astype(BF)
            s_ref[i] = scaled
            bias = bias + jnp.sum(scaled.astype(F32), axis=0, keepdims=True)
        bias_ref[...] = bias
        total[...] = jnp.zeros_like(total)

    part = weights[pl.ds(step * E_BLOCK * hidden, E_BLOCK * hidden), :]
    for i in range(row_dev):
        g = dot(part, s_ref[i], 1, 1).astype(BF)
        g_ref[:, pl.ds(i * hidden, hidden), :] = g.reshape(E_BLOCK, hidden, places)
    acc = total[...]
    for e in range(E_BLOCK):
        acc = acc + dot(r_ref[step * E_BLOCK + e], g_ref[e], 1, 1)
    total[...] = acc

    @pl.when(step == pl.num_programs(0) - 1)
    def _():
        for i in range(row_dev):
            block = acc[:, i * hidden : (i + 1) * hidden]
            left_ref[pl.ds(i, src, stride=row_dev), :] = jnp.concatenate(
                [block[s * src : (s + 1) * src] for s in range(seqs)], axis=1
            )


def second_kernel(dims, info, left_t, r_ref, s_ref, d_ref, weights_t, offset, pair_ref, keep, send, outer, before, held):
    src, seqs, hidden, row_dev, places, half = dims
    step = pl.program_id(0)
    block_lines = E_BLOCK * hidden

    @pl.when(step == 0)
    def _():
        before[...] = jnp.zeros_like(before)

    for e in range(E_BLOCK):
        outer[e] = dot(left_t[...], r_ref[e], 1, 0).astype(BF)
    acc = jnp.zeros((block_lines, half), F32)
    for i in range(row_dev):
        block = outer[:, pl.ds(i * hidden, hidden), :].reshape(block_lines, places)
        before[i] = before[i] + dot(weights_t[...], block, 1, 0)
        acc = acc + dot(block, s_ref[i], 1, 0)
    held[rows_at(step * block_lines, block_lines), :] = acc

    @pl.when(step == pl.num_programs(0) - 1)
    def _():
        core = lax.rem(info[0], 2)
        lines = hidden * hidden // 2
        keep[...] = held[rows_at(core * lines, lines), :]
        send[...] = held[rows_at((1 - core) * lines, lines), :].astype(BF)
        for i in range(row_dev):
            pair_ref[i] = ((before[i].T + offset[...]) / d_ref[i].astype(F32)).astype(BF)


def third_kernel(dims, info, left, g_ref, keep, send, held):
    src, seqs, hidden, row_dev, places, half = dims
    step = pl.program_id(0)
    base = seqs * hidden
    lines = src * base
    for e in range(E_BLOCK):
        grad = dot(left[...], g_ref[e], 1, 0)
        for h in range(2):
            for s in range(seqs):
                held[pl.ds(h * lines + s * hidden + step * E_BLOCK + e, src, stride=base), :] = grad[
                    s * src : (s + 1) * src, h * half : (h + 1) * half
                ]

    @pl.when(step == pl.num_programs(0) - 1)
    def _():
        core = lax.rem(info[0], 2)
        keep[...] = held[rows_at(core * lines, lines), :]
        send[...] = held[rows_at((1 - core) * lines, lines), :].astype(BF)


def pack_backward_kernel(dims, info, keep, came, w_keep, w_came, left, far_1, far_2, far_3, out):
    src, seqs, hidden, row_dev, places, half = dims
    pairs = src // 2
    lines = 2 * seqs * hidden
    w_lines = hidden * hidden // src
    total = left[...] + far_1[...].astype(F32) + far_2[...].astype(F32) + far_3[...].astype(F32)
    total = jnp.where(info[1] == 0, total, 0.0).astype(BF)
    for q in range(pairs):
        span = pl.ds(q * lines, lines)
        out[q, pl.ds(0, lines), :] = (keep[span, :] + came[span, :].astype(F32)).astype(BF)
        span = pl.ds(q * w_lines, w_lines)
        out[q, pl.ds(lines, w_lines), :] = (w_keep[span, :] + w_came[span, :].astype(F32)).astype(BF)
        out[q, pl.ds(lines + w_lines, 2 * row_dev), :] = total[q * 2 * row_dev : (q + 1) * 2 * row_dev]


def unpack_backward_kernel(dims, info, arrived, send, keep, chunk, held):
    src, seqs, hidden, row_dev, places, half = dims
    pairs = src // 2
    base = seqs * hidden
    w_lines = hidden * hidden // src
    core = lax.rem(info[0], 2)
    total = arrived[0, : 2 * base + w_lines, :].astype(F32)
    for q in range(1, pairs):
        total = total + arrived[q, : 2 * base + w_lines, :].astype(F32)
    held[...] = total[: 2 * base]
    chunk[...] = total[2 * base :].astype(BF)
    for ref, to in ((send, 1 - core), (keep, core)):
        ref[pl.ds(0, base), :] = held[rows_at(to * base, base), :].astype(BF)
        for q in range(pairs):
            ref[pl.ds(base + q * row_dev, row_dev), :] = arrived[
                q, rows_at(2 * base + w_lines + to * row_dev, row_dev), :
            ]


def projector_kernel(dims, info, keep, came, normed, live, bias, grads, w_keep, w_send, small, right, left):
    src, seqs, hidden, row_dev, places, half = dims
    base = seqs * hidden
    core = lax.rem(info[0], 2)
    for ref, who in ((keep, core), (came, 1 - core)):
        right[rows_at(who * base, base), :] = ref[pl.ds(0, base), :].astype(F32)
        for q in range(src // 2):
            left[rows_at(q * 2 * row_dev + who * row_dev, row_dev), :] = ref[
                pl.ds(base + q * row_dev, row_dev), :
            ].astype(F32)
    left_t = left[...].T
    weight = jnp.zeros((2 * hidden, places), F32)
    sums = jnp.zeros((8, 2 * hidden), F32)
    for s in range(seqs):
        span = slice(s * hidden, (s + 1) * hidden)
        right_s = jnp.concatenate([right[span, :], right[base + s * hidden : base + (s + 1) * hidden, :]], axis=1)
        grad = (jnp.concatenate([left_t[span], right_s], axis=0) * live[s : s + 1, :]).astype(BF)
        grads[pl.ds(s * 2 * hidden, 2 * hidden), :] = grad
        weight = weight + dot(grad, normed[s], 1, 0)
        sums = sums + dot(jnp.ones((8, places), BF), grad, 1, 1)
    low, high = weight[:, :half], weight[:, half:]
    w_keep[...] = jnp.where(core == 0, low, high)
    w_send[...] = jnp.where(core == 0, high, low).astype(BF)
    row = jnp.concatenate([sums[:1], jnp.zeros((1, half - 2 * hidden), F32)], axis=1)
    small[...] = bias_block(bias[...], row, half)


def bias_block(first, second, half):
    first_high, second_high = first.astype(BF).astype(F32), second.astype(BF).astype(F32)
    rows = [first_high, first - first_high, second_high, second - second_high]
    return jnp.concatenate(rows + [jnp.zeros((GROUP - 4, half), F32)], axis=0).astype(BF)


def align_kernel(dims, msa, grads, weights, out):
    src, seqs, hidden, row_dev, places, half = dims
    for s in range(seqs):
        grad = grads[pl.ds(s * 2 * hidden, 2 * hidden), :].astype(F32).T.astype(BF)
        grad = dot(grad, weights[...], 1, 0)
        value, scale = normal(msa[s].astype(F32))
        shift = jnp.mean(grad, axis=-1, keepdims=True)
        slope = jnp.mean(grad * value, axis=-1, keepdims=True)
        out[s] = (scale * (grad - shift - value * slope)).astype(BF)


def pack_column_kernel(dims, w_keep, w_came, chunk, small, out):
    weight = (w_keep[...] + w_came[...].astype(F32)).astype(BF)
    at = weight.shape[0]
    size = chunk.shape[0]
    for c in range(out.shape[0]):
        out[c, pl.ds(0, at), :] = weight
        out[c, pl.ds(at, size), :] = chunk[...]
        out[c, pl.ds(at + size, GROUP), :] = small[...]


def left_sum_kernel(dims, left, near_1, near_2, near_3, total, sent):
    value = left[...] + near_1[...].astype(F32) + near_2[...].astype(F32) + near_3[...].astype(F32)
    total[...] = value
    sent[...] = value.astype(BF)


def pack_row_kernel(dims, arrived, out):
    total = arrived[0].astype(F32)
    for c in range(1, arrived.shape[0]):
        total = total + arrived[c].astype(F32)
    at = total.shape[0] - GROUP
    last = total[at:]
    small = bias_block(last[0:1] + last[1:2], last[2:3] + last[3:4], last.shape[1])
    total = total[:at].astype(BF)
    for q in range(out.shape[0]):
        out[q, pl.ds(0, at), :] = total
        out[q, pl.ds(at, GROUP), :] = small


def finish_kernel(dims, info, mine, other, projector, projector_bias, weight, bias, held):
    src, seqs, hidden, row_dev, places, half = dims
    core = lax.rem(info[0], 2)
    w_lines = hidden * hidden // src
    at = 2 * hidden + w_lines
    sums = []
    small = jnp.zeros((GROUP, half), F32)
    for ref, who in ((mine, core), (other, 1 - core)):
        total = jnp.zeros((2 * hidden, half), F32)
        for q in range(src // 2):
            total = total + ref[q, : 2 * hidden, :].astype(F32)
            small = small + ref[q, at : at + GROUP, :].astype(F32)
            held[rows_at(who * (hidden * hidden // 2) + q * w_lines, w_lines), :] = ref[
                q, 2 * hidden : at, :
            ].astype(F32)
        sums.append(total)
    first = jnp.where(core == 0, sums[0], sums[1])
    second = jnp.where(core == 0, sums[1], sums[0])
    projector[...] = jnp.concatenate([first, second], axis=1)
    bias[...] = small[0:1] + small[1:2]
    projector_bias[...] = (small[2:3] + small[3:4])[:, : 2 * hidden]
    for c in range(hidden):
        weight[pl.ds(c * hidden, hidden), :] = held[pl.ds(c, hidden, stride=hidden), :]


def shape_of(dtype, *shape):
    return jax.ShapeDtypeStruct(shape, dtype)


def whole(*shape):
    return pl.BlockSpec(shape, lambda t: (0,) * len(shape))


SCALARS = pl.BlockSpec(memory_space=pltpu.SMEM)


def call(kernel, dims, name, args, outs, scratch=(), steps=1, in_specs=None, out_specs=None, macs=0, room=24):
    in_specs, out_specs = in_specs or {}, out_specs or {}
    specs = [
        SCALARS if a.dtype == jnp.int32 and a.ndim == 1 else in_specs.get(n, whole(*a.shape))
        for n, a in enumerate(args)
    ]
    size = sum(a.size * a.dtype.itemsize for a in args)
    size += sum(o.size * jnp.dtype(o.dtype).itemsize for o in outs)
    result = pl.pallas_call(
        functools.partial(kernel, dims),
        grid=(steps,),
        in_specs=specs,
        out_specs=[out_specs.get(n, whole(*o.shape)) for n, o in enumerate(outs)],
        out_shape=list(outs),
        scratch_shapes=[pltpu.VMEM(s, t) for s, t in scratch],
        compiler_params=pltpu.CompilerParams(
            dimension_semantics=("arbitrary",), vmem_limit_bytes=room * 2**20
        ),
        cost_estimate=pl.CostEstimate(flops=40 * macs, bytes_accessed=size, transcendentals=0),
        name=name,
    )(*args)
    return result


def near_parts(block, cols):
    return [
        lax.ppermute(block, "col", [(a, a + d) for a in range(0, cols, STEP)])
        for d in range(1, STEP)
    ]


def per_device(
    homolog_features,
    presence_indicator,
    polymer_label,
    lowering_matrix,
    lowering_offset,
    outgoing_matrix,
    outgoing_offset,
    update_adjoint,
):
    seqs, places, depth = homolog_features.shape
    hidden = lowering_matrix.shape[1] // 2
    channels = outgoing_matrix.shape[1]
    row_dev = update_adjoint.shape[0]
    rows, cols = lax.axis_size("row"), lax.axis_size("col")
    pairs, half = rows // 2, channels
    dims = (rows, seqs, hidden, row_dev, places, half)
    base = seqs * hidden
    total = rows * seqs
    lines = row_dev * hidden
    w_lines = hidden * hidden // rows
    info = jnp.stack([lax.axis_index("row"), lax.axis_index("col")]).astype(jnp.int32)
    swap = [(i, i ^ 1) for i in range(rows)]
    same_core = [list(range(c, rows, 2)) for c in range(2)]

    def partner(block):
        return lax.ppermute(block, "row", swap)

    def over_pairs(block):
        return lax.all_to_all(block, "row", 0, 0, axis_index_groups=same_core, tiled=True)

    size = base + GROUP + pairs * row_dev
    normed, live, send, keep = call(
        project_kernel,
        dims,
        "project",
        (info, homolog_features, presence_indicator, polymer_label[None], lowering_matrix.T, lowering_offset[None]),
        (
            shape_of(BF, seqs, places, depth),
            shape_of(F32, 8, places),
            shape_of(BF, size, half),
            shape_of(BF, size, half),
        ),
        [((2 * base, half), F32), ((places, base), F32)],
        macs=100_000_000,
    )
    came = partner(send)

    tree = jnp.concatenate([keep[base:], came[base:]], axis=0)
    far = [lax.ppermute(tree, "col", [(0, d)]) for d in range(STEP, cols, STEP)]
    tree = sum(far, tree)
    near = near_parts(tree, cols)
    packed = call(
        pack_right_kernel,
        dims,
        "pack_right",
        (info, keep, came),
        (shape_of(BF, pairs, 2 * (base + GROUP), half),),
    )[0]
    mine = over_pairs(packed)
    mine, *near = lax.optimization_barrier((mine, *near))
    packed = call(
        pack_left_kernel,
        dims,
        "pack_left",
        (info, tree, *near),
        (shape_of(BF, pairs, 2 * (GROUP + row_dev), half),),
    )[0]
    arrived = over_pairs(packed)
    other = partner(mine)
    right_cols, live_t, by_e, by_e_t = call(
        unpack_right_kernel,
        dims,
        "unpack_right",
        (info, mine, other, outgoing_matrix),
        (
            shape_of(BF, hidden, total, places),
            shape_of(BF, places, total),
            shape_of(BF, hidden * hidden, channels),
            shape_of(BF, channels, hidden * hidden),
        ),
        [
            ((2 * rows * base, half), F32),
            ((2 * rows * GROUP, half), F32),
            ((hidden * hidden, channels), F32),
        ],
        macs=300_000_000,
    )

    by_block = lambda *block: pl.BlockSpec((E_BLOCK, *block), lambda t: (t, 0, 0))
    outer_grad, scaled, divisor, left_grad, bias_grad, left_rows, left_t = call(
        first_kernel,
        dims,
        "scaled_outer_grad",
        (info, arrived, right_cols, live_t, update_adjoint, by_e),
        (
            shape_of(BF, hidden, lines, places),
            shape_of(BF, row_dev, places, channels),
            shape_of(BF, row_dev, places, channels),
            shape_of(F32, rows * row_dev, half),
            shape_of(F32, 1, channels),
            shape_of(BF, total, lines),
            shape_of(BF, lines, total),
        ),
        [((rows * GROUP, half), F32), ((total, lines), F32)],
        steps=hidden // E_BLOCK,
        out_specs={0: by_block(lines, places)},
        macs=800_000_000,
        room=32,
    )

    sent = left_grad.astype(BF)
    near = [
        lax.ppermute(sent, "col", [(a + d, a) for a in range(0, cols, STEP)])
        for d in range(1, STEP)
    ]
    right_keep, right_send = call(
        third_kernel,
        dims,
        "right_grad",
        (info, left_rows, outer_grad),
        (shape_of(F32, rows * base, half), shape_of(BF, rows * base, half)),
        [((2 * rows * base, half), F32)],
        steps=hidden // E_BLOCK,
        in_specs={2: by_block(lines, places)},
        macs=270_000_000,
        room=32,
    )
    *near, right_send = lax.optimization_barrier((*near, right_send))
    left_grad, sent = call(
        left_sum_kernel,
        dims,
        "left_sum",
        (left_grad, *near),
        (shape_of(F32, rows * row_dev, half), shape_of(BF, rows * row_dev, half)),
    )
    left_t, sent = lax.optimization_barrier((left_t, sent))
    far = [lax.ppermute(sent, "col", [(d, 0)]) for d in range(STEP, cols, STEP)]
    pair_increment, w_keep, w_send = call(
        second_kernel,
        dims,
        "outer_pair",
        (info, left_t, right_cols, scaled, divisor, by_e_t, outgoing_offset[None]),
        (
            shape_of(BF, row_dev, places, channels),
            shape_of(F32, hidden * hidden // 2, channels),
            shape_of(BF, hidden * hidden // 2, channels),
        ),
        [
            ((E_BLOCK, lines, places), BF),
            ((row_dev, channels, places), F32),
            ((hidden * hidden, channels), F32),
        ],
        steps=hidden // E_BLOCK,
        in_specs={
            2: by_block(total, places),
            5: pl.BlockSpec((channels, E_BLOCK * hidden), lambda t: (0, t)),
        },
        macs=1_300_000_000,
        room=32,
    )
    w_send, *far = lax.optimization_barrier((w_send, *far))
    w_came = partner(w_send)
    right_came = partner(right_send)
    packed = call(
        pack_backward_kernel,
        dims,
        "pack_backward",
        (info, right_keep, right_came, w_keep, w_came, left_grad, *far),
        (shape_of(BF, pairs, 2 * base + w_lines + 2 * row_dev, half),),
    )[0]
    arrived = over_pairs(packed)

    send, keep, chunk = call(
        unpack_backward_kernel,
        dims,
        "unpack_backward",
        (info, arrived),
        (
            shape_of(BF, base + pairs * row_dev, half),
            shape_of(BF, base + pairs * row_dev, half),
            shape_of(BF, w_lines, half),
        ),
        [((2 * base, half), F32)],
    )
    came = partner(send)
    grads, w_keep, w_send, small = call(
        projector_kernel,
        dims,
        "projector_grad",
        (info, keep, came, normed, live, bias_grad),
        (
            shape_of(BF, seqs * 2 * hidden, places),
            shape_of(F32, 2 * hidden, half),
            shape_of(BF, 2 * hidden, half),
            shape_of(BF, GROUP, half),
        ),
        [((2 * base, half), F32), ((places, base), F32)],
        macs=20_000_000,
    )
    w_came = partner(w_send)
    size = 2 * hidden + w_lines + GROUP
    packed = call(
        pack_column_kernel, dims, "pack_column", (w_keep, w_came, chunk, small), (shape_of(BF, cols, size, half),)
    )[0]
    arrived = lax.all_to_all(packed, "col", 0, 0, tiled=True)
    alignment_gradient = call(
        align_kernel,
        dims,
        "alignment",
        (homolog_features, grads, lowering_matrix.T),
        (shape_of(BF, seqs, places, depth),),
        macs=200_000_000,
    )[0]
    arrived, alignment_gradient = lax.optimization_barrier((arrived, alignment_gradient))
    packed = call(pack_row_kernel, dims, "pack_row", (arrived,), (shape_of(BF, pairs, size, half),))[0]
    mine = over_pairs(packed)
    other = partner(mine)
    projector, projector_bias, weight, bias = call(
        finish_kernel,
        dims,
        "finish",
        (info, mine, other),
        (
            shape_of(F32, 2 * hidden, depth),
            shape_of(F32, 1, 2 * hidden),
            shape_of(F32, hidden * hidden, channels),
            shape_of(F32, 1, channels),
        ),
        [((hidden * hidden, channels), F32)],
    )
    return (
        pair_increment,
        alignment_gradient,
        projector.T,
        projector_bias[0],
        weight,
        bias[0],
    )


def solution(mesh):
    in_specs = (
        P("row", "col", None),
        P("row", "col"),
        P("col"),
        P(),
        P(),
        P(),
        P(),
        P("row", "col", None),
    )
    out_specs = (P("row", "col", None), P("row", "col", None), P(), P(), P(), P())
    return jax.shard_map(
        per_device, mesh=mesh, in_specs=in_specs, out_specs=out_specs, check_vma=False
    )
```

time: 837 us -> 152 us (0.18)
  waiting for transfers between devices: 594 us -> 26.1 us
  blocking collectives: 155 us -> 27.3 us
  starting transfers between devices: 0.25 us -> 55 us
  Pallas kernels: 0 us -> 33.4 us
  matrix products: 29.3 us -> 0 us
  local copies, waits for them, and re-layouts: 33.6 us -> 8.4 us
  between operations: 14.3 us -> 0.95 us
    psum x3 -> x0, waiting for transfers between devices: 439 us -> none  [the longest x1 176 us: per_device(): lax.psum((projector_weight_gradient, projector_bias_gradient, weight_grad...]
    reduce_scatter x2 -> x0, waiting for transfers between devices: 155 us -> none  [the longest x1 81.8 us: per_device(): lax.psum_scatter(placed, 'row', scatter_dimension=0, tiled=True)]
    psum x2 -> x0, blocking collectives: 130 us -> none  [the longest x1 77.4 us: per_device(): lax.psum((projector_weight_gradient, projector_bias_gradient, weight_grad...]
    ppermute x0 -> x19, starting transfers between devices: none -> 36.1 us  [the longest x7 13.7 us: partner(): return lax.ppermute(block, 'row', swap)]
    pallas_call x0 -> x15, Pallas kernels: none -> 33.4 us  [call(): pl.pallas_call(functools.partial(kernel, dims), grid=(steps,), in_specs=s...]
    dot_general x16 -> x0, matrix products: 29.3 us -> none  [the longest x2 8.98 us: block_step(): jnp.einsum('icej,sej->sci', outer_grad, right_cols, preferred_element_typ...]
    all_to_all x0 -> x2, blocking collectives: none -> 27.3 us  [over_pairs(): lax.all_to_all(block, 'row', 0, 0, axis_index_groups=same_core, tiled=True)]
    all_gather x1 -> x0, blocking collectives: 25.7 us -> none  [per_device(): lax.all_gather(active_mask.astype(jnp.bfloat16), 'row', axis=0, tiled=True)]
  transfers between devices with their start and end apart: 6 -> 22, of which waited for: 5 -> 12; matrix products, arithmetic and copies ran while one was open for 3% -> 0% of each run, Pallas kernels for 0% -> 12%
where the time goes in v3:
time: 152 us; the launch traced here: 151 us
  starting transfers between devices  55 us (36%)
  Pallas kernels  33.4 us (22%)
  blocking collectives  27.3 us (18%)
  waiting for transfers between devices  26.1 us (17%)
  local copies, waits for them, and re-layouts  8.4 us (6%)
    pallas_call x15, Pallas kernels, call(): pl.pallas_call(functools.partial(kernel, dims), grid=(steps,), in_specs=s...  33.4 us
    all_to_all x2, blocking collectives, over_pairs(): lax.all_to_all(block, 'row', 0, 0, axis_index_groups=same_core, tiled=True)  27.3 us
    all_to_all x1, waiting for transfers between devices, per_device(): arrived = lax.all_to_all(packed, 'col', 0, 0, tiled=True)  15.5 us
    ppermute x7, starting transfers between devices, partner(): return lax.ppermute(block, 'row', swap)  13.7 us
    all_to_all x2, starting transfers between devices, over_pairs(): lax.all_to_all(block, 'row', 0, 0, axis_index_groups=same_core, tiled=True)  11.8 us
    ppermute x3, starting transfers between devices, per_device(): far = [lax.ppermute(tree, 'col', [(0, d)]) for d in range(STEP, cols, STEP)]  10.8 us
    unnamed x34, local copies, waits for them, and re-layouts  8.39 us
    all_to_all x1, starting transfers between devices, per_device(): arrived = lax.all_to_all(packed, 'col', 0, 0, tiled=True)  7.03 us
  transfers between devices with their start and end apart: 22, of which 12 were waited for; matrix products, arithmetic and copies ran while one was open for 0% of the time, Pallas kernels for 12%

profile of v3, /device:TPU:1, one launch (start us, length us, event | category | flops | bytes accessed | tf_op | source)
XLA Modules:
  0.0 151.3 jit_solution(16697803581871094895)
XLA Ops:
  4.5 1.4 project.1
  5.9 3.3 %collective-permute-start = (bf16[272,128]{1,0:T(8,128)(2,1)S(1)}, bf16[272,128]{1,0:T(8,128)(2,1)S(1)}, u32[]{:S(2)}, u32[]{:S(2)}) collective-permute-start(bf16[272,128]{1,0:T(8,128)(2,1)S(1)} %get-tuple-element.56), channel_id=1, source_target_pairs={{0,16},{16,0},{32,48},{48,32},{64,80},{80,64},{96,112},{112,96},{1... | collective-permute-start | bytes 208904 | tf_op jit(solution)/shard_map/ppermute | solution.py:427
  10.2 1.4 pack_right.1
  11.6 4.9 %all-to-all-start = ((bf16[8,288,128]{2,1,0:T(8,128)(2,1)}), bf16[8,288,128]{2,1,0:T(8,128)(2,1)S(1)}, u32[]{:S(2)}, u32[]{:S(2)}) async-start(bf16[8,288,128]{2,1,0:T(8,128)(2,1)} %pack_right.1), calls=%async_computation | async-start | bytes 1179648 | tf_op jit(solution)/shard_map/all_to_all | solution.py:430
  16.5 4.9 %collective-permute-start.1 = (bf16[288,128]{1,0:T(8,128)(2,1)S(1)}, bf16[288,128]{1,0:T(8,128)(2,1)S(1)}, u32[]{:S(2)}, u32[]{:S(2)}) collective-permute-start(bf16[288,128]{1,0:T(8,128)(2,1)S(1)} %pad_maximum_fusion), channel_id=1, source_target_pairs={{0,4},{16,20},{32,36},{48,52},{64,68},{80,84},{96,100},{112,116},{... | collective-permute-start | bytes 221192 | tf_op jit(solution)/shard_map/ppermute | solution.py:450
  21.5 4.6 %collective-permute-start.2 = (bf16[288,128]{1,0:T(8,128)(2,1)S(1)}, bf16[288,128]{1,0:T(8,128)(2,1)S(1)}, u32[]{:S(2)}, u32[]{:S(2)}) collective-permute-start(bf16[288,128]{1,0:T(8,128)(2,1)S(1)} %pad_maximum_fusion), channel_id=1, source_target_pairs={{0,8},{16,24},{32,40},{48,56},{64,72},{80,88},{96,104},{112,120},{... | collective-permute-start | bytes 221192 | tf_op jit(solution)/shard_map/ppermute | solution.py:450
  26.0 1.3 collective-permute-start.3
  27.4 1.3 collective-permute-done.3
  28.8 1.3 collective-permute-start.4
  30.1 1.3 collective-permute-start.5
  31.4 1.3 collective-permute-start.6
  32.8 1.7 %collective-permute-done.6.near_3 = bf16[288,128]{1,0:T(8,128)(2,1)S(1)} collective-permute-done((bf16[288,128]{1,0:T(8,128)(2,1)S(1)}, bf16[288,128]{1,0:T(8,128)(2,1)S(1)}, u32[]{:S(2)}, u32[]{:S(2)}) %collective-permute-start.6) | collective-permute-done | bytes 73760 | tf_op jit(solution)/shard_map/ppermute | solution.py:396
  34.5 1.7 %collective-permute-start.7 = (bf16[8,288,128]{2,1,0:T(8,128)(2,1)S(1)}, bf16[8,288,128]{2,1,0:T(8,128)(2,1)S(1)}, u32[]{:S(2)}, u32[]{:S(2)}) collective-permute-start(bf16[8,288,128]{2,1,0:T(8,128)(2,1)S(1)} %all-to-all-done.mine), channel_id=1, source_target_pairs={{0,16},{16,0},{32,48},{48,32},{64,80},{80,64},{96,112},{112,96},{1... | collective-permute-start | bytes 1769480 | tf_op jit(solution)/shard_map/ppermute | solution.py:427
  37.4 6.9 %all-to-all-start.1 = ((bf16[8,64,128]{2,1,0:T(8,128)(2,1)}), bf16[8,64,128]{2,1,0:T(8,128)(2,1)S(1)}, u32[]{:S(2)}, u32[]{:S(2)}) async-start(bf16[8,64,128]{2,1,0:T(8,128)(2,1)} %pack_left.1), calls=%async_computation.1 | async-start | bytes 262144 | tf_op jit(solution)/shard_map/all_to_all | solution.py:430
  44.3 2.8 %unpack_right.1 = (bf16[32,64,256]{2,1,0:T(8,128)(2,1)S(1)}, bf16[256,64]{1,0:T(8,128)(2,1)S(1)}, bf16[1024,128]{1,0:T(8,128)(2,1)S(1)}, bf16[128,1024]{1,0:T(8,128)(2,1)S(1)}) custom-call(s32[2]{0:T(128)S(1)} %pad_add_fusion.info, bf16[8,288,128]{2,1,0:T(8,128)(2,1)S(1)} %all-to-all-done.mine, bf16[8,288,128]{2,1,0:T(8,128)(2,1)S(1)} %collective-permute-done.7.other, ...), custom_call_target="tpu_custom_call" | custom-call | flops 12000000000 | bytes 3047432 | tf_op jit(solution)/shard_map/unpack_right/pallas_call | solution.py:378
  49.5 1.8 %all-to-all-done.1.arrived = bf16[8,64,128]{2,1,0:T(8,128)(2,1)S(1)} async-done(((bf16[8,64,128]{2,1,0:T(8,128)(2,1)}), bf16[8,64,128]{2,1,0:T(8,128)(2,1)S(1)}, u32[]{:S(2)}, u32[]{:S(2)}) %all-to-all-start.1) | async-done | bytes 131104 | tf_op jit(solution)/shard_map/all_to_all | solution.py:430
  53.4 7.8 %scaled_outer_grad.1 = (bf16[32,512,256]{2,1,0:T(8,128)(2,1)S(1)}, bf16[16,256,128]{2,1,0:T(8,128)(2,1)S(1)}, bf16[16,256,128]{2,1,0:T(8,128)(2,1)S(1)}, f32[256...) custom-call(s32[2]{0:T(128)S(1)} %pad_add_fusion.info, ...), custom_call_target="tpu_custom_call" | custom-call | flops 32000000000 | bytes 13271560 | tf_op jit(solution)/shard_map/scaled_outer_grad/pallas_call | solution.py:378
  61.2 1.3 collective-permute-start.10
  62.5 1.3 collective-permute-start.8
  63.8 1.3 collective-permute-start.9
  65.2 3.4 %right_grad.1 = (f32[2048,128]{1,0:T(8,128)S(1)}, bf16[2048,128]{1,0:T(8,128)(2,1)S(1)}) custom-call(s32[2]{0:T(128)S(1)} %pad_add_fusion.info, bf16[64,512]{1,0:T(8,128)(2,1)S(1)} %get-tuple-element.66.left, bf16[32,512,256]{2,1,0:T(8,128)(2,1)S(1)} %get-tuple-element.67.g_ref), custom_call_target="tpu_custom_call" | custom-call | flops 10800000000 | bytes 10027016 | tf_op jit(solution)/shard_map/right_grad/pallas_call | solution.py:378
  73.1 2.4 %collective-permute-start.11 = (bf16[2048,128]{1,0:T(8,128)(2,1)S(1)}, bf16[2048,128]{1,0:T(8,128)(2,1)S(1)}, u32[]{:S(2)}, u32[]{:S(2)}) collective-permute-start(bf16[2048,128]{1,0:T(8,128)(2,1)S(1)} %get-tuple-element.79), channel_id=1, source_target_pairs={{0,16},{16,0},{32,48},{48,32},{64,80},{80,64},{96,112},{112,96},{1... | collective-permute-start | bytes 1572872 | tf_op jit(solution)/shard_map/ppermute | solution.py:427
  75.4 8.7 %outer_pair.1 = (bf16[16,256,128]{2,1,0:T(8,128)(2,1)}, f32[512,128]{1,0:T(8,128)S(1)}, bf16[512,128]{1,0:T(8,128)(2,1)S(1)}) custom-call(s32[2]{0:T(128)S(1)} %pad_add_fusion.info, bf16[512,64]{1,0:T(8,128)(2,1)S(1)} %get-tuple-element.73.left_t, bf16[32,64,256]{2,1,0:T(8,128)(2,1)S(1)} %copy-done.12, bf16[16,256,128]{2,1,0:T(8,128)(2,1)S(1)} %get-tuple-element.74.s_ref, ...), custom_call_target="tpu_custom_call" | custom-call | flops 51999997952 | bytes 4915720 | tf_op jit(solution)/shard_map/outer_pair/pallas_call | solution.py:378
  84.5 1.3 collective-permute-done.15.w_came
  86.5 16.9 %all_to_all.25.arrived = bf16[8,352,128]{2,1,0:T(8,128)(2,1)S(1)} all-to-all(bf16[8,352,128]{2,1,0:T(8,128)(2,1)S(1)} %pack_backward.1), channel_id=1, replica_groups={{0,32,64,96,128,160,192,224},{16,48,80,112,144,176,208,240},{1,33,65,97..., dimensions={0} | all-to-all | bytes 1441792 | tf_op jit(solution)/shard_map/all_to_all | solution.py:430
  104.0 1.7 %collective-permute-start.16 = (bf16[256,128]{1,0:T(8,128)(2,1)S(1)}, bf16[256,128]{1,0:T(8,128)(2,1)S(1)}, u32[]{:S(2)}, u32[]{:S(2)}) collective-permute-start(bf16[256,128]{1,0:T(8,128)(2,1)S(1)} %get-tuple-element.89), channel_id=1, source_target_pairs={{0,16},{16,0},{32,48},{48,32},{64,80},{80,64},{96,112},{112,96},{1... | collective-permute-start | bytes 196616 | tf_op jit(solution)/shard_map/ppermute | solution.py:427
  109.6 7.0 %all-to-all-start.3 = ((bf16[16,144,128]{2,1,0:T(8,128)(2,1)}), bf16[16,144,128]{2,1,0:T(8,128)(2,1)S(1)}, u32[]{:S(2)}, u32[]{:S(2)}) async-start(bf16[16,144,128]{2,1,0:T(8,128)(2,1)} %pack_column.1), calls=%async_computation.3 | async-start | bytes 1179648 | tf_op jit(solution)/shard_map/all_to_all | solution.py:606
  116.7 1.8 %alignment.1 = bf16[4,256,256]{2,1,0:T(8,128)(2,1)} custom-call(bf16[4,256,256]{2,1,0:T(8,128)(2,1)S(1)} %copy-done.2, bf16[256,256]{1,0:T(8,128)(2,1)S(1)} %get-tuple-element.97.grads, bf16[64,256]{1,0:T(8,128)(2,1)S(1)} %bitcast.10), custom_call_target="tpu_custom_call" | custom-call | flops 8000000000 | bytes 1212416 | tf_op jit(solution)/shard_map/alignment/pallas_call | solution.py:378
  118.5 15.5 %all-to-all-done.3.arrived = bf16[16,144,128]{2,1,0:T(8,128)(2,1)S(1)} async-done(((bf16[16,144,128]{2,1,0:T(8,128)(2,1)}), bf16[16,144,128]{2,1,0:T(8,128)(2,1)S(1)}, u32[]{:S(2)}, u32[]{:S(2)}) %all-to-all-start.3) | async-done | bytes 589856 | tf_op jit(solution)/shard_map/all_to_all | solution.py:606
  134.0 10.4 %all_to_all.26.mine = bf16[8,144,128]{2,1,0:T(8,128)(2,1)S(1)} all-to-all(bf16[8,144,128]{2,1,0:T(8,128)(2,1)S(1)} %pack_row.1), channel_id=1, replica_groups={{0,32,64,96,128,160,192,224},{16,48,80,112,144,176,208,240},{1,33,65,97..., dimensions={0} | all-to-all | bytes 589824 | tf_op jit(solution)/shard_map/all_to_all | solution.py:430
  144.4 3.9 %collective-permute-start.18 = (bf16[8,144,128]{2,1,0:T(8,128)(2,1)S(1)}, bf16[8,144,128]{2,1,0:T(8,128)(2,1)S(1)}, u32[]{:S(2)}, u32[]{:S(2)}) collective-permute-start(bf16[8,144,128]{2,1,0:T(8,128)(2,1)S(1)} %all_to_all.26.mine), channel_id=1, source_target_pairs={{0,16},{16,0},{32,48},{48,32},{64,80},{80,64},{96,112},{112,96},{1... | collective-permute-start | bytes 884744 | tf_op jit(solution)/shard_map/ppermute | solution.py:427
  149.6 1.7 %finish.1 = (f32[64,256]{1,0:T(8,128)}, f32[1,64]{1,0:T(1,128)}, f32[1024,128]{1,0:T(8,128)}, f32[1,128]{1,0:T(1,128)}) custom-call(s32[2]{0:T(128)S(1)} %pad_add_fusion.info, bf16[8,144,128]{2,1,0:T(8,128)(2,1)S(1)} %all_to_all.26.mine, bf16[8,144,128]{2,1,0:T(8,128)(2,1)S(1)} %collective-permute-done.18.other), custom_call_target="tpu_custom_call" | custom-call | bytes 1180424 | tf_op jit(solution)/shard_map/finish/pallas_call | solution.py:378
  (69 shorter events, 22.2 us)
Async XLA Ops:
  0.7 1.0 copy-start.1
  4.5 39.8 %copy-start.3 = (bf16[1024,128]{1,0:T(8,128)(2,1)S(1)}, bf16[1024,128]{1,0:T(8,128)(2,1)}, u32[]{:S(2)}) copy-start(bf16[1024,128]{1,0:T(8,128)(2,1)} %weights.1) | copy-start | bytes 786436
  5.9 4.2 %collective-permute-start = (bf16[272,128]{1,0:T(8,128)(2,1)S(1)}, bf16[272,128]{1,0:T(8,128)(2,1)S(1)}, u32[]{:S(2)}, u32[]{:S(2)}) collective-permute-start(bf16[272,128]{1,0:T(8,128)(2,1)S(1)} %get-tuple-element.56), channel_id=1, source_target_pairs={{0,16},{16,0},{32,48},{48,32},{64,80},{80,64},{96,112},{112,96},{1... | collective-permute-start | bytes 208904 | tf_op jit(solution)/shard_map/ppermute | solution.py:427
  11.6 22.9 %all-to-all-start = ((bf16[8,288,128]{2,1,0:T(8,128)(2,1)}), bf16[8,288,128]{2,1,0:T(8,128)(2,1)S(1)}, u32[]{:S(2)}, u32[]{:S(2)}) async-start(bf16[8,288,128]{2,1,0:T(8,128)(2,1)} %pack_right.1), calls=%async_computation | async-start | bytes 1179648 | tf_op jit(solution)/shard_map/all_to_all | solution.py:430
  16.5 10.8 %collective-permute-start.1 = (bf16[288,128]{1,0:T(8,128)(2,1)S(1)}, bf16[288,128]{1,0:T(8,128)(2,1)S(1)}, u32[]{:S(2)}, u32[]{:S(2)}) collective-permute-start(bf16[288,128]{1,0:T(8,128)(2,1)S(1)} %pad_maximum_fusion), channel_id=1, source_target_pairs={{0,4},{16,20},{32,36},{48,52},{64,68},{80,84},{96,100},{112,116},{... | collective-permute-start | bytes 221192 | tf_op jit(solution)/shard_map/ppermute | solution.py:450
  21.5 6.0 %collective-permute-start.2 = (bf16[288,128]{1,0:T(8,128)(2,1)S(1)}, bf16[288,128]{1,0:T(8,128)(2,1)S(1)}, u32[]{:S(2)}, u32[]{:S(2)}) collective-permute-start(bf16[288,128]{1,0:T(8,128)(2,1)S(1)} %pad_maximum_fusion), channel_id=1, source_target_pairs={{0,8},{16,24},{32,40},{48,56},{64,72},{80,88},{96,104},{112,120},{... | collective-permute-start | bytes 221192 | tf_op jit(solution)/shard_map/ppermute | solution.py:450
  26.0 2.7 %collective-permute-start.3 = (bf16[288,128]{1,0:T(8,128)(2,1)S(1)}, bf16[288,128]{1,0:T(8,128)(2,1)S(1)}, u32[]{:S(2)}, u32[]{:S(2)}) collective-permute-start(bf16[288,128]{1,0:T(8,128)(2,1)S(1)} %pad_maximum_fusion), channel_id=1, source_target_pairs={{0,12},{16,28},{32,44},{48,60},{64,76},{80,92},{96,108},{112,124},... | collective-permute-start | bytes 221192 | tf_op jit(solution)/shard_map/ppermute | solution.py:450
  28.8 3.9 %collective-permute-start.4 = (bf16[288,128]{1,0:T(8,128)(2,1)S(1)}, bf16[288,128]{1,0:T(8,128)(2,1)S(1)}, u32[]{:S(2)}, u32[]{:S(2)}) collective-permute-start(bf16[288,128]{1,0:T(8,128)(2,1)S(1)} %add_add_fusion.tree), channel_id=1, source_target_pairs={{0,1},{4,5},{8,9},{12,13},{16,17},{20,21},{24,25},{28,29},{32,33},... | collective-permute-start | bytes 221192 | tf_op jit(solution)/shard_map/ppermute | solution.py:396
  30.1 2.7 %collective-permute-start.5 = (bf16[288,128]{1,0:T(8,128)(2,1)S(1)}, bf16[288,128]{1,0:T(8,128)(2,1)S(1)}, u32[]{:S(2)}, u32[]{:S(2)}) collective-permute-start(bf16[288,128]{1,0:T(8,128)(2,1)S(1)} %add_add_fusion.tree), channel_id=1, source_target_pairs={{0,2},{4,6},{8,10},{12,14},{16,18},{20,22},{24,26},{28,30},{32,34}... | collective-permute-start | bytes 221192 | tf_op jit(solution)/shard_map/ppermute | solution.py:396
  31.4 3.1 %collective-permute-start.6 = (bf16[288,128]{1,0:T(8,128)(2,1)S(1)}, bf16[288,128]{1,0:T(8,128)(2,1)S(1)}, u32[]{:S(2)}, u32[]{:S(2)}) collective-permute-start(bf16[288,128]{1,0:T(8,128)(2,1)S(1)} %add_add_fusion.tree), channel_id=1, source_target_pairs={{0,3},{4,7},{8,11},{12,15},{16,19},{20,23},{24,27},{28,31},{32,35}... | collective-permute-start | bytes 221192 | tf_op jit(solution)/shard_map/ppermute | solution.py:396
  34.5 9.8 %collective-permute-start.7 = (bf16[8,288,128]{2,1,0:T(8,128)(2,1)S(1)}, bf16[8,288,128]{2,1,0:T(8,128)(2,1)S(1)}, u32[]{:S(2)}, u32[]{:S(2)}) collective-permute-start(bf16[8,288,128]{2,1,0:T(8,128)(2,1)S(1)} %all-to-all-done.mine), channel_id=1, source_target_pairs={{0,16},{16,0},{32,48},{48,32},{64,80},{80,64},{96,112},{112,96},{1... | collective-permute-start | bytes 1769480 | tf_op jit(solution)/shard_map/ppermute | solution.py:427
  37.4 13.9 %all-to-all-start.1 = ((bf16[8,64,128]{2,1,0:T(8,128)(2,1)}), bf16[8,64,128]{2,1,0:T(8,128)(2,1)S(1)}, u32[]{:S(2)}, u32[]{:S(2)}) async-start(bf16[8,64,128]{2,1,0:T(8,128)(2,1)} %pack_left.1), calls=%async_computation.1 | async-start | bytes 262144 | tf_op jit(solution)/shard_map/all_to_all | solution.py:430
  44.3 6.9 %copy-start = (bf16[16,256,128]{2,1,0:T(8,128)(2,1)S(1)}, bf16[16,256,128]{2,1,0:T(8,128)(2,1)}, u32[]{:S(2)}) copy-start(bf16[16,256,128]{2,1,0:T(8,128)(2,1)} %adjoint.1) | copy-start | bytes 3145732
  47.1 1.0 copy-start.10
  51.2 1.2 copy-start.11
  61.2 7.4 %collective-permute-start.10 = (bf16[256,128]{1,0:T(8,128)(2,1)S(1)}, bf16[256,128]{1,0:T(8,128)(2,1)S(1)}, u32[]{:S(2)}, u32[]{:S(2)}) collective-permute-start(bf16[256,128]{1,0:T(8,128)(2,1)S(1)} %convert_element_type.3), channel_id=1, source_target_pairs={{3,0},{7,4},{11,8},{15,12},{19,16},{23,20},{27,24},{31,28},{35,32}... | collective-permute-start | bytes 196616 | tf_op jit(solution)/shard_map/ppermute | solution.py:514
  62.5 6.1 %collective-permute-start.8 = (bf16[256,128]{1,0:T(8,128)(2,1)S(1)}, bf16[256,128]{1,0:T(8,128)(2,1)S(1)}, u32[]{:S(2)}, u32[]{:S(2)}) collective-permute-start(bf16[256,128]{1,0:T(8,128)(2,1)S(1)} %convert_element_type.3), channel_id=1, source_target_pairs={{1,0},{5,4},{9,8},{13,12},{17,16},{21,20},{25,24},{29,28},{33,32},... | collective-permute-start | bytes 196616 | tf_op jit(solution)/shard_map/ppermute | solution.py:514
  63.8 5.3 %collective-permute-start.9 = (bf16[256,128]{1,0:T(8,128)(2,1)S(1)}, bf16[256,128]{1,0:T(8,128)(2,1)S(1)}, u32[]{:S(2)}, u32[]{:S(2)}) collective-permute-start(bf16[256,128]{1,0:T(8,128)(2,1)S(1)} %convert_element_type.3), channel_id=1, source_target_pairs={{2,0},{6,4},{10,8},{14,12},{18,16},{22,20},{26,24},{30,28},{34,32}... | collective-permute-start | bytes 196616 | tf_op jit(solution)/shard_map/ppermute | solution.py:514
  65.1 10.3 %copy-start.9 = (f32[128]{0:T(128)S(1)}, f32[128]{0:T(128)}, u32[]{:S(2)}) copy-start(f32[128]{0:T(128)} %param.14) | copy-start | bytes 1540
  65.1 10.3 %copy-start.12 = (bf16[32,64,256]{2,1,0:T(8,128)(2,1)S(1)}, bf16[32,64,256]{2,1,0:T(8,128)(2,1)}, u32[]{:S(2)}) copy-start(bf16[32,64,256]{2,1,0:T(8,128)(2,1)} %copy-done.10) | copy-start | bytes 3145732
  65.1 10.3 %copy-start.14 = (bf16[128,1024]{1,0:T(8,128)(2,1)S(1)}, bf16[128,1024]{1,0:T(8,128)(2,1)}, u32[]{:S(2)}) copy-start(bf16[128,1024]{1,0:T(8,128)(2,1)} %copy-done.13) | copy-start | bytes 786436
  69.2 15.0 %collective-permute-start.12 = (bf16[256,128]{1,0:T(8,128)(2,1)S(1)}, bf16[256,128]{1,0:T(8,128)(2,1)S(1)}, u32[]{:S(2)}, u32[]{:S(2)}) collective-permute-start(bf16[256,128]{1,0:T(8,128)(2,1)S(1)} %get-tuple-element.82), channel_id=1, source_target_pairs={{4,0},{20,16},{36,32},{52,48},{68,64},{84,80},{100,96},{116,112},{... | collective-permute-start | bytes 196616 | tf_op jit(solution)/shard_map/ppermute | solution.py:538
  70.5 13.7 %collective-permute-start.13 = (bf16[256,128]{1,0:T(8,128)(2,1)S(1)}, bf16[256,128]{1,0:T(8,128)(2,1)S(1)}, u32[]{:S(2)}, u32[]{:S(2)}) collective-permute-start(bf16[256,128]{1,0:T(8,128)(2,1)S(1)} %get-tuple-element.82), channel_id=1, source_target_pairs={{8,0},{24,16},{40,32},{56,48},{72,64},{88,80},{104,96},{120,112},{... | collective-permute-start | bytes 196616 | tf_op jit(solution)/shard_map/ppermute | solution.py:538
  71.8 12.4 %collective-permute-start.14 = (bf16[256,128]{1,0:T(8,128)(2,1)S(1)}, bf16[256,128]{1,0:T(8,128)(2,1)S(1)}, u32[]{:S(2)}, u32[]{:S(2)}) collective-permute-start(bf16[256,128]{1,0:T(8,128)(2,1)S(1)} %get-tuple-element.82), channel_id=1, source_target_pairs={{12,0},{28,16},{44,32},{60,48},{76,64},{92,80},{108,96},{124,112},... | collective-permute-start | bytes 196616 | tf_op jit(solution)/shard_map/ppermute | solution.py:538
  73.1 12.7 %collective-permute-start.11 = (bf16[2048,128]{1,0:T(8,128)(2,1)S(1)}, bf16[2048,128]{1,0:T(8,128)(2,1)S(1)}, u32[]{:S(2)}, u32[]{:S(2)}) collective-permute-start(bf16[2048,128]{1,0:T(8,128)(2,1)S(1)} %get-tuple-element.79), channel_id=1, source_target_pairs={{0,16},{16,0},{32,48},{48,32},{64,80},{80,64},{96,112},{112,96},{1... | collective-permute-start | bytes 1572872 | tf_op jit(solution)/shard_map/ppermute | solution.py:427
  84.1 32.5 %copy-start.2 = (bf16[4,256,256]{2,1,0:T(8,128)(2,1)S(1)}, bf16[4,256,256]{2,1,0:T(8,128)(2,1)}, u32[]{:S(2)}) copy-start(bf16[4,256,256]{2,1,0:T(8,128)(2,1)} %msa.3) | copy-start | bytes 1572868
  84.1 32.5 %copy-start.5 = (bf16[256,64]{0,1:T(8,128)(2,1)S(1)}, bf16[256,64]{0,1:T(8,128)(2,1)}, u32[]{:S(2)}) copy-start(bf16[256,64]{0,1:T(8,128)(2,1)} %param.11) | copy-start | bytes 98308
  84.1 1.6 %collective-permute-start.15 = (bf16[512,128]{1,0:T(8,128)(2,1)S(1)}, bf16[512,128]{1,0:T(8,128)(2,1)S(1)}, u32[]{:S(2)}, u32[]{:S(2)}) collective-permute-start(bf16[512,128]{1,0:T(8,128)(2,1)S(1)} %get-tuple-element.83), channel_id=1, source_target_pairs={{0,16},{16,0},{32,48},{48,32},{64,80},{80,64},{96,112},{112,96},{1... | collective-permute-start | bytes 393224 | tf_op jit(solution)/shard_map/ppermute | solution.py:427
  104.0 2.6 %collective-permute-start.16 = (bf16[256,128]{1,0:T(8,128)(2,1)S(1)}, bf16[256,128]{1,0:T(8,128)(2,1)S(1)}, u32[]{:S(2)}, u32[]{:S(2)}) collective-permute-start(bf16[256,128]{1,0:T(8,128)(2,1)S(1)} %get-tuple-element.89), channel_id=1, source_target_pairs={{0,16},{16,0},{32,48},{48,32},{64,80},{80,64},{96,112},{112,96},{1... | collective-permute-start | bytes 196616 | tf_op jit(solution)/shard_map/ppermute | solution.py:427
  107.4 1.3 collective-permute-start.17
  109.6 24.3 %all-to-all-start.3 = ((bf16[16,144,128]{2,1,0:T(8,128)(2,1)}), bf16[16,144,128]{2,1,0:T(8,128)(2,1)S(1)}, u32[]{:S(2)}, u32[]{:S(2)}) async-start(bf16[16,144,128]{2,1,0:T(8,128)(2,1)} %pack_column.1), calls=%async_computation.3 | async-start | bytes 1179648 | tf_op jit(solution)/shard_map/all_to_all | solution.py:606
  144.4 5.2 %collective-permute-start.18 = (bf16[8,144,128]{2,1,0:T(8,128)(2,1)S(1)}, bf16[8,144,128]{2,1,0:T(8,128)(2,1)S(1)}, u32[]{:S(2)}, u32[]{:S(2)}) collective-permute-start(bf16[8,144,128]{2,1,0:T(8,128)(2,1)S(1)} %all_to_all.26.mine), channel_id=1, source_target_pairs={{0,16},{16,0},{32,48},{48,32},{64,80},{80,64},{96,112},{112,96},{1... | collective-permute-start | bytes 884744 | tf_op jit(solution)/shard_map/ppermute | solution.py:427
  (7 other events, 5.1 us)

commit v4 on v3

--- a/solution.py
+++ b/solution.py
@@ -14,6 +14,8 @@
 STEP = 4
 GROUP = 16
 E_BLOCK = 8
+E_WIDE = 16
+FUSE = 4
 
 
 def dot(a, b, lhs, rhs):
@@ -77,7 +79,7 @@
             ].astype(BF)
 
 
-def pack_right_kernel(dims, info, keep, came, out):
+def pack_forward_kernel(dims, info, keep, came, out):
     src, seqs, hidden, row_dev, places, half = dims
     core = lax.rem(info[0], 2)
     base = seqs * hidden
@@ -87,19 +89,24 @@
         for q in range(src // 2):
             out[q, rows_at(who * base, base), :] = value
             out[q, rows_at(2 * base + who * GROUP, GROUP), :] = flags
-
-
-def pack_left_kernel(dims, info, tree, near_1, near_2, near_3, out):
-    src, seqs, hidden, row_dev, places, half = dims
-    pairs = src // 2
-    core = lax.rem(info[0], 2)
-    mixed = GROUP + pairs * row_dev
-    for n, who in enumerate((core, 1 - core)):
-        span = pl.ds(n * mixed, mixed)
-        spread = tree[span, :] + near_1[span, :] + near_2[span, :] + near_3[span, :]
-        for q in range(pairs):
-            out[q, rows_at(who * row_dev, row_dev), :] = spread[GROUP + q * row_dev : GROUP + (q + 1) * row_dev]
-            out[q, rows_at(2 * row_dev + who * GROUP, GROUP), :] = spread[:GROUP]
+            out[q, rows_at(2 * base + 2 * GROUP + who * row_dev, row_dev), :] = ref[
+                pl.ds(base + GROUP + q * row_dev, row_dev), :
+            ]
+
+
+def left_rows_kernel(dims, mine, out, tiles):
+    src, seqs, hidden, row_dev, places, half = dims
+    first = 2 * seqs * hidden
+    for q in range(src // 2):
+        tiles[pl.ds(q * 2 * GROUP, 2 * GROUP), :] = mine[q, first : first + 2 * GROUP, :].astype(F32)
+    rows = [tiles[pl.ds(seqs + s, src, stride=GROUP), :] for s in range(seqs)]
+    blocks = [jnp.concatenate(rows, axis=0)]
+    for q in range(src // 2):
+        tiles[pl.ds(q * 2 * row_dev, 2 * row_dev), :] = mine[q, first + 2 * GROUP :, :].astype(F32)
+    for i in range(row_dev):
+        tile = tiles[pl.ds(i, src, stride=row_dev), :]
+        blocks.append(jnp.concatenate([tile[:, s * hidden : (s + 1) * hidden] for s in range(seqs)], axis=0))
+    out[...] = jnp.concatenate(blocks, axis=1).astype(BF)
 
 
 def unpack_right_kernel(dims, info, mine, other, weights, r_ref, live_t_ref, by_e, by_e_t, r_all, flags, w_all):
@@ -110,7 +117,9 @@
     for ref, h in ((mine, core), (other, 1 - core)):
         for q in range(src // 2):
             r_all[rows_at(h * lines + q * 2 * base, 2 * base), :] = ref[q, : 2 * base, :].astype(F32)
-            flags[rows_at((h * src + 2 * q) * GROUP, 2 * GROUP), :] = ref[q, 2 * base :, :].astype(F32)
+            flags[rows_at((h * src + 2 * q) * GROUP, 2 * GROUP), :] = ref[
+                q, 2 * base : 2 * base + 2 * GROUP, :
+            ].astype(F32)
     w_all[...] = weights[...].astype(F32)
     for e in range(hidden):
         for h in range(2):
@@ -126,24 +135,16 @@
         live_t_ref[pl.ds(h * half, half), :] = jnp.concatenate(rows, axis=0).T.astype(BF)
 
 
-def first_kernel(dims, info, arrived, r_ref, live_t, adjoint, weights, g_ref, s_ref, d_ref, left_ref, bias_ref, left_out, left_t, tiles, total):
+def first_kernel(dims, info, tree, near_1, near_2, near_3, r_ref, live_t, adjoint, weights, g_ref, s_ref, d_ref, left_ref, bias_ref, left_out, left_t, total):
     src, seqs, hidden, row_dev, places, half = dims
     step = pl.program_id(0)
 
     @pl.when(step == 0)
     def _():
         pair = info[0] // 2
-        for q in range(src // 2):
-            tiles[pl.ds(q * 2 * GROUP, 2 * GROUP), :] = arrived[q, 2 * row_dev :, :].astype(F32)
-        rows = [tiles[pl.ds(seqs + s, src, stride=GROUP), :] for s in range(seqs)]
-        band = jnp.concatenate(rows, axis=0).astype(BF)
-        for q in range(src // 2):
-            tiles[pl.ds(q * 2 * row_dev, 2 * row_dev), :] = arrived[q, : 2 * row_dev, :].astype(F32)
-        blocks = []
-        for i in range(row_dev):
-            tile = tiles[pl.ds(i, src, stride=row_dev), :]
-            blocks.append(jnp.concatenate([tile[:, s * hidden : (s + 1) * hidden] for s in range(seqs)], axis=0))
-        left = jnp.concatenate(blocks, axis=1)
+        spread = tree[...].astype(F32) + near_1[...].astype(F32) + near_2[...].astype(F32) + near_3[...].astype(F32)
+        band = spread[:, :half].astype(BF)
+        left = spread[:, half:]
         left_out[...] = left.astype(BF)
         left_t[...] = left.T.astype(BF)
         spot = lax.broadcasted_iota(jnp.int32, (half, half), 0) - pair * row_dev
@@ -158,13 +159,15 @@
         bias_ref[...] = bias
         total[...] = jnp.zeros_like(total)
 
-    part = weights[pl.ds(step * E_BLOCK * hidden, E_BLOCK * hidden), :]
+    part = weights[pl.ds(step * E_WIDE * hidden, E_WIDE * hidden), :]
     for i in range(row_dev):
         g = dot(part, s_ref[i], 1, 1).astype(BF)
-        g_ref[:, pl.ds(i * hidden, hidden), :] = g.reshape(E_BLOCK, hidden, places)
+        g_ref[:, pl.ds(i * hidden, hidden), :] = g.reshape(E_WIDE, hidden, places)
     acc = total[...]
-    for e in range(E_BLOCK):
-        acc = acc + dot(r_ref[step * E_BLOCK + e], g_ref[e], 1, 1)
+    for e in range(0, E_WIDE, FUSE):
+        right = jnp.concatenate([r_ref[step * E_WIDE + e + n] for n in range(FUSE)], axis=1)
+        grad = jnp.concatenate([g_ref[e + n] for n in range(FUSE)], axis=1)
+        acc = acc + dot(right, grad, 1, 1)
     total[...] = acc
 
     @pl.when(step == pl.num_programs(0) - 1)
@@ -191,7 +194,12 @@
     for i in range(row_dev):
         block = outer[:, pl.ds(i * hidden, hidden), :].reshape(block_lines, places)
         before[i] = before[i] + dot(weights_t[...], block, 1, 0)
-        acc = acc + dot(block, s_ref[i], 1, 0)
+    for i in range(0, row_dev, FUSE):
+        blocks = [
+            outer[:, pl.ds((i + n) * hidden, hidden), :].reshape(block_lines, places) for n in range(FUSE)
+        ]
+        scaled = s_ref[pl.ds(i, FUSE)].reshape(FUSE * places, half)
+        acc = acc + dot(jnp.concatenate(blocks, axis=1), scaled, 1, 0)
     held[rows_at(step * block_lines, block_lines), :] = acc
 
     @pl.when(step == pl.num_programs(0) - 1)
@@ -209,11 +217,11 @@
     step = pl.program_id(0)
     base = seqs * hidden
     lines = src * base
-    for e in range(E_BLOCK):
+    for e in range(E_WIDE):
         grad = dot(left[...], g_ref[e], 1, 0)
         for h in range(2):
             for s in range(seqs):
-                held[pl.ds(h * lines + s * hidden + step * E_BLOCK + e, src, stride=base), :] = grad[
+                held[pl.ds(h * lines + s * hidden + step * E_WIDE + e, src, stride=base), :] = grad[
                     s * src : (s + 1) * src, h * half : (h + 1) * half
                 ]
 
@@ -306,10 +314,24 @@
     weight = (w_keep[...] + w_came[...].astype(F32)).astype(BF)
     at = weight.shape[0]
     size = chunk.shape[0]
-    for c in range(out.shape[0]):
-        out[c, pl.ds(0, at), :] = weight
-        out[c, pl.ds(at, size), :] = chunk[...]
-        out[c, pl.ds(at + size, GROUP), :] = small[...]
+    out[pl.ds(0, at), :] = weight
+    out[pl.ds(at, size), :] = chunk[...]
+    out[pl.ds(at + size, GROUP), :] = small[...]
+
+
+def sum_of_four(part_0, part_1, part_2, part_3):
+    parts = [p[...].astype(F32) for p in (part_0, part_1, part_2, part_3)]
+    total = (parts[0] + parts[1]) + (parts[2] + parts[3])
+    at = total.shape[0] - GROUP
+    last = total[at:]
+    small = bias_block(last[0:1] + last[1:2], last[2:3] + last[3:4], last.shape[1])
+    return total[:at].astype(BF), small
+
+
+def column_sum_kernel(dims, part_0, part_1, part_2, part_3, out):
+    total, small = sum_of_four(part_0, part_1, part_2, part_3)
+    out[pl.ds(0, total.shape[0]), :] = total
+    out[pl.ds(total.shape[0], GROUP), :] = small
 
 
 def left_sum_kernel(dims, left, near_1, near_2, near_3, total, sent):
@@ -318,17 +340,11 @@
     sent[...] = value.astype(BF)
 
 
-def pack_row_kernel(dims, arrived, out):
-    total = arrived[0].astype(F32)
-    for c in range(1, arrived.shape[0]):
-        total = total + arrived[c].astype(F32)
-    at = total.shape[0] - GROUP
-    last = total[at:]
-    small = bias_block(last[0:1] + last[1:2], last[2:3] + last[3:4], last.shape[1])
-    total = total[:at].astype(BF)
+def pack_row_kernel(dims, part_0, part_1, part_2, part_3, out):
+    total, small = sum_of_four(part_0, part_1, part_2, part_3)
     for q in range(out.shape[0]):
-        out[q, pl.ds(0, at), :] = total
-        out[q, pl.ds(at, GROUP), :] = small
+        out[q, pl.ds(0, total.shape[0]), :] = total
+        out[q, pl.ds(total.shape[0], GROUP), :] = small
 
 
 def finish_kernel(dims, info, mine, other, projector, projector_bias, weight, bias, held):
@@ -367,7 +383,7 @@
 SCALARS = pl.BlockSpec(memory_space=pltpu.SMEM)
 
 
-def call(kernel, dims, name, args, outs, scratch=(), steps=1, in_specs=None, out_specs=None, macs=0, room=24):
+def call(kernel, dims, name, args, outs, scratch=(), steps=1, in_specs=None, out_specs=None, macs=0, room=16):
     in_specs, out_specs = in_specs or {}, out_specs or {}
     specs = [
         SCALARS if a.dtype == jnp.int32 and a.ndim == 1 else in_specs.get(n, whole(*a.shape))
@@ -396,6 +412,11 @@
         lax.ppermute(block, "col", [(a, a + d) for a in range(0, cols, STEP)])
         for d in range(1, STEP)
     ]
+
+
+def swap_parts(block, cols, unit):
+    swaps = [lax.ppermute(block, "col", [(i, i ^ d * unit) for i in range(cols)]) for d in range(1, STEP)]
+    return [block, *swaps]
 
 
 def per_device(
@@ -443,30 +464,30 @@
         ),
         [((2 * base, half), F32), ((places, base), F32)],
         macs=100_000_000,
+        room=62,
     )
     came = partner(send)
 
-    tree = jnp.concatenate([keep[base:], came[base:]], axis=0)
+    packed = call(
+        pack_forward_kernel,
+        dims,
+        "pack_forward",
+        (info, keep, came),
+        (shape_of(BF, pairs, 2 * (base + GROUP + row_dev), half),),
+    )[0]
+    mine = over_pairs(packed)
+    tree = call(
+        left_rows_kernel,
+        dims,
+        "left_rows",
+        (mine,),
+        (shape_of(BF, total, half + lines),),
+        [((rows * GROUP, half), F32)],
+    )[0]
     far = [lax.ppermute(tree, "col", [(0, d)]) for d in range(STEP, cols, STEP)]
     tree = sum(far, tree)
     near = near_parts(tree, cols)
-    packed = call(
-        pack_right_kernel,
-        dims,
-        "pack_right",
-        (info, keep, came),
-        (shape_of(BF, pairs, 2 * (base + GROUP), half),),
-    )[0]
-    mine = over_pairs(packed)
-    mine, *near = lax.optimization_barrier((mine, *near))
-    packed = call(
-        pack_left_kernel,
-        dims,
-        "pack_left",
-        (info, tree, *near),
-        (shape_of(BF, pairs, 2 * (GROUP + row_dev), half),),
-    )[0]
-    arrived = over_pairs(packed)
+    mine, tree = lax.optimization_barrier((mine, tree))
     other = partner(mine)
     right_cols, live_t, by_e, by_e_t = call(
         unpack_right_kernel,
@@ -487,12 +508,12 @@
         macs=300_000_000,
     )
 
-    by_block = lambda *block: pl.BlockSpec((E_BLOCK, *block), lambda t: (t, 0, 0))
+    by_block = lambda size, *block: pl.BlockSpec((size, *block), lambda t: (t, 0, 0))
     outer_grad, scaled, divisor, left_grad, bias_grad, left_rows, left_t = call(
         first_kernel,
         dims,
         "scaled_outer_grad",
-        (info, arrived, right_cols, live_t, update_adjoint, by_e),
+        (info, tree, *near, right_cols, live_t, update_adjoint, by_e),
         (
             shape_of(BF, hidden, lines, places),
             shape_of(BF, row_dev, places, channels),
@@ -502,11 +523,11 @@
             shape_of(BF, total, lines),
             shape_of(BF, lines, total),
         ),
-        [((rows * GROUP, half), F32), ((total, lines), F32)],
-        steps=hidden // E_BLOCK,
-        out_specs={0: by_block(lines, places)},
+        [((total, lines), F32)],
+        steps=hidden // E_WIDE,
+        out_specs={0: by_block(E_WIDE, lines, places)},
         macs=800_000_000,
-        room=32,
+        room=24,
     )
 
     sent = left_grad.astype(BF)
@@ -521,10 +542,10 @@
         (info, left_rows, outer_grad),
         (shape_of(F32, rows * base, half), shape_of(BF, rows * base, half)),
         [((2 * rows * base, half), F32)],
-        steps=hidden // E_BLOCK,
-        in_specs={2: by_block(lines, places)},
+        steps=hidden // E_WIDE,
+        in_specs={2: by_block(E_WIDE, lines, places)},
         macs=270_000_000,
-        room=32,
+        room=24,
     )
     *near, right_send = lax.optimization_barrier((*near, right_send))
     left_grad, sent = call(
@@ -553,11 +574,11 @@
         ],
         steps=hidden // E_BLOCK,
         in_specs={
-            2: by_block(total, places),
+            2: by_block(E_BLOCK, total, places),
             5: pl.BlockSpec((channels, E_BLOCK * hidden), lambda t: (0, t)),
         },
         macs=1_300_000_000,
-        room=32,
+        room=20,
     )
     w_send, *far = lax.optimization_barrier((w_send, *far))
     w_came = partner(w_send)
@@ -600,10 +621,10 @@
     )
     w_came = partner(w_send)
     size = 2 * hidden + w_lines + GROUP
-    packed = call(
-        pack_column_kernel, dims, "pack_column", (w_keep, w_came, chunk, small), (shape_of(BF, cols, size, half),)
+    own = call(
+        pack_column_kernel, dims, "pack_column", (w_keep, w_came, chunk, small), (shape_of(BF, size, half),)
     )[0]
-    arrived = lax.all_to_all(packed, "col", 0, 0, tiled=True)
+    parts = swap_parts(own, cols, STEP)
     alignment_gradient = call(
         align_kernel,
         dims,
@@ -612,8 +633,10 @@
         (shape_of(BF, seqs, places, depth),),
         macs=200_000_000,
     )[0]
-    arrived, alignment_gradient = lax.optimization_barrier((arrived, alignment_gradient))
-    packed = call(pack_row_kernel, dims, "pack_row", (arrived,), (shape_of(BF, pairs, size, half),))[0]
+    *parts, alignment_gradient = lax.optimization_barrier((*parts, alignment_gradient))
+    own = call(column_sum_kernel, dims, "column_sum", parts, (shape_of(BF, size, half),))[0]
+    parts = swap_parts(own, cols, 1)
+    packed = call(pack_row_kernel, dims, "pack_row", parts, (shape_of(BF, pairs, size, half),))[0]
     mine = over_pairs(packed)
     other = partner(mine)
     projector, projector_bias, weight, bias = call(

time: 152 us -> 135 us (0.89)
  blocking collectives: 27.3 us -> 43.9 us
  waiting for transfers between devices: 26.1 us -> 12.9 us
  starting transfers between devices: 55 us -> 44.5 us
  local copies, waits for them, and re-layouts: 8.4 us -> 0.92 us
  Pallas kernels: 33.4 us -> 31.1 us
    all_to_all x3 -> x0, starting transfers between devices: 18.9 us -> none  [the longest x2 11.8 us: over_pairs(): lax.all_to_all(block, 'row', 0, 0, axis_index_groups=same_core, tiled=True)]
    all_to_all x3 -> x0, waiting for transfers between devices: 17.2 us -> none  [the longest x1 15.5 us: per_device(): arrived = lax.all_to_all(packed, 'col', 0, 0, tiled=True)]
    all_to_all x2 -> x3, blocking collectives: 27.3 us -> 43.9 us  [over_pairs(): lax.all_to_all(block, 'row', 0, 0, axis_index_groups=same_core, tiled=True)]
    ppermute x0 -> x6, starting transfers between devices: none -> 9.28 us  [swap_parts(): lax.ppermute(block, 'col', [(i, i ^ d * unit) for i in range(cols)])]
    unnamed x34 -> x18, local copies, waits for them, and re-layouts: 8.39 us -> 0.92 us
    ppermute x0 -> x6, waiting for transfers between devices: none -> 4.83 us  [swap_parts(): lax.ppermute(block, 'col', [(i, i ^ d * unit) for i in range(cols)])]
    pallas_call x15 -> x16, Pallas kernels: 33.4 us -> 31.1 us  [call(): pl.pallas_call(functools.partial(kernel, dims), grid=(steps,), in_specs=s...]
    ppermute x3, waiting for transfers between devices: 1.78 us -> 0.01 us  [near_parts(): lax.ppermute(block, 'col', [(a, a + d) for a in range(0, cols, STEP)])]
  transfers between devices with their start and end apart: 22 -> 25, of which waited for: 12 -> 13; matrix products, arithmetic and copies ran while one was open for 0% -> 0% of each run, Pallas kernels for 12% -> 12%
where the time goes in v4:
time: 135 us
  starting transfers between devices  44.5 us (33%)
  blocking collectives  43.9 us (33%)
  Pallas kernels  31.1 us (23%)
  waiting for transfers between devices  12.9 us (10%)
    all_to_all x3, blocking collectives, over_pairs(): lax.all_to_all(block, 'row', 0, 0, axis_index_groups=same_core, tiled=True)  43.9 us
    pallas_call x16, Pallas kernels, call(): pl.pallas_call(functools.partial(kernel, dims), grid=(steps,), in_specs=s...  31.1 us
    ppermute x7, starting transfers between devices, partner(): return lax.ppermute(block, 'row', swap)  12.8 us
    ppermute x3, starting transfers between devices, per_device(): far = [lax.ppermute(tree, 'col', [(0, d)]) for d in range(STEP, cols, STEP)]  10.8 us
    ppermute x6, starting transfers between devices, swap_parts(): lax.ppermute(block, 'col', [(i, i ^ d * unit) for i in range(cols)])  9.28 us
    ppermute x7, waiting for transfers between devices, partner(): return lax.ppermute(block, 'row', swap)  5.39 us
    ppermute x6, waiting for transfers between devices, swap_parts(): lax.ppermute(block, 'col', [(i, i ^ d * unit) for i in range(cols)])  4.83 us
    ppermute x3, starting transfers between devices, per_device(): lax.ppermute(sent, 'col', [(a + d, a) for a in range(0, cols, STEP)])  3.88 us
  transfers between devices with their start and end apart: 25, of which 13 were waited for; matrix products, arithmetic and copies ran while one was open for 0% of the time, Pallas kernels for 12%

profile of v4, /device:TPU:1, one launch (start us, length us, event | category | flops | bytes accessed | tf_op | source)
XLA Modules:
  0.0 134.9 jit_solution(9261714026059957146)
XLA Ops:
  1.2 2.6 %project.1 = (bf16[4,256,256]{2,1,0:T(8,128)(2,1)}, f32[8,256]{1,0:T(8,128)}, bf16[272,128]{1,0:T(8,128)(2,1)}, bf16[272,128]{1,0:T(8,128)(2,1)}) custom-call(s32[2]{0:T(128)} %pad_add_fusion.info, bf16[4,256,256]{2,1,0:T(8,128)(2,1)} %msa.3, s32[4,256]{1,0:T(4,128)} %present.1, s32[1,256]{1,0:T(1,128)} %bitcast.13, bf16[64,256]{1,0:T(8,128)(2,1)} %bitcast.9, ...), custom_call_target="tpu_custom_call" | custom-call | flops 4000000000 | bytes 1234184 | tf_op jit(solution)/shard_map/project/pallas_call | solution.py:394
  3.9 3.2 %collective-permute-start = (bf16[272,128]{1,0:T(8,128)(2,1)}, bf16[272,128]{1,0:T(8,128)(2,1)S(1)}, u32[]{:S(2)}, u32[]{:S(2)}) collective-permute-start(bf16[272,128]{1,0:T(8,128)(2,1)} %get-tuple-element.57), channel_id=1, source_target_pairs={{0,16},{16,0},{32,48},{48,32},{64,80},{80,64},{96,112},{112,96},{1... | collective-permute-start | bytes 208904 | tf_op jit(solution)/shard_map/ppermute | solution.py:448
  9.8 17.5 %all_to_all.15.mine = bf16[8,320,128]{2,1,0:T(8,128)(2,1)S(1)} all-to-all(bf16[8,320,128]{2,1,0:T(8,128)(2,1)S(1)} %pack_forward.1), channel_id=1, replica_groups={{0,32,64,96,128,160,192,224},{16,48,80,112,144,176,208,240},{1,33,65,97..., dimensions={0} | all-to-all | bytes 1310720 | tf_op jit(solution)/shard_map/all_to_all | solution.py:451
  27.5 4.9 %collective-permute-start.1 = (bf16[64,640]{1,0:T(8,128)(2,1)S(1)}, bf16[64,640]{1,0:T(8,128)(2,1)S(1)}, u32[]{:S(2)}, u32[]{:S(2)}) collective-permute-start(bf16[64,640]{1,0:T(8,128)(2,1)S(1)} %left_rows.1), channel_id=1, source_target_pairs={{0,4},{16,20},{32,36},{48,52},{64,68},{80,84},{96,100},{112,116},{... | collective-permute-start | bytes 245768 | tf_op jit(solution)/shard_map/ppermute | solution.py:487
  32.4 4.6 %collective-permute-start.2 = (bf16[64,640]{1,0:T(8,128)(2,1)S(1)}, bf16[64,640]{1,0:T(8,128)(2,1)S(1)}, u32[]{:S(2)}, u32[]{:S(2)}) collective-permute-start(bf16[64,640]{1,0:T(8,128)(2,1)S(1)} %left_rows.1), channel_id=1, source_target_pairs={{0,8},{16,24},{32,40},{48,56},{64,72},{80,88},{96,104},{112,120},{... | collective-permute-start | bytes 245768 | tf_op jit(solution)/shard_map/ppermute | solution.py:487
  37.0 1.3 collective-permute-start.3
  38.5 1.3 collective-permute-done.3
  39.8 2.1 %collective-permute-start.7 = (bf16[8,320,128]{2,1,0:T(8,128)(2,1)S(1)}, bf16[8,320,128]{2,1,0:T(8,128)(2,1)S(1)}, u32[]{:S(2)}, u32[]{:S(2)}) collective-permute-start(bf16[8,320,128]{2,1,0:T(8,128)(2,1)S(1)} %all_to_all.15.mine), channel_id=1, source_target_pairs={{0,16},{16,0},{32,48},{48,32},{64,80},{80,64},{96,112},{112,96},{1... | collective-permute-start | bytes 1966088 | tf_op jit(solution)/shard_map/ppermute | solution.py:448
  41.9 1.3 collective-permute-start.4
  43.2 1.3 collective-permute-start.5
  44.5 1.3 collective-permute-start.6
  45.8 2.8 %unpack_right.1 = (bf16[32,64,256]{2,1,0:T(8,128)(2,1)S(1)}, bf16[256,64]{1,0:T(8,128)(2,1)S(1)}, bf16[1024,128]{1,0:T(8,128)(2,1)S(1)}, bf16[128,1024]{1,0:T(8,128)(2,1)S(1)}) custom-call(s32[2]{0:T(128)S(1)} %copy-done.1, bf16[8,320,128]{2,1,0:T(8,128)(2,1)S(1)} %all_to_all.15.mine, bf16[8,320,128]{2,1,0:T(8,128)(2,1)S(1)} %collective-permute-done.7.other, ...), custom_call_target="tpu_custom_call" | custom-call | flops 12000000000 | bytes 3178504 | tf_op jit(solution)/shard_map/unpack_right/pallas_call | solution.py:394
  48.7 7.3 %scaled_outer_grad.1 = (bf16[32,512,256]{2,1,0:T(8,128)(2,1)S(1)}, bf16[16,256,128]{2,1,0:T(8,128)(2,1)S(1)}, bf16[16,256,128]{2,1,0:T(8,128)(2,1)S(1)}, f32[256...) custom-call(s32[2]{0:T(128)S(1)} %copy-done.1, ...), custom_call_target="tpu_custom_call" | custom-call | flops 32000000000 | bytes 13468168 | tf_op jit(solution)/shard_map/scaled_outer_grad/pallas_call | solution.py:394
  56.0 1.3 collective-permute-start.10
  57.3 1.3 collective-permute-start.8
  58.6 1.3 collective-permute-start.9
  59.9 3.1 %right_grad.1 = (f32[2048,128]{1,0:T(8,128)S(1)}, bf16[2048,128]{1,0:T(8,128)(2,1)S(1)}) custom-call(s32[2]{0:T(128)S(1)} %copy-done.1, bf16[64,512]{1,0:T(8,128)(2,1)S(1)} %get-tuple-element.65.left, bf16[32,512,256]{2,1,0:T(8,128)(2,1)S(1)} %get-tuple-element.66.g_ref), custom_call_target="tpu_custom_call" | custom-call | flops 10800000000 | bytes 10027016 | tf_op jit(solution)/shard_map/right_grad/pallas_call | solution.py:394
  64.3 1.3 collective-permute-start.12
  65.6 1.3 collective-permute-start.13
  66.9 1.3 collective-permute-start.14
  69.3 8.5 %outer_pair.1 = (bf16[16,256,128]{2,1,0:T(8,128)(2,1)}, f32[512,128]{1,0:T(8,128)S(1)}, bf16[512,128]{1,0:T(8,128)(2,1)S(1)}) custom-call(s32[2]{0:T(128)S(1)} %copy-done.1, bf16[512,64]{1,0:T(8,128)(2,1)S(1)} %get-tuple-element.72.left_t, bf16[32,64,256]{2,1,0:T(8,128)(2,1)S(1)} %get-tuple-element.60.r_ref, ...), custom_call_target="tpu_custom_call" | custom-call | flops 51999997952 | bytes 4915720 | tf_op jit(solution)/shard_map/outer_pair/pallas_call | solution.py:394
  77.9 1.3 collective-permute-done.15.w_came
  79.9 16.0 %all_to_all.16.arrived = bf16[8,352,128]{2,1,0:T(8,128)(2,1)S(1)} all-to-all(bf16[8,352,128]{2,1,0:T(8,128)(2,1)S(1)} %pack_backward.1), channel_id=1, replica_groups={{0,32,64,96,128,160,192,224},{16,48,80,112,144,176,208,240},{1,33,65,97..., dimensions={0} | all-to-all | bytes 1441792 | tf_op jit(solution)/shard_map/all_to_all | solution.py:451
  100.7 2.0 %collective-permute-start.18 = (bf16[144,128]{1,0:T(8,128)(2,1)S(1)}, bf16[144,128]{1,0:T(8,128)(2,1)S(1)}, u32[]{:S(2)}, u32[]{:S(2)}) collective-permute-start(bf16[144,128]{1,0:T(8,128)(2,1)S(1)} %pack_column.1.part_0), channel_id=1, source_target_pairs={{0,4},{1,5},{2,6},{3,7},{4,0},{5,1},{6,2},{7,3},{8,12},{9,13},{10,... | collective-permute-start | bytes 110600 | tf_op jit(solution)/shard_map/ppermute | solution.py:418
  102.7 4.6 %collective-permute-start.19 = (bf16[144,128]{1,0:T(8,128)(2,1)S(1)}, bf16[144,128]{1,0:T(8,128)(2,1)S(1)}, u32[]{:S(2)}, u32[]{:S(2)}) collective-permute-start(bf16[144,128]{1,0:T(8,128)(2,1)S(1)} %pack_column.1.part_0), channel_id=1, source_target_pairs={{0,8},{1,9},{2,10},{3,11},{4,12},{5,13},{6,14},{7,15},{8,0},{9,1},... | collective-permute-start | bytes 110600 | tf_op jit(solution)/shard_map/ppermute | solution.py:418
  107.3 1.8 %alignment.1 = bf16[4,256,256]{2,1,0:T(8,128)(2,1)} custom-call(bf16[4,256,256]{2,1,0:T(8,128)(2,1)S(1)} %copy-done.3, bf16[256,256]{1,0:T(8,128)(2,1)S(1)} %get-tuple-element.96.grads, bf16[64,256]{1,0:T(8,128)(2,1)S(1)} %bitcast.10), custom_call_target="tpu_custom_call" | custom-call | flops 8000000000 | bytes 1212416 | tf_op jit(solution)/shard_map/alignment/pallas_call | solution.py:394
  110.2 2.0 %collective-permute-done.20.part_3 = bf16[144,128]{1,0:T(8,128)(2,1)S(1)} collective-permute-done((bf16[144,128]{1,0:T(8,128)(2,1)S(1)}, bf16[144,128]{1,0:T(8,128)(2,1)S(1)}, u32[]{:S(2)}, u32[]{:S(2)}) %collective-permute-start.20) | collective-permute-done | bytes 36896 | tf_op jit(solution)/shard_map/ppermute | solution.py:418
  112.4 2.5 %collective-permute-start.23 = (bf16[144,128]{1,0:T(8,128)(2,1)S(1)}, bf16[144,128]{1,0:T(8,128)(2,1)S(1)}, u32[]{:S(2)}, u32[]{:S(2)}) collective-permute-start(bf16[144,128]{1,0:T(8,128)(2,1)S(1)} %column_sum.1.part_0), channel_id=1, source_target_pairs={{0,3},{1,2},{2,1},{3,0},{4,7},{5,6},{6,5},{7,4},{8,11},{9,10},{10,... | collective-permute-start | bytes 110600 | tf_op jit(solution)/shard_map/ppermute | solution.py:418
  115.2 1.5 %collective-permute-done.23.part_3 = bf16[144,128]{1,0:T(8,128)(2,1)S(1)} collective-permute-done((bf16[144,128]{1,0:T(8,128)(2,1)S(1)}, bf16[144,128]{1,0:T(8,128)(2,1)S(1)}, u32[]{:S(2)}, u32[]{:S(2)}) %collective-permute-start.23) | collective-permute-done | bytes 36896 | tf_op jit(solution)/shard_map/ppermute | solution.py:418
  116.8 10.4 %all_to_all.17.mine = bf16[8,144,128]{2,1,0:T(8,128)(2,1)S(1)} all-to-all(bf16[8,144,128]{2,1,0:T(8,128)(2,1)S(1)} %pack_row.1), channel_id=1, replica_groups={{0,32,64,96,128,160,192,224},{16,48,80,112,144,176,208,240},{1,33,65,97..., dimensions={0} | all-to-all | bytes 589824 | tf_op jit(solution)/shard_map/all_to_all | solution.py:451
  127.2 4.8 %collective-permute-start.24 = (bf16[8,144,128]{2,1,0:T(8,128)(2,1)S(1)}, bf16[8,144,128]{2,1,0:T(8,128)(2,1)S(1)}, u32[]{:S(2)}, u32[]{:S(2)}) collective-permute-start(bf16[8,144,128]{2,1,0:T(8,128)(2,1)S(1)} %all_to_all.17.mine), channel_id=1, source_target_pairs={{0,16},{16,0},{32,48},{48,32},{64,80},{80,64},{96,112},{112,96},{1... | collective-permute-start | bytes 884744 | tf_op jit(solution)/shard_map/ppermute | solution.py:448
  133.1 1.7 %finish.1 = (f32[64,256]{1,0:T(8,128)}, f32[1,64]{1,0:T(1,128)}, f32[1024,128]{1,0:T(8,128)}, f32[1,128]{1,0:T(1,128)}) custom-call(s32[2]{0:T(128)S(1)} %copy-done.1, bf16[8,144,128]{2,1,0:T(8,128)(2,1)S(1)} %all_to_all.17.mine, bf16[8,144,128]{2,1,0:T(8,128)(2,1)S(1)} %collective-permute-done.24.other), custom_call_target="tpu_custom_call" | custom-call | bytes 1180424 | tf_op jit(solution)/shard_map/finish/pallas_call | solution.py:394
  (58 shorter events, 14.4 us)
Async XLA Ops:
  1.2 44.6 %copy-start.4 = (bf16[1024,128]{1,0:T(8,128)(2,1)S(1)}, bf16[1024,128]{1,0:T(8,128)(2,1)}, u32[]{:S(2)}) copy-start(bf16[1024,128]{1,0:T(8,128)(2,1)} %weights.1) | copy-start | bytes 786436
  3.9 4.4 %collective-permute-start = (bf16[272,128]{1,0:T(8,128)(2,1)}, bf16[272,128]{1,0:T(8,128)(2,1)S(1)}, u32[]{:S(2)}, u32[]{:S(2)}) collective-permute-start(bf16[272,128]{1,0:T(8,128)(2,1)} %get-tuple-element.57), channel_id=1, source_target_pairs={{0,16},{16,0},{32,48},{48,32},{64,80},{80,64},{96,112},{112,96},{1... | collective-permute-start | bytes 208904 | tf_op jit(solution)/shard_map/ppermute | solution.py:448
  27.5 10.8 %collective-permute-start.1 = (bf16[64,640]{1,0:T(8,128)(2,1)S(1)}, bf16[64,640]{1,0:T(8,128)(2,1)S(1)}, u32[]{:S(2)}, u32[]{:S(2)}) collective-permute-start(bf16[64,640]{1,0:T(8,128)(2,1)S(1)} %left_rows.1), channel_id=1, source_target_pairs={{0,4},{16,20},{32,36},{48,52},{64,68},{80,84},{96,100},{112,116},{... | collective-permute-start | bytes 245768 | tf_op jit(solution)/shard_map/ppermute | solution.py:487
  32.4 6.1 %collective-permute-start.2 = (bf16[64,640]{1,0:T(8,128)(2,1)S(1)}, bf16[64,640]{1,0:T(8,128)(2,1)S(1)}, u32[]{:S(2)}, u32[]{:S(2)}) collective-permute-start(bf16[64,640]{1,0:T(8,128)(2,1)S(1)} %left_rows.1), channel_id=1, source_target_pairs={{0,8},{16,24},{32,40},{48,56},{64,72},{80,88},{96,104},{112,120},{... | collective-permute-start | bytes 245768 | tf_op jit(solution)/shard_map/ppermute | solution.py:487
  37.0 2.8 %collective-permute-start.3 = (bf16[64,640]{1,0:T(8,128)(2,1)S(1)}, bf16[64,640]{1,0:T(8,128)(2,1)S(1)}, u32[]{:S(2)}, u32[]{:S(2)}) collective-permute-start(bf16[64,640]{1,0:T(8,128)(2,1)S(1)} %left_rows.1), channel_id=1, source_target_pairs={{0,12},{16,28},{32,44},{48,60},{64,76},{80,92},{96,108},{112,124},... | collective-permute-start | bytes 245768 | tf_op jit(solution)/shard_map/ppermute | solution.py:487
  39.8 8.8 %copy-start.2 = (bf16[16,256,128]{2,1,0:T(8,128)(2,1)S(1)}, bf16[16,256,128]{2,1,0:T(8,128)(2,1)}, u32[]{:S(2)}) copy-start(bf16[16,256,128]{2,1,0:T(8,128)(2,1)} %adjoint.1) | copy-start | bytes 3145732
  39.8 6.0 %collective-permute-start.7 = (bf16[8,320,128]{2,1,0:T(8,128)(2,1)S(1)}, bf16[8,320,128]{2,1,0:T(8,128)(2,1)S(1)}, u32[]{:S(2)}, u32[]{:S(2)}) collective-permute-start(bf16[8,320,128]{2,1,0:T(8,128)(2,1)S(1)} %all_to_all.15.mine), channel_id=1, source_target_pairs={{0,16},{16,0},{32,48},{48,32},{64,80},{80,64},{96,112},{112,96},{1... | collective-permute-start | bytes 1966088 | tf_op jit(solution)/shard_map/ppermute | solution.py:448
  41.9 6.7 %collective-permute-start.4 = (bf16[64,640]{1,0:T(8,128)(2,1)S(1)}, bf16[64,640]{1,0:T(8,128)(2,1)S(1)}, u32[]{:S(2)}, u32[]{:S(2)}) collective-permute-start(bf16[64,640]{1,0:T(8,128)(2,1)S(1)} %add_add_fusion.tree), channel_id=1, source_target_pairs={{0,1},{4,5},{8,9},{12,13},{16,17},{20,21},{24,25},{28,29},{32,33},... | collective-permute-start | bytes 245768 | tf_op jit(solution)/shard_map/ppermute | solution.py:412
  43.2 5.4 %collective-permute-start.5 = (bf16[64,640]{1,0:T(8,128)(2,1)S(1)}, bf16[64,640]{1,0:T(8,128)(2,1)S(1)}, u32[]{:S(2)}, u32[]{:S(2)}) collective-permute-start(bf16[64,640]{1,0:T(8,128)(2,1)S(1)} %add_add_fusion.tree), channel_id=1, source_target_pairs={{0,2},{4,6},{8,10},{12,14},{16,18},{20,22},{24,26},{28,30},{32,34}... | collective-permute-start | bytes 245768 | tf_op jit(solution)/shard_map/ppermute | solution.py:412
  44.5 4.1 %collective-permute-start.6 = (bf16[64,640]{1,0:T(8,128)(2,1)S(1)}, bf16[64,640]{1,0:T(8,128)(2,1)S(1)}, u32[]{:S(2)}, u32[]{:S(2)}) collective-permute-start(bf16[64,640]{1,0:T(8,128)(2,1)S(1)} %add_add_fusion.tree), channel_id=1, source_target_pairs={{0,3},{4,7},{8,11},{12,15},{16,19},{20,23},{24,27},{28,31},{32,35}... | collective-permute-start | bytes 245768 | tf_op jit(solution)/shard_map/ppermute | solution.py:412
  56.0 7.1 %collective-permute-start.10 = (bf16[256,128]{1,0:T(8,128)(2,1)S(1)}, bf16[256,128]{1,0:T(8,128)(2,1)S(1)}, u32[]{:S(2)}, u32[]{:S(2)}) collective-permute-start(bf16[256,128]{1,0:T(8,128)(2,1)S(1)} %convert_element_type.3), channel_id=1, source_target_pairs={{3,0},{7,4},{11,8},{15,12},{19,16},{23,20},{27,24},{31,28},{35,32}... | collective-permute-start | bytes 196616 | tf_op jit(solution)/shard_map/ppermute | solution.py:535
  57.3 6.9 %collective-permute-start.8 = (bf16[256,128]{1,0:T(8,128)(2,1)S(1)}, bf16[256,128]{1,0:T(8,128)(2,1)S(1)}, u32[]{:S(2)}, u32[]{:S(2)}) collective-permute-start(bf16[256,128]{1,0:T(8,128)(2,1)S(1)} %convert_element_type.3), channel_id=1, source_target_pairs={{1,0},{5,4},{9,8},{13,12},{17,16},{21,20},{25,24},{29,28},{33,32},... | collective-permute-start | bytes 196616 | tf_op jit(solution)/shard_map/ppermute | solution.py:535
  58.6 5.6 %collective-permute-start.9 = (bf16[256,128]{1,0:T(8,128)(2,1)S(1)}, bf16[256,128]{1,0:T(8,128)(2,1)S(1)}, u32[]{:S(2)}, u32[]{:S(2)}) collective-permute-start(bf16[256,128]{1,0:T(8,128)(2,1)S(1)} %convert_element_type.3), channel_id=1, source_target_pairs={{2,0},{6,4},{10,8},{14,12},{18,16},{22,20},{26,24},{30,28},{34,32}... | collective-permute-start | bytes 196616 | tf_op jit(solution)/shard_map/ppermute | solution.py:535
  59.9 9.3 %copy-start.6 = (f32[128]{0:T(128)S(1)}, f32[128]{0:T(128)}, u32[]{:S(2)}) copy-start(f32[128]{0:T(128)} %param.14) | copy-start | bytes 1540
  64.3 13.4 %collective-permute-start.12 = (bf16[256,128]{1,0:T(8,128)(2,1)S(1)}, bf16[256,128]{1,0:T(8,128)(2,1)S(1)}, u32[]{:S(2)}, u32[]{:S(2)}) collective-permute-start(bf16[256,128]{1,0:T(8,128)(2,1)S(1)} %get-tuple-element.81), channel_id=1, source_target_pairs={{4,0},{20,16},{36,32},{52,48},{68,64},{84,80},{100,96},{116,112},{... | collective-permute-start | bytes 196616 | tf_op jit(solution)/shard_map/ppermute | solution.py:559
  65.6 12.1 %collective-permute-start.13 = (bf16[256,128]{1,0:T(8,128)(2,1)S(1)}, bf16[256,128]{1,0:T(8,128)(2,1)S(1)}, u32[]{:S(2)}, u32[]{:S(2)}) collective-permute-start(bf16[256,128]{1,0:T(8,128)(2,1)S(1)} %get-tuple-element.81), channel_id=1, source_target_pairs={{8,0},{24,16},{40,32},{56,48},{72,64},{88,80},{104,96},{120,112},{... | collective-permute-start | bytes 196616 | tf_op jit(solution)/shard_map/ppermute | solution.py:559
  66.9 10.8 %collective-permute-start.14 = (bf16[256,128]{1,0:T(8,128)(2,1)S(1)}, bf16[256,128]{1,0:T(8,128)(2,1)S(1)}, u32[]{:S(2)}, u32[]{:S(2)}) collective-permute-start(bf16[256,128]{1,0:T(8,128)(2,1)S(1)} %get-tuple-element.81), channel_id=1, source_target_pairs={{12,0},{28,16},{44,32},{60,48},{76,64},{92,80},{108,96},{124,112},... | collective-permute-start | bytes 196616 | tf_op jit(solution)/shard_map/ppermute | solution.py:559
  68.2 11.0 %collective-permute-start.11 = (bf16[2048,128]{1,0:T(8,128)(2,1)S(1)}, bf16[2048,128]{1,0:T(8,128)(2,1)S(1)}, u32[]{:S(2)}, u32[]{:S(2)}) collective-permute-start(bf16[2048,128]{1,0:T(8,128)(2,1)S(1)} %get-tuple-element.78), channel_id=1, source_target_pairs={{0,16},{16,0},{32,48},{48,32},{64,80},{80,64},{96,112},{112,96},{1... | collective-permute-start | bytes 1572872 | tf_op jit(solution)/shard_map/ppermute | solution.py:448
  69.2 29.4 %copy-start.7 = (bf16[4,256,256]{2,1,0:T(8,128)(2,1)S(1)}, bf16[4,256,256]{2,1,0:T(8,128)(2,1)}, u32[]{:S(2)}) copy-start(bf16[4,256,256]{2,1,0:T(8,128)(2,1)} %get-tuple-element.89.normed) | copy-start | bytes 1572868
  69.2 29.4 %copy-start.8 = (f32[8,256]{1,0:T(8,128)S(1)}, f32[8,256]{1,0:T(8,128)}, u32[]{:S(2)}) copy-start(f32[8,256]{1,0:T(8,128)} %get-tuple-element.90.live) | copy-start | bytes 24580
  69.2 38.1 %copy-start.3 = (bf16[4,256,256]{2,1,0:T(8,128)(2,1)S(1)}, bf16[4,256,256]{2,1,0:T(8,128)(2,1)}, u32[]{:S(2)}) copy-start(bf16[4,256,256]{2,1,0:T(8,128)(2,1)} %msa.3) | copy-start | bytes 1572868
  69.2 38.1 %copy-start.5 = (bf16[256,64]{0,1:T(8,128)(2,1)S(1)}, bf16[256,64]{0,1:T(8,128)(2,1)}, u32[]{:S(2)}) copy-start(bf16[256,64]{0,1:T(8,128)(2,1)} %param.11) | copy-start | bytes 98308
  77.7 1.4 %collective-permute-start.15 = (bf16[512,128]{1,0:T(8,128)(2,1)S(1)}, bf16[512,128]{1,0:T(8,128)(2,1)S(1)}, u32[]{:S(2)}, u32[]{:S(2)}) collective-permute-start(bf16[512,128]{1,0:T(8,128)(2,1)S(1)} %get-tuple-element.82), channel_id=1, source_target_pairs={{0,16},{16,0},{32,48},{48,32},{64,80},{80,64},{96,112},{112,96},{1... | collective-permute-start | bytes 393224 | tf_op jit(solution)/shard_map/ppermute | solution.py:448
  96.6 2.0 %collective-permute-start.16 = (bf16[256,128]{1,0:T(8,128)(2,1)S(1)}, bf16[256,128]{1,0:T(8,128)(2,1)S(1)}, u32[]{:S(2)}, u32[]{:S(2)}) collective-permute-start(bf16[256,128]{1,0:T(8,128)(2,1)S(1)} %get-tuple-element.88), channel_id=1, source_target_pairs={{0,16},{16,0},{32,48},{48,32},{64,80},{80,64},{96,112},{112,96},{1... | collective-permute-start | bytes 196616 | tf_op jit(solution)/shard_map/ppermute | solution.py:448
  99.5 1.3 collective-permute-start.17
  100.7 8.4 %collective-permute-start.18 = (bf16[144,128]{1,0:T(8,128)(2,1)S(1)}, bf16[144,128]{1,0:T(8,128)(2,1)S(1)}, u32[]{:S(2)}, u32[]{:S(2)}) collective-permute-start(bf16[144,128]{1,0:T(8,128)(2,1)S(1)} %pack_column.1.part_0), channel_id=1, source_target_pairs={{0,4},{1,5},{2,6},{3,7},{4,0},{5,1},{6,2},{7,3},{8,12},{9,13},{10,... | collective-permute-start | bytes 110600 | tf_op jit(solution)/shard_map/ppermute | solution.py:418
  102.7 7.5 %collective-permute-start.19 = (bf16[144,128]{1,0:T(8,128)(2,1)S(1)}, bf16[144,128]{1,0:T(8,128)(2,1)S(1)}, u32[]{:S(2)}, u32[]{:S(2)}) collective-permute-start(bf16[144,128]{1,0:T(8,128)(2,1)S(1)} %pack_column.1.part_0), channel_id=1, source_target_pairs={{0,8},{1,9},{2,10},{3,11},{4,12},{5,13},{6,14},{7,15},{8,0},{9,1},... | collective-permute-start | bytes 110600 | tf_op jit(solution)/shard_map/ppermute | solution.py:418
  107.3 4.9 %collective-permute-start.20 = (bf16[144,128]{1,0:T(8,128)(2,1)S(1)}, bf16[144,128]{1,0:T(8,128)(2,1)S(1)}, u32[]{:S(2)}, u32[]{:S(2)}) collective-permute-start(bf16[144,128]{1,0:T(8,128)(2,1)S(1)} %pack_column.1.part_0), channel_id=1, source_target_pairs={{0,12},{1,13},{2,14},{3,15},{4,8},{5,9},{6,10},{7,11},{8,4},{9,5},... | collective-permute-start | bytes 110600 | tf_op jit(solution)/shard_map/ppermute | solution.py:418
  112.2 2.9 %collective-permute-start.21 = (bf16[144,128]{1,0:T(8,128)(2,1)S(1)}, bf16[144,128]{1,0:T(8,128)(2,1)S(1)}, u32[]{:S(2)}, u32[]{:S(2)}) collective-permute-start(bf16[144,128]{1,0:T(8,128)(2,1)S(1)} %column_sum.1.part_0), channel_id=1, source_target_pairs={{0,1},{1,0},{2,3},{3,2},{4,5},{5,4},{6,7},{7,6},{8,9},{9,8},{10,11... | collective-permute-start | bytes 110600 | tf_op jit(solution)/shard_map/ppermute | solution.py:418
  112.3 2.9 %collective-permute-start.22 = (bf16[144,128]{1,0:T(8,128)(2,1)S(1)}, bf16[144,128]{1,0:T(8,128)(2,1)S(1)}, u32[]{:S(2)}, u32[]{:S(2)}) collective-permute-start(bf16[144,128]{1,0:T(8,128)(2,1)S(1)} %column_sum.1.part_0), channel_id=1, source_target_pairs={{0,2},{1,3},{2,0},{3,1},{4,6},{5,7},{6,4},{7,5},{8,10},{9,11},{10,... | collective-permute-start | bytes 110600 | tf_op jit(solution)/shard_map/ppermute | solution.py:418
  112.4 4.3 %collective-permute-start.23 = (bf16[144,128]{1,0:T(8,128)(2,1)S(1)}, bf16[144,128]{1,0:T(8,128)(2,1)S(1)}, u32[]{:S(2)}, u32[]{:S(2)}) collective-permute-start(bf16[144,128]{1,0:T(8,128)(2,1)S(1)} %column_sum.1.part_0), channel_id=1, source_target_pairs={{0,3},{1,2},{2,1},{3,0},{4,7},{5,6},{6,5},{7,4},{8,11},{9,10},{10,... | collective-permute-start | bytes 110600 | tf_op jit(solution)/shard_map/ppermute | solution.py:418
  127.2 6.0 %collective-permute-start.24 = (bf16[8,144,128]{2,1,0:T(8,128)(2,1)S(1)}, bf16[8,144,128]{2,1,0:T(8,128)(2,1)S(1)}, u32[]{:S(2)}, u32[]{:S(2)}) collective-permute-start(bf16[8,144,128]{2,1,0:T(8,128)(2,1)S(1)} %all_to_all.17.mine), channel_id=1, source_target_pairs={{0,16},{16,0},{32,48},{48,32},{64,80},{80,64},{96,112},{112,96},{1... | collective-permute-start | bytes 884744 | tf_op jit(solution)/shard_map/ppermute | solution.py:448
  (2 other events, 7.9 us)

commit v5 on v4

--- a/solution.py
+++ b/solution.py
@@ -33,11 +33,12 @@
     return center * scale, scale
 
 
-def project_kernel(dims, info, msa, present, label, weights, offset, normed, live_ref, send, keep, right, left):
+def project_kernel(dims, msa, present, label, weights, offset, normed, live_ref, send, keep, right, left):
     src, seqs, hidden, row_dev, places, half = dims
     pairs = src // 2
-    me, core = info[0], lax.rem(info[0], 2)
-    first = info[1] == 0
+    me = lax.axis_index("row")
+    core = lax.rem(me, 2)
+    first = lax.axis_index("col") == 0
     seq = me * seqs + lax.broadcasted_iota(jnp.int32, (seqs, places), 0)
     chain = lax.rem(seq + (CHAINS - PAIRED % CHAINS), CHAINS)
     permitted = (seq < PAIRED) | (chain == jnp.broadcast_to(label[...], (seqs, places)))
@@ -79,9 +80,9 @@
             ].astype(BF)
 
 
-def pack_forward_kernel(dims, info, keep, came, out):
-    src, seqs, hidden, row_dev, places, half = dims
-    core = lax.rem(info[0], 2)
+def pack_forward_kernel(dims, keep, came, out):
+    src, seqs, hidden, row_dev, places, half = dims
+    core = lax.rem(lax.axis_index("row"), 2)
     base = seqs * hidden
     for ref, who in ((keep, core), (came, 1 - core)):
         value = ref[pl.ds(0, base), :]
@@ -109,11 +110,11 @@
     out[...] = jnp.concatenate(blocks, axis=1).astype(BF)
 
 
-def unpack_right_kernel(dims, info, mine, other, weights, r_ref, live_t_ref, by_e, by_e_t, r_all, flags, w_all):
+def unpack_right_kernel(dims, mine, other, weights, r_ref, live_t_ref, by_e, by_e_t, r_all, flags, w_all):
     src, seqs, hidden, row_dev, places, half = dims
     base = seqs * hidden
     lines = src * base
-    core = lax.rem(info[0], 2)
+    core = lax.rem(lax.axis_index("row"), 2)
     for ref, h in ((mine, core), (other, 1 - core)):
         for q in range(src // 2):
             r_all[rows_at(h * lines + q * 2 * base, 2 * base), :] = ref[q, : 2 * base, :].astype(F32)
@@ -135,13 +136,13 @@
         live_t_ref[pl.ds(h * half, half), :] = jnp.concatenate(rows, axis=0).T.astype(BF)
 
 
-def first_kernel(dims, info, tree, near_1, near_2, near_3, r_ref, live_t, adjoint, weights, g_ref, s_ref, d_ref, left_ref, bias_ref, left_out, left_t, total):
+def first_kernel(dims, tree, near_1, near_2, near_3, r_ref, live_t, adjoint, weights, g_ref, s_ref, d_ref, left_ref, bias_ref, left_out, left_t, total):
     src, seqs, hidden, row_dev, places, half = dims
     step = pl.program_id(0)
 
     @pl.when(step == 0)
     def _():
-        pair = info[0] // 2
+        pair = lax.axis_index("row") // 2
         spread = tree[...].astype(F32) + near_1[...].astype(F32) + near_2[...].astype(F32) + near_3[...].astype(F32)
         band = spread[:, :half].astype(BF)
         left = spread[:, half:]
@@ -179,40 +180,54 @@
             )
 
 
-def second_kernel(dims, info, left_t, r_ref, s_ref, d_ref, weights_t, offset, pair_ref, keep, send, outer, before, held):
+def outer_of(left_t, r_ref, outer):
+    for e in range(E_BLOCK):
+        outer[e] = dot(left_t[...], r_ref[e], 1, 0).astype(BF)
+
+
+def outer_row(outer, i, hidden):
+    return outer[:, pl.ds(i * hidden, hidden), :].reshape(E_BLOCK * hidden, outer.shape[2])
+
+
+def second_kernel(dims, left_t, r_ref, s_ref, keep, send, outer, held):
     src, seqs, hidden, row_dev, places, half = dims
     step = pl.program_id(0)
     block_lines = E_BLOCK * hidden
+    outer_of(left_t, r_ref, outer)
+    acc = jnp.zeros((block_lines, half), F32)
+    for i in range(0, row_dev, FUSE):
+        blocks = [outer_row(outer, i + n, hidden) for n in range(FUSE)]
+        scaled = s_ref[pl.ds(i, FUSE)].reshape(FUSE * places, half)
+        acc = acc + dot(jnp.concatenate(blocks, axis=1), scaled, 1, 0)
+    held[rows_at(step * block_lines, block_lines), :] = acc
+
+    @pl.when(step == pl.num_programs(0) - 1)
+    def _():
+        core = lax.rem(lax.axis_index("row"), 2)
+        lines = hidden * hidden // 2
+        keep[...] = held[rows_at(core * lines, lines), :]
+        send[...] = held[rows_at((1 - core) * lines, lines), :].astype(BF)
+
+
+def pair_kernel(dims, left_t, r_ref, d_ref, weights_t, offset, pair_ref, outer, before):
+    src, seqs, hidden, row_dev, places, half = dims
+    step = pl.program_id(0)
 
     @pl.when(step == 0)
     def _():
         before[...] = jnp.zeros_like(before)
 
-    for e in range(E_BLOCK):
-        outer[e] = dot(left_t[...], r_ref[e], 1, 0).astype(BF)
-    acc = jnp.zeros((block_lines, half), F32)
+    outer_of(left_t, r_ref, outer)
     for i in range(row_dev):
-        block = outer[:, pl.ds(i * hidden, hidden), :].reshape(block_lines, places)
-        before[i] = before[i] + dot(weights_t[...], block, 1, 0)
-    for i in range(0, row_dev, FUSE):
-        blocks = [
-            outer[:, pl.ds((i + n) * hidden, hidden), :].reshape(block_lines, places) for n in range(FUSE)
-        ]
-        scaled = s_ref[pl.ds(i, FUSE)].reshape(FUSE * places, half)
-        acc = acc + dot(jnp.concatenate(blocks, axis=1), scaled, 1, 0)
-    held[rows_at(step * block_lines, block_lines), :] = acc
+        before[i] = before[i] + dot(weights_t[...], outer_row(outer, i, hidden), 1, 0)
 
     @pl.when(step == pl.num_programs(0) - 1)
     def _():
-        core = lax.rem(info[0], 2)
-        lines = hidden * hidden // 2
-        keep[...] = held[rows_at(core * lines, lines), :]
-        send[...] = held[rows_at((1 - core) * lines, lines), :].astype(BF)
         for i in range(row_dev):
             pair_ref[i] = ((before[i].T + offset[...]) / d_ref[i].astype(F32)).astype(BF)
 
 
-def third_kernel(dims, info, left, g_ref, keep, send, held):
+def third_kernel(dims, left, g_ref, keep, send, held):
     src, seqs, hidden, row_dev, places, half = dims
     step = pl.program_id(0)
     base = seqs * hidden
@@ -227,18 +242,18 @@
 
     @pl.when(step == pl.num_programs(0) - 1)
     def _():
-        core = lax.rem(info[0], 2)
+        core = lax.rem(lax.axis_index("row"), 2)
         keep[...] = held[rows_at(core * lines, lines), :]
         send[...] = held[rows_at((1 - core) * lines, lines), :].astype(BF)
 
 
-def pack_backward_kernel(dims, info, keep, came, w_keep, w_came, left, far_1, far_2, far_3, out):
+def pack_backward_kernel(dims, keep, came, w_keep, w_came, left, far_1, far_2, far_3, out):
     src, seqs, hidden, row_dev, places, half = dims
     pairs = src // 2
     lines = 2 * seqs * hidden
     w_lines = hidden * hidden // src
     total = left[...] + far_1[...].astype(F32) + far_2[...].astype(F32) + far_3[...].astype(F32)
-    total = jnp.where(info[1] == 0, total, 0.0).astype(BF)
+    total = jnp.where(lax.axis_index("col") == 0, total, 0.0).astype(BF)
     for q in range(pairs):
         span = pl.ds(q * lines, lines)
         out[q, pl.ds(0, lines), :] = (keep[span, :] + came[span, :].astype(F32)).astype(BF)
@@ -247,12 +262,12 @@
         out[q, pl.ds(lines + w_lines, 2 * row_dev), :] = total[q * 2 * row_dev : (q + 1) * 2 * row_dev]
 
 
-def unpack_backward_kernel(dims, info, arrived, send, keep, chunk, held):
+def unpack_backward_kernel(dims, arrived, send, keep, chunk, held):
     src, seqs, hidden, row_dev, places, half = dims
     pairs = src // 2
     base = seqs * hidden
     w_lines = hidden * hidden // src
-    core = lax.rem(info[0], 2)
+    core = lax.rem(lax.axis_index("row"), 2)
     total = arrived[0, : 2 * base + w_lines, :].astype(F32)
     for q in range(1, pairs):
         total = total + arrived[q, : 2 * base + w_lines, :].astype(F32)
@@ -266,10 +281,10 @@
             ]
 
 
-def projector_kernel(dims, info, keep, came, normed, live, bias, grads, w_keep, w_send, small, right, left):
+def projector_kernel(dims, keep, came, normed, live, bias, grads, w_keep, w_send, small, right, left):
     src, seqs, hidden, row_dev, places, half = dims
     base = seqs * hidden
-    core = lax.rem(info[0], 2)
+    core = lax.rem(lax.axis_index("row"), 2)
     for ref, who in ((keep, core), (came, 1 - core)):
         right[rows_at(who * base, base), :] = ref[pl.ds(0, base), :].astype(F32)
         for q in range(src // 2):
@@ -347,9 +362,9 @@
         out[q, pl.ds(total.shape[0], GROUP), :] = small
 
 
-def finish_kernel(dims, info, mine, other, projector, projector_bias, weight, bias, held):
-    src, seqs, hidden, row_dev, places, half = dims
-    core = lax.rem(info[0], 2)
+def finish_kernel(dims, mine, other, projector, projector_bias, weight, bias, held):
+    src, seqs, hidden, row_dev, places, half = dims
+    core = lax.rem(lax.axis_index("row"), 2)
     w_lines = hidden * hidden // src
     at = 2 * hidden + w_lines
     sums = []
@@ -380,15 +395,9 @@
     return pl.BlockSpec(shape, lambda t: (0,) * len(shape))
 
 
-SCALARS = pl.BlockSpec(memory_space=pltpu.SMEM)
-
-
 def call(kernel, dims, name, args, outs, scratch=(), steps=1, in_specs=None, out_specs=None, macs=0, room=16):
     in_specs, out_specs = in_specs or {}, out_specs or {}
-    specs = [
-        SCALARS if a.dtype == jnp.int32 and a.ndim == 1 else in_specs.get(n, whole(*a.shape))
-        for n, a in enumerate(args)
-    ]
+    specs = [in_specs.get(n, whole(*a.shape)) for n, a in enumerate(args)]
     size = sum(a.size * a.dtype.itemsize for a in args)
     size += sum(o.size * jnp.dtype(o.dtype).itemsize for o in outs)
     result = pl.pallas_call(
@@ -440,7 +449,6 @@
     total = rows * seqs
     lines = row_dev * hidden
     w_lines = hidden * hidden // rows
-    info = jnp.stack([lax.axis_index("row"), lax.axis_index("col")]).astype(jnp.int32)
     swap = [(i, i ^ 1) for i in range(rows)]
     same_core = [list(range(c, rows, 2)) for c in range(2)]
 
@@ -455,7 +463,7 @@
         project_kernel,
         dims,
         "project",
-        (info, homolog_features, presence_indicator, polymer_label[None], lowering_matrix.T, lowering_offset[None]),
+        (homolog_features, presence_indicator, polymer_label[None], lowering_matrix.T, lowering_offset[None]),
         (
             shape_of(BF, seqs, places, depth),
             shape_of(F32, 8, places),
@@ -472,7 +480,7 @@
         pack_forward_kernel,
         dims,
         "pack_forward",
-        (info, keep, came),
+        (keep, came),
         (shape_of(BF, pairs, 2 * (base + GROUP + row_dev), half),),
     )[0]
     mine = over_pairs(packed)
@@ -493,7 +501,7 @@
         unpack_right_kernel,
         dims,
         "unpack_right",
-        (info, mine, other, outgoing_matrix),
+        (mine, other, outgoing_matrix),
         (
             shape_of(BF, hidden, total, places),
             shape_of(BF, places, total),
@@ -513,7 +521,7 @@
         first_kernel,
         dims,
         "scaled_outer_grad",
-        (info, tree, *near, right_cols, live_t, update_adjoint, by_e),
+        (tree, *near, right_cols, live_t, update_adjoint, by_e),
         (
             shape_of(BF, hidden, lines, places),
             shape_of(BF, row_dev, places, channels),
@@ -539,11 +547,11 @@
         third_kernel,
         dims,
         "right_grad",
-        (info, left_rows, outer_grad),
+        (left_rows, outer_grad),
         (shape_of(F32, rows * base, half), shape_of(BF, rows * base, half)),
         [((2 * rows * base, half), F32)],
         steps=hidden // E_WIDE,
-        in_specs={2: by_block(E_WIDE, lines, places)},
+        in_specs={1: by_block(E_WIDE, lines, places)},
         macs=270_000_000,
         room=24,
     )
@@ -557,27 +565,16 @@
     )
     left_t, sent = lax.optimization_barrier((left_t, sent))
     far = [lax.ppermute(sent, "col", [(d, 0)]) for d in range(STEP, cols, STEP)]
-    pair_increment, w_keep, w_send = call(
+    w_keep, w_send = call(
         second_kernel,
         dims,
-        "outer_pair",
-        (info, left_t, right_cols, scaled, divisor, by_e_t, outgoing_offset[None]),
-        (
-            shape_of(BF, row_dev, places, channels),
-            shape_of(F32, hidden * hidden // 2, channels),
-            shape_of(BF, hidden * hidden // 2, channels),
-        ),
-        [
-            ((E_BLOCK, lines, places), BF),
-            ((row_dev, channels, places), F32),
-            ((hidden * hidden, channels), F32),
-        ],
+        "outer_weight_grad",
+        (left_t, right_cols, scaled),
+        (shape_of(F32, hidden * hidden // 2, channels), shape_of(BF, hidden * hidden // 2, channels)),
+        [((E_BLOCK, lines, places), BF), ((hidden * hidden, channels), F32)],
         steps=hidden // E_BLOCK,
-        in_specs={
-            2: by_block(E_BLOCK, total, places),
-            5: pl.BlockSpec((channels, E_BLOCK * hidden), lambda t: (0, t)),
-        },
-        macs=1_300_000_000,
+        in_specs={1: by_block(E_BLOCK, total, places)},
+        macs=800_000_000,
         room=20,
     )
     w_send, *far = lax.optimization_barrier((w_send, *far))
@@ -587,7 +584,7 @@
         pack_backward_kernel,
         dims,
         "pack_backward",
-        (info, right_keep, right_came, w_keep, w_came, left_grad, *far),
+        (right_keep, right_came, w_keep, w_came, left_grad, *far),
         (shape_of(BF, pairs, 2 * base + w_lines + 2 * row_dev, half),),
     )[0]
     arrived = over_pairs(packed)
@@ -596,7 +593,7 @@
         unpack_backward_kernel,
         dims,
         "unpack_backward",
-        (info, arrived),
+        (arrived,),
         (
             shape_of(BF, base + pairs * row_dev, half),
             shape_of(BF, base + pairs * row_dev, half),
@@ -609,7 +606,7 @@
         projector_kernel,
         dims,
         "projector_grad",
-        (info, keep, came, normed, live, bias_grad),
+        (keep, came, normed, live, bias_grad),
         (
             shape_of(BF, seqs * 2 * hidden, places),
             shape_of(F32, 2 * hidden, half),
@@ -625,6 +622,24 @@
         pack_column_kernel, dims, "pack_column", (w_keep, w_came, chunk, small), (shape_of(BF, size, half),)
     )[0]
     parts = swap_parts(own, cols, STEP)
+    pair_increment = call(
+        pair_kernel,
+        dims,
+        "outer_pair",
+        (left_t, right_cols, divisor, by_e_t, outgoing_offset[None]),
+        (shape_of(BF, row_dev, places, channels),),
+        [((E_BLOCK, lines, places), BF), ((row_dev, channels, places), F32)],
+        steps=hidden // E_BLOCK,
+        in_specs={
+            1: by_block(E_BLOCK, total, places),
+            3: pl.BlockSpec((channels, E_BLOCK * hidden), lambda t: (0, t)),
+        },
+        macs=800_000_000,
+        room=20,
+    )[0]
+    *parts, pair_increment = lax.optimization_barrier((*parts, pair_increment))
+    own = call(column_sum_kernel, dims, "column_sum", parts, (shape_of(BF, size, half),))[0]
+    parts = swap_parts(own, cols, 1)
     alignment_gradient = call(
         align_kernel,
         dims,
@@ -634,8 +649,6 @@
         macs=200_000_000,
     )[0]
     *parts, alignment_gradient = lax.optimization_barrier((*parts, alignment_gradient))
-    own = call(column_sum_kernel, dims, "column_sum", parts, (shape_of(BF, size, half),))[0]
-    parts = swap_parts(own, cols, 1)
     packed = call(pack_row_kernel, dims, "pack_row", parts, (shape_of(BF, pairs, size, half),))[0]
     mine = over_pairs(packed)
     other = partner(mine)
@@ -643,7 +656,7 @@
         finish_kernel,
         dims,
         "finish",
-        (info, mine, other),
+        (mine, other),
         (
             shape_of(F32, 2 * hidden, depth),
             shape_of(F32, 1, 2 * hidden),

time: 135 us -> 128 us (0.948)
  waiting for transfers between devices: 12.9 us -> 8.2 us
  Pallas kernels: 31.1 us -> 28.6 us
    ppermute x6, waiting for transfers between devices: 4.83 us -> 0.02 us  [swap_parts(): lax.ppermute(block, 'col', [(i, i ^ d * unit) for i in range(cols)])]
    pallas_call x16 -> x17, Pallas kernels: 31.1 us -> 28.6 us  [call(): pl.pallas_call(functools.partial(kernel, dims), grid=(steps,), in_specs=s...]
    ppermute x7, starting transfers between devices: 12.8 us -> 14.7 us  [partner(): return lax.ppermute(block, 'row', swap)]
  transfers between devices with their start and end apart: 25 -> 25, of which waited for: 13 -> 9; matrix products, arithmetic and copies ran while one was open for 0% -> 0% of each run, Pallas kernels for 12% -> 13%
where the time goes in v5:
time: 128 us
  starting transfers between devices  45.5 us (36%)
  blocking collectives  43.4 us (34%)
  Pallas kernels  28.6 us (22%)
  waiting for transfers between devices  8.2 us (6%)
    all_to_all x3, blocking collectives, over_pairs(): lax.all_to_all(block, 'row', 0, 0, axis_index_groups=same_core, tiled=True)  43.4 us
    pallas_call x17, Pallas kernels, call(): pl.pallas_call(functools.partial(kernel, dims), grid=(steps,), in_specs=s...  28.6 us
    ppermute x7, starting transfers between devices, partner(): return lax.ppermute(block, 'row', swap)  14.7 us
    ppermute x3, starting transfers between devices, per_device(): far = [lax.ppermute(tree, 'col', [(0, d)]) for d in range(STEP, cols, STEP)]  10.8 us
    ppermute x6, starting transfers between devices, swap_parts(): lax.ppermute(block, 'col', [(i, i ^ d * unit) for i in range(cols)])  8.38 us
    ppermute x7, waiting for transfers between devices, partner(): return lax.ppermute(block, 'row', swap)  5.06 us
    ppermute x3, starting transfers between devices, per_device(): lax.ppermute(sent, 'col', [(a + d, a) for a in range(0, cols, STEP)])  3.88 us
    ppermute x3, starting transfers between devices, per_device(): far = [lax.ppermute(sent, 'col', [(d, 0)]) for d in range(STEP, cols, STEP)]  3.88 us
  transfers between devices with their start and end apart: 25, of which 9 were waited for; matrix products, arithmetic and copies ran while one was open for 0% of the time, Pallas kernels for 13%

profile of v5, /device:TPU:1, one launch (start us, length us, event | category | flops | bytes accessed | tf_op | source)
XLA Modules:
  0.0 127.6 jit_solution(13250552603131818528)
XLA Ops:
  0.6 2.6 %project.1 = (bf16[4,256,256]{2,1,0:T(8,128)(2,1)}, f32[8,256]{1,0:T(8,128)}, bf16[272,128]{1,0:T(8,128)(2,1)}, bf16[272,128]{1,0:T(8,128)(2,1)}) custom-call(bf16[4,256,256]{2,1,0:T(8,128)(2,1)} %msa.3, s32[4,256]{1,0:T(4,128)} %present.1, s32[1,256]{1,0:T(1,128)} %bitcast.11, bf16[64,256]{1,0:T(8,128)(2,1)} %bitcast.7, f32[1,64]{1,0:T(1,128)} %bitcast.12), custom_call_target="tpu_custom_call" | custom-call | flops 4000000000 | bytes 1234176 | tf_op jit(solution)/shard_map/project/pallas_call | solution.py:403
  3.3 3.2 %collective-permute-start = (bf16[272,128]{1,0:T(8,128)(2,1)}, bf16[272,128]{1,0:T(8,128)(2,1)S(1)}, u32[]{:S(2)}, u32[]{:S(2)}) collective-permute-start(bf16[272,128]{1,0:T(8,128)(2,1)} %get-tuple-element.61), channel_id=1, source_target_pairs={{0,16},{16,0},{32,48},{48,32},{64,80},{80,64},{96,112},{112,96},{1... | collective-permute-start | bytes 208904 | tf_op jit(solution)/shard_map/ppermute | solution.py:456
  8.6 17.5 %all_to_all.15.mine = bf16[8,320,128]{2,1,0:T(8,128)(2,1)S(1)} all-to-all(bf16[8,320,128]{2,1,0:T(8,128)(2,1)S(1)} %pack_forward.1), channel_id=1, replica_groups={{0,32,64,96,128,160,192,224},{16,48,80,112,144,176,208,240},{1,33,65,97..., dimensions={0} | all-to-all | bytes 1310720 | tf_op jit(solution)/shard_map/all_to_all | solution.py:459
  26.4 7.9 %collective-permute-start.3 = (bf16[64,640]{1,0:T(8,128)(2,1)S(1)}, bf16[64,640]{1,0:T(8,128)(2,1)S(1)}, u32[]{:S(2)}, u32[]{:S(2)}) collective-permute-start(bf16[64,640]{1,0:T(8,128)(2,1)S(1)} %left_rows.1), channel_id=1, source_target_pairs={{0,12},{16,28},{32,44},{48,60},{64,76},{80,92},{96,108},{112,124},... | collective-permute-start | bytes 245768 | tf_op jit(solution)/shard_map/ppermute | solution.py:495
  34.3 1.6 %collective-permute-start.2 = (bf16[64,640]{1,0:T(8,128)(2,1)S(1)}, bf16[64,640]{1,0:T(8,128)(2,1)S(1)}, u32[]{:S(2)}, u32[]{:S(2)}) collective-permute-start(bf16[64,640]{1,0:T(8,128)(2,1)S(1)} %left_rows.1), channel_id=1, source_target_pairs={{0,8},{16,24},{32,40},{48,56},{64,72},{80,88},{96,104},{112,120},{... | collective-permute-start | bytes 245768 | tf_op jit(solution)/shard_map/ppermute | solution.py:495
  35.9 1.3 %collective-permute-start.1 = (bf16[64,640]{1,0:T(8,128)(2,1)S(1)}, bf16[64,640]{1,0:T(8,128)(2,1)S(1)}, u32[]{:S(2)}, u32[]{:S(2)}) collective-permute-start(bf16[64,640]{1,0:T(8,128)(2,1)S(1)} %left_rows.1), channel_id=1, source_target_pairs={{0,4},{16,20},{32,36},{48,52},{64,68},{80,84},{96,100},{112,116},{... | collective-permute-start | bytes 245768 | tf_op jit(solution)/shard_map/ppermute | solution.py:495
  37.4 1.8 %collective-permute-done.1 = bf16[64,640]{1,0:T(8,128)(2,1)S(1)} collective-permute-done((bf16[64,640]{1,0:T(8,128)(2,1)S(1)}, bf16[64,640]{1,0:T(8,128)(2,1)S(1)}, u32[]{:S(2)}, u32[]{:S(2)}) %collective-permute-start.1) | collective-permute-done | bytes 81952 | tf_op jit(solution)/shard_map/ppermute | solution.py:495
  39.2 1.7 %collective-permute-start.7 = (bf16[8,320,128]{2,1,0:T(8,128)(2,1)S(1)}, bf16[8,320,128]{2,1,0:T(8,128)(2,1)S(1)}, u32[]{:S(2)}, u32[]{:S(2)}) collective-permute-start(bf16[8,320,128]{2,1,0:T(8,128)(2,1)S(1)} %all_to_all.15.mine), channel_id=1, source_target_pairs={{0,16},{16,0},{32,48},{48,32},{64,80},{80,64},{96,112},{112,96},{1... | collective-permute-start | bytes 1966088 | tf_op jit(solution)/shard_map/ppermute | solution.py:456
  40.8 1.3 %collective-permute-start.6 = (bf16[64,640]{1,0:T(8,128)(2,1)S(1)}, bf16[64,640]{1,0:T(8,128)(2,1)S(1)}, u32[]{:S(2)}, u32[]{:S(2)}) collective-permute-start(bf16[64,640]{1,0:T(8,128)(2,1)S(1)} %add_add_fusion.tree), channel_id=1, source_target_pairs={{0,3},{4,7},{8,11},{12,15},{16,19},{20,23},{24,27},{28,31},{32,35}... | collective-permute-start | bytes 245768 | tf_op jit(solution)/shard_map/ppermute | solution.py:421
  42.1 1.3 %collective-permute-start.5 = (bf16[64,640]{1,0:T(8,128)(2,1)S(1)}, bf16[64,640]{1,0:T(8,128)(2,1)S(1)}, u32[]{:S(2)}, u32[]{:S(2)}) collective-permute-start(bf16[64,640]{1,0:T(8,128)(2,1)S(1)} %add_add_fusion.tree), channel_id=1, source_target_pairs={{0,2},{4,6},{8,10},{12,14},{16,18},{20,22},{24,26},{28,30},{32,34}... | collective-permute-start | bytes 245768 | tf_op jit(solution)/shard_map/ppermute | solution.py:421
  43.4 1.3 %collective-permute-start.4 = (bf16[64,640]{1,0:T(8,128)(2,1)S(1)}, bf16[64,640]{1,0:T(8,128)(2,1)S(1)}, u32[]{:S(2)}, u32[]{:S(2)}) collective-permute-start(bf16[64,640]{1,0:T(8,128)(2,1)S(1)} %add_add_fusion.tree), channel_id=1, source_target_pairs={{0,1},{4,5},{8,9},{12,13},{16,17},{20,21},{24,25},{28,29},{32,33},... | collective-permute-start | bytes 245768 | tf_op jit(solution)/shard_map/ppermute | solution.py:421
  44.7 1.9 %unpack_right.1 = (bf16[32,64,256]{2,1,0:T(8,128)(2,1)S(1)}, bf16[256,64]{1,0:T(8,128)(2,1)S(1)}, bf16[1024,128]{1,0:T(8,128)(2,1)S(1)}, bf16[128,1024]{1,0:T(8,128)(2,1)S(1)}) custom-call(bf16[8,320,128]{2,1,0:T(8,128)(2,1)S(1)} %all_to_all.15.mine, bf16[8,320,128]{2,1,0:T(8,128)(2,1)S(1)} %collective-permute-done.7.other, bf16[1024,128]{1,0:T(8,128)(2,1)S(1)} %copy-done.3), custom_call_target="tpu_custom_call" | custom-call | flops 12000000000 | bytes 3178496 | tf_op jit(solution)/shard_map/unpack_right/pallas_call | solution.py:403
  46.7 6.8 %scaled_outer_grad.1 = (bf16[32,512,256]{2,1,0:T(8,128)(2,1)S(1)}, bf16[16,256,128]{2,1,0:T(8,128)(2,1)S(1)}, bf16[16,256,128]{2,1,0:T(8,128)(2,1)S(1)}, f32[256...) custom-call(bf16[64,640]{1,0:T(8,128)(2,1)S(1)} %add_add_fusion.tree, ...), custom_call_target="tpu_custom_call" | custom-call | flops 32000000000 | bytes 13468160 | tf_op jit(solution)/shard_map/scaled_outer_grad/pallas_call | solution.py:403
  53.5 1.3 %collective-permute-start.10 = (bf16[256,128]{1,0:T(8,128)(2,1)S(1)}, bf16[256,128]{1,0:T(8,128)(2,1)S(1)}, u32[]{:S(2)}, u32[]{:S(2)}) collective-permute-start(bf16[256,128]{1,0:T(8,128)(2,1)S(1)} %convert_element_type.3), channel_id=1, source_target_pairs={{3,0},{7,4},{11,8},{15,12},{19,16},{23,20},{27,24},{31,28},{35,32}... | collective-permute-start | bytes 196616 | tf_op jit(solution)/shard_map/ppermute | solution.py:543
  54.8 1.3 %collective-permute-start.9 = (bf16[256,128]{1,0:T(8,128)(2,1)S(1)}, bf16[256,128]{1,0:T(8,128)(2,1)S(1)}, u32[]{:S(2)}, u32[]{:S(2)}) collective-permute-start(bf16[256,128]{1,0:T(8,128)(2,1)S(1)} %convert_element_type.3), channel_id=1, source_target_pairs={{2,0},{6,4},{10,8},{14,12},{18,16},{22,20},{26,24},{30,28},{34,32}... | collective-permute-start | bytes 196616 | tf_op jit(solution)/shard_map/ppermute | solution.py:543
  56.1 1.3 %collective-permute-start.8 = (bf16[256,128]{1,0:T(8,128)(2,1)S(1)}, bf16[256,128]{1,0:T(8,128)(2,1)S(1)}, u32[]{:S(2)}, u32[]{:S(2)}) collective-permute-start(bf16[256,128]{1,0:T(8,128)(2,1)S(1)} %convert_element_type.3), channel_id=1, source_target_pairs={{1,0},{5,4},{9,8},{13,12},{17,16},{21,20},{25,24},{29,28},{33,32},... | collective-permute-start | bytes 196616 | tf_op jit(solution)/shard_map/ppermute | solution.py:543
  57.4 2.6 %right_grad.1 = (f32[2048,128]{1,0:T(8,128)S(1)}, bf16[2048,128]{1,0:T(8,128)(2,1)S(1)}) custom-call(bf16[64,512]{1,0:T(8,128)(2,1)S(1)} %get-tuple-element.67.left, bf16[32,512,256]{2,1,0:T(8,128)(2,1)S(1)} %get-tuple-element.68.g_ref), custom_call_target="tpu_custom_call" | custom-call | flops 10800000000 | bytes 10027008 | tf_op jit(solution)/shard_map/right_grad/pallas_call | solution.py:403
  61.3 1.3 %collective-permute-start.14 = (bf16[256,128]{1,0:T(8,128)(2,1)S(1)}, bf16[256,128]{1,0:T(8,128)(2,1)S(1)}, u32[]{:S(2)}, u32[]{:S(2)}) collective-permute-start(bf16[256,128]{1,0:T(8,128)(2,1)S(1)} %get-tuple-element.82), channel_id=1, source_target_pairs={{12,0},{28,16},{44,32},{60,48},{76,64},{92,80},{108,96},{124,112},... | collective-permute-start | bytes 196616 | tf_op jit(solution)/shard_map/ppermute | solution.py:567
  62.6 1.3 %collective-permute-start.13 = (bf16[256,128]{1,0:T(8,128)(2,1)S(1)}, bf16[256,128]{1,0:T(8,128)(2,1)S(1)}, u32[]{:S(2)}, u32[]{:S(2)}) collective-permute-start(bf16[256,128]{1,0:T(8,128)(2,1)S(1)} %get-tuple-element.82), channel_id=1, source_target_pairs={{8,0},{24,16},{40,32},{56,48},{72,64},{88,80},{104,96},{120,112},{... | collective-permute-start | bytes 196616 | tf_op jit(solution)/shard_map/ppermute | solution.py:567
  63.9 1.3 %collective-permute-start.12 = (bf16[256,128]{1,0:T(8,128)(2,1)S(1)}, bf16[256,128]{1,0:T(8,128)(2,1)S(1)}, u32[]{:S(2)}, u32[]{:S(2)}) collective-permute-start(bf16[256,128]{1,0:T(8,128)(2,1)S(1)} %get-tuple-element.82), channel_id=1, source_target_pairs={{4,0},{20,16},{36,32},{52,48},{68,64},{84,80},{100,96},{116,112},{... | collective-permute-start | bytes 196616 | tf_op jit(solution)/shard_map/ppermute | solution.py:567
  65.2 1.8 %collective-permute-start.11 = (bf16[2048,128]{1,0:T(8,128)(2,1)S(1)}, bf16[2048,128]{1,0:T(8,128)(2,1)S(1)}, u32[]{:S(2)}, u32[]{:S(2)}) collective-permute-start(bf16[2048,128]{1,0:T(8,128)(2,1)S(1)} %get-tuple-element.72), channel_id=1, source_target_pairs={{0,16},{16,0},{32,48},{48,32},{64,80},{80,64},{96,112},{112,96},{1... | collective-permute-start | bytes 1572872 | tf_op jit(solution)/shard_map/ppermute | solution.py:456
  66.9 5.0 %outer_weight_grad.1 = (f32[512,128]{1,0:T(8,128)S(1)}, bf16[512,128]{1,0:T(8,128)(2,1)S(1)}) custom-call(bf16[512,64]{1,0:T(8,128)(2,1)S(1)} %get-tuple-element.78.left_t, bf16[32,64,256]{2,1,0:T(8,128)(2,1)S(1)} %get-tuple-element.64.r_ref, bf16[16,256,128]{2,1,0:T(8,128)(2,1)S(1)} %get-tuple-element.79.s_ref), custom_call_target="tpu_custom_call" | custom-call | flops 32000000000 | bytes 2555904 | tf_op jit(solution)/shard_map/outer_weight_grad/pallas_call | solution.py:403
  72.0 2.3 %collective-permute-start.15 = (bf16[512,128]{1,0:T(8,128)(2,1)S(1)}, bf16[512,128]{1,0:T(8,128)(2,1)S(1)}, u32[]{:S(2)}, u32[]{:S(2)}) collective-permute-start(bf16[512,128]{1,0:T(8,128)(2,1)S(1)} %get-tuple-element.83), channel_id=1, source_target_pairs={{0,16},{16,0},{32,48},{48,32},{64,80},{80,64},{96,112},{112,96},{1... | collective-permute-start | bytes 393224 | tf_op jit(solution)/shard_map/ppermute | solution.py:456
  75.5 15.5 %all_to_all.16.arrived = bf16[8,352,128]{2,1,0:T(8,128)(2,1)S(1)} all-to-all(bf16[8,352,128]{2,1,0:T(8,128)(2,1)S(1)} %pack_backward.1), channel_id=1, replica_groups={{0,32,64,96,128,160,192,224},{16,48,80,112,144,176,208,240},{1,33,65,97..., dimensions={0} | all-to-all | bytes 1441792 | tf_op jit(solution)/shard_map/all_to_all | solution.py:459
  91.1 1.8 %collective-permute-start.16 = (bf16[256,128]{1,0:T(8,128)(2,1)S(1)}, bf16[256,128]{1,0:T(8,128)(2,1)S(1)}, u32[]{:S(2)}, u32[]{:S(2)}) collective-permute-start(bf16[256,128]{1,0:T(8,128)(2,1)S(1)} %get-tuple-element.89), channel_id=1, source_target_pairs={{0,16},{16,0},{32,48},{48,32},{64,80},{80,64},{96,112},{112,96},{1... | collective-permute-start | bytes 196616 | tf_op jit(solution)/shard_map/ppermute | solution.py:456
  95.4 1.3 %collective-permute-start.20 = (bf16[144,128]{1,0:T(8,128)(2,1)S(1)}, bf16[144,128]{1,0:T(8,128)(2,1)S(1)}, u32[]{:S(2)}, u32[]{:S(2)}) collective-permute-start(bf16[144,128]{1,0:T(8,128)(2,1)S(1)} %pack_column.1.part_0), channel_id=1, source_target_pairs={{0,12},{1,13},{2,14},{3,15},{4,8},{5,9},{6,10},{7,11},{8,4},{9,5},... | collective-permute-start | bytes 110600 | tf_op jit(solution)/shard_map/ppermute | solution.py:427
  96.7 3.3 %collective-permute-start.19 = (bf16[144,128]{1,0:T(8,128)(2,1)S(1)}, bf16[144,128]{1,0:T(8,128)(2,1)S(1)}, u32[]{:S(2)}, u32[]{:S(2)}) collective-permute-start(bf16[144,128]{1,0:T(8,128)(2,1)S(1)} %pack_column.1.part_0), channel_id=1, source_target_pairs={{0,8},{1,9},{2,10},{3,11},{4,12},{5,13},{6,14},{7,15},{8,0},{9,1},... | collective-permute-start | bytes 110600 | tf_op jit(solution)/shard_map/ppermute | solution.py:427
  101.1 5.7 %outer_pair.1 = bf16[16,256,128]{2,1,0:T(8,128)(2,1)} custom-call(bf16[512,64]{1,0:T(8,128)(2,1)S(1)} %get-tuple-element.78.left_t, bf16[32,64,256]{2,1,0:T(8,128)(2,1)S(1)} %get-tuple-element.64.r_ref, bf16[16,256,128]{2,1,0:T(8,128)(2,1)S(1)} %get-tuple-element.97.d_ref, bf16[128,1024]{1,0:T(8,128)(2,1)S(1)} %get-tuple-element.98.weights_t, ...), custom_call_target="tpu_custom_call" | custom-call | flops 32000000000 | bytes 3473920 | tf_op jit(solution)/shard_map/outer_pair/pallas_call | solution.py:403
  107.0 2.5 %collective-permute-start.21 = (bf16[144,128]{1,0:T(8,128)(2,1)S(1)}, bf16[144,128]{1,0:T(8,128)(2,1)S(1)}, u32[]{:S(2)}, u32[]{:S(2)}) collective-permute-start(bf16[144,128]{1,0:T(8,128)(2,1)S(1)} %column_sum.1.part_0), channel_id=1, source_target_pairs={{0,1},{1,0},{2,3},{3,2},{4,5},{5,4},{6,7},{7,6},{8,9},{9,8},{10,11... | collective-permute-start | bytes 110600 | tf_op jit(solution)/shard_map/ppermute | solution.py:427
  109.5 1.8 %alignment.1 = bf16[4,256,256]{2,1,0:T(8,128)(2,1)} custom-call(bf16[4,256,256]{2,1,0:T(8,128)(2,1)S(1)} %copy-done.2, bf16[256,256]{1,0:T(8,128)(2,1)S(1)} %get-tuple-element.104.grads, bf16[64,256]{1,0:T(8,128)(2,1)S(1)} %bitcast.8), custom_call_target="tpu_custom_call" | custom-call | flops 8000000000 | bytes 1212416 | tf_op jit(solution)/shard_map/alignment/pallas_call | solution.py:403
  111.4 10.4 %all_to_all.17.mine = bf16[8,144,128]{2,1,0:T(8,128)(2,1)S(1)} all-to-all(bf16[8,144,128]{2,1,0:T(8,128)(2,1)S(1)} %pack_row.1), channel_id=1, replica_groups={{0,32,64,96,128,160,192,224},{16,48,80,112,144,176,208,240},{1,33,65,97..., dimensions={0} | all-to-all | bytes 589824 | tf_op jit(solution)/shard_map/all_to_all | solution.py:459
  121.8 3.4 %collective-permute-start.24 = (bf16[8,144,128]{2,1,0:T(8,128)(2,1)S(1)}, bf16[8,144,128]{2,1,0:T(8,128)(2,1)S(1)}, u32[]{:S(2)}, u32[]{:S(2)}) collective-permute-start(bf16[8,144,128]{2,1,0:T(8,128)(2,1)S(1)} %all_to_all.17.mine), channel_id=1, source_target_pairs={{0,16},{16,0},{32,48},{48,32},{64,80},{80,64},{96,112},{112,96},{1... | collective-permute-start | bytes 884744 | tf_op jit(solution)/shard_map/ppermute | solution.py:456
  (56 shorter events, 11.2 us)
Async XLA Ops:
  0.6 44.1 %copy-start.3 = (bf16[1024,128]{1,0:T(8,128)(2,1)S(1)}, bf16[1024,128]{1,0:T(8,128)(2,1)}, u32[]{:S(2)}) copy-start(bf16[1024,128]{1,0:T(8,128)(2,1)} %weights.1) | copy-start | bytes 786436
  3.3 4.4 %collective-permute-start = (bf16[272,128]{1,0:T(8,128)(2,1)}, bf16[272,128]{1,0:T(8,128)(2,1)S(1)}, u32[]{:S(2)}, u32[]{:S(2)}) collective-permute-start(bf16[272,128]{1,0:T(8,128)(2,1)} %get-tuple-element.61), channel_id=1, source_target_pairs={{0,16},{16,0},{32,48},{48,32},{64,80},{80,64},{96,112},{112,96},{1... | collective-permute-start | bytes 208904 | tf_op jit(solution)/shard_map/ppermute | solution.py:456
  26.4 10.8 %collective-permute-start.3 = (bf16[64,640]{1,0:T(8,128)(2,1)S(1)}, bf16[64,640]{1,0:T(8,128)(2,1)S(1)}, u32[]{:S(2)}, u32[]{:S(2)}) collective-permute-start(bf16[64,640]{1,0:T(8,128)(2,1)S(1)} %left_rows.1), channel_id=1, source_target_pairs={{0,12},{16,28},{32,44},{48,60},{64,76},{80,92},{96,108},{112,124},... | collective-permute-start | bytes 245768 | tf_op jit(solution)/shard_map/ppermute | solution.py:495
  34.3 3.0 %collective-permute-start.2 = (bf16[64,640]{1,0:T(8,128)(2,1)S(1)}, bf16[64,640]{1,0:T(8,128)(2,1)S(1)}, u32[]{:S(2)}, u32[]{:S(2)}) collective-permute-start(bf16[64,640]{1,0:T(8,128)(2,1)S(1)} %left_rows.1), channel_id=1, source_target_pairs={{0,8},{16,24},{32,40},{48,56},{64,72},{80,88},{96,104},{112,120},{... | collective-permute-start | bytes 245768 | tf_op jit(solution)/shard_map/ppermute | solution.py:495
  35.9 3.2 %collective-permute-start.1 = (bf16[64,640]{1,0:T(8,128)(2,1)S(1)}, bf16[64,640]{1,0:T(8,128)(2,1)S(1)}, u32[]{:S(2)}, u32[]{:S(2)}) collective-permute-start(bf16[64,640]{1,0:T(8,128)(2,1)S(1)} %left_rows.1), channel_id=1, source_target_pairs={{0,4},{16,20},{32,36},{48,52},{64,68},{80,84},{96,100},{112,116},{... | collective-permute-start | bytes 245768 | tf_op jit(solution)/shard_map/ppermute | solution.py:495
  39.1 7.6 %copy-start.1 = (bf16[16,256,128]{2,1,0:T(8,128)(2,1)S(1)}, bf16[16,256,128]{2,1,0:T(8,128)(2,1)}, u32[]{:S(2)}) copy-start(bf16[16,256,128]{2,1,0:T(8,128)(2,1)} %adjoint.1) | copy-start | bytes 3145732
  39.2 5.6 %collective-permute-start.7 = (bf16[8,320,128]{2,1,0:T(8,128)(2,1)S(1)}, bf16[8,320,128]{2,1,0:T(8,128)(2,1)S(1)}, u32[]{:S(2)}, u32[]{:S(2)}) collective-permute-start(bf16[8,320,128]{2,1,0:T(8,128)(2,1)S(1)} %all_to_all.15.mine), channel_id=1, source_target_pairs={{0,16},{16,0},{32,48},{48,32},{64,80},{80,64},{96,112},{112,96},{1... | collective-permute-start | bytes 1966088 | tf_op jit(solution)/shard_map/ppermute | solution.py:456
  40.8 5.8 %collective-permute-start.6 = (bf16[64,640]{1,0:T(8,128)(2,1)S(1)}, bf16[64,640]{1,0:T(8,128)(2,1)S(1)}, u32[]{:S(2)}, u32[]{:S(2)}) collective-permute-start(bf16[64,640]{1,0:T(8,128)(2,1)S(1)} %add_add_fusion.tree), channel_id=1, source_target_pairs={{0,3},{4,7},{8,11},{12,15},{16,19},{20,23},{24,27},{28,31},{32,35}... | collective-permute-start | bytes 245768 | tf_op jit(solution)/shard_map/ppermute | solution.py:421
  42.1 4.6 %collective-permute-start.5 = (bf16[64,640]{1,0:T(8,128)(2,1)S(1)}, bf16[64,640]{1,0:T(8,128)(2,1)S(1)}, u32[]{:S(2)}, u32[]{:S(2)}) collective-permute-start(bf16[64,640]{1,0:T(8,128)(2,1)S(1)} %add_add_fusion.tree), channel_id=1, source_target_pairs={{0,2},{4,6},{8,10},{12,14},{16,18},{20,22},{24,26},{28,30},{32,34}... | collective-permute-start | bytes 245768 | tf_op jit(solution)/shard_map/ppermute | solution.py:421
  43.4 3.3 %collective-permute-start.4 = (bf16[64,640]{1,0:T(8,128)(2,1)S(1)}, bf16[64,640]{1,0:T(8,128)(2,1)S(1)}, u32[]{:S(2)}, u32[]{:S(2)}) collective-permute-start(bf16[64,640]{1,0:T(8,128)(2,1)S(1)} %add_add_fusion.tree), channel_id=1, source_target_pairs={{0,1},{4,5},{8,9},{12,13},{16,17},{20,21},{24,25},{28,29},{32,33},... | collective-permute-start | bytes 245768 | tf_op jit(solution)/shard_map/ppermute | solution.py:421
  53.5 6.5 %collective-permute-start.10 = (bf16[256,128]{1,0:T(8,128)(2,1)S(1)}, bf16[256,128]{1,0:T(8,128)(2,1)S(1)}, u32[]{:S(2)}, u32[]{:S(2)}) collective-permute-start(bf16[256,128]{1,0:T(8,128)(2,1)S(1)} %convert_element_type.3), channel_id=1, source_target_pairs={{3,0},{7,4},{11,8},{15,12},{19,16},{23,20},{27,24},{31,28},{35,32}... | collective-permute-start | bytes 196616 | tf_op jit(solution)/shard_map/ppermute | solution.py:543
  54.8 5.3 %collective-permute-start.9 = (bf16[256,128]{1,0:T(8,128)(2,1)S(1)}, bf16[256,128]{1,0:T(8,128)(2,1)S(1)}, u32[]{:S(2)}, u32[]{:S(2)}) collective-permute-start(bf16[256,128]{1,0:T(8,128)(2,1)S(1)} %convert_element_type.3), channel_id=1, source_target_pairs={{2,0},{6,4},{10,8},{14,12},{18,16},{22,20},{26,24},{30,28},{34,32}... | collective-permute-start | bytes 196616 | tf_op jit(solution)/shard_map/ppermute | solution.py:543
  56.1 5.1 %collective-permute-start.8 = (bf16[256,128]{1,0:T(8,128)(2,1)S(1)}, bf16[256,128]{1,0:T(8,128)(2,1)S(1)}, u32[]{:S(2)}, u32[]{:S(2)}) collective-permute-start(bf16[256,128]{1,0:T(8,128)(2,1)S(1)} %convert_element_type.3), channel_id=1, source_target_pairs={{1,0},{5,4},{9,8},{13,12},{17,16},{21,20},{25,24},{29,28},{33,32},... | collective-permute-start | bytes 196616 | tf_op jit(solution)/shard_map/ppermute | solution.py:543
  61.3 10.7 %collective-permute-start.14 = (bf16[256,128]{1,0:T(8,128)(2,1)S(1)}, bf16[256,128]{1,0:T(8,128)(2,1)S(1)}, u32[]{:S(2)}, u32[]{:S(2)}) collective-permute-start(bf16[256,128]{1,0:T(8,128)(2,1)S(1)} %get-tuple-element.82), channel_id=1, source_target_pairs={{12,0},{28,16},{44,32},{60,48},{76,64},{92,80},{108,96},{124,112},... | collective-permute-start | bytes 196616 | tf_op jit(solution)/shard_map/ppermute | solution.py:567
  62.6 9.4 %collective-permute-start.13 = (bf16[256,128]{1,0:T(8,128)(2,1)S(1)}, bf16[256,128]{1,0:T(8,128)(2,1)S(1)}, u32[]{:S(2)}, u32[]{:S(2)}) collective-permute-start(bf16[256,128]{1,0:T(8,128)(2,1)S(1)} %get-tuple-element.82), channel_id=1, source_target_pairs={{8,0},{24,16},{40,32},{56,48},{72,64},{88,80},{104,96},{120,112},{... | collective-permute-start | bytes 196616 | tf_op jit(solution)/shard_map/ppermute | solution.py:567
  63.9 8.1 %collective-permute-start.12 = (bf16[256,128]{1,0:T(8,128)(2,1)S(1)}, bf16[256,128]{1,0:T(8,128)(2,1)S(1)}, u32[]{:S(2)}, u32[]{:S(2)}) collective-permute-start(bf16[256,128]{1,0:T(8,128)(2,1)S(1)} %get-tuple-element.82), channel_id=1, source_target_pairs={{4,0},{20,16},{36,32},{52,48},{68,64},{84,80},{100,96},{116,112},{... | collective-permute-start | bytes 196616 | tf_op jit(solution)/shard_map/ppermute | solution.py:567
  65.2 10.2 %collective-permute-start.11 = (bf16[2048,128]{1,0:T(8,128)(2,1)S(1)}, bf16[2048,128]{1,0:T(8,128)(2,1)S(1)}, u32[]{:S(2)}, u32[]{:S(2)}) collective-permute-start(bf16[2048,128]{1,0:T(8,128)(2,1)S(1)} %get-tuple-element.72), channel_id=1, source_target_pairs={{0,16},{16,0},{32,48},{48,32},{64,80},{80,64},{96,112},{112,96},{1... | collective-permute-start | bytes 1572872 | tf_op jit(solution)/shard_map/ppermute | solution.py:456
  66.9 26.9 %copy-start.6 = (bf16[4,256,256]{2,1,0:T(8,128)(2,1)S(1)}, bf16[4,256,256]{2,1,0:T(8,128)(2,1)}, u32[]{:S(2)}) copy-start(bf16[4,256,256]{2,1,0:T(8,128)(2,1)} %get-tuple-element.90.normed) | copy-start | bytes 1572868
  66.9 26.9 %copy-start.7 = (f32[8,256]{1,0:T(8,128)S(1)}, f32[8,256]{1,0:T(8,128)}, u32[]{:S(2)}) copy-start(f32[8,256]{1,0:T(8,128)} %get-tuple-element.91.live) | copy-start | bytes 24580
  66.9 34.1 %copy-start.5 = (f32[128]{0:T(128)S(1)}, f32[128]{0:T(128)}, u32[]{:S(2)}) copy-start(f32[128]{0:T(128)} %param.14) | copy-start | bytes 1540
  72.0 3.3 %collective-permute-start.15 = (bf16[512,128]{1,0:T(8,128)(2,1)S(1)}, bf16[512,128]{1,0:T(8,128)(2,1)S(1)}, u32[]{:S(2)}, u32[]{:S(2)}) collective-permute-start(bf16[512,128]{1,0:T(8,128)(2,1)S(1)} %get-tuple-element.83), channel_id=1, source_target_pairs={{0,16},{16,0},{32,48},{48,32},{64,80},{80,64},{96,112},{112,96},{1... | collective-permute-start | bytes 393224 | tf_op jit(solution)/shard_map/ppermute | solution.py:456
  91.1 2.7 %collective-permute-start.16 = (bf16[256,128]{1,0:T(8,128)(2,1)S(1)}, bf16[256,128]{1,0:T(8,128)(2,1)S(1)}, u32[]{:S(2)}, u32[]{:S(2)}) collective-permute-start(bf16[256,128]{1,0:T(8,128)(2,1)S(1)} %get-tuple-element.89), channel_id=1, source_target_pairs={{0,16},{16,0},{32,48},{48,32},{64,80},{80,64},{96,112},{112,96},{1... | collective-permute-start | bytes 196616 | tf_op jit(solution)/shard_map/ppermute | solution.py:456
  94.1 1.3 %collective-permute-start.17 = (bf16[64,128]{1,0:T(8,128)(2,1)S(1)}, bf16[64,128]{1,0:T(8,128)(2,1)S(1)}, u32[]{:S(2)}, u32[]{:S(2)}) collective-permute-start(bf16[64,128]{1,0:T(8,128)(2,1)S(1)} %get-tuple-element.94), channel_id=1, source_target_pairs={{0,16},{16,0},{32,48},{48,32},{64,80},{80,64},{96,112},{112,96},{1... | collective-permute-start | bytes 49160 | tf_op jit(solution)/shard_map/ppermute | solution.py:456
  95.4 11.3 %collective-permute-start.20 = (bf16[144,128]{1,0:T(8,128)(2,1)S(1)}, bf16[144,128]{1,0:T(8,128)(2,1)S(1)}, u32[]{:S(2)}, u32[]{:S(2)}) collective-permute-start(bf16[144,128]{1,0:T(8,128)(2,1)S(1)} %pack_column.1.part_0), channel_id=1, source_target_pairs={{0,12},{1,13},{2,14},{3,15},{4,8},{5,9},{6,10},{7,11},{8,4},{9,5},... | collective-permute-start | bytes 110600 | tf_op jit(solution)/shard_map/ppermute | solution.py:427
  96.7 10.0 %collective-permute-start.19 = (bf16[144,128]{1,0:T(8,128)(2,1)S(1)}, bf16[144,128]{1,0:T(8,128)(2,1)S(1)}, u32[]{:S(2)}, u32[]{:S(2)}) collective-permute-start(bf16[144,128]{1,0:T(8,128)(2,1)S(1)} %pack_column.1.part_0), channel_id=1, source_target_pairs={{0,8},{1,9},{2,10},{3,11},{4,12},{5,13},{6,14},{7,15},{8,0},{9,1},... | collective-permute-start | bytes 110600 | tf_op jit(solution)/shard_map/ppermute | solution.py:427
  100.1 6.7 %collective-permute-start.18 = (bf16[144,128]{1,0:T(8,128)(2,1)S(1)}, bf16[144,128]{1,0:T(8,128)(2,1)S(1)}, u32[]{:S(2)}, u32[]{:S(2)}) collective-permute-start(bf16[144,128]{1,0:T(8,128)(2,1)S(1)} %pack_column.1.part_0), channel_id=1, source_target_pairs={{0,4},{1,5},{2,6},{3,7},{4,0},{5,1},{6,2},{7,3},{8,12},{9,13},{10,... | collective-permute-start | bytes 110600 | tf_op jit(solution)/shard_map/ppermute | solution.py:427
  101.1 8.5 %copy-start.2 = (bf16[4,256,256]{2,1,0:T(8,128)(2,1)S(1)}, bf16[4,256,256]{2,1,0:T(8,128)(2,1)}, u32[]{:S(2)}) copy-start(bf16[4,256,256]{2,1,0:T(8,128)(2,1)} %msa.3) | copy-start | bytes 1572868
  101.1 8.5 %copy-start.4 = (bf16[256,64]{0,1:T(8,128)(2,1)S(1)}, bf16[256,64]{0,1:T(8,128)(2,1)}, u32[]{:S(2)}) copy-start(bf16[256,64]{0,1:T(8,128)(2,1)} %param.11) | copy-start | bytes 98308
  106.8 4.6 %collective-permute-start.23 = (bf16[144,128]{1,0:T(8,128)(2,1)S(1)}, bf16[144,128]{1,0:T(8,128)(2,1)S(1)}, u32[]{:S(2)}, u32[]{:S(2)}) collective-permute-start(bf16[144,128]{1,0:T(8,128)(2,1)S(1)} %column_sum.1.part_0), channel_id=1, source_target_pairs={{0,3},{1,2},{2,1},{3,0},{4,7},{5,6},{6,5},{7,4},{8,11},{9,10},{10,... | collective-permute-start | bytes 110600 | tf_op jit(solution)/shard_map/ppermute | solution.py:427
  106.9 4.5 %collective-permute-start.22 = (bf16[144,128]{1,0:T(8,128)(2,1)S(1)}, bf16[144,128]{1,0:T(8,128)(2,1)S(1)}, u32[]{:S(2)}, u32[]{:S(2)}) collective-permute-start(bf16[144,128]{1,0:T(8,128)(2,1)S(1)} %column_sum.1.part_0), channel_id=1, source_target_pairs={{0,2},{1,3},{2,0},{3,1},{4,6},{5,7},{6,4},{7,5},{8,10},{9,11},{10,... | collective-permute-start | bytes 110600 | tf_op jit(solution)/shard_map/ppermute | solution.py:427
  107.0 4.4 %collective-permute-start.21 = (bf16[144,128]{1,0:T(8,128)(2,1)S(1)}, bf16[144,128]{1,0:T(8,128)(2,1)S(1)}, u32[]{:S(2)}, u32[]{:S(2)}) collective-permute-start(bf16[144,128]{1,0:T(8,128)(2,1)S(1)} %column_sum.1.part_0), channel_id=1, source_target_pairs={{0,1},{1,0},{2,3},{3,2},{4,5},{5,4},{6,7},{7,6},{8,9},{9,8},{10,11... | collective-permute-start | bytes 110600 | tf_op jit(solution)/shard_map/ppermute | solution.py:427
  121.8 4.6 %collective-permute-start.24 = (bf16[8,144,128]{2,1,0:T(8,128)(2,1)S(1)}, bf16[8,144,128]{2,1,0:T(8,128)(2,1)S(1)}, u32[]{:S(2)}, u32[]{:S(2)}) collective-permute-start(bf16[8,144,128]{2,1,0:T(8,128)(2,1)S(1)} %all_to_all.17.mine), channel_id=1, source_target_pairs={{0,16},{16,0},{32,48},{48,32},{64,80},{80,64},{96,112},{112,96},{1... | collective-permute-start | bytes 884744 | tf_op jit(solution)/shard_map/ppermute | solution.py:456
  (1 other events, 0.9 us)

commit v6 on v5

--- a/solution.py
+++ b/solution.py
@@ -13,9 +13,8 @@
 F32 = jnp.float32
 STEP = 4
 GROUP = 16
-E_BLOCK = 8
-E_WIDE = 16
-FUSE = 4
+FUSE_E = 8
+FUSE_I = 8
 
 
 def dot(a, b, lhs, rhs):
@@ -80,6 +79,10 @@
             ].astype(BF)
 
 
+def move_kernel(dims, block, out):
+    out[...] = block[...]
+
+
 def pack_forward_kernel(dims, keep, came, out):
     src, seqs, hidden, row_dev, places, half = dims
     core = lax.rem(lax.axis_index("row"), 2)
@@ -136,115 +139,85 @@
         live_t_ref[pl.ds(h * half, half), :] = jnp.concatenate(rows, axis=0).T.astype(BF)
 
 
-def first_kernel(dims, tree, near_1, near_2, near_3, r_ref, live_t, adjoint, weights, g_ref, s_ref, d_ref, left_ref, bias_ref, left_out, left_t, total):
-    src, seqs, hidden, row_dev, places, half = dims
-    step = pl.program_id(0)
-
-    @pl.when(step == 0)
-    def _():
-        pair = lax.axis_index("row") // 2
-        spread = tree[...].astype(F32) + near_1[...].astype(F32) + near_2[...].astype(F32) + near_3[...].astype(F32)
-        band = spread[:, :half].astype(BF)
-        left = spread[:, half:]
-        left_out[...] = left.astype(BF)
-        left_t[...] = left.T.astype(BF)
-        spot = lax.broadcasted_iota(jnp.int32, (half, half), 0) - pair * row_dev
-        bias = jnp.zeros((1, half), F32)
-        for i in range(row_dev):
-            column = dot(band, jnp.where(spot == i, 1.0, 0.0).astype(BF), 1, 0).astype(BF)
-            divisor = jnp.maximum(dot(live_t[...], column, 1, 0), 1.0)
-            scaled = (adjoint[i].astype(F32) / divisor).astype(BF)
-            d_ref[i] = divisor.astype(BF)
-            s_ref[i] = scaled
-            bias = bias + jnp.sum(scaled.astype(F32), axis=0, keepdims=True)
-        bias_ref[...] = bias
-        total[...] = jnp.zeros_like(total)
-
-    part = weights[pl.ds(step * E_WIDE * hidden, E_WIDE * hidden), :]
+def first_kernel(dims, tree, near_1, near_2, near_3, r_ref, live_t, adjoint, weights, g_ref, s_ref, d_ref, left_ref, bias_ref, left_out, left_t):
+    src, seqs, hidden, row_dev, places, half = dims
+    pair = lax.axis_index("row") // 2
+    spread = tree[...].astype(F32) + near_1[...].astype(F32) + near_2[...].astype(F32) + near_3[...].astype(F32)
+    band = spread[:, :half].astype(BF)
+    left = spread[:, half:]
+    left_out[...] = left.astype(BF)
+    left_t[...] = left.T.astype(BF)
+    spot = lax.broadcasted_iota(jnp.int32, (half, half), 0) - pair * row_dev
+    bias = jnp.zeros((1, half), F32)
     for i in range(row_dev):
-        g = dot(part, s_ref[i], 1, 1).astype(BF)
-        g_ref[:, pl.ds(i * hidden, hidden), :] = g.reshape(E_WIDE, hidden, places)
-    acc = total[...]
-    for e in range(0, E_WIDE, FUSE):
-        right = jnp.concatenate([r_ref[step * E_WIDE + e + n] for n in range(FUSE)], axis=1)
-        grad = jnp.concatenate([g_ref[e + n] for n in range(FUSE)], axis=1)
+        column = dot(band, jnp.where(spot == i, 1.0, 0.0).astype(BF), 1, 0).astype(BF)
+        divisor = jnp.maximum(dot(live_t[...], column, 1, 0), 1.0)
+        scaled = (adjoint[i].astype(F32) / divisor).astype(BF)
+        d_ref[i] = divisor.astype(BF)
+        s_ref[i] = scaled
+        bias = bias + jnp.sum(scaled.astype(F32), axis=0, keepdims=True)
+    bias_ref[...] = bias
+    for i in range(row_dev):
+        g = dot(weights[...], s_ref[i], 1, 1).astype(BF)
+        g_ref[:, pl.ds(i * hidden, hidden), :] = g.reshape(hidden, hidden, places)
+    acc = jnp.zeros((src * seqs, row_dev * hidden), F32)
+    for e in range(0, hidden, FUSE_E):
+        right = jnp.concatenate([r_ref[e + n] for n in range(FUSE_E)], axis=1)
+        grad = jnp.concatenate([g_ref[e + n] for n in range(FUSE_E)], axis=1)
         acc = acc + dot(right, grad, 1, 1)
-    total[...] = acc
-
-    @pl.when(step == pl.num_programs(0) - 1)
-    def _():
-        for i in range(row_dev):
-            block = acc[:, i * hidden : (i + 1) * hidden]
-            left_ref[pl.ds(i, src, stride=row_dev), :] = jnp.concatenate(
-                [block[s * src : (s + 1) * src] for s in range(seqs)], axis=1
-            )
+    for i in range(row_dev):
+        block = acc[:, i * hidden : (i + 1) * hidden]
+        left_ref[pl.ds(i, src, stride=row_dev), :] = jnp.concatenate(
+            [block[s * src : (s + 1) * src] for s in range(seqs)], axis=1
+        )
 
 
 def outer_of(left_t, r_ref, outer):
-    for e in range(E_BLOCK):
+    for e in range(outer.shape[0]):
         outer[e] = dot(left_t[...], r_ref[e], 1, 0).astype(BF)
 
 
 def outer_row(outer, i, hidden):
-    return outer[:, pl.ds(i * hidden, hidden), :].reshape(E_BLOCK * hidden, outer.shape[2])
+    return outer[:, pl.ds(i * hidden, hidden), :].reshape(hidden * hidden, outer.shape[2])
 
 
 def second_kernel(dims, left_t, r_ref, s_ref, keep, send, outer, held):
     src, seqs, hidden, row_dev, places, half = dims
-    step = pl.program_id(0)
-    block_lines = E_BLOCK * hidden
     outer_of(left_t, r_ref, outer)
-    acc = jnp.zeros((block_lines, half), F32)
-    for i in range(0, row_dev, FUSE):
-        blocks = [outer_row(outer, i + n, hidden) for n in range(FUSE)]
-        scaled = s_ref[pl.ds(i, FUSE)].reshape(FUSE * places, half)
+    acc = jnp.zeros((hidden * hidden, half), F32)
+    for i in range(0, row_dev, FUSE_I):
+        blocks = [outer_row(outer, i + n, hidden) for n in range(FUSE_I)]
+        scaled = s_ref[pl.ds(i, FUSE_I)].reshape(FUSE_I * places, half)
         acc = acc + dot(jnp.concatenate(blocks, axis=1), scaled, 1, 0)
-    held[rows_at(step * block_lines, block_lines), :] = acc
-
-    @pl.when(step == pl.num_programs(0) - 1)
-    def _():
-        core = lax.rem(lax.axis_index("row"), 2)
-        lines = hidden * hidden // 2
-        keep[...] = held[rows_at(core * lines, lines), :]
-        send[...] = held[rows_at((1 - core) * lines, lines), :].astype(BF)
-
-
-def pair_kernel(dims, left_t, r_ref, d_ref, weights_t, offset, pair_ref, outer, before):
-    src, seqs, hidden, row_dev, places, half = dims
-    step = pl.program_id(0)
-
-    @pl.when(step == 0)
-    def _():
-        before[...] = jnp.zeros_like(before)
-
+    held[...] = acc
+    core = lax.rem(lax.axis_index("row"), 2)
+    lines = hidden * hidden // 2
+    keep[...] = held[rows_at(core * lines, lines), :]
+    send[...] = held[rows_at((1 - core) * lines, lines), :].astype(BF)
+
+
+def pair_kernel(dims, left_t, r_ref, d_ref, weights_t, offset, pair_ref, outer):
+    src, seqs, hidden, row_dev, places, half = dims
     outer_of(left_t, r_ref, outer)
     for i in range(row_dev):
-        before[i] = before[i] + dot(weights_t[...], outer_row(outer, i, hidden), 1, 0)
-
-    @pl.when(step == pl.num_programs(0) - 1)
-    def _():
-        for i in range(row_dev):
-            pair_ref[i] = ((before[i].T + offset[...]) / d_ref[i].astype(F32)).astype(BF)
+        before = dot(weights_t[...], outer_row(outer, i, hidden), 1, 0)
+        pair_ref[i] = ((before.T + offset[...]) / d_ref[i].astype(F32)).astype(BF)
 
 
 def third_kernel(dims, left, g_ref, keep, send, held):
     src, seqs, hidden, row_dev, places, half = dims
-    step = pl.program_id(0)
     base = seqs * hidden
     lines = src * base
-    for e in range(E_WIDE):
+    for e in range(hidden):
         grad = dot(left[...], g_ref[e], 1, 0)
         for h in range(2):
             for s in range(seqs):
-                held[pl.ds(h * lines + s * hidden + step * E_WIDE + e, src, stride=base), :] = grad[
+                held[pl.ds(h * lines + s * hidden + e, src, stride=base), :] = grad[
                     s * src : (s + 1) * src, h * half : (h + 1) * half
                 ]
-
-    @pl.when(step == pl.num_programs(0) - 1)
-    def _():
-        core = lax.rem(lax.axis_index("row"), 2)
-        keep[...] = held[rows_at(core * lines, lines), :]
-        send[...] = held[rows_at((1 - core) * lines, lines), :].astype(BF)
+    core = lax.rem(lax.axis_index("row"), 2)
+    keep[...] = held[rows_at(core * lines, lines), :]
+    send[...] = held[rows_at((1 - core) * lines, lines), :].astype(BF)
 
 
 def pack_backward_kernel(dims, keep, came, w_keep, w_came, left, far_1, far_2, far_3, out):
@@ -395,16 +368,14 @@
     return pl.BlockSpec(shape, lambda t: (0,) * len(shape))
 
 
-def call(kernel, dims, name, args, outs, scratch=(), steps=1, in_specs=None, out_specs=None, macs=0, room=16):
-    in_specs, out_specs = in_specs or {}, out_specs or {}
-    specs = [in_specs.get(n, whole(*a.shape)) for n, a in enumerate(args)]
+def call(kernel, dims, name, args, outs, scratch=(), macs=0, room=16):
     size = sum(a.size * a.dtype.itemsize for a in args)
     size += sum(o.size * jnp.dtype(o.dtype).itemsize for o in outs)
     result = pl.pallas_call(
         functools.partial(kernel, dims),
-        grid=(steps,),
-        in_specs=specs,
-        out_specs=[out_specs.get(n, whole(*o.shape)) for n, o in enumerate(outs)],
+        grid=(1,),
+        in_specs=[whole(*a.shape) for a in args],
+        out_specs=[whole(*o.shape) for o in outs],
         out_shape=list(outs),
         scratch_shapes=[pltpu.VMEM(s, t) for s, t in scratch],
         compiler_params=pltpu.CompilerParams(
@@ -475,6 +446,8 @@
         room=62,
     )
     came = partner(send)
+    keep = call(move_kernel, dims, "move", (keep,), (shape_of(BF, size, half),))[0]
+    came, keep = lax.optimization_barrier((came, keep))
 
     packed = call(
         pack_forward_kernel,
@@ -516,7 +489,6 @@
         macs=300_000_000,
     )
 
-    by_block = lambda size, *block: pl.BlockSpec((size, *block), lambda t: (t, 0, 0))
     outer_grad, scaled, divisor, left_grad, bias_grad, left_rows, left_t = call(
         first_kernel,
         dims,
@@ -531,11 +503,8 @@
             shape_of(BF, total, lines),
             shape_of(BF, lines, total),
         ),
-        [((total, lines), F32)],
-        steps=hidden // E_WIDE,
-        out_specs={0: by_block(E_WIDE, lines, places)},
         macs=800_000_000,
-        room=24,
+        room=32,
     )
 
     sent = left_grad.astype(BF)
@@ -550,10 +519,8 @@
         (left_rows, outer_grad),
         (shape_of(F32, rows * base, half), shape_of(BF, rows * base, half)),
         [((2 * rows * base, half), F32)],
-        steps=hidden // E_WIDE,
-        in_specs={1: by_block(E_WIDE, lines, places)},
         macs=270_000_000,
-        room=24,
+        room=32,
     )
     *near, right_send = lax.optimization_barrier((*near, right_send))
     left_grad, sent = call(
@@ -571,11 +538,9 @@
         "outer_weight_grad",
         (left_t, right_cols, scaled),
         (shape_of(F32, hidden * hidden // 2, channels), shape_of(BF, hidden * hidden // 2, channels)),
-        [((E_BLOCK, lines, places), BF), ((hidden * hidden, channels), F32)],
-        steps=hidden // E_BLOCK,
-        in_specs={1: by_block(E_BLOCK, total, places)},
+        [((hidden, lines, places), BF), ((hidden * hidden, channels), F32)],
         macs=800_000_000,
-        room=20,
+        room=26,
     )
     w_send, *far = lax.optimization_barrier((w_send, *far))
     w_came = partner(w_send)
@@ -628,14 +593,9 @@
         "outer_pair",
         (left_t, right_cols, divisor, by_e_t, outgoing_offset[None]),
         (shape_of(BF, row_dev, places, channels),),
-        [((E_BLOCK, lines, places), BF), ((row_dev, channels, places), F32)],
-        steps=hidden // E_BLOCK,
-        in_specs={
-            1: by_block(E_BLOCK, total, places),
-            3: pl.BlockSpec((channels, E_BLOCK * hidden), lambda t: (0, t)),
-        },
+        [((hidden, lines, places), BF)],
         macs=800_000_000,
-        room=20,
+        room=26,
     )[0]
     *parts, pair_increment = lax.optimization_barrier((*parts, pair_increment))
     own = call(column_sum_kernel, dims, "column_sum", parts, (shape_of(BF, size, half),))[0]

time: 128 us -> 126 us (0.984)
  Pallas kernels: 28.6 us -> 26.6 us
    pallas_call x17 -> x18, Pallas kernels: 28.6 us -> 26.6 us  [call(): pl.pallas_call(functools.partial(kernel, dims), grid=(1,), in_specs=[whol...]
  transfers between devices with their start and end apart: 25 -> 25, of which waited for: 9 -> 9; matrix products, arithmetic and copies ran while one was open for 0% -> 0% of each run, Pallas kernels for 13% -> 12%
where the time goes in v6:
time: 126 us; the launch traced here: 125 us
  starting transfers between devices  46 us (37%)
  blocking collectives  43.4 us (34%)
  Pallas kernels  26.6 us (21%)
  waiting for transfers between devices  7.34 us (6%)
    all_to_all x3, blocking collectives, over_pairs(): lax.all_to_all(block, 'row', 0, 0, axis_index_groups=same_core, tiled=True)  43.4 us
    pallas_call x18, Pallas kernels, call(): pl.pallas_call(functools.partial(kernel, dims), grid=(1,), in_specs=[whol...  26.6 us
    ppermute x7, starting transfers between devices, partner(): return lax.ppermute(block, 'row', swap)  15 us
    ppermute x3, starting transfers between devices, per_device(): far = [lax.ppermute(tree, 'col', [(0, d)]) for d in range(STEP, cols, STEP)]  10.8 us
    ppermute x6, starting transfers between devices, swap_parts(): lax.ppermute(block, 'col', [(i, i ^ d * unit) for i in range(cols)])  8.6 us
    ppermute x7, waiting for transfers between devices, partner(): return lax.ppermute(block, 'row', swap)  4.17 us
    ppermute x3, starting transfers between devices, per_device(): lax.ppermute(sent, 'col', [(a + d, a) for a in range(0, cols, STEP)])  3.88 us
    ppermute x3, starting transfers between devices, per_device(): far = [lax.ppermute(sent, 'col', [(d, 0)]) for d in range(STEP, cols, STEP)]  3.88 us
  transfers between devices with their start and end apart: 25, of which 9 were waited for; matrix products, arithmetic and copies ran while one was open for 0% of the time, Pallas kernels for 12%

profile of v6, /device:TPU:1, one launch (start us, length us, event | category | flops | bytes accessed | tf_op | source)
XLA Modules:
  0.0 125.3 jit_solution(7090571157588430977)
XLA Ops:
  0.6 2.6 %project.1 = (bf16[4,256,256]{2,1,0:T(8,128)(2,1)}, f32[8,256]{1,0:T(8,128)}, bf16[272,128]{1,0:T(8,128)(2,1)}, bf16[272,128]{1,0:T(8,128)(2,1)}) custom-call(bf16[4,256,256]{2,1,0:T(8,128)(2,1)} %msa.3, s32[4,256]{1,0:T(4,128)} %present.1, s32[1,256]{1,0:T(1,128)} %bitcast.11, bf16[64,256]{1,0:T(8,128)(2,1)} %bitcast.7, f32[1,64]{1,0:T(1,128)} %bitcast.12), custom_call_target="tpu_custom_call" | custom-call | flops 4000000000 | bytes 1234176 | tf_op jit(solution)/shard_map/project/pallas_call | solution.py:374
  3.3 3.2 %collective-permute-start = (bf16[272,128]{1,0:T(8,128)(2,1)}, bf16[272,128]{1,0:T(8,128)(2,1)S(1)}, u32[]{:S(2)}, u32[]{:S(2)}) collective-permute-start(bf16[272,128]{1,0:T(8,128)(2,1)} %get-tuple-element.62), channel_id=1, source_target_pairs={{0,16},{16,0},{32,48},{48,32},{64,80},{80,64},{96,112},{112,96},{1... | collective-permute-start | bytes 208904 | tf_op jit(solution)/shard_map/ppermute | solution.py:427
  7.7 17.5 %all_to_all.15.mine = bf16[8,320,128]{2,1,0:T(8,128)(2,1)S(1)} all-to-all(bf16[8,320,128]{2,1,0:T(8,128)(2,1)S(1)} %pack_forward.1), channel_id=1, replica_groups={{0,32,64,96,128,160,192,224},{16,48,80,112,144,176,208,240},{1,33,65,97..., dimensions={0} | all-to-all | bytes 1310720 | tf_op jit(solution)/shard_map/all_to_all | solution.py:430
  25.5 7.9 %collective-permute-start.3 = (bf16[64,640]{1,0:T(8,128)(2,1)S(1)}, bf16[64,640]{1,0:T(8,128)(2,1)S(1)}, u32[]{:S(2)}, u32[]{:S(2)}) collective-permute-start(bf16[64,640]{1,0:T(8,128)(2,1)S(1)} %left_rows.1), channel_id=1, source_target_pairs={{0,12},{16,28},{32,44},{48,60},{64,76},{80,92},{96,108},{112,124},... | collective-permute-start | bytes 245768 | tf_op jit(solution)/shard_map/ppermute | solution.py:468
  33.4 1.6 %collective-permute-start.2 = (bf16[64,640]{1,0:T(8,128)(2,1)S(1)}, bf16[64,640]{1,0:T(8,128)(2,1)S(1)}, u32[]{:S(2)}, u32[]{:S(2)}) collective-permute-start(bf16[64,640]{1,0:T(8,128)(2,1)S(1)} %left_rows.1), channel_id=1, source_target_pairs={{0,8},{16,24},{32,40},{48,56},{64,72},{80,88},{96,104},{112,120},{... | collective-permute-start | bytes 245768 | tf_op jit(solution)/shard_map/ppermute | solution.py:468
  35.0 1.3 %collective-permute-start.1 = (bf16[64,640]{1,0:T(8,128)(2,1)S(1)}, bf16[64,640]{1,0:T(8,128)(2,1)S(1)}, u32[]{:S(2)}, u32[]{:S(2)}) collective-permute-start(bf16[64,640]{1,0:T(8,128)(2,1)S(1)} %left_rows.1), channel_id=1, source_target_pairs={{0,4},{16,20},{32,36},{48,52},{64,68},{80,84},{96,100},{112,116},{... | collective-permute-start | bytes 245768 | tf_op jit(solution)/shard_map/ppermute | solution.py:468
  36.5 1.8 %collective-permute-done.1 = bf16[64,640]{1,0:T(8,128)(2,1)S(1)} collective-permute-done((bf16[64,640]{1,0:T(8,128)(2,1)S(1)}, bf16[64,640]{1,0:T(8,128)(2,1)S(1)}, u32[]{:S(2)}, u32[]{:S(2)}) %collective-permute-start.1) | collective-permute-done | bytes 81952 | tf_op jit(solution)/shard_map/ppermute | solution.py:468
  38.3 1.7 %collective-permute-start.7 = (bf16[8,320,128]{2,1,0:T(8,128)(2,1)S(1)}, bf16[8,320,128]{2,1,0:T(8,128)(2,1)S(1)}, u32[]{:S(2)}, u32[]{:S(2)}) collective-permute-start(bf16[8,320,128]{2,1,0:T(8,128)(2,1)S(1)} %all_to_all.15.mine), channel_id=1, source_target_pairs={{0,16},{16,0},{32,48},{48,32},{64,80},{80,64},{96,112},{112,96},{1... | collective-permute-start | bytes 1966088 | tf_op jit(solution)/shard_map/ppermute | solution.py:427
  39.9 1.3 %collective-permute-start.6 = (bf16[64,640]{1,0:T(8,128)(2,1)S(1)}, bf16[64,640]{1,0:T(8,128)(2,1)S(1)}, u32[]{:S(2)}, u32[]{:S(2)}) collective-permute-start(bf16[64,640]{1,0:T(8,128)(2,1)S(1)} %add_add_fusion.tree), channel_id=1, source_target_pairs={{0,3},{4,7},{8,11},{12,15},{16,19},{20,23},{24,27},{28,31},{32,35}... | collective-permute-start | bytes 245768 | tf_op jit(solution)/shard_map/ppermute | solution.py:392
  41.2 1.3 %collective-permute-start.5 = (bf16[64,640]{1,0:T(8,128)(2,1)S(1)}, bf16[64,640]{1,0:T(8,128)(2,1)S(1)}, u32[]{:S(2)}, u32[]{:S(2)}) collective-permute-start(bf16[64,640]{1,0:T(8,128)(2,1)S(1)} %add_add_fusion.tree), channel_id=1, source_target_pairs={{0,2},{4,6},{8,10},{12,14},{16,18},{20,22},{24,26},{28,30},{32,34}... | collective-permute-start | bytes 245768 | tf_op jit(solution)/shard_map/ppermute | solution.py:392
  42.5 1.3 %collective-permute-start.4 = (bf16[64,640]{1,0:T(8,128)(2,1)S(1)}, bf16[64,640]{1,0:T(8,128)(2,1)S(1)}, u32[]{:S(2)}, u32[]{:S(2)}) collective-permute-start(bf16[64,640]{1,0:T(8,128)(2,1)S(1)} %add_add_fusion.tree), channel_id=1, source_target_pairs={{0,1},{4,5},{8,9},{12,13},{16,17},{20,21},{24,25},{28,29},{32,33},... | collective-permute-start | bytes 245768 | tf_op jit(solution)/shard_map/ppermute | solution.py:392
  43.9 1.9 %unpack_right.1 = (bf16[32,64,256]{2,1,0:T(8,128)(2,1)S(1)}, bf16[256,64]{1,0:T(8,128)(2,1)S(1)}, bf16[1024,128]{1,0:T(8,128)(2,1)S(1)}, bf16[128,1024]{1,0:T(8,128)(2,1)S(1)}) custom-call(bf16[8,320,128]{2,1,0:T(8,128)(2,1)S(1)} %all_to_all.15.mine, bf16[8,320,128]{2,1,0:T(8,128)(2,1)S(1)} %collective-permute-done.7.other, bf16[1024,128]{1,0:T(8,128)(2,1)S(1)} %copy-done.3), custom_call_target="tpu_custom_call" | custom-call | flops 12000000000 | bytes 3178496 | tf_op jit(solution)/shard_map/unpack_right/pallas_call | solution.py:374
  45.8 6.5 %scaled_outer_grad.1 = (bf16[32,512,256]{2,1,0:T(8,128)(2,1)S(1)}, bf16[16,256,128]{2,1,0:T(8,128)(2,1)S(1)}, bf16[16,256,128]{2,1,0:T(8,128)(2,1)S(1)}, f32[256...) custom-call(bf16[64,640]{1,0:T(8,128)(2,1)S(1)} %add_add_fusion.tree, ...), custom_call_target="tpu_custom_call" | custom-call | flops 32000000000 | bytes 13468160 | tf_op jit(solution)/shard_map/scaled_outer_grad/pallas_call | solution.py:374
  52.3 1.3 %collective-permute-start.10 = (bf16[256,128]{1,0:T(8,128)(2,1)S(1)}, bf16[256,128]{1,0:T(8,128)(2,1)S(1)}, u32[]{:S(2)}, u32[]{:S(2)}) collective-permute-start(bf16[256,128]{1,0:T(8,128)(2,1)S(1)} %convert_element_type.3), channel_id=1, source_target_pairs={{3,0},{7,4},{11,8},{15,12},{19,16},{23,20},{27,24},{31,28},{35,32}... | collective-permute-start | bytes 196616 | tf_op jit(solution)/shard_map/ppermute | solution.py:512
  53.6 1.3 %collective-permute-start.9 = (bf16[256,128]{1,0:T(8,128)(2,1)S(1)}, bf16[256,128]{1,0:T(8,128)(2,1)S(1)}, u32[]{:S(2)}, u32[]{:S(2)}) collective-permute-start(bf16[256,128]{1,0:T(8,128)(2,1)S(1)} %convert_element_type.3), channel_id=1, source_target_pairs={{2,0},{6,4},{10,8},{14,12},{18,16},{22,20},{26,24},{30,28},{34,32}... | collective-permute-start | bytes 196616 | tf_op jit(solution)/shard_map/ppermute | solution.py:512
  54.9 1.3 %collective-permute-start.8 = (bf16[256,128]{1,0:T(8,128)(2,1)S(1)}, bf16[256,128]{1,0:T(8,128)(2,1)S(1)}, u32[]{:S(2)}, u32[]{:S(2)}) collective-permute-start(bf16[256,128]{1,0:T(8,128)(2,1)S(1)} %convert_element_type.3), channel_id=1, source_target_pairs={{1,0},{5,4},{9,8},{13,12},{17,16},{21,20},{25,24},{29,28},{33,32},... | collective-permute-start | bytes 196616 | tf_op jit(solution)/shard_map/ppermute | solution.py:512
  56.2 2.6 %right_grad.1 = (f32[2048,128]{1,0:T(8,128)S(1)}, bf16[2048,128]{1,0:T(8,128)(2,1)S(1)}) custom-call(bf16[64,512]{1,0:T(8,128)(2,1)S(1)} %get-tuple-element.71.left, bf16[32,512,256]{2,1,0:T(8,128)(2,1)S(1)} %get-tuple-element.72.g_ref), custom_call_target="tpu_custom_call" | custom-call | flops 10800000000 | bytes 10027008 | tf_op jit(solution)/shard_map/right_grad/pallas_call | solution.py:374
  60.0 1.3 %collective-permute-start.14 = (bf16[256,128]{1,0:T(8,128)(2,1)S(1)}, bf16[256,128]{1,0:T(8,128)(2,1)S(1)}, u32[]{:S(2)}, u32[]{:S(2)}) collective-permute-start(bf16[256,128]{1,0:T(8,128)(2,1)S(1)} %get-tuple-element.86), channel_id=1, source_target_pairs={{12,0},{28,16},{44,32},{60,48},{76,64},{92,80},{108,96},{124,112},... | collective-permute-start | bytes 196616 | tf_op jit(solution)/shard_map/ppermute | solution.py:534
  61.3 1.3 %collective-permute-start.13 = (bf16[256,128]{1,0:T(8,128)(2,1)S(1)}, bf16[256,128]{1,0:T(8,128)(2,1)S(1)}, u32[]{:S(2)}, u32[]{:S(2)}) collective-permute-start(bf16[256,128]{1,0:T(8,128)(2,1)S(1)} %get-tuple-element.86), channel_id=1, source_target_pairs={{8,0},{24,16},{40,32},{56,48},{72,64},{88,80},{104,96},{120,112},{... | collective-permute-start | bytes 196616 | tf_op jit(solution)/shard_map/ppermute | solution.py:534
  62.6 1.3 %collective-permute-start.12 = (bf16[256,128]{1,0:T(8,128)(2,1)S(1)}, bf16[256,128]{1,0:T(8,128)(2,1)S(1)}, u32[]{:S(2)}, u32[]{:S(2)}) collective-permute-start(bf16[256,128]{1,0:T(8,128)(2,1)S(1)} %get-tuple-element.86), channel_id=1, source_target_pairs={{4,0},{20,16},{36,32},{52,48},{68,64},{84,80},{100,96},{116,112},{... | collective-permute-start | bytes 196616 | tf_op jit(solution)/shard_map/ppermute | solution.py:534
  63.9 2.0 %collective-permute-start.11 = (bf16[2048,128]{1,0:T(8,128)(2,1)S(1)}, bf16[2048,128]{1,0:T(8,128)(2,1)S(1)}, u32[]{:S(2)}, u32[]{:S(2)}) collective-permute-start(bf16[2048,128]{1,0:T(8,128)(2,1)S(1)} %get-tuple-element.76), channel_id=1, source_target_pairs={{0,16},{16,0},{32,48},{48,32},{64,80},{80,64},{96,112},{112,96},{1... | collective-permute-start | bytes 1572872 | tf_op jit(solution)/shard_map/ppermute | solution.py:427
  65.9 4.6 %outer_weight_grad.1 = (f32[512,128]{1,0:T(8,128)S(1)}, bf16[512,128]{1,0:T(8,128)(2,1)S(1)}) custom-call(bf16[512,64]{1,0:T(8,128)(2,1)S(1)} %get-tuple-element.82.left_t, bf16[32,64,256]{2,1,0:T(8,128)(2,1)S(1)} %get-tuple-element.68.r_ref, bf16[16,256,128]{2,1,0:T(8,128)(2,1)S(1)} %get-tuple-element.83.s_ref), custom_call_target="tpu_custom_call" | custom-call | flops 32000000000 | bytes 2555904 | tf_op jit(solution)/shard_map/outer_weight_grad/pallas_call | solution.py:374
  70.5 2.6 %collective-permute-start.15 = (bf16[512,128]{1,0:T(8,128)(2,1)S(1)}, bf16[512,128]{1,0:T(8,128)(2,1)S(1)}, u32[]{:S(2)}, u32[]{:S(2)}) collective-permute-start(bf16[512,128]{1,0:T(8,128)(2,1)S(1)} %get-tuple-element.87), channel_id=1, source_target_pairs={{0,16},{16,0},{32,48},{48,32},{64,80},{80,64},{96,112},{112,96},{1... | collective-permute-start | bytes 393224 | tf_op jit(solution)/shard_map/ppermute | solution.py:427
  74.2 15.5 %all_to_all.16.arrived = bf16[8,352,128]{2,1,0:T(8,128)(2,1)S(1)} all-to-all(bf16[8,352,128]{2,1,0:T(8,128)(2,1)S(1)} %pack_backward.1), channel_id=1, replica_groups={{0,32,64,96,128,160,192,224},{16,48,80,112,144,176,208,240},{1,33,65,97..., dimensions={0} | all-to-all | bytes 1441792 | tf_op jit(solution)/shard_map/all_to_all | solution.py:430
  89.8 1.7 %collective-permute-start.16 = (bf16[256,128]{1,0:T(8,128)(2,1)S(1)}, bf16[256,128]{1,0:T(8,128)(2,1)S(1)}, u32[]{:S(2)}, u32[]{:S(2)}) collective-permute-start(bf16[256,128]{1,0:T(8,128)(2,1)S(1)} %get-tuple-element.93), channel_id=1, source_target_pairs={{0,16},{16,0},{32,48},{48,32},{64,80},{80,64},{96,112},{112,96},{1... | collective-permute-start | bytes 196616 | tf_op jit(solution)/shard_map/ppermute | solution.py:427
  95.1 3.3 %collective-permute-start.19 = (bf16[144,128]{1,0:T(8,128)(2,1)S(1)}, bf16[144,128]{1,0:T(8,128)(2,1)S(1)}, u32[]{:S(2)}, u32[]{:S(2)}) collective-permute-start(bf16[144,128]{1,0:T(8,128)(2,1)S(1)} %pack_column.1.part_0), channel_id=1, source_target_pairs={{0,8},{1,9},{2,10},{3,11},{4,12},{5,13},{6,14},{7,15},{8,0},{9,1},... | collective-permute-start | bytes 110600 | tf_op jit(solution)/shard_map/ppermute | solution.py:398
  98.4 1.3 %collective-permute-start.18 = (bf16[144,128]{1,0:T(8,128)(2,1)S(1)}, bf16[144,128]{1,0:T(8,128)(2,1)S(1)}, u32[]{:S(2)}, u32[]{:S(2)}) collective-permute-start(bf16[144,128]{1,0:T(8,128)(2,1)S(1)} %pack_column.1.part_0), channel_id=1, source_target_pairs={{0,4},{1,5},{2,6},{3,7},{4,0},{5,1},{6,2},{7,3},{8,12},{9,13},{10,... | collective-permute-start | bytes 110600 | tf_op jit(solution)/shard_map/ppermute | solution.py:398
  99.7 4.5 %outer_pair.1 = bf16[16,256,128]{2,1,0:T(8,128)(2,1)} custom-call(bf16[512,64]{1,0:T(8,128)(2,1)S(1)} %get-tuple-element.82.left_t, bf16[32,64,256]{2,1,0:T(8,128)(2,1)S(1)} %get-tuple-element.68.r_ref, bf16[16,256,128]{2,1,0:T(8,128)(2,1)S(1)} %get-tuple-element.101.d_ref, bf16[128,1024]{1,0:T(8,128)(2,1)S(1)} %get-tuple-element.102.weights_t, ...), custom_call_target="tpu_custom_call" | custom-call | flops 32000000000 | bytes 3473920 | tf_op jit(solution)/shard_map/outer_pair/pallas_call | solution.py:374
  104.6 2.5 %collective-permute-start.21 = (bf16[144,128]{1,0:T(8,128)(2,1)S(1)}, bf16[144,128]{1,0:T(8,128)(2,1)S(1)}, u32[]{:S(2)}, u32[]{:S(2)}) collective-permute-start(bf16[144,128]{1,0:T(8,128)(2,1)S(1)} %column_sum.1.part_0), channel_id=1, source_target_pairs={{0,1},{1,0},{2,3},{3,2},{4,5},{5,4},{6,7},{7,6},{8,9},{9,8},{10,11... | collective-permute-start | bytes 110600 | tf_op jit(solution)/shard_map/ppermute | solution.py:398
  107.2 1.8 %alignment.1 = bf16[4,256,256]{2,1,0:T(8,128)(2,1)} custom-call(bf16[4,256,256]{2,1,0:T(8,128)(2,1)S(1)} %copy-done.2, bf16[256,256]{1,0:T(8,128)(2,1)S(1)} %get-tuple-element.108.grads, bf16[64,256]{1,0:T(8,128)(2,1)S(1)} %bitcast.8), custom_call_target="tpu_custom_call" | custom-call | flops 8000000000 | bytes 1212416 | tf_op jit(solution)/shard_map/alignment/pallas_call | solution.py:374
  109.0 10.4 %all_to_all.17.mine = bf16[8,144,128]{2,1,0:T(8,128)(2,1)S(1)} all-to-all(bf16[8,144,128]{2,1,0:T(8,128)(2,1)S(1)} %pack_row.1), channel_id=1, replica_groups={{0,32,64,96,128,160,192,224},{16,48,80,112,144,176,208,240},{1,33,65,97..., dimensions={0} | all-to-all | bytes 589824 | tf_op jit(solution)/shard_map/all_to_all | solution.py:430
  119.4 3.4 %collective-permute-start.24 = (bf16[8,144,128]{2,1,0:T(8,128)(2,1)S(1)}, bf16[8,144,128]{2,1,0:T(8,128)(2,1)S(1)}, u32[]{:S(2)}, u32[]{:S(2)}) collective-permute-start(bf16[8,144,128]{2,1,0:T(8,128)(2,1)S(1)} %all_to_all.17.mine), channel_id=1, source_target_pairs={{0,16},{16,0},{32,48},{48,32},{64,80},{80,64},{96,112},{112,96},{1... | collective-permute-start | bytes 884744 | tf_op jit(solution)/shard_map/ppermute | solution.py:427
  (57 shorter events, 10.6 us)
Async XLA Ops:
  0.6 43.2 %copy-start.3 = (bf16[1024,128]{1,0:T(8,128)(2,1)S(1)}, bf16[1024,128]{1,0:T(8,128)(2,1)}, u32[]{:S(2)}) copy-start(bf16[1024,128]{1,0:T(8,128)(2,1)} %weights.1) | copy-start | bytes 786436
  3.3 4.4 %collective-permute-start = (bf16[272,128]{1,0:T(8,128)(2,1)}, bf16[272,128]{1,0:T(8,128)(2,1)S(1)}, u32[]{:S(2)}, u32[]{:S(2)}) collective-permute-start(bf16[272,128]{1,0:T(8,128)(2,1)} %get-tuple-element.62), channel_id=1, source_target_pairs={{0,16},{16,0},{32,48},{48,32},{64,80},{80,64},{96,112},{112,96},{1... | collective-permute-start | bytes 208904 | tf_op jit(solution)/shard_map/ppermute | solution.py:427
  25.5 10.8 %collective-permute-start.3 = (bf16[64,640]{1,0:T(8,128)(2,1)S(1)}, bf16[64,640]{1,0:T(8,128)(2,1)S(1)}, u32[]{:S(2)}, u32[]{:S(2)}) collective-permute-start(bf16[64,640]{1,0:T(8,128)(2,1)S(1)} %left_rows.1), channel_id=1, source_target_pairs={{0,12},{16,28},{32,44},{48,60},{64,76},{80,92},{96,108},{112,124},... | collective-permute-start | bytes 245768 | tf_op jit(solution)/shard_map/ppermute | solution.py:468
  33.4 3.0 %collective-permute-start.2 = (bf16[64,640]{1,0:T(8,128)(2,1)S(1)}, bf16[64,640]{1,0:T(8,128)(2,1)S(1)}, u32[]{:S(2)}, u32[]{:S(2)}) collective-permute-start(bf16[64,640]{1,0:T(8,128)(2,1)S(1)} %left_rows.1), channel_id=1, source_target_pairs={{0,8},{16,24},{32,40},{48,56},{64,72},{80,88},{96,104},{112,120},{... | collective-permute-start | bytes 245768 | tf_op jit(solution)/shard_map/ppermute | solution.py:468
  35.0 3.2 %collective-permute-start.1 = (bf16[64,640]{1,0:T(8,128)(2,1)S(1)}, bf16[64,640]{1,0:T(8,128)(2,1)S(1)}, u32[]{:S(2)}, u32[]{:S(2)}) collective-permute-start(bf16[64,640]{1,0:T(8,128)(2,1)S(1)} %left_rows.1), channel_id=1, source_target_pairs={{0,4},{16,20},{32,36},{48,52},{64,68},{80,84},{96,100},{112,116},{... | collective-permute-start | bytes 245768 | tf_op jit(solution)/shard_map/ppermute | solution.py:468
  38.3 7.6 %copy-start.1 = (bf16[16,256,128]{2,1,0:T(8,128)(2,1)S(1)}, bf16[16,256,128]{2,1,0:T(8,128)(2,1)}, u32[]{:S(2)}) copy-start(bf16[16,256,128]{2,1,0:T(8,128)(2,1)} %adjoint.1) | copy-start | bytes 3145732
  38.3 5.6 %collective-permute-start.7 = (bf16[8,320,128]{2,1,0:T(8,128)(2,1)S(1)}, bf16[8,320,128]{2,1,0:T(8,128)(2,1)S(1)}, u32[]{:S(2)}, u32[]{:S(2)}) collective-permute-start(bf16[8,320,128]{2,1,0:T(8,128)(2,1)S(1)} %all_to_all.15.mine), channel_id=1, source_target_pairs={{0,16},{16,0},{32,48},{48,32},{64,80},{80,64},{96,112},{112,96},{1... | collective-permute-start | bytes 1966088 | tf_op jit(solution)/shard_map/ppermute | solution.py:427
  39.9 5.8 %collective-permute-start.6 = (bf16[64,640]{1,0:T(8,128)(2,1)S(1)}, bf16[64,640]{1,0:T(8,128)(2,1)S(1)}, u32[]{:S(2)}, u32[]{:S(2)}) collective-permute-start(bf16[64,640]{1,0:T(8,128)(2,1)S(1)} %add_add_fusion.tree), channel_id=1, source_target_pairs={{0,3},{4,7},{8,11},{12,15},{16,19},{20,23},{24,27},{28,31},{32,35}... | collective-permute-start | bytes 245768 | tf_op jit(solution)/shard_map/ppermute | solution.py:392
  41.2 4.6 %collective-permute-start.5 = (bf16[64,640]{1,0:T(8,128)(2,1)S(1)}, bf16[64,640]{1,0:T(8,128)(2,1)S(1)}, u32[]{:S(2)}, u32[]{:S(2)}) collective-permute-start(bf16[64,640]{1,0:T(8,128)(2,1)S(1)} %add_add_fusion.tree), channel_id=1, source_target_pairs={{0,2},{4,6},{8,10},{12,14},{16,18},{20,22},{24,26},{28,30},{32,34}... | collective-permute-start | bytes 245768 | tf_op jit(solution)/shard_map/ppermute | solution.py:392
  42.5 3.3 %collective-permute-start.4 = (bf16[64,640]{1,0:T(8,128)(2,1)S(1)}, bf16[64,640]{1,0:T(8,128)(2,1)S(1)}, u32[]{:S(2)}, u32[]{:S(2)}) collective-permute-start(bf16[64,640]{1,0:T(8,128)(2,1)S(1)} %add_add_fusion.tree), channel_id=1, source_target_pairs={{0,1},{4,5},{8,9},{12,13},{16,17},{20,21},{24,25},{28,29},{32,33},... | collective-permute-start | bytes 245768 | tf_op jit(solution)/shard_map/ppermute | solution.py:392
  52.3 6.5 %collective-permute-start.10 = (bf16[256,128]{1,0:T(8,128)(2,1)S(1)}, bf16[256,128]{1,0:T(8,128)(2,1)S(1)}, u32[]{:S(2)}, u32[]{:S(2)}) collective-permute-start(bf16[256,128]{1,0:T(8,128)(2,1)S(1)} %convert_element_type.3), channel_id=1, source_target_pairs={{3,0},{7,4},{11,8},{15,12},{19,16},{23,20},{27,24},{31,28},{35,32}... | collective-permute-start | bytes 196616 | tf_op jit(solution)/shard_map/ppermute | solution.py:512
  53.6 5.3 %collective-permute-start.9 = (bf16[256,128]{1,0:T(8,128)(2,1)S(1)}, bf16[256,128]{1,0:T(8,128)(2,1)S(1)}, u32[]{:S(2)}, u32[]{:S(2)}) collective-permute-start(bf16[256,128]{1,0:T(8,128)(2,1)S(1)} %convert_element_type.3), channel_id=1, source_target_pairs={{2,0},{6,4},{10,8},{14,12},{18,16},{22,20},{26,24},{30,28},{34,32}... | collective-permute-start | bytes 196616 | tf_op jit(solution)/shard_map/ppermute | solution.py:512
  54.9 5.1 %collective-permute-start.8 = (bf16[256,128]{1,0:T(8,128)(2,1)S(1)}, bf16[256,128]{1,0:T(8,128)(2,1)S(1)}, u32[]{:S(2)}, u32[]{:S(2)}) collective-permute-start(bf16[256,128]{1,0:T(8,128)(2,1)S(1)} %convert_element_type.3), channel_id=1, source_target_pairs={{1,0},{5,4},{9,8},{13,12},{17,16},{21,20},{25,24},{29,28},{33,32},... | collective-permute-start | bytes 196616 | tf_op jit(solution)/shard_map/ppermute | solution.py:512
  60.0 10.4 %collective-permute-start.14 = (bf16[256,128]{1,0:T(8,128)(2,1)S(1)}, bf16[256,128]{1,0:T(8,128)(2,1)S(1)}, u32[]{:S(2)}, u32[]{:S(2)}) collective-permute-start(bf16[256,128]{1,0:T(8,128)(2,1)S(1)} %get-tuple-element.86), channel_id=1, source_target_pairs={{12,0},{28,16},{44,32},{60,48},{76,64},{92,80},{108,96},{124,112},... | collective-permute-start | bytes 196616 | tf_op jit(solution)/shard_map/ppermute | solution.py:534
  61.3 9.1 %collective-permute-start.13 = (bf16[256,128]{1,0:T(8,128)(2,1)S(1)}, bf16[256,128]{1,0:T(8,128)(2,1)S(1)}, u32[]{:S(2)}, u32[]{:S(2)}) collective-permute-start(bf16[256,128]{1,0:T(8,128)(2,1)S(1)} %get-tuple-element.86), channel_id=1, source_target_pairs={{8,0},{24,16},{40,32},{56,48},{72,64},{88,80},{104,96},{120,112},{... | collective-permute-start | bytes 196616 | tf_op jit(solution)/shard_map/ppermute | solution.py:534
  62.6 7.8 %collective-permute-start.12 = (bf16[256,128]{1,0:T(8,128)(2,1)S(1)}, bf16[256,128]{1,0:T(8,128)(2,1)S(1)}, u32[]{:S(2)}, u32[]{:S(2)}) collective-permute-start(bf16[256,128]{1,0:T(8,128)(2,1)S(1)} %get-tuple-element.86), channel_id=1, source_target_pairs={{4,0},{20,16},{36,32},{52,48},{68,64},{84,80},{100,96},{116,112},{... | collective-permute-start | bytes 196616 | tf_op jit(solution)/shard_map/ppermute | solution.py:534
  63.9 10.2 %collective-permute-start.11 = (bf16[2048,128]{1,0:T(8,128)(2,1)S(1)}, bf16[2048,128]{1,0:T(8,128)(2,1)S(1)}, u32[]{:S(2)}, u32[]{:S(2)}) collective-permute-start(bf16[2048,128]{1,0:T(8,128)(2,1)S(1)} %get-tuple-element.76), channel_id=1, source_target_pairs={{0,16},{16,0},{32,48},{48,32},{64,80},{80,64},{96,112},{112,96},{1... | collective-permute-start | bytes 1572872 | tf_op jit(solution)/shard_map/ppermute | solution.py:427
  65.9 26.5 %copy-start.6 = (bf16[4,256,256]{2,1,0:T(8,128)(2,1)S(1)}, bf16[4,256,256]{2,1,0:T(8,128)(2,1)}, u32[]{:S(2)}) copy-start(bf16[4,256,256]{2,1,0:T(8,128)(2,1)} %get-tuple-element.94.normed) | copy-start | bytes 1572868
  65.9 26.5 %copy-start.7 = (f32[8,256]{1,0:T(8,128)S(1)}, f32[8,256]{1,0:T(8,128)}, u32[]{:S(2)}) copy-start(f32[8,256]{1,0:T(8,128)} %get-tuple-element.95.live) | copy-start | bytes 24580
  65.9 33.8 %copy-start.5 = (f32[128]{0:T(128)S(1)}, f32[128]{0:T(128)}, u32[]{:S(2)}) copy-start(f32[128]{0:T(128)} %param.14) | copy-start | bytes 1540
  70.5 3.6 %collective-permute-start.15 = (bf16[512,128]{1,0:T(8,128)(2,1)S(1)}, bf16[512,128]{1,0:T(8,128)(2,1)S(1)}, u32[]{:S(2)}, u32[]{:S(2)}) collective-permute-start(bf16[512,128]{1,0:T(8,128)(2,1)S(1)} %get-tuple-element.87), channel_id=1, source_target_pairs={{0,16},{16,0},{32,48},{48,32},{64,80},{80,64},{96,112},{112,96},{1... | collective-permute-start | bytes 393224 | tf_op jit(solution)/shard_map/ppermute | solution.py:427
  89.8 2.6 %collective-permute-start.16 = (bf16[256,128]{1,0:T(8,128)(2,1)S(1)}, bf16[256,128]{1,0:T(8,128)(2,1)S(1)}, u32[]{:S(2)}, u32[]{:S(2)}) collective-permute-start(bf16[256,128]{1,0:T(8,128)(2,1)S(1)} %get-tuple-element.93), channel_id=1, source_target_pairs={{0,16},{16,0},{32,48},{48,32},{64,80},{80,64},{96,112},{112,96},{1... | collective-permute-start | bytes 196616 | tf_op jit(solution)/shard_map/ppermute | solution.py:427
  92.7 1.3 %collective-permute-start.17 = (bf16[64,128]{1,0:T(8,128)(2,1)S(1)}, bf16[64,128]{1,0:T(8,128)(2,1)S(1)}, u32[]{:S(2)}, u32[]{:S(2)}) collective-permute-start(bf16[64,128]{1,0:T(8,128)(2,1)S(1)} %get-tuple-element.98), channel_id=1, source_target_pairs={{0,16},{16,0},{32,48},{48,32},{64,80},{80,64},{96,112},{112,96},{1... | collective-permute-start | bytes 49160 | tf_op jit(solution)/shard_map/ppermute | solution.py:427
  94.0 10.2 %collective-permute-start.20 = (bf16[144,128]{1,0:T(8,128)(2,1)S(1)}, bf16[144,128]{1,0:T(8,128)(2,1)S(1)}, u32[]{:S(2)}, u32[]{:S(2)}) collective-permute-start(bf16[144,128]{1,0:T(8,128)(2,1)S(1)} %pack_column.1.part_0), channel_id=1, source_target_pairs={{0,12},{1,13},{2,14},{3,15},{4,8},{5,9},{6,10},{7,11},{8,4},{9,5},... | collective-permute-start | bytes 110600 | tf_op jit(solution)/shard_map/ppermute | solution.py:398
  95.1 9.1 %collective-permute-start.19 = (bf16[144,128]{1,0:T(8,128)(2,1)S(1)}, bf16[144,128]{1,0:T(8,128)(2,1)S(1)}, u32[]{:S(2)}, u32[]{:S(2)}) collective-permute-start(bf16[144,128]{1,0:T(8,128)(2,1)S(1)} %pack_column.1.part_0), channel_id=1, source_target_pairs={{0,8},{1,9},{2,10},{3,11},{4,12},{5,13},{6,14},{7,15},{8,0},{9,1},... | collective-permute-start | bytes 110600 | tf_op jit(solution)/shard_map/ppermute | solution.py:398
  98.4 5.8 %collective-permute-start.18 = (bf16[144,128]{1,0:T(8,128)(2,1)S(1)}, bf16[144,128]{1,0:T(8,128)(2,1)S(1)}, u32[]{:S(2)}, u32[]{:S(2)}) collective-permute-start(bf16[144,128]{1,0:T(8,128)(2,1)S(1)} %pack_column.1.part_0), channel_id=1, source_target_pairs={{0,4},{1,5},{2,6},{3,7},{4,0},{5,1},{6,2},{7,3},{8,12},{9,13},{10,... | collective-permute-start | bytes 110600 | tf_op jit(solution)/shard_map/ppermute | solution.py:398
  99.7 7.5 %copy-start.2 = (bf16[4,256,256]{2,1,0:T(8,128)(2,1)S(1)}, bf16[4,256,256]{2,1,0:T(8,128)(2,1)}, u32[]{:S(2)}) copy-start(bf16[4,256,256]{2,1,0:T(8,128)(2,1)} %msa.3) | copy-start | bytes 1572868
  99.7 7.5 %copy-start.4 = (bf16[256,64]{0,1:T(8,128)(2,1)S(1)}, bf16[256,64]{0,1:T(8,128)(2,1)}, u32[]{:S(2)}) copy-start(bf16[256,64]{0,1:T(8,128)(2,1)} %param.11) | copy-start | bytes 98308
  104.2 4.8 %collective-permute-start.23 = (bf16[144,128]{1,0:T(8,128)(2,1)S(1)}, bf16[144,128]{1,0:T(8,128)(2,1)S(1)}, u32[]{:S(2)}, u32[]{:S(2)}) collective-permute-start(bf16[144,128]{1,0:T(8,128)(2,1)S(1)} %column_sum.1.part_0), channel_id=1, source_target_pairs={{0,3},{1,2},{2,1},{3,0},{4,7},{5,6},{6,5},{7,4},{8,11},{9,10},{10,... | collective-permute-start | bytes 110600 | tf_op jit(solution)/shard_map/ppermute | solution.py:398
  104.5 4.5 %collective-permute-start.22 = (bf16[144,128]{1,0:T(8,128)(2,1)S(1)}, bf16[144,128]{1,0:T(8,128)(2,1)S(1)}, u32[]{:S(2)}, u32[]{:S(2)}) collective-permute-start(bf16[144,128]{1,0:T(8,128)(2,1)S(1)} %column_sum.1.part_0), channel_id=1, source_target_pairs={{0,2},{1,3},{2,0},{3,1},{4,6},{5,7},{6,4},{7,5},{8,10},{9,11},{10,... | collective-permute-start | bytes 110600 | tf_op jit(solution)/shard_map/ppermute | solution.py:398
  104.6 4.4 %collective-permute-start.21 = (bf16[144,128]{1,0:T(8,128)(2,1)S(1)}, bf16[144,128]{1,0:T(8,128)(2,1)S(1)}, u32[]{:S(2)}, u32[]{:S(2)}) collective-permute-start(bf16[144,128]{1,0:T(8,128)(2,1)S(1)} %column_sum.1.part_0), channel_id=1, source_target_pairs={{0,1},{1,0},{2,3},{3,2},{4,5},{5,4},{6,7},{7,6},{8,9},{9,8},{10,11... | collective-permute-start | bytes 110600 | tf_op jit(solution)/shard_map/ppermute | solution.py:398
  119.4 4.6 %collective-permute-start.24 = (bf16[8,144,128]{2,1,0:T(8,128)(2,1)S(1)}, bf16[8,144,128]{2,1,0:T(8,128)(2,1)S(1)}, u32[]{:S(2)}, u32[]{:S(2)}) collective-permute-start(bf16[8,144,128]{2,1,0:T(8,128)(2,1)S(1)} %all_to_all.17.mine), channel_id=1, source_target_pairs={{0,16},{16,0},{32,48},{48,32},{64,80},{80,64},{96,112},{112,96},{1... | collective-permute-start | bytes 884744 | tf_op jit(solution)/shard_map/ppermute | solution.py:427
  (1 other events, 0.9 us)

commit v7 on v6

--- a/solution.py
+++ b/solution.py
@@ -387,13 +387,6 @@
     return result
 
 
-def near_parts(block, cols):
-    return [
-        lax.ppermute(block, "col", [(a, a + d) for a in range(0, cols, STEP)])
-        for d in range(1, STEP)
-    ]
-
-
 def swap_parts(block, cols, unit):
     swaps = [lax.ppermute(block, "col", [(i, i ^ d * unit) for i in range(cols)]) for d in range(1, STEP)]
     return [block, *swaps]
@@ -465,9 +458,10 @@
         (shape_of(BF, total, half + lines),),
         [((rows * GROUP, half), F32)],
     )[0]
-    far = [lax.ppermute(tree, "col", [(0, d)]) for d in range(STEP, cols, STEP)]
+    leads = sorted(range(STEP, cols, STEP), key=lambda d: min(d, cols - d))
+    far = [lax.ppermute(tree, "col", [(0, d)]) for d in leads]
     tree = sum(far, tree)
-    near = near_parts(tree, cols)
+    near = swap_parts(tree, cols, 1)[1:]
     mine, tree = lax.optimization_barrier((mine, tree))
     other = partner(mine)
     right_cols, live_t, by_e, by_e_t = call(
@@ -508,10 +502,7 @@
     )
 
     sent = left_grad.astype(BF)
-    near = [
-        lax.ppermute(sent, "col", [(a + d, a) for a in range(0, cols, STEP)])
-        for d in range(1, STEP)
-    ]
+    near = swap_parts(sent, cols, 1)[1:]
     right_keep, right_send = call(
         third_kernel,
         dims,
@@ -531,7 +522,7 @@
         (shape_of(F32, rows * row_dev, half), shape_of(BF, rows * row_dev, half)),
     )
     left_t, sent = lax.optimization_barrier((left_t, sent))
-    far = [lax.ppermute(sent, "col", [(d, 0)]) for d in range(STEP, cols, STEP)]
+    far = [lax.ppermute(sent, "col", [(d, 0)]) for d in leads]
     w_keep, w_send = call(
         second_kernel,
         dims,

time: 126 us -> 124 us (0.984)
  starting transfers between devices: 46 us -> 43.1 us
    ppermute x12 -> x6, starting transfers between devices: 22.4 us -> 15.3 us  [the longest x3 11.4 us: per_device(): far = [lax.ppermute(tree, 'col', [(0, d)]) for d in leads]]
    ppermute x6 -> x12, starting transfers between devices: 8.6 us -> 13.8 us  [swap_parts(): lax.ppermute(block, 'col', [(i, i ^ d * unit) for i in range(cols)])]
    ppermute x6 -> x12, waiting for transfers between devices: 0.02 us -> 2.72 us  [swap_parts(): lax.ppermute(block, 'col', [(i, i ^ d * unit) for i in range(cols)])]
    ppermute x12 -> x6, waiting for transfers between devices: 3.15 us -> 1.46 us  [the longest x3 1.46 us: per_device(): far = [lax.ppermute(tree, 'col', [(0, d)]) for d in leads]]
  transfers between devices with their start and end apart: 25 -> 25, of which waited for: 9 -> 10; matrix products, arithmetic and copies ran while one was open for 0% -> 0% of each run, Pallas kernels for 12% -> 12%
where the time goes in v7:
time: 124 us; the launch traced here: 123 us
  blocking collectives  43.4 us (35%)
  starting transfers between devices  43.1 us (35%)
  Pallas kernels  26.6 us (21%)
  waiting for transfers between devices  8.35 us (7%)
    all_to_all x3, blocking collectives, over_pairs(): lax.all_to_all(block, 'row', 0, 0, axis_index_groups=same_core, tiled=True)  43.4 us
    pallas_call x18, Pallas kernels, call(): pl.pallas_call(functools.partial(kernel, dims), grid=(1,), in_specs=[whol...  26.6 us
    ppermute x7, starting transfers between devices, partner(): return lax.ppermute(block, 'row', swap)  14 us
    ppermute x12, starting transfers between devices, swap_parts(): lax.ppermute(block, 'col', [(i, i ^ d * unit) for i in range(cols)])  13.8 us
    ppermute x3, starting transfers between devices, per_device(): far = [lax.ppermute(tree, 'col', [(0, d)]) for d in leads]  11.4 us
    ppermute x7, waiting for transfers between devices, partner(): return lax.ppermute(block, 'row', swap)  4.17 us
    ppermute x3, starting transfers between devices, per_device(): far = [lax.ppermute(sent, 'col', [(d, 0)]) for d in leads]  3.88 us
    ppermute x12, waiting for transfers between devices, swap_parts(): lax.ppermute(block, 'col', [(i, i ^ d * unit) for i in range(cols)])  2.72 us
  transfers between devices with their start and end apart: 25, of which 10 were waited for; matrix products, arithmetic and copies ran while one was open for 0% of the time, Pallas kernels for 12%

profile of v7, /device:TPU:1, one launch (start us, length us, event | category | flops | bytes accessed | tf_op | source)
XLA Modules:
  0.0 123.2 jit_solution(5467826970316415355)
XLA Ops:
  0.6 2.6 %project.1 = (bf16[4,256,256]{2,1,0:T(8,128)(2,1)}, f32[8,256]{1,0:T(8,128)}, bf16[272,128]{1,0:T(8,128)(2,1)}, bf16[272,128]{1,0:T(8,128)(2,1)}) custom-call(bf16[4,256,256]{2,1,0:T(8,128)(2,1)} %msa.3, s32[4,256]{1,0:T(4,128)} %present.1, s32[1,256]{1,0:T(1,128)} %bitcast.11, bf16[64,256]{1,0:T(8,128)(2,1)} %bitcast.7, f32[1,64]{1,0:T(1,128)} %bitcast.12), custom_call_target="tpu_custom_call" | custom-call | flops 4000000000 | bytes 1234176 | tf_op jit(solution)/shard_map/project/pallas_call | solution.py:374
  3.3 3.2 %collective-permute-start = (bf16[272,128]{1,0:T(8,128)(2,1)}, bf16[272,128]{1,0:T(8,128)(2,1)S(1)}, u32[]{:S(2)}, u32[]{:S(2)}) collective-permute-start(bf16[272,128]{1,0:T(8,128)(2,1)} %get-tuple-element.62), channel_id=1, source_target_pairs={{0,16},{16,0},{32,48},{48,32},{64,80},{80,64},{96,112},{112,96},{1... | collective-permute-start | bytes 208904 | tf_op jit(solution)/shard_map/ppermute | solution.py:420
  7.7 17.5 %all_to_all.15.mine = bf16[8,320,128]{2,1,0:T(8,128)(2,1)S(1)} all-to-all(bf16[8,320,128]{2,1,0:T(8,128)(2,1)S(1)} %pack_forward.1), channel_id=1, replica_groups={{0,32,64,96,128,160,192,224},{16,48,80,112,144,176,208,240},{1,33,65,97..., dimensions={0} | all-to-all | bytes 1310720 | tf_op jit(solution)/shard_map/all_to_all | solution.py:423
  25.5 8.8 %collective-permute-start.3 = (bf16[64,640]{1,0:T(8,128)(2,1)S(1)}, bf16[64,640]{1,0:T(8,128)(2,1)S(1)}, u32[]{:S(2)}, u32[]{:S(2)}) collective-permute-start(bf16[64,640]{1,0:T(8,128)(2,1)S(1)} %left_rows.1), channel_id=1, source_target_pairs={{0,8},{16,24},{32,40},{48,56},{64,72},{80,88},{96,104},{112,120},{... | collective-permute-start | bytes 245768 | tf_op jit(solution)/shard_map/ppermute | solution.py:462
  34.3 1.3 %collective-permute-start.2 = (bf16[64,640]{1,0:T(8,128)(2,1)S(1)}, bf16[64,640]{1,0:T(8,128)(2,1)S(1)}, u32[]{:S(2)}, u32[]{:S(2)}) collective-permute-start(bf16[64,640]{1,0:T(8,128)(2,1)S(1)} %left_rows.1), channel_id=1, source_target_pairs={{0,12},{16,28},{32,44},{48,60},{64,76},{80,92},{96,108},{112,124},... | collective-permute-start | bytes 245768 | tf_op jit(solution)/shard_map/ppermute | solution.py:462
  35.6 1.3 %collective-permute-start.1 = (bf16[64,640]{1,0:T(8,128)(2,1)S(1)}, bf16[64,640]{1,0:T(8,128)(2,1)S(1)}, u32[]{:S(2)}, u32[]{:S(2)}) collective-permute-start(bf16[64,640]{1,0:T(8,128)(2,1)S(1)} %left_rows.1), channel_id=1, source_target_pairs={{0,4},{16,20},{32,36},{48,52},{64,68},{80,84},{96,100},{112,116},{... | collective-permute-start | bytes 245768 | tf_op jit(solution)/shard_map/ppermute | solution.py:462
  37.1 1.3 %collective-permute-done.1 = bf16[64,640]{1,0:T(8,128)(2,1)S(1)} collective-permute-done((bf16[64,640]{1,0:T(8,128)(2,1)S(1)}, bf16[64,640]{1,0:T(8,128)(2,1)S(1)}, u32[]{:S(2)}, u32[]{:S(2)}) %collective-permute-start.1) | collective-permute-done | bytes 81952 | tf_op jit(solution)/shard_map/ppermute | solution.py:462
  38.4 2.1 %collective-permute-start.7 = (bf16[8,320,128]{2,1,0:T(8,128)(2,1)S(1)}, bf16[8,320,128]{2,1,0:T(8,128)(2,1)S(1)}, u32[]{:S(2)}, u32[]{:S(2)}) collective-permute-start(bf16[8,320,128]{2,1,0:T(8,128)(2,1)S(1)} %all_to_all.15.mine), channel_id=1, source_target_pairs={{0,16},{16,0},{32,48},{48,32},{64,80},{80,64},{96,112},{112,96},{1... | collective-permute-start | bytes 1966088 | tf_op jit(solution)/shard_map/ppermute | solution.py:420
  40.5 2.7 %collective-permute-start.4 = (bf16[64,640]{1,0:T(8,128)(2,1)S(1)}, bf16[64,640]{1,0:T(8,128)(2,1)S(1)}, u32[]{:S(2)}, u32[]{:S(2)}) collective-permute-start(bf16[64,640]{1,0:T(8,128)(2,1)S(1)} %add_add_fusion.tree), channel_id=1, source_target_pairs={{0,1},{1,0},{2,3},{3,2},{4,5},{5,4},{6,7},{7,6},{8,9},{9,8},{10,11... | collective-permute-start | bytes 245768 | tf_op jit(solution)/shard_map/ppermute | solution.py:391
  43.2 1.9 %unpack_right.1 = (bf16[32,64,256]{2,1,0:T(8,128)(2,1)S(1)}, bf16[256,64]{1,0:T(8,128)(2,1)S(1)}, bf16[1024,128]{1,0:T(8,128)(2,1)S(1)}, bf16[128,1024]{1,0:T(8,128)(2,1)S(1)}) custom-call(bf16[8,320,128]{2,1,0:T(8,128)(2,1)S(1)} %all_to_all.15.mine, bf16[8,320,128]{2,1,0:T(8,128)(2,1)S(1)} %collective-permute-done.7.other, bf16[1024,128]{1,0:T(8,128)(2,1)S(1)} %copy-done.3), custom_call_target="tpu_custom_call" | custom-call | flops 12000000000 | bytes 3178496 | tf_op jit(solution)/shard_map/unpack_right/pallas_call | solution.py:374
  45.4 2.2 %collective-permute-done.4.near_1 = bf16[64,640]{1,0:T(8,128)(2,1)S(1)} collective-permute-done((bf16[64,640]{1,0:T(8,128)(2,1)S(1)}, bf16[64,640]{1,0:T(8,128)(2,1)S(1)}, u32[]{:S(2)}, u32[]{:S(2)}) %collective-permute-start.4) | collective-permute-done | bytes 81952 | tf_op jit(solution)/shard_map/ppermute | solution.py:391
  47.6 6.4 %scaled_outer_grad.1 = (bf16[32,512,256]{2,1,0:T(8,128)(2,1)S(1)}, bf16[16,256,128]{2,1,0:T(8,128)(2,1)S(1)}, bf16[16,256,128]{2,1,0:T(8,128)(2,1)S(1)}, f32[256...) custom-call(bf16[64,640]{1,0:T(8,128)(2,1)S(1)} %add_add_fusion.tree, ...), custom_call_target="tpu_custom_call" | custom-call | flops 32000000000 | bytes 13468160 | tf_op jit(solution)/shard_map/scaled_outer_grad/pallas_call | solution.py:374
  54.2 1.1 collective-permute-start.9
  55.2 1.6 %collective-permute-start.8 = (bf16[256,128]{1,0:T(8,128)(2,1)S(1)}, bf16[256,128]{1,0:T(8,128)(2,1)S(1)}, u32[]{:S(2)}, u32[]{:S(2)}) collective-permute-start(bf16[256,128]{1,0:T(8,128)(2,1)S(1)} %convert_element_type.3), channel_id=1, source_target_pairs={{0,1},{1,0},{2,3},{3,2},{4,5},{5,4},{6,7},{7,6},{8,9},{9,8},{10,11... | collective-permute-start | bytes 196616 | tf_op jit(solution)/shard_map/ppermute | solution.py:391
  56.8 2.6 %right_grad.1 = (f32[2048,128]{1,0:T(8,128)S(1)}, bf16[2048,128]{1,0:T(8,128)(2,1)S(1)}) custom-call(bf16[64,512]{1,0:T(8,128)(2,1)S(1)} %get-tuple-element.71.left, bf16[32,512,256]{2,1,0:T(8,128)(2,1)S(1)} %get-tuple-element.72.g_ref), custom_call_target="tpu_custom_call" | custom-call | flops 10800000000 | bytes 10027008 | tf_op jit(solution)/shard_map/right_grad/pallas_call | solution.py:374
  59.7 1.3 %collective-permute-start.14 = (bf16[256,128]{1,0:T(8,128)(2,1)S(1)}, bf16[256,128]{1,0:T(8,128)(2,1)S(1)}, u32[]{:S(2)}, u32[]{:S(2)}) collective-permute-start(bf16[256,128]{1,0:T(8,128)(2,1)S(1)} %get-tuple-element.86), channel_id=1, source_target_pairs={{8,0},{24,16},{40,32},{56,48},{72,64},{88,80},{104,96},{120,112},{... | collective-permute-start | bytes 196616 | tf_op jit(solution)/shard_map/ppermute | solution.py:525
  61.0 1.3 %collective-permute-start.13 = (bf16[256,128]{1,0:T(8,128)(2,1)S(1)}, bf16[256,128]{1,0:T(8,128)(2,1)S(1)}, u32[]{:S(2)}, u32[]{:S(2)}) collective-permute-start(bf16[256,128]{1,0:T(8,128)(2,1)S(1)} %get-tuple-element.86), channel_id=1, source_target_pairs={{12,0},{28,16},{44,32},{60,48},{76,64},{92,80},{108,96},{124,112},... | collective-permute-start | bytes 196616 | tf_op jit(solution)/shard_map/ppermute | solution.py:525
  62.3 1.3 %collective-permute-start.12 = (bf16[256,128]{1,0:T(8,128)(2,1)S(1)}, bf16[256,128]{1,0:T(8,128)(2,1)S(1)}, u32[]{:S(2)}, u32[]{:S(2)}) collective-permute-start(bf16[256,128]{1,0:T(8,128)(2,1)S(1)} %get-tuple-element.86), channel_id=1, source_target_pairs={{4,0},{20,16},{36,32},{52,48},{68,64},{84,80},{100,96},{116,112},{... | collective-permute-start | bytes 196616 | tf_op jit(solution)/shard_map/ppermute | solution.py:525
  63.6 1.4 %collective-permute-start.11 = (bf16[2048,128]{1,0:T(8,128)(2,1)S(1)}, bf16[2048,128]{1,0:T(8,128)(2,1)S(1)}, u32[]{:S(2)}, u32[]{:S(2)}) collective-permute-start(bf16[2048,128]{1,0:T(8,128)(2,1)S(1)} %get-tuple-element.76), channel_id=1, source_target_pairs={{0,16},{16,0},{32,48},{48,32},{64,80},{80,64},{96,112},{112,96},{1... | collective-permute-start | bytes 1572872 | tf_op jit(solution)/shard_map/ppermute | solution.py:420
  65.0 4.6 %outer_weight_grad.1 = (f32[512,128]{1,0:T(8,128)S(1)}, bf16[512,128]{1,0:T(8,128)(2,1)S(1)}) custom-call(bf16[512,64]{1,0:T(8,128)(2,1)S(1)} %get-tuple-element.82.left_t, bf16[32,64,256]{2,1,0:T(8,128)(2,1)S(1)} %get-tuple-element.68.r_ref, bf16[16,256,128]{2,1,0:T(8,128)(2,1)S(1)} %get-tuple-element.83.s_ref), custom_call_target="tpu_custom_call" | custom-call | flops 32000000000 | bytes 2555904 | tf_op jit(solution)/shard_map/outer_weight_grad/pallas_call | solution.py:374
  69.6 1.7 %collective-permute-start.15 = (bf16[512,128]{1,0:T(8,128)(2,1)S(1)}, bf16[512,128]{1,0:T(8,128)(2,1)S(1)}, u32[]{:S(2)}, u32[]{:S(2)}) collective-permute-start(bf16[512,128]{1,0:T(8,128)(2,1)S(1)} %get-tuple-element.87), channel_id=1, source_target_pairs={{0,16},{16,0},{32,48},{48,32},{64,80},{80,64},{96,112},{112,96},{1... | collective-permute-start | bytes 393224 | tf_op jit(solution)/shard_map/ppermute | solution.py:420
  72.4 15.5 %all_to_all.16.arrived = bf16[8,352,128]{2,1,0:T(8,128)(2,1)S(1)} all-to-all(bf16[8,352,128]{2,1,0:T(8,128)(2,1)S(1)} %pack_backward.1), channel_id=1, replica_groups={{0,32,64,96,128,160,192,224},{16,48,80,112,144,176,208,240},{1,33,65,97..., dimensions={0} | all-to-all | bytes 1441792 | tf_op jit(solution)/shard_map/all_to_all | solution.py:423
  88.0 1.7 %collective-permute-start.16 = (bf16[256,128]{1,0:T(8,128)(2,1)S(1)}, bf16[256,128]{1,0:T(8,128)(2,1)S(1)}, u32[]{:S(2)}, u32[]{:S(2)}) collective-permute-start(bf16[256,128]{1,0:T(8,128)(2,1)S(1)} %get-tuple-element.93), channel_id=1, source_target_pairs={{0,16},{16,0},{32,48},{48,32},{64,80},{80,64},{96,112},{112,96},{1... | collective-permute-start | bytes 196616 | tf_op jit(solution)/shard_map/ppermute | solution.py:420
  92.2 2.6 %collective-permute-start.20 = (bf16[144,128]{1,0:T(8,128)(2,1)S(1)}, bf16[144,128]{1,0:T(8,128)(2,1)S(1)}, u32[]{:S(2)}, u32[]{:S(2)}) collective-permute-start(bf16[144,128]{1,0:T(8,128)(2,1)S(1)} %pack_column.1.part_0), channel_id=1, source_target_pairs={{0,12},{1,13},{2,14},{3,15},{4,8},{5,9},{6,10},{7,11},{8,4},{9,5},... | collective-permute-start | bytes 110600 | tf_op jit(solution)/shard_map/ppermute | solution.py:391
  94.8 2.7 %collective-permute-start.19 = (bf16[144,128]{1,0:T(8,128)(2,1)S(1)}, bf16[144,128]{1,0:T(8,128)(2,1)S(1)}, u32[]{:S(2)}, u32[]{:S(2)}) collective-permute-start(bf16[144,128]{1,0:T(8,128)(2,1)S(1)} %pack_column.1.part_0), channel_id=1, source_target_pairs={{0,8},{1,9},{2,10},{3,11},{4,12},{5,13},{6,14},{7,15},{8,0},{9,1},... | collective-permute-start | bytes 110600 | tf_op jit(solution)/shard_map/ppermute | solution.py:391
  97.9 4.5 %outer_pair.1 = bf16[16,256,128]{2,1,0:T(8,128)(2,1)} custom-call(bf16[512,64]{1,0:T(8,128)(2,1)S(1)} %get-tuple-element.82.left_t, bf16[32,64,256]{2,1,0:T(8,128)(2,1)S(1)} %get-tuple-element.68.r_ref, bf16[16,256,128]{2,1,0:T(8,128)(2,1)S(1)} %get-tuple-element.101.d_ref, bf16[128,1024]{1,0:T(8,128)(2,1)S(1)} %get-tuple-element.102.weights_t, ...), custom_call_target="tpu_custom_call" | custom-call | flops 32000000000 | bytes 3473920 | tf_op jit(solution)/shard_map/outer_pair/pallas_call | solution.py:374
  102.6 2.5 %collective-permute-start.21 = (bf16[144,128]{1,0:T(8,128)(2,1)S(1)}, bf16[144,128]{1,0:T(8,128)(2,1)S(1)}, u32[]{:S(2)}, u32[]{:S(2)}) collective-permute-start(bf16[144,128]{1,0:T(8,128)(2,1)S(1)} %column_sum.1.part_0), channel_id=1, source_target_pairs={{0,1},{1,0},{2,3},{3,2},{4,5},{5,4},{6,7},{7,6},{8,9},{9,8},{10,11... | collective-permute-start | bytes 110600 | tf_op jit(solution)/shard_map/ppermute | solution.py:391
  105.1 1.8 %alignment.1 = bf16[4,256,256]{2,1,0:T(8,128)(2,1)} custom-call(bf16[4,256,256]{2,1,0:T(8,128)(2,1)S(1)} %copy-done.2, bf16[256,256]{1,0:T(8,128)(2,1)S(1)} %get-tuple-element.108.grads, bf16[64,256]{1,0:T(8,128)(2,1)S(1)} %bitcast.8), custom_call_target="tpu_custom_call" | custom-call | flops 8000000000 | bytes 1212416 | tf_op jit(solution)/shard_map/alignment/pallas_call | solution.py:374
  107.0 10.4 %all_to_all.17.mine = bf16[8,144,128]{2,1,0:T(8,128)(2,1)S(1)} all-to-all(bf16[8,144,128]{2,1,0:T(8,128)(2,1)S(1)} %pack_row.1), channel_id=1, replica_groups={{0,32,64,96,128,160,192,224},{16,48,80,112,144,176,208,240},{1,33,65,97..., dimensions={0} | all-to-all | bytes 589824 | tf_op jit(solution)/shard_map/all_to_all | solution.py:423
  117.4 3.4 %collective-permute-start.24 = (bf16[8,144,128]{2,1,0:T(8,128)(2,1)S(1)}, bf16[8,144,128]{2,1,0:T(8,128)(2,1)S(1)}, u32[]{:S(2)}, u32[]{:S(2)}) collective-permute-start(bf16[8,144,128]{2,1,0:T(8,128)(2,1)S(1)} %all_to_all.17.mine), channel_id=1, source_target_pairs={{0,16},{16,0},{32,48},{48,32},{64,80},{80,64},{96,112},{112,96},{1... | collective-permute-start | bytes 884744 | tf_op jit(solution)/shard_map/ppermute | solution.py:420
  120.8 1.2 collective-permute-done.24.other
  122.0 1.2 finish.1
  (57 shorter events, 6.7 us)
Async XLA Ops:
  0.6 42.6 %copy-start.3 = (bf16[1024,128]{1,0:T(8,128)(2,1)S(1)}, bf16[1024,128]{1,0:T(8,128)(2,1)}, u32[]{:S(2)}) copy-start(bf16[1024,128]{1,0:T(8,128)(2,1)} %weights.1) | copy-start | bytes 786436
  3.3 4.4 %collective-permute-start = (bf16[272,128]{1,0:T(8,128)(2,1)}, bf16[272,128]{1,0:T(8,128)(2,1)S(1)}, u32[]{:S(2)}, u32[]{:S(2)}) collective-permute-start(bf16[272,128]{1,0:T(8,128)(2,1)} %get-tuple-element.62), channel_id=1, source_target_pairs={{0,16},{16,0},{32,48},{48,32},{64,80},{80,64},{96,112},{112,96},{1... | collective-permute-start | bytes 208904 | tf_op jit(solution)/shard_map/ppermute | solution.py:420
  25.5 11.4 %collective-permute-start.3 = (bf16[64,640]{1,0:T(8,128)(2,1)S(1)}, bf16[64,640]{1,0:T(8,128)(2,1)S(1)}, u32[]{:S(2)}, u32[]{:S(2)}) collective-permute-start(bf16[64,640]{1,0:T(8,128)(2,1)S(1)} %left_rows.1), channel_id=1, source_target_pairs={{0,8},{16,24},{32,40},{48,56},{64,72},{80,88},{96,104},{112,120},{... | collective-permute-start | bytes 245768 | tf_op jit(solution)/shard_map/ppermute | solution.py:462
  34.3 2.8 %collective-permute-start.2 = (bf16[64,640]{1,0:T(8,128)(2,1)S(1)}, bf16[64,640]{1,0:T(8,128)(2,1)S(1)}, u32[]{:S(2)}, u32[]{:S(2)}) collective-permute-start(bf16[64,640]{1,0:T(8,128)(2,1)S(1)} %left_rows.1), channel_id=1, source_target_pairs={{0,12},{16,28},{32,44},{48,60},{64,76},{80,92},{96,108},{112,124},... | collective-permute-start | bytes 245768 | tf_op jit(solution)/shard_map/ppermute | solution.py:462
  35.6 2.8 %collective-permute-start.1 = (bf16[64,640]{1,0:T(8,128)(2,1)S(1)}, bf16[64,640]{1,0:T(8,128)(2,1)S(1)}, u32[]{:S(2)}, u32[]{:S(2)}) collective-permute-start(bf16[64,640]{1,0:T(8,128)(2,1)S(1)} %left_rows.1), channel_id=1, source_target_pairs={{0,4},{16,20},{32,36},{48,52},{64,68},{80,84},{96,100},{112,116},{... | collective-permute-start | bytes 245768 | tf_op jit(solution)/shard_map/ppermute | solution.py:462
  38.4 9.2 %copy-start.1 = (bf16[16,256,128]{2,1,0:T(8,128)(2,1)S(1)}, bf16[16,256,128]{2,1,0:T(8,128)(2,1)}, u32[]{:S(2)}) copy-start(bf16[16,256,128]{2,1,0:T(8,128)(2,1)} %adjoint.1) | copy-start | bytes 3145732
  38.4 4.8 %collective-permute-start.7 = (bf16[8,320,128]{2,1,0:T(8,128)(2,1)S(1)}, bf16[8,320,128]{2,1,0:T(8,128)(2,1)S(1)}, u32[]{:S(2)}, u32[]{:S(2)}) collective-permute-start(bf16[8,320,128]{2,1,0:T(8,128)(2,1)S(1)} %all_to_all.15.mine), channel_id=1, source_target_pairs={{0,16},{16,0},{32,48},{48,32},{64,80},{80,64},{96,112},{112,96},{1... | collective-permute-start | bytes 1966088 | tf_op jit(solution)/shard_map/ppermute | solution.py:420
  40.5 4.9 %collective-permute-start.6 = (bf16[64,640]{1,0:T(8,128)(2,1)S(1)}, bf16[64,640]{1,0:T(8,128)(2,1)S(1)}, u32[]{:S(2)}, u32[]{:S(2)}) collective-permute-start(bf16[64,640]{1,0:T(8,128)(2,1)S(1)} %add_add_fusion.tree), channel_id=1, source_target_pairs={{0,3},{1,2},{2,1},{3,0},{4,7},{5,6},{6,5},{7,4},{8,11},{9,10},{10,... | collective-permute-start | bytes 245768 | tf_op jit(solution)/shard_map/ppermute | solution.py:391
  40.5 4.9 %collective-permute-start.5 = (bf16[64,640]{1,0:T(8,128)(2,1)S(1)}, bf16[64,640]{1,0:T(8,128)(2,1)S(1)}, u32[]{:S(2)}, u32[]{:S(2)}) collective-permute-start(bf16[64,640]{1,0:T(8,128)(2,1)S(1)} %add_add_fusion.tree), channel_id=1, source_target_pairs={{0,2},{1,3},{2,0},{3,1},{4,6},{5,7},{6,4},{7,5},{8,10},{9,11},{10,... | collective-permute-start | bytes 245768 | tf_op jit(solution)/shard_map/ppermute | solution.py:391
  40.5 7.1 %collective-permute-start.4 = (bf16[64,640]{1,0:T(8,128)(2,1)S(1)}, bf16[64,640]{1,0:T(8,128)(2,1)S(1)}, u32[]{:S(2)}, u32[]{:S(2)}) collective-permute-start(bf16[64,640]{1,0:T(8,128)(2,1)S(1)} %add_add_fusion.tree), channel_id=1, source_target_pairs={{0,1},{1,0},{2,3},{3,2},{4,5},{5,4},{6,7},{7,6},{8,9},{9,8},{10,11... | collective-permute-start | bytes 245768 | tf_op jit(solution)/shard_map/ppermute | solution.py:391
  54.1 5.3 %collective-permute-start.10 = (bf16[256,128]{1,0:T(8,128)(2,1)S(1)}, bf16[256,128]{1,0:T(8,128)(2,1)S(1)}, u32[]{:S(2)}, u32[]{:S(2)}) collective-permute-start(bf16[256,128]{1,0:T(8,128)(2,1)S(1)} %convert_element_type.3), channel_id=1, source_target_pairs={{0,3},{1,2},{2,1},{3,0},{4,7},{5,6},{6,5},{7,4},{8,11},{9,10},{10,... | collective-permute-start | bytes 196616 | tf_op jit(solution)/shard_map/ppermute | solution.py:391
  54.2 5.2 %collective-permute-start.9 = (bf16[256,128]{1,0:T(8,128)(2,1)S(1)}, bf16[256,128]{1,0:T(8,128)(2,1)S(1)}, u32[]{:S(2)}, u32[]{:S(2)}) collective-permute-start(bf16[256,128]{1,0:T(8,128)(2,1)S(1)} %convert_element_type.3), channel_id=1, source_target_pairs={{0,2},{1,3},{2,0},{3,1},{4,6},{5,7},{6,4},{7,5},{8,10},{9,11},{10,... | collective-permute-start | bytes 196616 | tf_op jit(solution)/shard_map/ppermute | solution.py:391
  55.2 4.4 %collective-permute-start.8 = (bf16[256,128]{1,0:T(8,128)(2,1)S(1)}, bf16[256,128]{1,0:T(8,128)(2,1)S(1)}, u32[]{:S(2)}, u32[]{:S(2)}) collective-permute-start(bf16[256,128]{1,0:T(8,128)(2,1)S(1)} %convert_element_type.3), channel_id=1, source_target_pairs={{0,1},{1,0},{2,3},{3,2},{4,5},{5,4},{6,7},{7,6},{8,9},{9,8},{10,11... | collective-permute-start | bytes 196616 | tf_op jit(solution)/shard_map/ppermute | solution.py:391
  59.7 9.9 %collective-permute-start.14 = (bf16[256,128]{1,0:T(8,128)(2,1)S(1)}, bf16[256,128]{1,0:T(8,128)(2,1)S(1)}, u32[]{:S(2)}, u32[]{:S(2)}) collective-permute-start(bf16[256,128]{1,0:T(8,128)(2,1)S(1)} %get-tuple-element.86), channel_id=1, source_target_pairs={{8,0},{24,16},{40,32},{56,48},{72,64},{88,80},{104,96},{120,112},{... | collective-permute-start | bytes 196616 | tf_op jit(solution)/shard_map/ppermute | solution.py:525
  61.0 8.6 %collective-permute-start.13 = (bf16[256,128]{1,0:T(8,128)(2,1)S(1)}, bf16[256,128]{1,0:T(8,128)(2,1)S(1)}, u32[]{:S(2)}, u32[]{:S(2)}) collective-permute-start(bf16[256,128]{1,0:T(8,128)(2,1)S(1)} %get-tuple-element.86), channel_id=1, source_target_pairs={{12,0},{28,16},{44,32},{60,48},{76,64},{92,80},{108,96},{124,112},... | collective-permute-start | bytes 196616 | tf_op jit(solution)/shard_map/ppermute | solution.py:525
  62.3 7.3 %collective-permute-start.12 = (bf16[256,128]{1,0:T(8,128)(2,1)S(1)}, bf16[256,128]{1,0:T(8,128)(2,1)S(1)}, u32[]{:S(2)}, u32[]{:S(2)}) collective-permute-start(bf16[256,128]{1,0:T(8,128)(2,1)S(1)} %get-tuple-element.86), channel_id=1, source_target_pairs={{4,0},{20,16},{36,32},{52,48},{68,64},{84,80},{100,96},{116,112},{... | collective-permute-start | bytes 196616 | tf_op jit(solution)/shard_map/ppermute | solution.py:525
  63.6 8.7 %collective-permute-start.11 = (bf16[2048,128]{1,0:T(8,128)(2,1)S(1)}, bf16[2048,128]{1,0:T(8,128)(2,1)S(1)}, u32[]{:S(2)}, u32[]{:S(2)}) collective-permute-start(bf16[2048,128]{1,0:T(8,128)(2,1)S(1)} %get-tuple-element.76), channel_id=1, source_target_pairs={{0,16},{16,0},{32,48},{48,32},{64,80},{80,64},{96,112},{112,96},{1... | collective-permute-start | bytes 1572872 | tf_op jit(solution)/shard_map/ppermute | solution.py:420
  65.0 25.6 %copy-start.6 = (bf16[4,256,256]{2,1,0:T(8,128)(2,1)S(1)}, bf16[4,256,256]{2,1,0:T(8,128)(2,1)}, u32[]{:S(2)}) copy-start(bf16[4,256,256]{2,1,0:T(8,128)(2,1)} %get-tuple-element.94.normed) | copy-start | bytes 1572868
  65.0 25.6 %copy-start.7 = (f32[8,256]{1,0:T(8,128)S(1)}, f32[8,256]{1,0:T(8,128)}, u32[]{:S(2)}) copy-start(f32[8,256]{1,0:T(8,128)} %get-tuple-element.95.live) | copy-start | bytes 24580
  65.0 32.9 %copy-start.5 = (f32[128]{0:T(128)S(1)}, f32[128]{0:T(128)}, u32[]{:S(2)}) copy-start(f32[128]{0:T(128)} %param.14) | copy-start | bytes 1540
  69.6 2.7 %collective-permute-start.15 = (bf16[512,128]{1,0:T(8,128)(2,1)S(1)}, bf16[512,128]{1,0:T(8,128)(2,1)S(1)}, u32[]{:S(2)}, u32[]{:S(2)}) collective-permute-start(bf16[512,128]{1,0:T(8,128)(2,1)S(1)} %get-tuple-element.87), channel_id=1, source_target_pairs={{0,16},{16,0},{32,48},{48,32},{64,80},{80,64},{96,112},{112,96},{1... | collective-permute-start | bytes 393224 | tf_op jit(solution)/shard_map/ppermute | solution.py:420
  88.0 2.6 %collective-permute-start.16 = (bf16[256,128]{1,0:T(8,128)(2,1)S(1)}, bf16[256,128]{1,0:T(8,128)(2,1)S(1)}, u32[]{:S(2)}, u32[]{:S(2)}) collective-permute-start(bf16[256,128]{1,0:T(8,128)(2,1)S(1)} %get-tuple-element.93), channel_id=1, source_target_pairs={{0,16},{16,0},{32,48},{48,32},{64,80},{80,64},{96,112},{112,96},{1... | collective-permute-start | bytes 196616 | tf_op jit(solution)/shard_map/ppermute | solution.py:420
  90.9 1.3 %collective-permute-start.17 = (bf16[64,128]{1,0:T(8,128)(2,1)S(1)}, bf16[64,128]{1,0:T(8,128)(2,1)S(1)}, u32[]{:S(2)}, u32[]{:S(2)}) collective-permute-start(bf16[64,128]{1,0:T(8,128)(2,1)S(1)} %get-tuple-element.98), channel_id=1, source_target_pairs={{0,16},{16,0},{32,48},{48,32},{64,80},{80,64},{96,112},{112,96},{1... | collective-permute-start | bytes 49160 | tf_op jit(solution)/shard_map/ppermute | solution.py:420
  92.2 10.2 %collective-permute-start.20 = (bf16[144,128]{1,0:T(8,128)(2,1)S(1)}, bf16[144,128]{1,0:T(8,128)(2,1)S(1)}, u32[]{:S(2)}, u32[]{:S(2)}) collective-permute-start(bf16[144,128]{1,0:T(8,128)(2,1)S(1)} %pack_column.1.part_0), channel_id=1, source_target_pairs={{0,12},{1,13},{2,14},{3,15},{4,8},{5,9},{6,10},{7,11},{8,4},{9,5},... | collective-permute-start | bytes 110600 | tf_op jit(solution)/shard_map/ppermute | solution.py:391
  94.8 7.6 %collective-permute-start.19 = (bf16[144,128]{1,0:T(8,128)(2,1)S(1)}, bf16[144,128]{1,0:T(8,128)(2,1)S(1)}, u32[]{:S(2)}, u32[]{:S(2)}) collective-permute-start(bf16[144,128]{1,0:T(8,128)(2,1)S(1)} %pack_column.1.part_0), channel_id=1, source_target_pairs={{0,8},{1,9},{2,10},{3,11},{4,12},{5,13},{6,14},{7,15},{8,0},{9,1},... | collective-permute-start | bytes 110600 | tf_op jit(solution)/shard_map/ppermute | solution.py:391
  97.5 4.9 %collective-permute-start.18 = (bf16[144,128]{1,0:T(8,128)(2,1)S(1)}, bf16[144,128]{1,0:T(8,128)(2,1)S(1)}, u32[]{:S(2)}, u32[]{:S(2)}) collective-permute-start(bf16[144,128]{1,0:T(8,128)(2,1)S(1)} %pack_column.1.part_0), channel_id=1, source_target_pairs={{0,4},{1,5},{2,6},{3,7},{4,0},{5,1},{6,2},{7,3},{8,12},{9,13},{10,... | collective-permute-start | bytes 110600 | tf_op jit(solution)/shard_map/ppermute | solution.py:391
  97.8 7.3 %copy-start.2 = (bf16[4,256,256]{2,1,0:T(8,128)(2,1)S(1)}, bf16[4,256,256]{2,1,0:T(8,128)(2,1)}, u32[]{:S(2)}) copy-start(bf16[4,256,256]{2,1,0:T(8,128)(2,1)} %msa.3) | copy-start | bytes 1572868
  97.8 7.3 %copy-start.4 = (bf16[256,64]{0,1:T(8,128)(2,1)S(1)}, bf16[256,64]{0,1:T(8,128)(2,1)}, u32[]{:S(2)}) copy-start(bf16[256,64]{0,1:T(8,128)(2,1)} %param.11) | copy-start | bytes 98308
  102.4 4.6 %collective-permute-start.23 = (bf16[144,128]{1,0:T(8,128)(2,1)S(1)}, bf16[144,128]{1,0:T(8,128)(2,1)S(1)}, u32[]{:S(2)}, u32[]{:S(2)}) collective-permute-start(bf16[144,128]{1,0:T(8,128)(2,1)S(1)} %column_sum.1.part_0), channel_id=1, source_target_pairs={{0,3},{1,2},{2,1},{3,0},{4,7},{5,6},{6,5},{7,4},{8,11},{9,10},{10,... | collective-permute-start | bytes 110600 | tf_op jit(solution)/shard_map/ppermute | solution.py:391
  102.5 4.5 %collective-permute-start.22 = (bf16[144,128]{1,0:T(8,128)(2,1)S(1)}, bf16[144,128]{1,0:T(8,128)(2,1)S(1)}, u32[]{:S(2)}, u32[]{:S(2)}) collective-permute-start(bf16[144,128]{1,0:T(8,128)(2,1)S(1)} %column_sum.1.part_0), channel_id=1, source_target_pairs={{0,2},{1,3},{2,0},{3,1},{4,6},{5,7},{6,4},{7,5},{8,10},{9,11},{10,... | collective-permute-start | bytes 110600 | tf_op jit(solution)/shard_map/ppermute | solution.py:391
  102.6 4.4 %collective-permute-start.21 = (bf16[144,128]{1,0:T(8,128)(2,1)S(1)}, bf16[144,128]{1,0:T(8,128)(2,1)S(1)}, u32[]{:S(2)}, u32[]{:S(2)}) collective-permute-start(bf16[144,128]{1,0:T(8,128)(2,1)S(1)} %column_sum.1.part_0), channel_id=1, source_target_pairs={{0,1},{1,0},{2,3},{3,2},{4,5},{5,4},{6,7},{7,6},{8,9},{9,8},{10,11... | collective-permute-start | bytes 110600 | tf_op jit(solution)/shard_map/ppermute | solution.py:391
  117.4 4.6 %collective-permute-start.24 = (bf16[8,144,128]{2,1,0:T(8,128)(2,1)S(1)}, bf16[8,144,128]{2,1,0:T(8,128)(2,1)S(1)}, u32[]{:S(2)}, u32[]{:S(2)}) collective-permute-start(bf16[8,144,128]{2,1,0:T(8,128)(2,1)S(1)} %all_to_all.17.mine), channel_id=1, source_target_pairs={{0,16},{16,0},{32,48},{48,32},{64,80},{80,64},{96,112},{112,96},{1... | collective-permute-start | bytes 884744 | tf_op jit(solution)/shard_map/ppermute | solution.py:420
  (1 other events, 0.9 us)

commit v8 on v7

--- a/solution.py
+++ b/solution.py
@@ -87,13 +87,17 @@
     src, seqs, hidden, row_dev, places, half = dims
     core = lax.rem(lax.axis_index("row"), 2)
     base = seqs * hidden
+    own, partner = [ref[pl.ds(base, GROUP), :].astype(F32)[: GROUP // 2] for ref in (keep, came)]
+    flags = jnp.where(
+        core == 0, jnp.concatenate([own, partner], axis=0), jnp.concatenate([partner, own], axis=0)
+    ).astype(BF)
+    for q in range(src // 2):
+        out[q, pl.ds(2 * base, GROUP), :] = flags
     for ref, who in ((keep, core), (came, 1 - core)):
         value = ref[pl.ds(0, base), :]
-        flags = ref[pl.ds(base, GROUP), :]
         for q in range(src // 2):
             out[q, rows_at(who * base, base), :] = value
-            out[q, rows_at(2 * base + who * GROUP, GROUP), :] = flags
-            out[q, rows_at(2 * base + 2 * GROUP + who * row_dev, row_dev), :] = ref[
+            out[q, rows_at(2 * base + GROUP + who * row_dev, row_dev), :] = ref[
                 pl.ds(base + GROUP + q * row_dev, row_dev), :
             ]
 
@@ -102,11 +106,11 @@
     src, seqs, hidden, row_dev, places, half = dims
     first = 2 * seqs * hidden
     for q in range(src // 2):
-        tiles[pl.ds(q * 2 * GROUP, 2 * GROUP), :] = mine[q, first : first + 2 * GROUP, :].astype(F32)
-    rows = [tiles[pl.ds(seqs + s, src, stride=GROUP), :] for s in range(seqs)]
+        tiles[pl.ds(q * GROUP, GROUP), :] = mine[q, first : first + GROUP, :].astype(F32)
+    rows = [tiles[pl.ds(seqs + s, src, stride=GROUP // 2), :] for s in range(seqs)]
     blocks = [jnp.concatenate(rows, axis=0)]
     for q in range(src // 2):
-        tiles[pl.ds(q * 2 * row_dev, 2 * row_dev), :] = mine[q, first + 2 * GROUP :, :].astype(F32)
+        tiles[pl.ds(q * 2 * row_dev, 2 * row_dev), :] = mine[q, first + GROUP :, :].astype(F32)
     for i in range(row_dev):
         tile = tiles[pl.ds(i, src, stride=row_dev), :]
         blocks.append(jnp.concatenate([tile[:, s * hidden : (s + 1) * hidden] for s in range(seqs)], axis=0))
@@ -121,8 +125,8 @@
     for ref, h in ((mine, core), (other, 1 - core)):
         for q in range(src // 2):
             r_all[rows_at(h * lines + q * 2 * base, 2 * base), :] = ref[q, : 2 * base, :].astype(F32)
-            flags[rows_at((h * src + 2 * q) * GROUP, 2 * GROUP), :] = ref[
-                q, 2 * base : 2 * base + 2 * GROUP, :
+            flags[rows_at((h * src // 2 + q) * GROUP, GROUP), :] = ref[
+                q, 2 * base : 2 * base + GROUP, :
             ].astype(F32)
     w_all[...] = weights[...].astype(F32)
     for e in range(hidden):
@@ -135,7 +139,7 @@
         by_e[pl.ds(e * hidden, 4 * hidden), :] = part.astype(BF)
         by_e_t[:, pl.ds(e * hidden, 4 * hidden)] = part.T.astype(BF)
     for h in range(2):
-        rows = [flags[pl.ds(h * src * GROUP + s, src, stride=GROUP), :] for s in range(seqs)]
+        rows = [flags[pl.ds(h * src * GROUP // 2 + s, src, stride=GROUP // 2), :] for s in range(seqs)]
         live_t_ref[pl.ds(h * half, half), :] = jnp.concatenate(rows, axis=0).T.astype(BF)
 
 
@@ -335,7 +339,7 @@
         out[q, pl.ds(total.shape[0], GROUP), :] = small
 
 
-def finish_kernel(dims, mine, other, projector, projector_bias, weight, bias, held):
+def finish_kernel(dims, mine, other, projector, projector_bias, weight, bias):
     src, seqs, hidden, row_dev, places, half = dims
     core = lax.rem(lax.axis_index("row"), 2)
     w_lines = hidden * hidden // src
@@ -347,17 +351,16 @@
         for q in range(src // 2):
             total = total + ref[q, : 2 * hidden, :].astype(F32)
             small = small + ref[q, at : at + GROUP, :].astype(F32)
-            held[rows_at(who * (hidden * hidden // 2) + q * w_lines, w_lines), :] = ref[
-                q, 2 * hidden : at, :
-            ].astype(F32)
+            for n in range(w_lines // hidden):
+                e = (who * (src // 2) + q) * (w_lines // hidden) + n
+                line = 2 * hidden + n * hidden
+                weight[pl.ds(e, hidden, stride=hidden), :] = ref[q, line : line + hidden, :].astype(F32)
         sums.append(total)
     first = jnp.where(core == 0, sums[0], sums[1])
     second = jnp.where(core == 0, sums[1], sums[0])
     projector[...] = jnp.concatenate([first, second], axis=1)
     bias[...] = small[0:1] + small[1:2]
     projector_bias[...] = (small[2:3] + small[3:4])[:, : 2 * hidden]
-    for c in range(hidden):
-        weight[pl.ds(c * hidden, hidden), :] = held[pl.ds(c, hidden, stride=hidden), :]
 
 
 def shape_of(dtype, *shape):
@@ -447,7 +450,7 @@
         dims,
         "pack_forward",
         (keep, came),
-        (shape_of(BF, pairs, 2 * (base + GROUP + row_dev), half),),
+        (shape_of(BF, pairs, 2 * (base + row_dev) + GROUP, half),),
     )[0]
     mine = over_pairs(packed)
     tree = call(
@@ -477,7 +480,7 @@
         ),
         [
             ((2 * rows * base, half), F32),
-            ((2 * rows * GROUP, half), F32),
+            ((rows * GROUP, half), F32),
             ((hidden * hidden, channels), F32),
         ],
         macs=300_000_000,
@@ -614,7 +617,6 @@
             shape_of(F32, hidden * hidden, channels),
             shape_of(F32, 1, channels),
         ),
-        [((hidden * hidden, channels), F32)],
     )
     return (
         pair_increment,

time: 124 us -> 123 us (level)
  no operation moved by 1% of the time
where the time goes in v8:
time: 123 us
  blocking collectives  43.1 us (35%)
  starting transfers between devices  43 us (35%)
  Pallas kernels  26.5 us (22%)
  waiting for transfers between devices  8.37 us (7%)
    all_to_all x3, blocking collectives, over_pairs(): lax.all_to_all(block, 'row', 0, 0, axis_index_groups=same_core, tiled=True)  43.1 us
    pallas_call x18, Pallas kernels, call(): pl.pallas_call(functools.partial(kernel, dims), grid=(1,), in_specs=[whol...  26.5 us
    ppermute x7, starting transfers between devices, partner(): return lax.ppermute(block, 'row', swap)  13.9 us
    ppermute x12, starting transfers between devices, swap_parts(): lax.ppermute(block, 'col', [(i, i ^ d * unit) for i in range(cols)])  13.8 us
    ppermute x3, starting transfers between devices, per_device(): far = [lax.ppermute(tree, 'col', [(0, d)]) for d in leads]  11.4 us
    ppermute x7, waiting for transfers between devices, partner(): return lax.ppermute(block, 'row', swap)  4.17 us
    ppermute x3, starting transfers between devices, per_device(): far = [lax.ppermute(sent, 'col', [(d, 0)]) for d in leads]  3.88 us
    ppermute x12, waiting for transfers between devices, swap_parts(): lax.ppermute(block, 'col', [(i, i ^ d * unit) for i in range(cols)])  2.74 us
  transfers between devices with their start and end apart: 25, of which 10 were waited for; matrix products, arithmetic and copies ran while one was open for 0% of the time, Pallas kernels for 12%

profile of v8, /device:TPU:1, one launch (start us, length us, event | category | flops | bytes accessed | tf_op | source)
XLA Modules:
  0.0 122.8 jit_solution(2978406413411354778)
XLA Ops:
  0.6 2.6 %project.1 = (bf16[4,256,256]{2,1,0:T(8,128)(2,1)}, f32[8,256]{1,0:T(8,128)}, bf16[272,128]{1,0:T(8,128)(2,1)}, bf16[272,128]{1,0:T(8,128)(2,1)}) custom-call(bf16[4,256,256]{2,1,0:T(8,128)(2,1)} %msa.3, s32[4,256]{1,0:T(4,128)} %present.1, s32[1,256]{1,0:T(1,128)} %bitcast.11, bf16[64,256]{1,0:T(8,128)(2,1)} %bitcast.7, f32[1,64]{1,0:T(1,128)} %bitcast.12), custom_call_target="tpu_custom_call" | custom-call | flops 4000000000 | bytes 1234176 | tf_op jit(solution)/shard_map/project/pallas_call | solution.py:377
  3.3 3.2 %collective-permute-start = (bf16[272,128]{1,0:T(8,128)(2,1)}, bf16[272,128]{1,0:T(8,128)(2,1)S(1)}, u32[]{:S(2)}, u32[]{:S(2)}) collective-permute-start(bf16[272,128]{1,0:T(8,128)(2,1)} %get-tuple-element.62), channel_id=1, source_target_pairs={{0,16},{16,0},{32,48},{48,32},{64,80},{80,64},{96,112},{112,96},{1... | collective-permute-start | bytes 208904 | tf_op jit(solution)/shard_map/ppermute | solution.py:423
  7.7 17.2 %all_to_all.15.mine = bf16[8,304,128]{2,1,0:T(8,128)(2,1)S(1)} all-to-all(bf16[8,304,128]{2,1,0:T(8,128)(2,1)S(1)} %pack_forward.1), channel_id=1, replica_groups={{0,32,64,96,128,160,192,224},{16,48,80,112,144,176,208,240},{1,33,65,97..., dimensions={0} | all-to-all | bytes 1245184 | tf_op jit(solution)/shard_map/all_to_all | solution.py:426
  25.2 8.8 %collective-permute-start.3 = (bf16[64,640]{1,0:T(8,128)(2,1)S(1)}, bf16[64,640]{1,0:T(8,128)(2,1)S(1)}, u32[]{:S(2)}, u32[]{:S(2)}) collective-permute-start(bf16[64,640]{1,0:T(8,128)(2,1)S(1)} %left_rows.1), channel_id=1, source_target_pairs={{0,8},{16,24},{32,40},{48,56},{64,72},{80,88},{96,104},{112,120},{... | collective-permute-start | bytes 245768 | tf_op jit(solution)/shard_map/ppermute | solution.py:465
  34.0 1.3 %collective-permute-start.2 = (bf16[64,640]{1,0:T(8,128)(2,1)S(1)}, bf16[64,640]{1,0:T(8,128)(2,1)S(1)}, u32[]{:S(2)}, u32[]{:S(2)}) collective-permute-start(bf16[64,640]{1,0:T(8,128)(2,1)S(1)} %left_rows.1), channel_id=1, source_target_pairs={{0,12},{16,28},{32,44},{48,60},{64,76},{80,92},{96,108},{112,124},... | collective-permute-start | bytes 245768 | tf_op jit(solution)/shard_map/ppermute | solution.py:465
  35.3 1.3 %collective-permute-start.1 = (bf16[64,640]{1,0:T(8,128)(2,1)S(1)}, bf16[64,640]{1,0:T(8,128)(2,1)S(1)}, u32[]{:S(2)}, u32[]{:S(2)}) collective-permute-start(bf16[64,640]{1,0:T(8,128)(2,1)S(1)} %left_rows.1), channel_id=1, source_target_pairs={{0,4},{16,20},{32,36},{48,52},{64,68},{80,84},{96,100},{112,116},{... | collective-permute-start | bytes 245768 | tf_op jit(solution)/shard_map/ppermute | solution.py:465
  36.8 1.3 %collective-permute-done.1 = bf16[64,640]{1,0:T(8,128)(2,1)S(1)} collective-permute-done((bf16[64,640]{1,0:T(8,128)(2,1)S(1)}, bf16[64,640]{1,0:T(8,128)(2,1)S(1)}, u32[]{:S(2)}, u32[]{:S(2)}) %collective-permute-start.1) | collective-permute-done | bytes 81952 | tf_op jit(solution)/shard_map/ppermute | solution.py:465
  38.1 2.0 %collective-permute-start.7 = (bf16[8,304,128]{2,1,0:T(8,128)(2,1)S(1)}, bf16[8,304,128]{2,1,0:T(8,128)(2,1)S(1)}, u32[]{:S(2)}, u32[]{:S(2)}) collective-permute-start(bf16[8,304,128]{2,1,0:T(8,128)(2,1)S(1)} %all_to_all.15.mine), channel_id=1, source_target_pairs={{0,16},{16,0},{32,48},{48,32},{64,80},{80,64},{96,112},{112,96},{1... | collective-permute-start | bytes 1867784 | tf_op jit(solution)/shard_map/ppermute | solution.py:423
  40.2 2.7 %collective-permute-start.4 = (bf16[64,640]{1,0:T(8,128)(2,1)S(1)}, bf16[64,640]{1,0:T(8,128)(2,1)S(1)}, u32[]{:S(2)}, u32[]{:S(2)}) collective-permute-start(bf16[64,640]{1,0:T(8,128)(2,1)S(1)} %add_add_fusion.tree), channel_id=1, source_target_pairs={{0,1},{1,0},{2,3},{3,2},{4,5},{5,4},{6,7},{7,6},{8,9},{9,8},{10,11... | collective-permute-start | bytes 245768 | tf_op jit(solution)/shard_map/ppermute | solution.py:394
  42.8 1.9 %unpack_right.1 = (bf16[32,64,256]{2,1,0:T(8,128)(2,1)S(1)}, bf16[256,64]{1,0:T(8,128)(2,1)S(1)}, bf16[1024,128]{1,0:T(8,128)(2,1)S(1)}, bf16[128,1024]{1,0:T(8,128)(2,1)S(1)}) custom-call(bf16[8,304,128]{2,1,0:T(8,128)(2,1)S(1)} %all_to_all.15.mine, bf16[8,304,128]{2,1,0:T(8,128)(2,1)S(1)} %collective-permute-done.7.other, bf16[1024,128]{1,0:T(8,128)(2,1)S(1)} %copy-done.3), custom_call_target="tpu_custom_call" | custom-call | flops 12000000000 | bytes 3112960 | tf_op jit(solution)/shard_map/unpack_right/pallas_call | solution.py:377
  45.1 2.2 %collective-permute-done.4.near_1 = bf16[64,640]{1,0:T(8,128)(2,1)S(1)} collective-permute-done((bf16[64,640]{1,0:T(8,128)(2,1)S(1)}, bf16[64,640]{1,0:T(8,128)(2,1)S(1)}, u32[]{:S(2)}, u32[]{:S(2)}) %collective-permute-start.4) | collective-permute-done | bytes 81952 | tf_op jit(solution)/shard_map/ppermute | solution.py:394
  47.2 6.4 %scaled_outer_grad.1 = (bf16[32,512,256]{2,1,0:T(8,128)(2,1)S(1)}, bf16[16,256,128]{2,1,0:T(8,128)(2,1)S(1)}, bf16[16,256,128]{2,1,0:T(8,128)(2,1)S(1)}, f32[256...) custom-call(bf16[64,640]{1,0:T(8,128)(2,1)S(1)} %add_add_fusion.tree, ...), custom_call_target="tpu_custom_call" | custom-call | flops 32000000000 | bytes 13468160 | tf_op jit(solution)/shard_map/scaled_outer_grad/pallas_call | solution.py:377
  53.8 1.1 collective-permute-start.9
  54.9 1.6 %collective-permute-start.8 = (bf16[256,128]{1,0:T(8,128)(2,1)S(1)}, bf16[256,128]{1,0:T(8,128)(2,1)S(1)}, u32[]{:S(2)}, u32[]{:S(2)}) collective-permute-start(bf16[256,128]{1,0:T(8,128)(2,1)S(1)} %convert_element_type.3), channel_id=1, source_target_pairs={{0,1},{1,0},{2,3},{3,2},{4,5},{5,4},{6,7},{7,6},{8,9},{9,8},{10,11... | collective-permute-start | bytes 196616 | tf_op jit(solution)/shard_map/ppermute | solution.py:394
  56.4 2.6 %right_grad.1 = (f32[2048,128]{1,0:T(8,128)S(1)}, bf16[2048,128]{1,0:T(8,128)(2,1)S(1)}) custom-call(bf16[64,512]{1,0:T(8,128)(2,1)S(1)} %get-tuple-element.71.left, bf16[32,512,256]{2,1,0:T(8,128)(2,1)S(1)} %get-tuple-element.72.g_ref), custom_call_target="tpu_custom_call" | custom-call | flops 10800000000 | bytes 10027008 | tf_op jit(solution)/shard_map/right_grad/pallas_call | solution.py:377
  59.3 1.3 %collective-permute-start.14 = (bf16[256,128]{1,0:T(8,128)(2,1)S(1)}, bf16[256,128]{1,0:T(8,128)(2,1)S(1)}, u32[]{:S(2)}, u32[]{:S(2)}) collective-permute-start(bf16[256,128]{1,0:T(8,128)(2,1)S(1)} %get-tuple-element.86), channel_id=1, source_target_pairs={{8,0},{24,16},{40,32},{56,48},{72,64},{88,80},{104,96},{120,112},{... | collective-permute-start | bytes 196616 | tf_op jit(solution)/shard_map/ppermute | solution.py:528
  60.6 1.3 %collective-permute-start.13 = (bf16[256,128]{1,0:T(8,128)(2,1)S(1)}, bf16[256,128]{1,0:T(8,128)(2,1)S(1)}, u32[]{:S(2)}, u32[]{:S(2)}) collective-permute-start(bf16[256,128]{1,0:T(8,128)(2,1)S(1)} %get-tuple-element.86), channel_id=1, source_target_pairs={{12,0},{28,16},{44,32},{60,48},{76,64},{92,80},{108,96},{124,112},... | collective-permute-start | bytes 196616 | tf_op jit(solution)/shard_map/ppermute | solution.py:528
  61.9 1.3 %collective-permute-start.12 = (bf16[256,128]{1,0:T(8,128)(2,1)S(1)}, bf16[256,128]{1,0:T(8,128)(2,1)S(1)}, u32[]{:S(2)}, u32[]{:S(2)}) collective-permute-start(bf16[256,128]{1,0:T(8,128)(2,1)S(1)} %get-tuple-element.86), channel_id=1, source_target_pairs={{4,0},{20,16},{36,32},{52,48},{68,64},{84,80},{100,96},{116,112},{... | collective-permute-start | bytes 196616 | tf_op jit(solution)/shard_map/ppermute | solution.py:528
  63.2 1.4 %collective-permute-start.11 = (bf16[2048,128]{1,0:T(8,128)(2,1)S(1)}, bf16[2048,128]{1,0:T(8,128)(2,1)S(1)}, u32[]{:S(2)}, u32[]{:S(2)}) collective-permute-start(bf16[2048,128]{1,0:T(8,128)(2,1)S(1)} %get-tuple-element.76), channel_id=1, source_target_pairs={{0,16},{16,0},{32,48},{48,32},{64,80},{80,64},{96,112},{112,96},{1... | collective-permute-start | bytes 1572872 | tf_op jit(solution)/shard_map/ppermute | solution.py:423
  64.6 4.6 %outer_weight_grad.1 = (f32[512,128]{1,0:T(8,128)S(1)}, bf16[512,128]{1,0:T(8,128)(2,1)S(1)}) custom-call(bf16[512,64]{1,0:T(8,128)(2,1)S(1)} %get-tuple-element.82.left_t, bf16[32,64,256]{2,1,0:T(8,128)(2,1)S(1)} %get-tuple-element.68.r_ref, bf16[16,256,128]{2,1,0:T(8,128)(2,1)S(1)} %get-tuple-element.83.s_ref), custom_call_target="tpu_custom_call" | custom-call | flops 32000000000 | bytes 2555904 | tf_op jit(solution)/shard_map/outer_weight_grad/pallas_call | solution.py:377
  69.2 1.7 %collective-permute-start.15 = (bf16[512,128]{1,0:T(8,128)(2,1)S(1)}, bf16[512,128]{1,0:T(8,128)(2,1)S(1)}, u32[]{:S(2)}, u32[]{:S(2)}) collective-permute-start(bf16[512,128]{1,0:T(8,128)(2,1)S(1)} %get-tuple-element.87), channel_id=1, source_target_pairs={{0,16},{16,0},{32,48},{48,32},{64,80},{80,64},{96,112},{112,96},{1... | collective-permute-start | bytes 393224 | tf_op jit(solution)/shard_map/ppermute | solution.py:423
  72.0 15.5 %all_to_all.16.arrived = bf16[8,352,128]{2,1,0:T(8,128)(2,1)S(1)} all-to-all(bf16[8,352,128]{2,1,0:T(8,128)(2,1)S(1)} %pack_backward.1), channel_id=1, replica_groups={{0,32,64,96,128,160,192,224},{16,48,80,112,144,176,208,240},{1,33,65,97..., dimensions={0} | all-to-all | bytes 1441792 | tf_op jit(solution)/shard_map/all_to_all | solution.py:426
  87.6 1.7 %collective-permute-start.16 = (bf16[256,128]{1,0:T(8,128)(2,1)S(1)}, bf16[256,128]{1,0:T(8,128)(2,1)S(1)}, u32[]{:S(2)}, u32[]{:S(2)}) collective-permute-start(bf16[256,128]{1,0:T(8,128)(2,1)S(1)} %get-tuple-element.93), channel_id=1, source_target_pairs={{0,16},{16,0},{32,48},{48,32},{64,80},{80,64},{96,112},{112,96},{1... | collective-permute-start | bytes 196616 | tf_op jit(solution)/shard_map/ppermute | solution.py:423
  91.8 2.6 %collective-permute-start.20 = (bf16[144,128]{1,0:T(8,128)(2,1)S(1)}, bf16[144,128]{1,0:T(8,128)(2,1)S(1)}, u32[]{:S(2)}, u32[]{:S(2)}) collective-permute-start(bf16[144,128]{1,0:T(8,128)(2,1)S(1)} %pack_column.1.part_0), channel_id=1, source_target_pairs={{0,12},{1,13},{2,14},{3,15},{4,8},{5,9},{6,10},{7,11},{8,4},{9,5},... | collective-permute-start | bytes 110600 | tf_op jit(solution)/shard_map/ppermute | solution.py:394
  94.4 2.7 %collective-permute-start.19 = (bf16[144,128]{1,0:T(8,128)(2,1)S(1)}, bf16[144,128]{1,0:T(8,128)(2,1)S(1)}, u32[]{:S(2)}, u32[]{:S(2)}) collective-permute-start(bf16[144,128]{1,0:T(8,128)(2,1)S(1)} %pack_column.1.part_0), channel_id=1, source_target_pairs={{0,8},{1,9},{2,10},{3,11},{4,12},{5,13},{6,14},{7,15},{8,0},{9,1},... | collective-permute-start | bytes 110600 | tf_op jit(solution)/shard_map/ppermute | solution.py:394
  97.5 4.5 %outer_pair.1 = bf16[16,256,128]{2,1,0:T(8,128)(2,1)} custom-call(bf16[512,64]{1,0:T(8,128)(2,1)S(1)} %get-tuple-element.82.left_t, bf16[32,64,256]{2,1,0:T(8,128)(2,1)S(1)} %get-tuple-element.68.r_ref, bf16[16,256,128]{2,1,0:T(8,128)(2,1)S(1)} %get-tuple-element.101.d_ref, bf16[128,1024]{1,0:T(8,128)(2,1)S(1)} %get-tuple-element.102.weights_t, ...), custom_call_target="tpu_custom_call" | custom-call | flops 32000000000 | bytes 3473920 | tf_op jit(solution)/shard_map/outer_pair/pallas_call | solution.py:377
  102.2 2.5 %collective-permute-start.21 = (bf16[144,128]{1,0:T(8,128)(2,1)S(1)}, bf16[144,128]{1,0:T(8,128)(2,1)S(1)}, u32[]{:S(2)}, u32[]{:S(2)}) collective-permute-start(bf16[144,128]{1,0:T(8,128)(2,1)S(1)} %column_sum.1.part_0), channel_id=1, source_target_pairs={{0,1},{1,0},{2,3},{3,2},{4,5},{5,4},{6,7},{7,6},{8,9},{9,8},{10,11... | collective-permute-start | bytes 110600 | tf_op jit(solution)/shard_map/ppermute | solution.py:394
  104.8 1.8 %alignment.1 = bf16[4,256,256]{2,1,0:T(8,128)(2,1)} custom-call(bf16[4,256,256]{2,1,0:T(8,128)(2,1)S(1)} %copy-done.2, bf16[256,256]{1,0:T(8,128)(2,1)S(1)} %get-tuple-element.108.grads, bf16[64,256]{1,0:T(8,128)(2,1)S(1)} %bitcast.8), custom_call_target="tpu_custom_call" | custom-call | flops 8000000000 | bytes 1212416 | tf_op jit(solution)/shard_map/alignment/pallas_call | solution.py:377
  106.6 10.4 %all_to_all.17.mine = bf16[8,144,128]{2,1,0:T(8,128)(2,1)S(1)} all-to-all(bf16[8,144,128]{2,1,0:T(8,128)(2,1)S(1)} %pack_row.1), channel_id=1, replica_groups={{0,32,64,96,128,160,192,224},{16,48,80,112,144,176,208,240},{1,33,65,97..., dimensions={0} | all-to-all | bytes 589824 | tf_op jit(solution)/shard_map/all_to_all | solution.py:426
  117.0 3.4 %collective-permute-start.24 = (bf16[8,144,128]{2,1,0:T(8,128)(2,1)S(1)}, bf16[8,144,128]{2,1,0:T(8,128)(2,1)S(1)}, u32[]{:S(2)}, u32[]{:S(2)}) collective-permute-start(bf16[8,144,128]{2,1,0:T(8,128)(2,1)S(1)} %all_to_all.17.mine), channel_id=1, source_target_pairs={{0,16},{16,0},{32,48},{48,32},{64,80},{80,64},{96,112},{112,96},{1... | collective-permute-start | bytes 884744 | tf_op jit(solution)/shard_map/ppermute | solution.py:423
  120.5 1.2 collective-permute-done.24.other
  121.7 1.1 finish.1
  (57 shorter events, 6.7 us)
Async XLA Ops:
  0.6 42.2 %copy-start.3 = (bf16[1024,128]{1,0:T(8,128)(2,1)S(1)}, bf16[1024,128]{1,0:T(8,128)(2,1)}, u32[]{:S(2)}) copy-start(bf16[1024,128]{1,0:T(8,128)(2,1)} %weights.1) | copy-start | bytes 786436
  3.3 4.4 %collective-permute-start = (bf16[272,128]{1,0:T(8,128)(2,1)}, bf16[272,128]{1,0:T(8,128)(2,1)S(1)}, u32[]{:S(2)}, u32[]{:S(2)}) collective-permute-start(bf16[272,128]{1,0:T(8,128)(2,1)} %get-tuple-element.62), channel_id=1, source_target_pairs={{0,16},{16,0},{32,48},{48,32},{64,80},{80,64},{96,112},{112,96},{1... | collective-permute-start | bytes 208904 | tf_op jit(solution)/shard_map/ppermute | solution.py:423
  25.2 11.4 %collective-permute-start.3 = (bf16[64,640]{1,0:T(8,128)(2,1)S(1)}, bf16[64,640]{1,0:T(8,128)(2,1)S(1)}, u32[]{:S(2)}, u32[]{:S(2)}) collective-permute-start(bf16[64,640]{1,0:T(8,128)(2,1)S(1)} %left_rows.1), channel_id=1, source_target_pairs={{0,8},{16,24},{32,40},{48,56},{64,72},{80,88},{96,104},{112,120},{... | collective-permute-start | bytes 245768 | tf_op jit(solution)/shard_map/ppermute | solution.py:465
  34.0 2.8 %collective-permute-start.2 = (bf16[64,640]{1,0:T(8,128)(2,1)S(1)}, bf16[64,640]{1,0:T(8,128)(2,1)S(1)}, u32[]{:S(2)}, u32[]{:S(2)}) collective-permute-start(bf16[64,640]{1,0:T(8,128)(2,1)S(1)} %left_rows.1), channel_id=1, source_target_pairs={{0,12},{16,28},{32,44},{48,60},{64,76},{80,92},{96,108},{112,124},... | collective-permute-start | bytes 245768 | tf_op jit(solution)/shard_map/ppermute | solution.py:465
  35.3 2.8 %collective-permute-start.1 = (bf16[64,640]{1,0:T(8,128)(2,1)S(1)}, bf16[64,640]{1,0:T(8,128)(2,1)S(1)}, u32[]{:S(2)}, u32[]{:S(2)}) collective-permute-start(bf16[64,640]{1,0:T(8,128)(2,1)S(1)} %left_rows.1), channel_id=1, source_target_pairs={{0,4},{16,20},{32,36},{48,52},{64,68},{80,84},{96,100},{112,116},{... | collective-permute-start | bytes 245768 | tf_op jit(solution)/shard_map/ppermute | solution.py:465
  38.1 9.1 %copy-start.1 = (bf16[16,256,128]{2,1,0:T(8,128)(2,1)S(1)}, bf16[16,256,128]{2,1,0:T(8,128)(2,1)}, u32[]{:S(2)}) copy-start(bf16[16,256,128]{2,1,0:T(8,128)(2,1)} %adjoint.1) | copy-start | bytes 3145732
  38.1 4.7 %collective-permute-start.7 = (bf16[8,304,128]{2,1,0:T(8,128)(2,1)S(1)}, bf16[8,304,128]{2,1,0:T(8,128)(2,1)S(1)}, u32[]{:S(2)}, u32[]{:S(2)}) collective-permute-start(bf16[8,304,128]{2,1,0:T(8,128)(2,1)S(1)} %all_to_all.15.mine), channel_id=1, source_target_pairs={{0,16},{16,0},{32,48},{48,32},{64,80},{80,64},{96,112},{112,96},{1... | collective-permute-start | bytes 1867784 | tf_op jit(solution)/shard_map/ppermute | solution.py:423
  40.2 4.9 %collective-permute-start.6 = (bf16[64,640]{1,0:T(8,128)(2,1)S(1)}, bf16[64,640]{1,0:T(8,128)(2,1)S(1)}, u32[]{:S(2)}, u32[]{:S(2)}) collective-permute-start(bf16[64,640]{1,0:T(8,128)(2,1)S(1)} %add_add_fusion.tree), channel_id=1, source_target_pairs={{0,3},{1,2},{2,1},{3,0},{4,7},{5,6},{6,5},{7,4},{8,11},{9,10},{10,... | collective-permute-start | bytes 245768 | tf_op jit(solution)/shard_map/ppermute | solution.py:394
  40.2 4.9 %collective-permute-start.5 = (bf16[64,640]{1,0:T(8,128)(2,1)S(1)}, bf16[64,640]{1,0:T(8,128)(2,1)S(1)}, u32[]{:S(2)}, u32[]{:S(2)}) collective-permute-start(bf16[64,640]{1,0:T(8,128)(2,1)S(1)} %add_add_fusion.tree), channel_id=1, source_target_pairs={{0,2},{1,3},{2,0},{3,1},{4,6},{5,7},{6,4},{7,5},{8,10},{9,11},{10,... | collective-permute-start | bytes 245768 | tf_op jit(solution)/shard_map/ppermute | solution.py:394
  40.2 7.1 %collective-permute-start.4 = (bf16[64,640]{1,0:T(8,128)(2,1)S(1)}, bf16[64,640]{1,0:T(8,128)(2,1)S(1)}, u32[]{:S(2)}, u32[]{:S(2)}) collective-permute-start(bf16[64,640]{1,0:T(8,128)(2,1)S(1)} %add_add_fusion.tree), channel_id=1, source_target_pairs={{0,1},{1,0},{2,3},{3,2},{4,5},{5,4},{6,7},{7,6},{8,9},{9,8},{10,11... | collective-permute-start | bytes 245768 | tf_op jit(solution)/shard_map/ppermute | solution.py:394
  53.7 5.3 %collective-permute-start.10 = (bf16[256,128]{1,0:T(8,128)(2,1)S(1)}, bf16[256,128]{1,0:T(8,128)(2,1)S(1)}, u32[]{:S(2)}, u32[]{:S(2)}) collective-permute-start(bf16[256,128]{1,0:T(8,128)(2,1)S(1)} %convert_element_type.3), channel_id=1, source_target_pairs={{0,3},{1,2},{2,1},{3,0},{4,7},{5,6},{6,5},{7,4},{8,11},{9,10},{10,... | collective-permute-start | bytes 196616 | tf_op jit(solution)/shard_map/ppermute | solution.py:394
  53.8 5.2 %collective-permute-start.9 = (bf16[256,128]{1,0:T(8,128)(2,1)S(1)}, bf16[256,128]{1,0:T(8,128)(2,1)S(1)}, u32[]{:S(2)}, u32[]{:S(2)}) collective-permute-start(bf16[256,128]{1,0:T(8,128)(2,1)S(1)} %convert_element_type.3), channel_id=1, source_target_pairs={{0,2},{1,3},{2,0},{3,1},{4,6},{5,7},{6,4},{7,5},{8,10},{9,11},{10,... | collective-permute-start | bytes 196616 | tf_op jit(solution)/shard_map/ppermute | solution.py:394
  54.9 4.4 %collective-permute-start.8 = (bf16[256,128]{1,0:T(8,128)(2,1)S(1)}, bf16[256,128]{1,0:T(8,128)(2,1)S(1)}, u32[]{:S(2)}, u32[]{:S(2)}) collective-permute-start(bf16[256,128]{1,0:T(8,128)(2,1)S(1)} %convert_element_type.3), channel_id=1, source_target_pairs={{0,1},{1,0},{2,3},{3,2},{4,5},{5,4},{6,7},{7,6},{8,9},{9,8},{10,11... | collective-permute-start | bytes 196616 | tf_op jit(solution)/shard_map/ppermute | solution.py:394
  59.3 9.9 %collective-permute-start.14 = (bf16[256,128]{1,0:T(8,128)(2,1)S(1)}, bf16[256,128]{1,0:T(8,128)(2,1)S(1)}, u32[]{:S(2)}, u32[]{:S(2)}) collective-permute-start(bf16[256,128]{1,0:T(8,128)(2,1)S(1)} %get-tuple-element.86), channel_id=1, source_target_pairs={{8,0},{24,16},{40,32},{56,48},{72,64},{88,80},{104,96},{120,112},{... | collective-permute-start | bytes 196616 | tf_op jit(solution)/shard_map/ppermute | solution.py:528
  60.6 8.6 %collective-permute-start.13 = (bf16[256,128]{1,0:T(8,128)(2,1)S(1)}, bf16[256,128]{1,0:T(8,128)(2,1)S(1)}, u32[]{:S(2)}, u32[]{:S(2)}) collective-permute-start(bf16[256,128]{1,0:T(8,128)(2,1)S(1)} %get-tuple-element.86), channel_id=1, source_target_pairs={{12,0},{28,16},{44,32},{60,48},{76,64},{92,80},{108,96},{124,112},... | collective-permute-start | bytes 196616 | tf_op jit(solution)/shard_map/ppermute | solution.py:528
  61.9 7.3 %collective-permute-start.12 = (bf16[256,128]{1,0:T(8,128)(2,1)S(1)}, bf16[256,128]{1,0:T(8,128)(2,1)S(1)}, u32[]{:S(2)}, u32[]{:S(2)}) collective-permute-start(bf16[256,128]{1,0:T(8,128)(2,1)S(1)} %get-tuple-element.86), channel_id=1, source_target_pairs={{4,0},{20,16},{36,32},{52,48},{68,64},{84,80},{100,96},{116,112},{... | collective-permute-start | bytes 196616 | tf_op jit(solution)/shard_map/ppermute | solution.py:528
  63.2 8.7 %collective-permute-start.11 = (bf16[2048,128]{1,0:T(8,128)(2,1)S(1)}, bf16[2048,128]{1,0:T(8,128)(2,1)S(1)}, u32[]{:S(2)}, u32[]{:S(2)}) collective-permute-start(bf16[2048,128]{1,0:T(8,128)(2,1)S(1)} %get-tuple-element.76), channel_id=1, source_target_pairs={{0,16},{16,0},{32,48},{48,32},{64,80},{80,64},{96,112},{112,96},{1... | collective-permute-start | bytes 1572872 | tf_op jit(solution)/shard_map/ppermute | solution.py:423
  64.6 25.6 %copy-start.6 = (bf16[4,256,256]{2,1,0:T(8,128)(2,1)S(1)}, bf16[4,256,256]{2,1,0:T(8,128)(2,1)}, u32[]{:S(2)}) copy-start(bf16[4,256,256]{2,1,0:T(8,128)(2,1)} %get-tuple-element.94.normed) | copy-start | bytes 1572868
  64.6 25.6 %copy-start.7 = (f32[8,256]{1,0:T(8,128)S(1)}, f32[8,256]{1,0:T(8,128)}, u32[]{:S(2)}) copy-start(f32[8,256]{1,0:T(8,128)} %get-tuple-element.95.live) | copy-start | bytes 24580
  64.6 32.9 %copy-start.5 = (f32[128]{0:T(128)S(1)}, f32[128]{0:T(128)}, u32[]{:S(2)}) copy-start(f32[128]{0:T(128)} %param.14) | copy-start | bytes 1540
  69.2 2.7 %collective-permute-start.15 = (bf16[512,128]{1,0:T(8,128)(2,1)S(1)}, bf16[512,128]{1,0:T(8,128)(2,1)S(1)}, u32[]{:S(2)}, u32[]{:S(2)}) collective-permute-start(bf16[512,128]{1,0:T(8,128)(2,1)S(1)} %get-tuple-element.87), channel_id=1, source_target_pairs={{0,16},{16,0},{32,48},{48,32},{64,80},{80,64},{96,112},{112,96},{1... | collective-permute-start | bytes 393224 | tf_op jit(solution)/shard_map/ppermute | solution.py:423
  87.6 2.6 %collective-permute-start.16 = (bf16[256,128]{1,0:T(8,128)(2,1)S(1)}, bf16[256,128]{1,0:T(8,128)(2,1)S(1)}, u32[]{:S(2)}, u32[]{:S(2)}) collective-permute-start(bf16[256,128]{1,0:T(8,128)(2,1)S(1)} %get-tuple-element.93), channel_id=1, source_target_pairs={{0,16},{16,0},{32,48},{48,32},{64,80},{80,64},{96,112},{112,96},{1... | collective-permute-start | bytes 196616 | tf_op jit(solution)/shard_map/ppermute | solution.py:423
  90.5 1.3 %collective-permute-start.17 = (bf16[64,128]{1,0:T(8,128)(2,1)S(1)}, bf16[64,128]{1,0:T(8,128)(2,1)S(1)}, u32[]{:S(2)}, u32[]{:S(2)}) collective-permute-start(bf16[64,128]{1,0:T(8,128)(2,1)S(1)} %get-tuple-element.98), channel_id=1, source_target_pairs={{0,16},{16,0},{32,48},{48,32},{64,80},{80,64},{96,112},{112,96},{1... | collective-permute-start | bytes 49160 | tf_op jit(solution)/shard_map/ppermute | solution.py:423
  91.8 10.2 %collective-permute-start.20 = (bf16[144,128]{1,0:T(8,128)(2,1)S(1)}, bf16[144,128]{1,0:T(8,128)(2,1)S(1)}, u32[]{:S(2)}, u32[]{:S(2)}) collective-permute-start(bf16[144,128]{1,0:T(8,128)(2,1)S(1)} %pack_column.1.part_0), channel_id=1, source_target_pairs={{0,12},{1,13},{2,14},{3,15},{4,8},{5,9},{6,10},{7,11},{8,4},{9,5},... | collective-permute-start | bytes 110600 | tf_op jit(solution)/shard_map/ppermute | solution.py:394
  94.4 7.6 %collective-permute-start.19 = (bf16[144,128]{1,0:T(8,128)(2,1)S(1)}, bf16[144,128]{1,0:T(8,128)(2,1)S(1)}, u32[]{:S(2)}, u32[]{:S(2)}) collective-permute-start(bf16[144,128]{1,0:T(8,128)(2,1)S(1)} %pack_column.1.part_0), channel_id=1, source_target_pairs={{0,8},{1,9},{2,10},{3,11},{4,12},{5,13},{6,14},{7,15},{8,0},{9,1},... | collective-permute-start | bytes 110600 | tf_op jit(solution)/shard_map/ppermute | solution.py:394
  97.1 4.9 %collective-permute-start.18 = (bf16[144,128]{1,0:T(8,128)(2,1)S(1)}, bf16[144,128]{1,0:T(8,128)(2,1)S(1)}, u32[]{:S(2)}, u32[]{:S(2)}) collective-permute-start(bf16[144,128]{1,0:T(8,128)(2,1)S(1)} %pack_column.1.part_0), channel_id=1, source_target_pairs={{0,4},{1,5},{2,6},{3,7},{4,0},{5,1},{6,2},{7,3},{8,12},{9,13},{10,... | collective-permute-start | bytes 110600 | tf_op jit(solution)/shard_map/ppermute | solution.py:394
  97.5 7.3 %copy-start.2 = (bf16[4,256,256]{2,1,0:T(8,128)(2,1)S(1)}, bf16[4,256,256]{2,1,0:T(8,128)(2,1)}, u32[]{:S(2)}) copy-start(bf16[4,256,256]{2,1,0:T(8,128)(2,1)} %msa.3) | copy-start | bytes 1572868
  97.5 7.3 %copy-start.4 = (bf16[256,64]{0,1:T(8,128)(2,1)S(1)}, bf16[256,64]{0,1:T(8,128)(2,1)}, u32[]{:S(2)}) copy-start(bf16[256,64]{0,1:T(8,128)(2,1)} %param.11) | copy-start | bytes 98308
  102.0 4.6 %collective-permute-start.23 = (bf16[144,128]{1,0:T(8,128)(2,1)S(1)}, bf16[144,128]{1,0:T(8,128)(2,1)S(1)}, u32[]{:S(2)}, u32[]{:S(2)}) collective-permute-start(bf16[144,128]{1,0:T(8,128)(2,1)S(1)} %column_sum.1.part_0), channel_id=1, source_target_pairs={{0,3},{1,2},{2,1},{3,0},{4,7},{5,6},{6,5},{7,4},{8,11},{9,10},{10,... | collective-permute-start | bytes 110600 | tf_op jit(solution)/shard_map/ppermute | solution.py:394
  102.1 4.5 %collective-permute-start.22 = (bf16[144,128]{1,0:T(8,128)(2,1)S(1)}, bf16[144,128]{1,0:T(8,128)(2,1)S(1)}, u32[]{:S(2)}, u32[]{:S(2)}) collective-permute-start(bf16[144,128]{1,0:T(8,128)(2,1)S(1)} %column_sum.1.part_0), channel_id=1, source_target_pairs={{0,2},{1,3},{2,0},{3,1},{4,6},{5,7},{6,4},{7,5},{8,10},{9,11},{10,... | collective-permute-start | bytes 110600 | tf_op jit(solution)/shard_map/ppermute | solution.py:394
  102.2 4.4 %collective-permute-start.21 = (bf16[144,128]{1,0:T(8,128)(2,1)S(1)}, bf16[144,128]{1,0:T(8,128)(2,1)S(1)}, u32[]{:S(2)}, u32[]{:S(2)}) collective-permute-start(bf16[144,128]{1,0:T(8,128)(2,1)S(1)} %column_sum.1.part_0), channel_id=1, source_target_pairs={{0,1},{1,0},{2,3},{3,2},{4,5},{5,4},{6,7},{7,6},{8,9},{9,8},{10,11... | collective-permute-start | bytes 110600 | tf_op jit(solution)/shard_map/ppermute | solution.py:394
  117.0 4.6 %collective-permute-start.24 = (bf16[8,144,128]{2,1,0:T(8,128)(2,1)S(1)}, bf16[8,144,128]{2,1,0:T(8,128)(2,1)S(1)}, u32[]{:S(2)}, u32[]{:S(2)}) collective-permute-start(bf16[8,144,128]{2,1,0:T(8,128)(2,1)S(1)} %all_to_all.17.mine), channel_id=1, source_target_pairs={{0,16},{16,0},{32,48},{48,32},{64,80},{80,64},{96,112},{112,96},{1... | collective-permute-start | bytes 884744 | tf_op jit(solution)/shard_map/ppermute | solution.py:423
  (1 other events, 0.9 us)

commit v9 on v8

--- a/solution.py
+++ b/solution.py
@@ -391,7 +391,8 @@
 
 
 def swap_parts(block, cols, unit):
-    swaps = [lax.ppermute(block, "col", [(i, i ^ d * unit) for i in range(cols)]) for d in range(1, STEP)]
+    order = sorted(range(1, STEP), key=lambda d: min(d * unit, cols - d * unit))
+    swaps = [lax.ppermute(block, "col", [(i, i ^ d * unit) for i in range(cols)]) for d in order]
     return [block, *swaps]
 
 

time: 123 us -> 123 us (level)
  no operation moved by 1% of the time
where the time goes in v9:
time: 123 us
  blocking collectives  43.1 us (35%)
  starting transfers between devices  43 us (35%)
  Pallas kernels  26.5 us (22%)
  waiting for transfers between devices  8.37 us (7%)
    all_to_all x3, blocking collectives, over_pairs(): lax.all_to_all(block, 'row', 0, 0, axis_index_groups=same_core, tiled=True)  43.1 us
    pallas_call x18, Pallas kernels, call(): pl.pallas_call(functools.partial(kernel, dims), grid=(1,), in_specs=[whol...  26.5 us
    ppermute x7, starting transfers between devices, partner(): return lax.ppermute(block, 'row', swap)  13.9 us
    ppermute x12, starting transfers between devices, swap_parts(): lax.ppermute(block, 'col', [(i, i ^ d * unit) for i in range(cols)])  13.8 us
    ppermute x3, starting transfers between devices, per_device(): far = [lax.ppermute(tree, 'col', [(0, d)]) for d in leads]  11.4 us
    ppermute x7, waiting for transfers between devices, partner(): return lax.ppermute(block, 'row', swap)  4.17 us
    ppermute x3, starting transfers between devices, per_device(): far = [lax.ppermute(sent, 'col', [(d, 0)]) for d in leads]  3.88 us
    ppermute x12, waiting for transfers between devices, swap_parts(): lax.ppermute(block, 'col', [(i, i ^ d * unit) for i in range(cols)])  2.74 us
  transfers between devices with their start and end apart: 25, of which 10 were waited for; matrix products, arithmetic and copies ran while one was open for 0% of the time, Pallas kernels for 12%

profile of v9, /device:TPU:1, one launch (start us, length us, event | category | flops | bytes accessed | tf_op | source)
XLA Modules:
  0.0 122.8 jit_solution(10024429304910669825)
XLA Ops:
  0.6 2.6 %project.1 = (bf16[4,256,256]{2,1,0:T(8,128)(2,1)}, f32[8,256]{1,0:T(8,128)}, bf16[272,128]{1,0:T(8,128)(2,1)}, bf16[272,128]{1,0:T(8,128)(2,1)}) custom-call(bf16[4,256,256]{2,1,0:T(8,128)(2,1)} %msa.3, s32[4,256]{1,0:T(4,128)} %present.1, s32[1,256]{1,0:T(1,128)} %bitcast.11, bf16[64,256]{1,0:T(8,128)(2,1)} %bitcast.7, f32[1,64]{1,0:T(1,128)} %bitcast.12), custom_call_target="tpu_custom_call" | custom-call | flops 4000000000 | bytes 1234176 | tf_op jit(solution)/shard_map/project/pallas_call | solution.py:377
  3.3 3.2 %collective-permute-start = (bf16[272,128]{1,0:T(8,128)(2,1)}, bf16[272,128]{1,0:T(8,128)(2,1)S(1)}, u32[]{:S(2)}, u32[]{:S(2)}) collective-permute-start(bf16[272,128]{1,0:T(8,128)(2,1)} %get-tuple-element.62), channel_id=1, source_target_pairs={{0,16},{16,0},{32,48},{48,32},{64,80},{80,64},{96,112},{112,96},{1... | collective-permute-start | bytes 208904 | tf_op jit(solution)/shard_map/ppermute | solution.py:424
  7.7 17.2 %all_to_all.15.mine = bf16[8,304,128]{2,1,0:T(8,128)(2,1)S(1)} all-to-all(bf16[8,304,128]{2,1,0:T(8,128)(2,1)S(1)} %pack_forward.1), channel_id=1, replica_groups={{0,32,64,96,128,160,192,224},{16,48,80,112,144,176,208,240},{1,33,65,97..., dimensions={0} | all-to-all | bytes 1245184 | tf_op jit(solution)/shard_map/all_to_all | solution.py:427
  25.2 8.8 %collective-permute-start.3 = (bf16[64,640]{1,0:T(8,128)(2,1)S(1)}, bf16[64,640]{1,0:T(8,128)(2,1)S(1)}, u32[]{:S(2)}, u32[]{:S(2)}) collective-permute-start(bf16[64,640]{1,0:T(8,128)(2,1)S(1)} %left_rows.1), channel_id=1, source_target_pairs={{0,8},{16,24},{32,40},{48,56},{64,72},{80,88},{96,104},{112,120},{... | collective-permute-start | bytes 245768 | tf_op jit(solution)/shard_map/ppermute | solution.py:466
  34.0 1.3 %collective-permute-start.2 = (bf16[64,640]{1,0:T(8,128)(2,1)S(1)}, bf16[64,640]{1,0:T(8,128)(2,1)S(1)}, u32[]{:S(2)}, u32[]{:S(2)}) collective-permute-start(bf16[64,640]{1,0:T(8,128)(2,1)S(1)} %left_rows.1), channel_id=1, source_target_pairs={{0,12},{16,28},{32,44},{48,60},{64,76},{80,92},{96,108},{112,124},... | collective-permute-start | bytes 245768 | tf_op jit(solution)/shard_map/ppermute | solution.py:466
  35.3 1.3 %collective-permute-start.1 = (bf16[64,640]{1,0:T(8,128)(2,1)S(1)}, bf16[64,640]{1,0:T(8,128)(2,1)S(1)}, u32[]{:S(2)}, u32[]{:S(2)}) collective-permute-start(bf16[64,640]{1,0:T(8,128)(2,1)S(1)} %left_rows.1), channel_id=1, source_target_pairs={{0,4},{16,20},{32,36},{48,52},{64,68},{80,84},{96,100},{112,116},{... | collective-permute-start | bytes 245768 | tf_op jit(solution)/shard_map/ppermute | solution.py:466
  36.8 1.3 %collective-permute-done.1 = bf16[64,640]{1,0:T(8,128)(2,1)S(1)} collective-permute-done((bf16[64,640]{1,0:T(8,128)(2,1)S(1)}, bf16[64,640]{1,0:T(8,128)(2,1)S(1)}, u32[]{:S(2)}, u32[]{:S(2)}) %collective-permute-start.1) | collective-permute-done | bytes 81952 | tf_op jit(solution)/shard_map/ppermute | solution.py:466
  38.1 2.0 %collective-permute-start.7 = (bf16[8,304,128]{2,1,0:T(8,128)(2,1)S(1)}, bf16[8,304,128]{2,1,0:T(8,128)(2,1)S(1)}, u32[]{:S(2)}, u32[]{:S(2)}) collective-permute-start(bf16[8,304,128]{2,1,0:T(8,128)(2,1)S(1)} %all_to_all.15.mine), channel_id=1, source_target_pairs={{0,16},{16,0},{32,48},{48,32},{64,80},{80,64},{96,112},{112,96},{1... | collective-permute-start | bytes 1867784 | tf_op jit(solution)/shard_map/ppermute | solution.py:424
  40.2 2.7 %collective-permute-start.4 = (bf16[64,640]{1,0:T(8,128)(2,1)S(1)}, bf16[64,640]{1,0:T(8,128)(2,1)S(1)}, u32[]{:S(2)}, u32[]{:S(2)}) collective-permute-start(bf16[64,640]{1,0:T(8,128)(2,1)S(1)} %add_add_fusion.tree), channel_id=1, source_target_pairs={{0,1},{1,0},{2,3},{3,2},{4,5},{5,4},{6,7},{7,6},{8,9},{9,8},{10,11... | collective-permute-start | bytes 245768 | tf_op jit(solution)/shard_map/ppermute | solution.py:395
  42.8 1.9 %unpack_right.1 = (bf16[32,64,256]{2,1,0:T(8,128)(2,1)S(1)}, bf16[256,64]{1,0:T(8,128)(2,1)S(1)}, bf16[1024,128]{1,0:T(8,128)(2,1)S(1)}, bf16[128,1024]{1,0:T(8,128)(2,1)S(1)}) custom-call(bf16[8,304,128]{2,1,0:T(8,128)(2,1)S(1)} %all_to_all.15.mine, bf16[8,304,128]{2,1,0:T(8,128)(2,1)S(1)} %collective-permute-done.7.other, bf16[1024,128]{1,0:T(8,128)(2,1)S(1)} %copy-done.3), custom_call_target="tpu_custom_call" | custom-call | flops 12000000000 | bytes 3112960 | tf_op jit(solution)/shard_map/unpack_right/pallas_call | solution.py:377
  45.1 2.2 %collective-permute-done.4.near_1 = bf16[64,640]{1,0:T(8,128)(2,1)S(1)} collective-permute-done((bf16[64,640]{1,0:T(8,128)(2,1)S(1)}, bf16[64,640]{1,0:T(8,128)(2,1)S(1)}, u32[]{:S(2)}, u32[]{:S(2)}) %collective-permute-start.4) | collective-permute-done | bytes 81952 | tf_op jit(solution)/shard_map/ppermute | solution.py:395
  47.2 6.4 %scaled_outer_grad.1 = (bf16[32,512,256]{2,1,0:T(8,128)(2,1)S(1)}, bf16[16,256,128]{2,1,0:T(8,128)(2,1)S(1)}, bf16[16,256,128]{2,1,0:T(8,128)(2,1)S(1)}, f32[256...) custom-call(bf16[64,640]{1,0:T(8,128)(2,1)S(1)} %add_add_fusion.tree, ...), custom_call_target="tpu_custom_call" | custom-call | flops 32000000000 | bytes 13468160 | tf_op jit(solution)/shard_map/scaled_outer_grad/pallas_call | solution.py:377
  53.8 1.1 collective-permute-start.9
  54.9 1.6 %collective-permute-start.8 = (bf16[256,128]{1,0:T(8,128)(2,1)S(1)}, bf16[256,128]{1,0:T(8,128)(2,1)S(1)}, u32[]{:S(2)}, u32[]{:S(2)}) collective-permute-start(bf16[256,128]{1,0:T(8,128)(2,1)S(1)} %convert_element_type.3), channel_id=1, source_target_pairs={{0,1},{1,0},{2,3},{3,2},{4,5},{5,4},{6,7},{7,6},{8,9},{9,8},{10,11... | collective-permute-start | bytes 196616 | tf_op jit(solution)/shard_map/ppermute | solution.py:395
  56.4 2.6 %right_grad.1 = (f32[2048,128]{1,0:T(8,128)S(1)}, bf16[2048,128]{1,0:T(8,128)(2,1)S(1)}) custom-call(bf16[64,512]{1,0:T(8,128)(2,1)S(1)} %get-tuple-element.71.left, bf16[32,512,256]{2,1,0:T(8,128)(2,1)S(1)} %get-tuple-element.72.g_ref), custom_call_target="tpu_custom_call" | custom-call | flops 10800000000 | bytes 10027008 | tf_op jit(solution)/shard_map/right_grad/pallas_call | solution.py:377
  59.3 1.3 %collective-permute-start.14 = (bf16[256,128]{1,0:T(8,128)(2,1)S(1)}, bf16[256,128]{1,0:T(8,128)(2,1)S(1)}, u32[]{:S(2)}, u32[]{:S(2)}) collective-permute-start(bf16[256,128]{1,0:T(8,128)(2,1)S(1)} %get-tuple-element.86), channel_id=1, source_target_pairs={{8,0},{24,16},{40,32},{56,48},{72,64},{88,80},{104,96},{120,112},{... | collective-permute-start | bytes 196616 | tf_op jit(solution)/shard_map/ppermute | solution.py:529
  60.6 1.3 %collective-permute-start.13 = (bf16[256,128]{1,0:T(8,128)(2,1)S(1)}, bf16[256,128]{1,0:T(8,128)(2,1)S(1)}, u32[]{:S(2)}, u32[]{:S(2)}) collective-permute-start(bf16[256,128]{1,0:T(8,128)(2,1)S(1)} %get-tuple-element.86), channel_id=1, source_target_pairs={{12,0},{28,16},{44,32},{60,48},{76,64},{92,80},{108,96},{124,112},... | collective-permute-start | bytes 196616 | tf_op jit(solution)/shard_map/ppermute | solution.py:529
  61.9 1.3 %collective-permute-start.12 = (bf16[256,128]{1,0:T(8,128)(2,1)S(1)}, bf16[256,128]{1,0:T(8,128)(2,1)S(1)}, u32[]{:S(2)}, u32[]{:S(2)}) collective-permute-start(bf16[256,128]{1,0:T(8,128)(2,1)S(1)} %get-tuple-element.86), channel_id=1, source_target_pairs={{4,0},{20,16},{36,32},{52,48},{68,64},{84,80},{100,96},{116,112},{... | collective-permute-start | bytes 196616 | tf_op jit(solution)/shard_map/ppermute | solution.py:529
  63.2 1.4 %collective-permute-start.11 = (bf16[2048,128]{1,0:T(8,128)(2,1)S(1)}, bf16[2048,128]{1,0:T(8,128)(2,1)S(1)}, u32[]{:S(2)}, u32[]{:S(2)}) collective-permute-start(bf16[2048,128]{1,0:T(8,128)(2,1)S(1)} %get-tuple-element.76), channel_id=1, source_target_pairs={{0,16},{16,0},{32,48},{48,32},{64,80},{80,64},{96,112},{112,96},{1... | collective-permute-start | bytes 1572872 | tf_op jit(solution)/shard_map/ppermute | solution.py:424
  64.6 4.6 %outer_weight_grad.1 = (f32[512,128]{1,0:T(8,128)S(1)}, bf16[512,128]{1,0:T(8,128)(2,1)S(1)}) custom-call(bf16[512,64]{1,0:T(8,128)(2,1)S(1)} %get-tuple-element.82.left_t, bf16[32,64,256]{2,1,0:T(8,128)(2,1)S(1)} %get-tuple-element.68.r_ref, bf16[16,256,128]{2,1,0:T(8,128)(2,1)S(1)} %get-tuple-element.83.s_ref), custom_call_target="tpu_custom_call" | custom-call | flops 32000000000 | bytes 2555904 | tf_op jit(solution)/shard_map/outer_weight_grad/pallas_call | solution.py:377
  69.2 1.7 %collective-permute-start.15 = (bf16[512,128]{1,0:T(8,128)(2,1)S(1)}, bf16[512,128]{1,0:T(8,128)(2,1)S(1)}, u32[]{:S(2)}, u32[]{:S(2)}) collective-permute-start(bf16[512,128]{1,0:T(8,128)(2,1)S(1)} %get-tuple-element.87), channel_id=1, source_target_pairs={{0,16},{16,0},{32,48},{48,32},{64,80},{80,64},{96,112},{112,96},{1... | collective-permute-start | bytes 393224 | tf_op jit(solution)/shard_map/ppermute | solution.py:424
  72.0 15.5 %all_to_all.16.arrived = bf16[8,352,128]{2,1,0:T(8,128)(2,1)S(1)} all-to-all(bf16[8,352,128]{2,1,0:T(8,128)(2,1)S(1)} %pack_backward.1), channel_id=1, replica_groups={{0,32,64,96,128,160,192,224},{16,48,80,112,144,176,208,240},{1,33,65,97..., dimensions={0} | all-to-all | bytes 1441792 | tf_op jit(solution)/shard_map/all_to_all | solution.py:427
  87.6 1.7 %collective-permute-start.16 = (bf16[256,128]{1,0:T(8,128)(2,1)S(1)}, bf16[256,128]{1,0:T(8,128)(2,1)S(1)}, u32[]{:S(2)}, u32[]{:S(2)}) collective-permute-start(bf16[256,128]{1,0:T(8,128)(2,1)S(1)} %get-tuple-element.93), channel_id=1, source_target_pairs={{0,16},{16,0},{32,48},{48,32},{64,80},{80,64},{96,112},{112,96},{1... | collective-permute-start | bytes 196616 | tf_op jit(solution)/shard_map/ppermute | solution.py:424
  91.8 3.8 %collective-permute-start.20 = (bf16[144,128]{1,0:T(8,128)(2,1)S(1)}, bf16[144,128]{1,0:T(8,128)(2,1)S(1)}, u32[]{:S(2)}, u32[]{:S(2)}) collective-permute-start(bf16[144,128]{1,0:T(8,128)(2,1)S(1)} %pack_column.1.part_0), channel_id=1, source_target_pairs={{0,8},{1,9},{2,10},{3,11},{4,12},{5,13},{6,14},{7,15},{8,0},{9,1},... | collective-permute-start | bytes 110600 | tf_op jit(solution)/shard_map/ppermute | solution.py:395
  95.6 1.5 %collective-permute-start.19 = (bf16[144,128]{1,0:T(8,128)(2,1)S(1)}, bf16[144,128]{1,0:T(8,128)(2,1)S(1)}, u32[]{:S(2)}, u32[]{:S(2)}) collective-permute-start(bf16[144,128]{1,0:T(8,128)(2,1)S(1)} %pack_column.1.part_0), channel_id=1, source_target_pairs={{0,12},{1,13},{2,14},{3,15},{4,8},{5,9},{6,10},{7,11},{8,4},{9,5},... | collective-permute-start | bytes 110600 | tf_op jit(solution)/shard_map/ppermute | solution.py:395
  97.5 4.5 %outer_pair.1 = bf16[16,256,128]{2,1,0:T(8,128)(2,1)} custom-call(bf16[512,64]{1,0:T(8,128)(2,1)S(1)} %get-tuple-element.82.left_t, bf16[32,64,256]{2,1,0:T(8,128)(2,1)S(1)} %get-tuple-element.68.r_ref, bf16[16,256,128]{2,1,0:T(8,128)(2,1)S(1)} %get-tuple-element.101.d_ref, bf16[128,1024]{1,0:T(8,128)(2,1)S(1)} %get-tuple-element.102.weights_t, ...), custom_call_target="tpu_custom_call" | custom-call | flops 32000000000 | bytes 3473920 | tf_op jit(solution)/shard_map/outer_pair/pallas_call | solution.py:377
  102.2 2.5 %collective-permute-start.21 = (bf16[144,128]{1,0:T(8,128)(2,1)S(1)}, bf16[144,128]{1,0:T(8,128)(2,1)S(1)}, u32[]{:S(2)}, u32[]{:S(2)}) collective-permute-start(bf16[144,128]{1,0:T(8,128)(2,1)S(1)} %column_sum.1.part_0), channel_id=1, source_target_pairs={{0,1},{1,0},{2,3},{3,2},{4,5},{5,4},{6,7},{7,6},{8,9},{9,8},{10,11... | collective-permute-start | bytes 110600 | tf_op jit(solution)/shard_map/ppermute | solution.py:395
  104.8 1.8 %alignment.1 = bf16[4,256,256]{2,1,0:T(8,128)(2,1)} custom-call(bf16[4,256,256]{2,1,0:T(8,128)(2,1)S(1)} %copy-done.2, bf16[256,256]{1,0:T(8,128)(2,1)S(1)} %get-tuple-element.108.grads, bf16[64,256]{1,0:T(8,128)(2,1)S(1)} %bitcast.8), custom_call_target="tpu_custom_call" | custom-call | flops 8000000000 | bytes 1212416 | tf_op jit(solution)/shard_map/alignment/pallas_call | solution.py:377
  106.6 10.4 %all_to_all.17.mine = bf16[8,144,128]{2,1,0:T(8,128)(2,1)S(1)} all-to-all(bf16[8,144,128]{2,1,0:T(8,128)(2,1)S(1)} %pack_row.1), channel_id=1, replica_groups={{0,32,64,96,128,160,192,224},{16,48,80,112,144,176,208,240},{1,33,65,97..., dimensions={0} | all-to-all | bytes 589824 | tf_op jit(solution)/shard_map/all_to_all | solution.py:427
  117.0 3.4 %collective-permute-start.24 = (bf16[8,144,128]{2,1,0:T(8,128)(2,1)S(1)}, bf16[8,144,128]{2,1,0:T(8,128)(2,1)S(1)}, u32[]{:S(2)}, u32[]{:S(2)}) collective-permute-start(bf16[8,144,128]{2,1,0:T(8,128)(2,1)S(1)} %all_to_all.17.mine), channel_id=1, source_target_pairs={{0,16},{16,0},{32,48},{48,32},{64,80},{80,64},{96,112},{112,96},{1... | collective-permute-start | bytes 884744 | tf_op jit(solution)/shard_map/ppermute | solution.py:424
  120.5 1.2 collective-permute-done.24.other
  121.7 1.1 finish.1
  (57 shorter events, 6.7 us)
Async XLA Ops:
  0.6 42.2 %copy-start.3 = (bf16[1024,128]{1,0:T(8,128)(2,1)S(1)}, bf16[1024,128]{1,0:T(8,128)(2,1)}, u32[]{:S(2)}) copy-start(bf16[1024,128]{1,0:T(8,128)(2,1)} %weights.1) | copy-start | bytes 786436
  3.3 4.4 %collective-permute-start = (bf16[272,128]{1,0:T(8,128)(2,1)}, bf16[272,128]{1,0:T(8,128)(2,1)S(1)}, u32[]{:S(2)}, u32[]{:S(2)}) collective-permute-start(bf16[272,128]{1,0:T(8,128)(2,1)} %get-tuple-element.62), channel_id=1, source_target_pairs={{0,16},{16,0},{32,48},{48,32},{64,80},{80,64},{96,112},{112,96},{1... | collective-permute-start | bytes 208904 | tf_op jit(solution)/shard_map/ppermute | solution.py:424
  25.2 11.4 %collective-permute-start.3 = (bf16[64,640]{1,0:T(8,128)(2,1)S(1)}, bf16[64,640]{1,0:T(8,128)(2,1)S(1)}, u32[]{:S(2)}, u32[]{:S(2)}) collective-permute-start(bf16[64,640]{1,0:T(8,128)(2,1)S(1)} %left_rows.1), channel_id=1, source_target_pairs={{0,8},{16,24},{32,40},{48,56},{64,72},{80,88},{96,104},{112,120},{... | collective-permute-start | bytes 245768 | tf_op jit(solution)/shard_map/ppermute | solution.py:466
  34.0 2.8 %collective-permute-start.2 = (bf16[64,640]{1,0:T(8,128)(2,1)S(1)}, bf16[64,640]{1,0:T(8,128)(2,1)S(1)}, u32[]{:S(2)}, u32[]{:S(2)}) collective-permute-start(bf16[64,640]{1,0:T(8,128)(2,1)S(1)} %left_rows.1), channel_id=1, source_target_pairs={{0,12},{16,28},{32,44},{48,60},{64,76},{80,92},{96,108},{112,124},... | collective-permute-start | bytes 245768 | tf_op jit(solution)/shard_map/ppermute | solution.py:466
  35.3 2.8 %collective-permute-start.1 = (bf16[64,640]{1,0:T(8,128)(2,1)S(1)}, bf16[64,640]{1,0:T(8,128)(2,1)S(1)}, u32[]{:S(2)}, u32[]{:S(2)}) collective-permute-start(bf16[64,640]{1,0:T(8,128)(2,1)S(1)} %left_rows.1), channel_id=1, source_target_pairs={{0,4},{16,20},{32,36},{48,52},{64,68},{80,84},{96,100},{112,116},{... | collective-permute-start | bytes 245768 | tf_op jit(solution)/shard_map/ppermute | solution.py:466
  38.1 9.1 %copy-start.1 = (bf16[16,256,128]{2,1,0:T(8,128)(2,1)S(1)}, bf16[16,256,128]{2,1,0:T(8,128)(2,1)}, u32[]{:S(2)}) copy-start(bf16[16,256,128]{2,1,0:T(8,128)(2,1)} %adjoint.1) | copy-start | bytes 3145732
  38.1 4.7 %collective-permute-start.7 = (bf16[8,304,128]{2,1,0:T(8,128)(2,1)S(1)}, bf16[8,304,128]{2,1,0:T(8,128)(2,1)S(1)}, u32[]{:S(2)}, u32[]{:S(2)}) collective-permute-start(bf16[8,304,128]{2,1,0:T(8,128)(2,1)S(1)} %all_to_all.15.mine), channel_id=1, source_target_pairs={{0,16},{16,0},{32,48},{48,32},{64,80},{80,64},{96,112},{112,96},{1... | collective-permute-start | bytes 1867784 | tf_op jit(solution)/shard_map/ppermute | solution.py:424
  40.2 4.9 %collective-permute-start.6 = (bf16[64,640]{1,0:T(8,128)(2,1)S(1)}, bf16[64,640]{1,0:T(8,128)(2,1)S(1)}, u32[]{:S(2)}, u32[]{:S(2)}) collective-permute-start(bf16[64,640]{1,0:T(8,128)(2,1)S(1)} %add_add_fusion.tree), channel_id=1, source_target_pairs={{0,3},{1,2},{2,1},{3,0},{4,7},{5,6},{6,5},{7,4},{8,11},{9,10},{10,... | collective-permute-start | bytes 245768 | tf_op jit(solution)/shard_map/ppermute | solution.py:395
  40.2 4.9 %collective-permute-start.5 = (bf16[64,640]{1,0:T(8,128)(2,1)S(1)}, bf16[64,640]{1,0:T(8,128)(2,1)S(1)}, u32[]{:S(2)}, u32[]{:S(2)}) collective-permute-start(bf16[64,640]{1,0:T(8,128)(2,1)S(1)} %add_add_fusion.tree), channel_id=1, source_target_pairs={{0,2},{1,3},{2,0},{3,1},{4,6},{5,7},{6,4},{7,5},{8,10},{9,11},{10,... | collective-permute-start | bytes 245768 | tf_op jit(solution)/shard_map/ppermute | solution.py:395
  40.2 7.1 %collective-permute-start.4 = (bf16[64,640]{1,0:T(8,128)(2,1)S(1)}, bf16[64,640]{1,0:T(8,128)(2,1)S(1)}, u32[]{:S(2)}, u32[]{:S(2)}) collective-permute-start(bf16[64,640]{1,0:T(8,128)(2,1)S(1)} %add_add_fusion.tree), channel_id=1, source_target_pairs={{0,1},{1,0},{2,3},{3,2},{4,5},{5,4},{6,7},{7,6},{8,9},{9,8},{10,11... | collective-permute-start | bytes 245768 | tf_op jit(solution)/shard_map/ppermute | solution.py:395
  53.7 5.3 %collective-permute-start.10 = (bf16[256,128]{1,0:T(8,128)(2,1)S(1)}, bf16[256,128]{1,0:T(8,128)(2,1)S(1)}, u32[]{:S(2)}, u32[]{:S(2)}) collective-permute-start(bf16[256,128]{1,0:T(8,128)(2,1)S(1)} %convert_element_type.3), channel_id=1, source_target_pairs={{0,3},{1,2},{2,1},{3,0},{4,7},{5,6},{6,5},{7,4},{8,11},{9,10},{10,... | collective-permute-start | bytes 196616 | tf_op jit(solution)/shard_map/ppermute | solution.py:395
  53.8 5.2 %collective-permute-start.9 = (bf16[256,128]{1,0:T(8,128)(2,1)S(1)}, bf16[256,128]{1,0:T(8,128)(2,1)S(1)}, u32[]{:S(2)}, u32[]{:S(2)}) collective-permute-start(bf16[256,128]{1,0:T(8,128)(2,1)S(1)} %convert_element_type.3), channel_id=1, source_target_pairs={{0,2},{1,3},{2,0},{3,1},{4,6},{5,7},{6,4},{7,5},{8,10},{9,11},{10,... | collective-permute-start | bytes 196616 | tf_op jit(solution)/shard_map/ppermute | solution.py:395
  54.9 4.4 %collective-permute-start.8 = (bf16[256,128]{1,0:T(8,128)(2,1)S(1)}, bf16[256,128]{1,0:T(8,128)(2,1)S(1)}, u32[]{:S(2)}, u32[]{:S(2)}) collective-permute-start(bf16[256,128]{1,0:T(8,128)(2,1)S(1)} %convert_element_type.3), channel_id=1, source_target_pairs={{0,1},{1,0},{2,3},{3,2},{4,5},{5,4},{6,7},{7,6},{8,9},{9,8},{10,11... | collective-permute-start | bytes 196616 | tf_op jit(solution)/shard_map/ppermute | solution.py:395
  59.3 9.9 %collective-permute-start.14 = (bf16[256,128]{1,0:T(8,128)(2,1)S(1)}, bf16[256,128]{1,0:T(8,128)(2,1)S(1)}, u32[]{:S(2)}, u32[]{:S(2)}) collective-permute-start(bf16[256,128]{1,0:T(8,128)(2,1)S(1)} %get-tuple-element.86), channel_id=1, source_target_pairs={{8,0},{24,16},{40,32},{56,48},{72,64},{88,80},{104,96},{120,112},{... | collective-permute-start | bytes 196616 | tf_op jit(solution)/shard_map/ppermute | solution.py:529
  60.6 8.6 %collective-permute-start.13 = (bf16[256,128]{1,0:T(8,128)(2,1)S(1)}, bf16[256,128]{1,0:T(8,128)(2,1)S(1)}, u32[]{:S(2)}, u32[]{:S(2)}) collective-permute-start(bf16[256,128]{1,0:T(8,128)(2,1)S(1)} %get-tuple-element.86), channel_id=1, source_target_pairs={{12,0},{28,16},{44,32},{60,48},{76,64},{92,80},{108,96},{124,112},... | collective-permute-start | bytes 196616 | tf_op jit(solution)/shard_map/ppermute | solution.py:529
  61.9 7.3 %collective-permute-start.12 = (bf16[256,128]{1,0:T(8,128)(2,1)S(1)}, bf16[256,128]{1,0:T(8,128)(2,1)S(1)}, u32[]{:S(2)}, u32[]{:S(2)}) collective-permute-start(bf16[256,128]{1,0:T(8,128)(2,1)S(1)} %get-tuple-element.86), channel_id=1, source_target_pairs={{4,0},{20,16},{36,32},{52,48},{68,64},{84,80},{100,96},{116,112},{... | collective-permute-start | bytes 196616 | tf_op jit(solution)/shard_map/ppermute | solution.py:529
  63.2 8.7 %collective-permute-start.11 = (bf16[2048,128]{1,0:T(8,128)(2,1)S(1)}, bf16[2048,128]{1,0:T(8,128)(2,1)S(1)}, u32[]{:S(2)}, u32[]{:S(2)}) collective-permute-start(bf16[2048,128]{1,0:T(8,128)(2,1)S(1)} %get-tuple-element.76), channel_id=1, source_target_pairs={{0,16},{16,0},{32,48},{48,32},{64,80},{80,64},{96,112},{112,96},{1... | collective-permute-start | bytes 1572872 | tf_op jit(solution)/shard_map/ppermute | solution.py:424
  64.6 25.6 %copy-start.6 = (bf16[4,256,256]{2,1,0:T(8,128)(2,1)S(1)}, bf16[4,256,256]{2,1,0:T(8,128)(2,1)}, u32[]{:S(2)}) copy-start(bf16[4,256,256]{2,1,0:T(8,128)(2,1)} %get-tuple-element.94.normed) | copy-start | bytes 1572868
  64.6 25.6 %copy-start.7 = (f32[8,256]{1,0:T(8,128)S(1)}, f32[8,256]{1,0:T(8,128)}, u32[]{:S(2)}) copy-start(f32[8,256]{1,0:T(8,128)} %get-tuple-element.95.live) | copy-start | bytes 24580
  64.6 32.9 %copy-start.5 = (f32[128]{0:T(128)S(1)}, f32[128]{0:T(128)}, u32[]{:S(2)}) copy-start(f32[128]{0:T(128)} %param.14) | copy-start | bytes 1540
  69.2 2.7 %collective-permute-start.15 = (bf16[512,128]{1,0:T(8,128)(2,1)S(1)}, bf16[512,128]{1,0:T(8,128)(2,1)S(1)}, u32[]{:S(2)}, u32[]{:S(2)}) collective-permute-start(bf16[512,128]{1,0:T(8,128)(2,1)S(1)} %get-tuple-element.87), channel_id=1, source_target_pairs={{0,16},{16,0},{32,48},{48,32},{64,80},{80,64},{96,112},{112,96},{1... | collective-permute-start | bytes 393224 | tf_op jit(solution)/shard_map/ppermute | solution.py:424
  87.6 2.6 %collective-permute-start.16 = (bf16[256,128]{1,0:T(8,128)(2,1)S(1)}, bf16[256,128]{1,0:T(8,128)(2,1)S(1)}, u32[]{:S(2)}, u32[]{:S(2)}) collective-permute-start(bf16[256,128]{1,0:T(8,128)(2,1)S(1)} %get-tuple-element.93), channel_id=1, source_target_pairs={{0,16},{16,0},{32,48},{48,32},{64,80},{80,64},{96,112},{112,96},{1... | collective-permute-start | bytes 196616 | tf_op jit(solution)/shard_map/ppermute | solution.py:424
  90.5 1.3 %collective-permute-start.17 = (bf16[64,128]{1,0:T(8,128)(2,1)S(1)}, bf16[64,128]{1,0:T(8,128)(2,1)S(1)}, u32[]{:S(2)}, u32[]{:S(2)}) collective-permute-start(bf16[64,128]{1,0:T(8,128)(2,1)S(1)} %get-tuple-element.98), channel_id=1, source_target_pairs={{0,16},{16,0},{32,48},{48,32},{64,80},{80,64},{96,112},{112,96},{1... | collective-permute-start | bytes 49160 | tf_op jit(solution)/shard_map/ppermute | solution.py:424
  91.8 10.2 %collective-permute-start.20 = (bf16[144,128]{1,0:T(8,128)(2,1)S(1)}, bf16[144,128]{1,0:T(8,128)(2,1)S(1)}, u32[]{:S(2)}, u32[]{:S(2)}) collective-permute-start(bf16[144,128]{1,0:T(8,128)(2,1)S(1)} %pack_column.1.part_0), channel_id=1, source_target_pairs={{0,8},{1,9},{2,10},{3,11},{4,12},{5,13},{6,14},{7,15},{8,0},{9,1},... | collective-permute-start | bytes 110600 | tf_op jit(solution)/shard_map/ppermute | solution.py:395
  95.6 6.4 %collective-permute-start.19 = (bf16[144,128]{1,0:T(8,128)(2,1)S(1)}, bf16[144,128]{1,0:T(8,128)(2,1)S(1)}, u32[]{:S(2)}, u32[]{:S(2)}) collective-permute-start(bf16[144,128]{1,0:T(8,128)(2,1)S(1)} %pack_column.1.part_0), channel_id=1, source_target_pairs={{0,12},{1,13},{2,14},{3,15},{4,8},{5,9},{6,10},{7,11},{8,4},{9,5},... | collective-permute-start | bytes 110600 | tf_op jit(solution)/shard_map/ppermute | solution.py:395
  97.1 4.9 %collective-permute-start.18 = (bf16[144,128]{1,0:T(8,128)(2,1)S(1)}, bf16[144,128]{1,0:T(8,128)(2,1)S(1)}, u32[]{:S(2)}, u32[]{:S(2)}) collective-permute-start(bf16[144,128]{1,0:T(8,128)(2,1)S(1)} %pack_column.1.part_0), channel_id=1, source_target_pairs={{0,4},{1,5},{2,6},{3,7},{4,0},{5,1},{6,2},{7,3},{8,12},{9,13},{10,... | collective-permute-start | bytes 110600 | tf_op jit(solution)/shard_map/ppermute | solution.py:395
  97.5 7.3 %copy-start.2 = (bf16[4,256,256]{2,1,0:T(8,128)(2,1)S(1)}, bf16[4,256,256]{2,1,0:T(8,128)(2,1)}, u32[]{:S(2)}) copy-start(bf16[4,256,256]{2,1,0:T(8,128)(2,1)} %msa.3) | copy-start | bytes 1572868
  97.5 7.3 %copy-start.4 = (bf16[256,64]{0,1:T(8,128)(2,1)S(1)}, bf16[256,64]{0,1:T(8,128)(2,1)}, u32[]{:S(2)}) copy-start(bf16[256,64]{0,1:T(8,128)(2,1)} %param.11) | copy-start | bytes 98308
  102.0 4.6 %collective-permute-start.23 = (bf16[144,128]{1,0:T(8,128)(2,1)S(1)}, bf16[144,128]{1,0:T(8,128)(2,1)S(1)}, u32[]{:S(2)}, u32[]{:S(2)}) collective-permute-start(bf16[144,128]{1,0:T(8,128)(2,1)S(1)} %column_sum.1.part_0), channel_id=1, source_target_pairs={{0,3},{1,2},{2,1},{3,0},{4,7},{5,6},{6,5},{7,4},{8,11},{9,10},{10,... | collective-permute-start | bytes 110600 | tf_op jit(solution)/shard_map/ppermute | solution.py:395
  102.1 4.5 %collective-permute-start.22 = (bf16[144,128]{1,0:T(8,128)(2,1)S(1)}, bf16[144,128]{1,0:T(8,128)(2,1)S(1)}, u32[]{:S(2)}, u32[]{:S(2)}) collective-permute-start(bf16[144,128]{1,0:T(8,128)(2,1)S(1)} %column_sum.1.part_0), channel_id=1, source_target_pairs={{0,2},{1,3},{2,0},{3,1},{4,6},{5,7},{6,4},{7,5},{8,10},{9,11},{10,... | collective-permute-start | bytes 110600 | tf_op jit(solution)/shard_map/ppermute | solution.py:395
  102.2 4.4 %collective-permute-start.21 = (bf16[144,128]{1,0:T(8,128)(2,1)S(1)}, bf16[144,128]{1,0:T(8,128)(2,1)S(1)}, u32[]{:S(2)}, u32[]{:S(2)}) collective-permute-start(bf16[144,128]{1,0:T(8,128)(2,1)S(1)} %column_sum.1.part_0), channel_id=1, source_target_pairs={{0,1},{1,0},{2,3},{3,2},{4,5},{5,4},{6,7},{7,6},{8,9},{9,8},{10,11... | collective-permute-start | bytes 110600 | tf_op jit(solution)/shard_map/ppermute | solution.py:395
  117.0 4.6 %collective-permute-start.24 = (bf16[8,144,128]{2,1,0:T(8,128)(2,1)S(1)}, bf16[8,144,128]{2,1,0:T(8,128)(2,1)S(1)}, u32[]{:S(2)}, u32[]{:S(2)}) collective-permute-start(bf16[8,144,128]{2,1,0:T(8,128)(2,1)S(1)} %all_to_all.17.mine), channel_id=1, source_target_pairs={{0,16},{16,0},{32,48},{48,32},{64,80},{80,64},{96,112},{112,96},{1... | collective-permute-start | bytes 884744 | tf_op jit(solution)/shard_map/ppermute | solution.py:424
  (1 other events, 0.9 us)
